TPU v7x, 256 devices: a whole 4x4x8 slice. The times are simulated.
256 devices in a mesh: dp: 4 (over y), ctx: 64 (over x, z, core).
Axes of the slice: x: 4, y: 4, z: 8, core: 2. Of those that a mesh axis runs over, the one named last changes fastest.
Arguments:
- queries: bfloat16 [2, 16384, 1024], P(None, ('dp', 'ctx')), parts along dimension 1, may hold values from -6 to 6
- keys: bfloat16 [1, 16384, 1024], P(None, ('dp', 'ctx')), parts along dimension 1, may hold values from -48 to 48
- values: bfloat16 [1, 16384, 1024], P(None, ('dp', 'ctx')), parts along dimension 1, may hold values from -48 to 48
- rates: float32 [1, 2, 16384], P(None, None, ('dp', 'ctx')), parts along dimension 2, may hold values from 0.05 to 1
- fast_weights: bfloat16 [3, 2, 512, 1024], replicated, may hold values from -0.25 to 0.25
Outputs:
- outputs: bfloat16 [2, 16384, 1024], P(None, ('dp', 'ctx')), parts along dimension 1
There are 4 independent parts, one for each index of `dp`. A program takes and returns all parts, laid end to end along the dimension named above; an argument that names none is the same for every part. Nothing has to cross between parts.
All inputs are finite; a program needn't handle non-finite values.
Results may differ from a plain program's by a relative error of at most 0.007.
The roundings to bfloat16 on the way count: a program that leaves them out, or rounds other values in their place, can miss the bound.
Values may be sent and summed in bfloat16 or wider, within the bound.
No kernel may reach another device: no remote copies, remote signals or barrier semaphores. Data moves between devices by JAX's collectives and lax.ppermute only.
A program may use at most 128 MiB of HBM per device.

v0:
```python
import jax
import jax.numpy as jnp
from jax import lax
from jax.sharding import PartitionSpec as P

upd_scale = 2.0
norm_eps = 1e-07


def apply_block(weights, query_block):
    row_count = query_block.shape[0]
    head_count = weights.shape[1]
    head_size = weights.shape[2]
    split_q = query_block.reshape(row_count, head_count, head_size)
    first_proj = jnp.einsum("thd,hdf->thf", split_q, weights[0], preferred_element_type=jnp.float32)
    third_proj = jnp.einsum("thd,hdf->thf", split_q, weights[1], preferred_element_type=jnp.float32)
    gated_hidden = (jax.nn.silu(first_proj) * third_proj).astype(jnp.bfloat16)
    result = jnp.einsum(
        "thf,hdf->thd", gated_hidden, weights[2], preferred_element_type=jnp.float32
    )
    return result.reshape(row_count, head_count * head_size).astype(jnp.bfloat16)


def block_gradient(weights, key_block, value_block, rate_block):
    row_count = key_block.shape[0]
    head_count = weights.shape[1]
    head_size = weights.shape[2]
    split_k = key_block.reshape(row_count, head_count, head_size)
    split_v = value_block.reshape(row_count, head_count, head_size)
    scaled_values = (split_v.astype(jnp.float32) * jnp.transpose(rate_block)[:, :, None]).astype(
        jnp.bfloat16
    )
    key_first = jnp.einsum("thd,hdf->thf", split_k, weights[0], preferred_element_type=jnp.float32)
    key_third = jnp.einsum("thd,hdf->thf", split_k, weights[1], preferred_element_type=jnp.float32)
    sigmoid_first = jax.nn.sigmoid(key_first)
    key_act = key_first * sigmoid_first
    key_gated = (key_act * key_third).astype(jnp.bfloat16)
    back_grad = -jnp.einsum(
        "thd,hdf->thf", scaled_values, weights[2], preferred_element_type=jnp.float32
    )
    d_first = (
        back_grad * key_third * sigmoid_first * (1.0 + key_first * (1.0 - sigmoid_first))
    ).astype(jnp.bfloat16)
    d_third = (back_grad * key_act).astype(jnp.bfloat16)
    grad_first = jnp.einsum("thd,thf->hdf", split_k, d_first, preferred_element_type=jnp.float32)
    grad_third = jnp.einsum("thd,thf->hdf", split_k, d_third, preferred_element_type=jnp.float32)
    grad_down = -jnp.einsum(
        "thd,thf->hdf", scaled_values, key_gated, preferred_element_type=jnp.float32
    )
    return jnp.stack([grad_first, grad_third, grad_down])


def renew(weights, key_block, value_block, rate_block):
    partial_value = block_gradient(weights, key_block, value_block, rate_block)
    grad_rows = lax.psum_scatter(partial_value, "ctx", scatter_dimension=2, tiled=True)
    scaled_part = grad_rows.astype(jnp.bfloat16)
    rows_each = grad_rows.shape[2]
    head_size = weights.shape[2]
    offset = lax.axis_index("ctx") * rows_each
    scaled = lax.all_gather(scaled_part, "ctx", axis=2, tiled=True)
    gram_full = jnp.einsum(
        "mhdf,mhef->mhde", scaled, scaled, preferred_element_type=jnp.float32
    ).astype(jnp.bfloat16)
    gram_float = gram_full.astype(jnp.float32)
    gram_level = jnp.sqrt(jnp.sum(gram_float * gram_float, axis=(2, 3), keepdims=True)) + norm_eps
    identity = jnp.eye(head_size, dtype=jnp.float32)
    first_poly = (1.5 * identity - 0.5 * gram_float / gram_level).astype(jnp.bfloat16)
    first_part = lax.dynamic_slice_in_dim(first_poly, offset, rows_each, 2)
    squared_part = jnp.einsum(
        "mhde,mhek->mhdk", first_part, first_poly, preferred_element_type=jnp.float32
    ).astype(jnp.bfloat16)
    moved_part = jnp.einsum(
        "mhde,mhek->mhdk", squared_part, gram_full, preferred_element_type=jnp.float32
    )
    identity_part = lax.dynamic_slice_in_dim(identity, offset, rows_each, 0)
    second_part = (1.5 * identity_part - 0.5 * moved_part / gram_level).astype(jnp.bfloat16)
    combined_part = jnp.einsum(
        "mhde,mhek->mhdk", second_part, first_poly, preferred_element_type=jnp.float32
    ).astype(jnp.bfloat16)
    update_part = jnp.einsum(
        "mhde,mhef->mhdf", combined_part, scaled, preferred_element_type=jnp.float32
    ) / jnp.sqrt(gram_level)
    weight_part = lax.dynamic_slice_in_dim(weights, offset, rows_each, 2)
    renewed_part = (weight_part.astype(jnp.float32) - upd_scale * update_part).astype(jnp.bfloat16)
    return lax.all_gather(renewed_part, "ctx", axis=2, tiled=True)


def body(queries, keys, values, rates, fast_weights):
    weights = fast_weights
    results = []
    block_count = queries.shape[0]
    for block_index in range(block_count):
        results.append(apply_block(weights, queries[block_index]))
        if block_index + 1 < block_count:
            weights = renew(weights, keys[block_index], values[block_index], rates[block_index])
    return jnp.stack(results)


def solution(mesh):
    in_specs = (
        P(None, ("dp", "ctx"), None),
        P(None, ("dp", "ctx"), None),
        P(None, ("dp", "ctx"), None),
        P(None, None, ("dp", "ctx")),
        P(),
    )
    out_specs = P(None, ("dp", "ctx"), None)
    return jax.shard_map(body, mesh=mesh, in_specs=in_specs, out_specs=out_specs, check_vma=False)
```

profile of v0, /device:TPU:1, one launch (start us, length us, event | category | flops | bytes accessed | tf_op | source)
XLA Modules:
  0.0 536.0 jit_solution(424761085800470408)
XLA Ops:
  6.5 0.0 all-gather.3.cloned.1.call-start
  6.5 1.0 reshape_squeeze.11
  7.5 2.1 fusion.32
  9.6 2.1 fusion.38
  11.7 1.2 reshape.46
  12.9 2.1 fusion.50
  15.0 0.0 copy-start.3
  15.0 0.8 convolution_bitcast_fusion
  15.8 0.8 convolution_bitcast_fusion.1
  16.6 0.0 copy-done.3
  16.6 0.8 negate_bitcast_fusion
  17.4 5.6 %pad_maximum_fusion = f32[3,2,512,1024]{2,3,1,0:T(8,128)} fusion(f32[1,2,512,1024]{2,3,1,0:T(8,128)S(1)} %negate_bitcast_fusion, f32[1,2,512,1024]{2,3,1,0:T(8,128)S(1)} %convolution_bitcast_fusion, f32[1,2,512,1024]{2,3,1,0:T(8,128)S(1)} %convolution_bitcast_fusion.1), kind=kLoop, calls=%fused_computation | loop fusion | flops 6291456 | bytes 25165824 | tf_op jit(solution)/shard_map/stack | solution.py:50
  22.9 19.5 %copy.37 = f32[3,2,512,1024]{3,1,0,2:T(2,128)} copy(f32[3,2,512,1024]{2,3,1,0:T(8,128)} %pad_maximum_fusion) | data formatting | bytes 25165824 | tf_op jit(solution)/shard_map/stack | solution.py:50
  42.4 0.0 copy-start.4
  42.4 299.0 %all-reduce.2 = bf16[3,2,512,1024]{3,1,0,2:T(2,128)(2,1)} all-reduce(f32[3,2,512,1024]{3,1,0,2:T(2,128)} %copy.37), channel_id=2, replica_groups=mesh['dp'=4,'ctx'=64] {'ctx'}, use_global_device_ids=true, to_apply=%region_0.1.clone | all-reduce | flops 3145728 | bytes 18874368
  341.4 0.0 copy-done.4
  341.4 0.6 dynamic-slice
  342.6 1.6 dynamic-slice_convert_fusion
  344.2 0.0 all-gather.3.cloned.1.call-update
  344.2 0.2 all-gather.5.cloned.1.call-start
  344.5 0.1 iota_compare_fusion
  344.6 1.1 broadcast_select_fusion
  345.7 79.2 %all-gather.3.cloned.1.call-done = bf16[3,2,512,1024]{3,1,0,2:T(2,128)(2,1)} async-done(((bf16[3,2,8,1024]{3,1,0,2:T(2,128)(2,1)}), bf16[3,2,512,1024]{3,1,0,2:T(2,128)(2,1)}) %all-gather.3.cloned.1.call-update) | async-done | bytes 6291472 | tf_op jit(solution)/shard_map/all_gather | solution.py:60
  424.9 0.0 copy-start.1
  424.9 8.8 %fusion.3 = (f32[3,2]{1,0:T(4,128)S(1)}, bf16[3,2,512,512]{3,2,1,0:T(8,128)(2,1)S(1)}) fusion(bf16[3,2,512,1024]{3,1,0,2:T(2,128)(2,1)} %all-gather.3.cloned.1.call-done), kind=kOutput, calls=%fused_computation.6 | convolution fusion | flops 3227516928 | bytes 9437208 | tf_op jit(solution)/shard_map/mhdf,mhef->mhde/dot_general | solution.py:61
  433.7 0.0 copy-start
  433.7 1.7 copy-done
  435.4 0.0 copy-done.1
  435.4 1.1 fusion.2
  436.5 2.8 fusion.76
  439.3 0.0 copy-start.2
  439.3 5.6 %fusion.86 = bf16[3,2,8,1024]{3,2,1,0:T(8,128)(2,1)} fusion(bf16[3,2,512,1024]{3,1,0,2:T(2,128)(2,1)} %all-gather.3.cloned.1.call-done, bf16[3,2,8,512]{3,2,1,0:T(8,128)(2,1)S(1)} %fusion.76, bf16[3,2,512,512]{3,2,1,0:T(8,128)(2,1)S(1)} %fusion.2, f32[3,2]{1,0:T(4,128)S(1)} %get-tuple-element.7, bf16[3,2,512,1024]{3,2,1,0:T(8,128)(2,1)} %param.9, ...), kind=kOutput, calls=%fused_computation.64 | convolution fusion | flops 75767808 | bytes 9682972 | tf_op jit(solution)/shard_map/mhde,mhef->mhdf/dot_general | solution.py:80
  445.0 0.0 all-gather.5.cloned.1.call-update
  445.0 0.0 copy-done.2
  445.0 0.1 reshape_squeeze.12
  445.1 0.1 reshape_squeeze.10
  445.2 2.1 fusion.35
  447.3 3.4 fusion.69
  450.6 0.1 copy.30
  450.8 0.1 convert_element_type.89
  450.8 72.0 %all-gather.5.cloned.1.call-done = bf16[3,2,512,1024]{3,2,1,0:T(8,128)(2,1)} async-done(((bf16[3,2,8,1024]{3,2,1,0:T(8,128)(2,1)}), bf16[3,2,512,1024]{3,2,1,0:T(8,128)(2,1)}) %all-gather.5.cloned.1.call-update) | async-done | bytes 6291472 | tf_op jit(solution)/shard_map/all_gather | solution.py:85
  522.8 2.1 fusion.53
  524.9 3.3 fusion.68
  528.2 0.1 copy.43
  528.4 0.1 convert_element_type.109
  528.4 0.7 pad_maximum_fusion.1
  (3 shorter events, 0.0 us)
Async XLA Ops:
  6.5 418.4 %all-gather.3.cloned.1.call-start = ((), (), s32[]{:S(2)}) async-start(), calls=%async_computation | async-start | bytes 6389760 | tf_op jit(solution)/shard_map/all_gather | solution.py:60
  15.0 1.6 copy-start.3
  42.4 299.0 %copy-start.4 = (u32[256]{0:T(256)S(1)}, u32[256]{0:T(256)}, u32[]{:S(2)}) copy-start(u32[256]{0:T(256)} %constant.34) | copy-start | bytes 3076
  344.2 178.6 %all-gather.5.cloned.1.call-start = ((), (), s32[]{:S(2)}) async-start(), calls=%async_computation.1 | async-start | bytes 6389760 | tf_op jit(solution)/shard_map/all_gather | solution.py:85
  424.9 10.5 %copy-start.1 = (f32[512,512]{1,0:T(8,128)S(1)}, f32[512,512]{1,0:T(8,128)}, u32[]{:S(2)}) copy-start(f32[512,512]{1,0:T(8,128)} %broadcast_select_fusion) | copy-start | bytes 3145732
  433.7 1.7 copy-start
  439.3 5.7 %copy-start.2 = (bf16[2,64,1024]{2,1,0:T(8,128)(2,1)S(1)}, bf16[2,64,1024]{2,1,0:T(8,128)(2,1)}, u32[]{:S(2)}) copy-start(bf16[2,64,1024]{2,1,0:T(8,128)(2,1)} %param.5) | copy-start | bytes 786436
Sparse Core Ops, SparseCore 0:
  344.4 80.4 all-gather.2
  445.1 77.6 all-gather.4
where the time goes:
time: 537 us; the launch traced here: 536 us
  blocking collectives  299 us (56%)
  waiting for transfers between devices  151 us (28%)
  matrix products  36.7 us (7%)
  local copies, waits for them, and re-layouts  26.1 us (5%)
  between operations  14.2 us (3%)
  other arithmetic  8.53 us (2%)
    unnamed x1, blocking collectives  299 us
    all_gather x1, waiting for transfers between devices, renew(): scaled = lax.all_gather(scaled_part, 'ctx', axis=2, tiled=True)  79.2 us
    all_gather x1, waiting for transfers between devices, renew(): return lax.all_gather(renewed_part, 'ctx', axis=2, tiled=True)  72 us
    another operation x1, local copies, waits for them, and re-layouts, block_gradient(): return jnp.stack([grad_first, grad_third, grad_down])  19.5 us
  transfers between devices with their start and end apart: 2, of which 2 were waited for; matrix products, arithmetic and copies ran while one was open for 1% of the time, Pallas kernels for 0%

commit v1 on v0

v1 whole, which is shorter than its diff:
```python
import functools

import jax
import jax.numpy as jnp
from jax import lax
from jax.experimental import pallas as pl
from jax.experimental.pallas import tpu as pltpu
from jax.sharding import PartitionSpec as P

X, Z, C = 4, 8, 2
DIM, FF, COLS = 512, 1024, 256
ROWS = DIM // Z
BF, F32 = jnp.bfloat16, jnp.float32
VMEM_LIMIT = 48 * 1024 * 1024
upd_scale = 2.0
norm_eps = 1e-07
VMEM = pl.BlockSpec(memory_space=pltpu.VMEM)
ANY = pl.BlockSpec(memory_space=pl.ANY)


def place():
    index = lax.axis_index("ctx")
    return index // (Z * C), (index // C) % Z, index % C


def move(array, to):
    perm = []
    for x in range(X):
        for z in range(Z):
            for c in range(C):
                tx, tz, tc = to(x, z, c)
                perm.append(((x * Z + z) * C + c, (tx % X * Z + tz % Z) * C + tc % C))
    return lax.ppermute(array, "ctx", perm)


def dot(left, right, dims):
    return lax.dot_general(left, right, (dims, ((), ())), preferred_element_type=F32)


def prepare_kernel(keys, values, rates, query, own, far1, far2, far3, query_own, query_far):
    x, _, _ = place()
    tokens = keys.shape[0]
    diagonal = lax.broadcasted_iota(jnp.int32, (tokens, tokens), 0) == lax.broadcasted_iota(
        jnp.int32, (tokens, tokens), 1
    )

    def fill(head):
        row = rates[head : head + 1, :]
        rate = jnp.sum(jnp.where(diagonal, row, 0.0), axis=1, keepdims=True)
        cols = slice(head * DIM, (head + 1) * DIM)
        scaled = (values[:, cols].astype(F32) * rate).astype(BF)
        for distance, ref in enumerate((own, far1, far2, far3)):

            @pl.when(lax.rem(x + distance, X) // 2 == head)
            def _():
                ref[:tokens, :] = keys[:, cols]
                ref[tokens:, :] = scaled

        @pl.when(x // 2 == head)
        def _():
            query_own[...] = query[:, cols]

        @pl.when(x // 2 != head)
        def _():
            query_far[...] = query[:, cols]

    fill(0)
    fill(1)


def prepare(keys, values, rates, query):
    tokens = keys.shape[0]
    pair = jax.ShapeDtypeStruct((2 * tokens, DIM), BF)
    half = jax.ShapeDtypeStruct((tokens, DIM), BF)
    return pl.pallas_call(
        prepare_kernel,
        out_shape=(pair, pair, pair, pair, half, half),
        in_specs=[VMEM] * 4,
        out_specs=(VMEM,) * 6,
        name="prepare",
    )(keys, values, rates, query)


def gradient_kernel(*refs):
    pieces, weights = refs[:8], refs[8]
    outs = refs[9:17]
    w, k, v, total, sem = refs[17:]
    x, z, c = place()
    column = pl.multiple_of((lax.rem(x, 2) * 2 + c) * COLS, COLS)
    copies = []
    for m in range(3):
        copy = pltpu.make_async_copy(
            weights.at[m, x // 2, :, pl.ds(column, COLS)], w.at[m], sem.at[m]
        )
        copy.start()
        copies.append(copy)
    tokens = pieces[0].shape[0] // 2
    for i, piece in enumerate(pieces):
        k[i * tokens : (i + 1) * tokens, :] = piece[:tokens, :]
        v[i * tokens : (i + 1) * tokens, :] = piece[tokens:, :]
    for copy in copies:
        copy.wait()
    key_first = dot(k[...], w[0], ((1,), (0,)))
    key_third = dot(k[...], w[1], ((1,), (0,)))
    back_grad = -dot(v[...], w[2], ((1,), (0,)))
    sig = jax.nn.sigmoid(key_first)
    key_act = key_first * sig
    key_gated = (key_act * key_third).astype(BF)
    d_first = (back_grad * key_third * sig * (1.0 + key_first * (1.0 - sig))).astype(BF)
    d_third = (back_grad * key_act).astype(BF)
    total[0] = dot(k[...], d_first, ((0,), (0,)))
    total[1] = dot(k[...], d_third, ((0,), (0,)))
    total[2] = -dot(v[...], key_gated, ((0,), (0,)))
    for distance in range(Z):
        row = pl.multiple_of(lax.rem(z + distance, Z) * ROWS, ROWS)
        for m in range(3):
            outs[distance][m] = total[m, pl.ds(row, ROWS), :].astype(outs[distance].dtype)


def gradient(pieces, weights):
    tokens = 8 * pieces[0].shape[0] // 2
    out_shape = [jax.ShapeDtypeStruct((3, ROWS, COLS), F32 if d == 0 else BF) for d in range(Z)]
    return pl.pallas_call(
        gradient_kernel,
        out_shape=out_shape,
        in_specs=[VMEM] * 8 + [ANY],
        out_specs=[VMEM] * Z,
        scratch_shapes=[
            pltpu.VMEM((3, DIM, COLS), BF),
            pltpu.VMEM((tokens, DIM), BF),
            pltpu.VMEM((tokens, DIM), BF),
            pltpu.VMEM((3, DIM, COLS), F32),
            pltpu.SemaphoreType.DMA((3,)),
        ],
        compiler_params=pltpu.CompilerParams(vmem_limit_bytes=VMEM_LIMIT),
        cost_estimate=pl.CostEstimate(
            flops=12 * tokens * DIM * COLS, bytes_accessed=4 << 20, transcendentals=tokens * COLS
        ),
        name="gradient",
    )(*pieces, weights)


def renew_kernel(*refs):
    pieces, weights, query_own, query_far = refs[:32], refs[32], refs[33], refs[34]
    out_own, out_far = refs[35], refs[36]
    scaled, w, sem, wsem = refs[37:]
    x, z, c = place()
    copies = []
    for i in range(4):
        part = lax.rem(x + i // 2, 2) * 2 + lax.rem(c + i % 2, 2)
        for distance in range(Z):
            row = pl.multiple_of(lax.rem(z - distance + Z, Z) * ROWS, ROWS)
            copy = pltpu.make_async_copy(
                pieces[i * Z + distance],
                scaled.at[part, :, pl.ds(row, ROWS), :],
                sem.at[i * Z + distance],
            )
            copy.start()
            copies.append(copy)
    load = pltpu.make_async_copy(weights.at[:, x // 2], w, wsem)
    load.start()
    for copy in copies:
        copy.wait()
    load.wait()
    identity = (
        lax.broadcasted_iota(jnp.int32, (DIM, DIM), 0)
        == lax.broadcasted_iota(jnp.int32, (DIM, DIM), 1)
    ).astype(F32)

    @pl.loop(0, 3)
    def _(m):
        gram = dot(scaled[0, m], scaled[0, m], ((1,), (1,)))
        for part in range(1, 4):
            gram += dot(scaled[part, m], scaled[part, m], ((1,), (1,)))
        gram = gram.astype(BF)
        gram_float = gram.astype(F32)
        level = jnp.sqrt(jnp.sum(gram_float * gram_float, keepdims=True)) + norm_eps
        half = 0.5 / level
        first_poly = (1.5 * identity - gram_float * half).astype(BF)
        squared = dot(first_poly, first_poly, ((1,), (0,))).astype(BF)
        moved = dot(squared, gram, ((1,), (0,)))
        second_poly = (1.5 * identity - moved * half).astype(BF)
        combined = dot(second_poly, first_poly, ((1,), (0,))).astype(BF)
        factor = upd_scale / jnp.sqrt(level)
        for part in range(4):
            cols = slice(part * COLS, (part + 1) * COLS)
            update = dot(combined, scaled[part, m], ((1,), (0,))) * factor
            w[m, :, cols] = (w[m, :, cols].astype(F32) - update).astype(BF)

    query = jnp.concatenate([query_own[...], query_far[...]], axis=0)
    first_proj = dot(query, w[0], ((1,), (0,)))
    third_proj = dot(query, w[1], ((1,), (0,)))
    gated = (first_proj * jax.nn.sigmoid(first_proj) * third_proj).astype(BF)
    result = dot(gated, w[2], ((1,), (1,))).astype(BF)
    tokens = query_own.shape[0]
    out_own[...] = result[:tokens]
    out_far[...] = result[tokens:]


def renew_apply(pieces, weights, query_own, query_far):
    half = jax.ShapeDtypeStruct(query_own.shape, BF)
    return pl.pallas_call(
        renew_kernel,
        out_shape=(half, half),
        in_specs=[ANY] * 33 + [VMEM] * 2,
        out_specs=(VMEM, VMEM),
        scratch_shapes=[
            pltpu.VMEM((4, 3, DIM, COLS), BF),
            pltpu.VMEM((3, DIM, FF), BF),
            pltpu.SemaphoreType.DMA((32,)),
            pltpu.SemaphoreType.DMA,
        ],
        compiler_params=pltpu.CompilerParams(vmem_limit_bytes=VMEM_LIMIT),
        cost_estimate=pl.CostEstimate(
            flops=6 * 10**9, bytes_accessed=7 << 20, transcendentals=1 << 17
        ),
        name="renew_apply",
    )(*pieces, weights, query_own, query_far)


def apply_block(weights, query):
    tokens = query.shape[0]
    split_q = query.reshape(tokens, 2, DIM)
    first_proj = jnp.einsum("thd,hdf->thf", split_q, weights[0], preferred_element_type=F32)
    third_proj = jnp.einsum("thd,hdf->thf", split_q, weights[1], preferred_element_type=F32)
    gated_hidden = (jax.nn.silu(first_proj) * third_proj).astype(BF)
    result = jnp.einsum("thf,hdf->thd", gated_hidden, weights[2], preferred_element_type=F32)
    return result.reshape(tokens, 2 * DIM).astype(BF)


def body(queries, keys, values, rates, weights):
    own, far1, far2, far3, query_own, query_far = prepare(keys[0], values[0], rates[0], queries[1])
    got = [own]
    for distance, payload in ((1, far1), (2, far2), (3, far3)):
        got.append(move(payload, lambda x, z, c: (x + distance, z, c)))
    got += [move(piece, lambda x, z, c: (x, z, c + 1)) for piece in got]
    query_got = move(query_far, lambda x, z, c: (X - 1 - x, z, c))
    chunks = gradient(got, weights)
    query_zero, chunks = lax.optimization_barrier((queries[0], chunks))
    total = chunks[0]
    for distance in (4, 3, 5, 2, 6, 1, 7):
        total = total + move(chunks[distance], lambda x, z, c: (x, z + distance, c)).astype(F32)
    scaled = total.astype(BF)
    first_out = apply_block(weights, query_zero)
    mine = [scaled] + [move(scaled, lambda x, z, c: (x, z + d, c)) for d in range(1, Z)]
    near = [move(piece, lambda x, z, c: (x, z, c + 1)) for piece in mine]
    across = [move(piece, lambda x, z, c: (x ^ 1, z, c)) for piece in mine]
    last = [move(piece, lambda x, z, c: (x, z, c + 1)) for piece in across]
    out_own, out_far = renew_apply(mine + near + across + last, weights, query_own, query_got)
    out_got = move(out_far, lambda x, z, c: (X - 1 - x, z, c))
    x, _, _ = place()
    second_out = jnp.where(
        x // 2 == 0,
        jnp.concatenate([out_own, out_got], axis=1),
        jnp.concatenate([out_got, out_own], axis=1),
    )
    return jnp.stack([first_out, second_out])


def solution(mesh):
    in_specs = (
        P(None, ("dp", "ctx"), None),
        P(None, ("dp", "ctx"), None),
        P(None, ("dp", "ctx"), None),
        P(None, None, ("dp", "ctx")),
        P(),
    )
    out_specs = P(None, ("dp", "ctx"), None)
    return jax.shard_map(body, mesh=mesh, in_specs=in_specs, out_specs=out_specs, check_vma=False)
```

time: 537 us -> 112 us (0.21)
  blocking collectives: 299 us -> 0 us
  waiting for transfers between devices: 151 us -> 17.8 us
  starting transfers between devices: 0.22 us -> 67 us
  matrix products: 36.7 us -> 5.45 us
  local copies, waits for them, and re-layouts: 26.1 us -> 2.76 us
  Pallas kernels: 0 us -> 17.3 us
  between operations: 14.2 us -> 0.17 us
  other arithmetic: 8.53 us -> 0.86 us
    unnamed x1 -> x0, blocking collectives: 299 us -> none
    all_gather x2 -> x0, waiting for transfers between devices: 151 us -> none  [the longest x1 79.2 us: renew(): scaled = lax.all_gather(scaled_part, 'ctx', axis=2, tiled=True)]
    ppermute x0 -> x47, starting transfers between devices: none -> 67 us  [move(): return lax.ppermute(array, 'ctx', perm)]
    dot_general x11 -> x1, matrix products: 30 us -> 2.07 us  [apply_block(): jnp.einsum('thd,hdf->thf', split_q, weights[0], preferred_element_type=F32)]
    another operation x4 -> x0, local copies, waits for them, and re-layouts: 20.6 us -> none  [the longest x1 19.5 us: block_gradient(): return jnp.stack([grad_first, grad_third, grad_down])]
    ppermute x0 -> x47, waiting for transfers between devices: none -> 17.8 us  [move(): return lax.ppermute(array, 'ctx', perm)]
    pallas_call x0 -> x3, Pallas kernels: none -> 17.3 us  [the longest x1 12.4 us: renew_apply(): pl.pallas_call(renew_kernel, out_shape=(half, half), in_specs=[ANY] * 33...]
    another operation x2 -> x1, other arithmetic: 6.29 us -> 0.73 us  [body(): return jnp.stack([first_out, second_out])]
  transfers between devices with their start and end apart: 2 -> 47, of which waited for: 2 -> 8; matrix products, arithmetic and copies ran while one was open for 1% -> 5% of each run, Pallas kernels for 0% -> 0%
where the time goes in v1:
time: 112 us; the launch traced here: 111 us
  starting transfers between devices  67 us (60%)
  waiting for transfers between devices  17.8 us (16%)
  Pallas kernels  17.3 us (15%)
  matrix products  5.45 us (5%)
  local copies, waits for them, and re-layouts  2.76 us (2%)
    ppermute x47, starting transfers between devices, move(): return lax.ppermute(array, 'ctx', perm)  67 us
    ppermute x47, waiting for transfers between devices, move(): return lax.ppermute(array, 'ctx', perm)  17.8 us
    pallas_call x1, Pallas kernels, renew_apply(): pl.pallas_call(renew_kernel, out_shape=(half, half), in_specs=[ANY] * 33...  12.4 us
    dot_general x1, matrix products, apply_block(): jnp.einsum('thf,hdf->thd', gated_hidden, weights[2], preferred_element_ty...  3.39 us
    pallas_call x1, Pallas kernels, gradient(): pl.pallas_call(gradient_kernel, out_shape=out_shape, in_specs=[VMEM] * 8...  2.68 us
  transfers between devices with their start and end apart: 47, of which 8 were waited for; matrix products, arithmetic and copies ran while one was open for 5% of the time, Pallas kernels for 0%

profile of v1, /device:TPU:1, one launch (start us, length us, event | category | flops | bytes accessed | tf_op | source)
XLA Modules:
  0.0 111.4 jit_solution(8155947943476070793)
XLA Ops:
  0.0 1.6 %slice_bitcast_fusion = (bf16[64,1024]{1,0:T(8,128)(2,1)}, bf16[64,1024]{1,0:T(8,128)(2,1)S(1)}) fusion(bf16[2,64,1024]{2,1,0:T(8,128)(2,1)} %param.5), kind=kLoop, calls=%fused_computation.26 | loop fusion | bytes 524288 | tf_op jit(solution)/shard_map/squeeze | solution.py:232
  1.6 2.2 %prepare.1 = (bf16[128,512]{1,0:T(8,128)(2,1)}, bf16[128,512]{1,0:T(8,128)(2,1)}, bf16[128,512]{1,0:T(8,128)(2,1)}, bf16[128,512]{1,0:T(8,128)(2,1)}, bf16[64,512]{1,0:T(8,128)(2,1)}, /*index=5*/bf16[64,512]{1,0:T(8,128)(2,1)}) custom-call(bf16[64,1024]{1,0:T(8,128)(2,1)} %bitcast.62, bf16[64,1024]{1,0:T(8,128)(2,1)} %bitcast.63, f32[2,64]{1,0:T(2,128)} %bitcast.65, ...), custom_call_target="tpu_custom_call" | custom-call | tf_op jit(solution)/shard_map/prepare/pallas_call | solution.py:75
  3.8 2.0 %collective-permute-start = (bf16[128,512]{1,0:T(8,128)(2,1)}, bf16[128,512]{1,0:T(8,128)(2,1)S(1)}, u32[]{:S(2)}, u32[]{:S(2)}) collective-permute-start(bf16[128,512]{1,0:T(8,128)(2,1)} %get-tuple-element.31), channel_id=1, source_target_pairs={{0,16},{1,17},{2,18},{3,19},{4,20},{5,21},{6,22},{7,23},{8,24},{9,... | collective-permute-start | bytes 393224 | tf_op jit(solution)/shard_map/ppermute | solution.py:33
  5.9 2.4 %collective-permute-start.1 = (bf16[128,512]{1,0:T(8,128)(2,1)}, bf16[128,512]{1,0:T(8,128)(2,1)S(1)}, u32[]{:S(2)}, u32[]{:S(2)}) collective-permute-start(bf16[128,512]{1,0:T(8,128)(2,1)} %get-tuple-element.32), channel_id=1, source_target_pairs={{0,32},{1,33},{2,34},{3,35},{4,36},{5,37},{6,38},{7,39},{8,40},{9,... | collective-permute-start | bytes 393224 | tf_op jit(solution)/shard_map/ppermute | solution.py:33
  8.3 1.1 %collective-permute-start.2 = (bf16[128,512]{1,0:T(8,128)(2,1)}, bf16[128,512]{1,0:T(8,128)(2,1)S(1)}, u32[]{:S(2)}, u32[]{:S(2)}) collective-permute-start(bf16[128,512]{1,0:T(8,128)(2,1)} %get-tuple-element.33), channel_id=1, source_target_pairs={{0,48},{1,49},{2,50},{3,51},{4,52},{5,53},{6,54},{7,55},{8,56},{9,... | collective-permute-start | bytes 393224 | tf_op jit(solution)/shard_map/ppermute | solution.py:33
  9.5 1.5 %collective-permute-start.3 = (bf16[128,512]{1,0:T(8,128)(2,1)}, bf16[128,512]{1,0:T(8,128)(2,1)S(1)}, u32[]{:S(2)}, u32[]{:S(2)}) collective-permute-start(bf16[128,512]{1,0:T(8,128)(2,1)} %get-tuple-element.30.refs_0_), channel_id=1, source_target_pairs={{0,1},{1,0},{2,3},{3,2},{4,5},{5,4},{6,7},{7,6},{8,9},{9,8},{10,11... | collective-permute-start | bytes 393224 | tf_op jit(solution)/shard_map/ppermute | solution.py:33
  11.0 5.2 %collective-permute-start.4 = (bf16[128,512]{1,0:T(8,128)(2,1)S(1)}, bf16[128,512]{1,0:T(8,128)(2,1)S(1)}, u32[]{:S(2)}, u32[]{:S(2)}) collective-permute-start(bf16[128,512]{1,0:T(8,128)(2,1)S(1)} %collective-permute-done.refs_1_), channel_id=1, source_target_pairs={{0,1},{1,0},{2,3},{3,2},{4,5},{5,4},{6,7},{7,6},{8,9},{9,8},{10,11... | collective-permute-start | bytes 393224 | tf_op jit(solution)/shard_map/ppermute | solution.py:33
  16.2 0.5 collective-permute-start.6
  16.7 0.5 collective-permute-done.4.refs_5_
  17.7 0.9 copy-done
  18.6 2.7 %gradient.1 = (f32[3,64,256]{2,1,0:T(8,128)S(1)}, bf16[3,64,256]{2,1,0:T(8,128)(2,1)S(1)}, bf16[3,64,256]{2,1,0:T(8,128)(2,1)S(1)}, bf16[3,64,256]{2,1,0:T(8,128...) custom-call(bf16[128,512]{1,0:T(8,128)(2,1)S(1)} %copy-done, ...), custom_call_target="tpu_custom_call" | custom-call | flops 805306368 | bytes 4194304 | tf_op jit(solution)/shard_map/gradient/pallas_call | solution.py:123
  21.3 2.5 %collective-permute-start.10 = (bf16[3,64,256]{2,1,0:T(8,128)(2,1)S(1)}, bf16[3,64,256]{2,1,0:T(8,128)(2,1)S(1)}, u32[]{:S(2)}, u32[]{:S(2)}) collective-permute-start(bf16[3,64,256]{2,1,0:T(8,128)(2,1)S(1)} %get-tuple-element.47), channel_id=1, source_target_pairs={{0,4},{1,5},{2,6},{3,7},{4,8},{5,9},{6,10},{7,11},{8,12},{9,13},{1... | collective-permute-start | bytes 294920 | tf_op jit(solution)/shard_map/ppermute | solution.py:33
  23.8 3.1 %collective-permute-start.11 = (bf16[3,64,256]{2,1,0:T(8,128)(2,1)S(1)}, bf16[3,64,256]{2,1,0:T(8,128)(2,1)S(1)}, u32[]{:S(2)}, u32[]{:S(2)}) collective-permute-start(bf16[3,64,256]{2,1,0:T(8,128)(2,1)S(1)} %get-tuple-element.48), channel_id=1, source_target_pairs={{0,12},{1,13},{2,14},{3,15},{4,0},{5,1},{6,2},{7,3},{8,4},{9,5},{1... | collective-permute-start | bytes 294920 | tf_op jit(solution)/shard_map/ppermute | solution.py:33
  26.9 0.7 collective-permute-start.12
  27.7 1.9 %collective-permute-start.13 = (bf16[3,64,256]{2,1,0:T(8,128)(2,1)S(1)}, bf16[3,64,256]{2,1,0:T(8,128)(2,1)S(1)}, u32[]{:S(2)}, u32[]{:S(2)}) collective-permute-start(bf16[3,64,256]{2,1,0:T(8,128)(2,1)S(1)} %get-tuple-element.50), channel_id=1, source_target_pairs={{0,14},{1,15},{2,0},{3,1},{4,2},{5,3},{6,4},{7,5},{8,6},{9,7},{10,... | collective-permute-start | bytes 294920 | tf_op jit(solution)/shard_map/ppermute | solution.py:33
  29.6 4.4 %collective-permute-start.7 = (bf16[3,64,256]{2,1,0:T(8,128)(2,1)S(1)}, bf16[3,64,256]{2,1,0:T(8,128)(2,1)S(1)}, u32[]{:S(2)}, u32[]{:S(2)}) collective-permute-start(bf16[3,64,256]{2,1,0:T(8,128)(2,1)S(1)} %get-tuple-element.44), channel_id=1, source_target_pairs={{0,8},{1,9},{2,10},{3,11},{4,12},{5,13},{6,14},{7,15},{8,0},{9,1},... | collective-permute-start | bytes 294920 | tf_op jit(solution)/shard_map/ppermute | solution.py:33
  34.0 4.5 %collective-permute-start.9 = (bf16[3,64,256]{2,1,0:T(8,128)(2,1)S(1)}, bf16[3,64,256]{2,1,0:T(8,128)(2,1)S(1)}, u32[]{:S(2)}, u32[]{:S(2)}) collective-permute-start(bf16[3,64,256]{2,1,0:T(8,128)(2,1)S(1)} %get-tuple-element.46), channel_id=1, source_target_pairs={{0,10},{1,11},{2,12},{3,13},{4,14},{5,15},{6,0},{7,1},{8,2},{9,3},... | collective-permute-start | bytes 294920 | tf_op jit(solution)/shard_map/ppermute | solution.py:33
  38.5 6.0 %collective-permute-done.8 = bf16[3,64,256]{2,1,0:T(8,128)(2,1)S(1)} collective-permute-done((bf16[3,64,256]{2,1,0:T(8,128)(2,1)S(1)}, bf16[3,64,256]{2,1,0:T(8,128)(2,1)S(1)}, u32[]{:S(2)}, u32[]{:S(2)}) %collective-permute-start.8) | collective-permute-done | bytes 98336 | tf_op jit(solution)/shard_map/ppermute | solution.py:33
  44.6 0.5 collective-permute-start.14
  45.1 1.6 %collective-permute-start.45 = (bf16[64,512]{1,0:T(8,128)(2,1)S(1)}, bf16[64,512]{1,0:T(8,128)(2,1)S(1)}, u32[]{:S(2)}, u32[]{:S(2)}) collective-permute-start(bf16[64,512]{1,0:T(8,128)(2,1)S(1)} %copy-done.3), channel_id=1, source_target_pairs={{0,48},{1,49},{2,50},{3,51},{4,52},{5,53},{6,54},{7,55},{8,56},{9,... | collective-permute-start | bytes 196616 | tf_op jit(solution)/shard_map/ppermute | solution.py:33
  46.8 4.3 %collective-permute-start.15 = (bf16[3,64,256]{2,1,0:T(8,128)(2,1)S(1)}, bf16[3,64,256]{2,1,0:T(8,128)(2,1)S(1)}, u32[]{:S(2)}, u32[]{:S(2)}) collective-permute-start(bf16[3,64,256]{2,1,0:T(8,128)(2,1)S(1)} %add_convert_fusion.refs_0_), channel_id=1, source_target_pairs={{0,4},{1,5},{2,6},{3,7},{4,8},{5,9},{6,10},{7,11},{8,12},{9,13},{1... | collective-permute-start | bytes 294920 | tf_op jit(solution)/shard_map/ppermute | solution.py:33
  51.1 1.9 %collective-permute-start.16 = (bf16[3,64,256]{2,1,0:T(8,128)(2,1)S(1)}, bf16[3,64,256]{2,1,0:T(8,128)(2,1)S(1)}, u32[]{:S(2)}, u32[]{:S(2)}) collective-permute-start(bf16[3,64,256]{2,1,0:T(8,128)(2,1)S(1)} %add_convert_fusion.refs_0_), channel_id=1, source_target_pairs={{0,6},{1,7},{2,8},{3,9},{4,10},{5,11},{6,12},{7,13},{8,14},{9,15},... | collective-permute-start | bytes 294920 | tf_op jit(solution)/shard_map/ppermute | solution.py:33
  53.0 2.7 %collective-permute-start.17 = (bf16[3,64,256]{2,1,0:T(8,128)(2,1)S(1)}, bf16[3,64,256]{2,1,0:T(8,128)(2,1)S(1)}, u32[]{:S(2)}, u32[]{:S(2)}) collective-permute-start(bf16[3,64,256]{2,1,0:T(8,128)(2,1)S(1)} %add_convert_fusion.refs_0_), channel_id=1, source_target_pairs={{0,8},{1,9},{2,10},{3,11},{4,12},{5,13},{6,14},{7,15},{8,0},{9,1},... | collective-permute-start | bytes 294920 | tf_op jit(solution)/shard_map/ppermute | solution.py:33
  55.6 3.0 %collective-permute-start.18 = (bf16[3,64,256]{2,1,0:T(8,128)(2,1)S(1)}, bf16[3,64,256]{2,1,0:T(8,128)(2,1)S(1)}, u32[]{:S(2)}, u32[]{:S(2)}) collective-permute-start(bf16[3,64,256]{2,1,0:T(8,128)(2,1)S(1)} %add_convert_fusion.refs_0_), channel_id=1, source_target_pairs={{0,10},{1,11},{2,12},{3,13},{4,14},{5,15},{6,0},{7,1},{8,2},{9,3},... | collective-permute-start | bytes 294920 | tf_op jit(solution)/shard_map/ppermute | solution.py:33
  58.6 1.9 %collective-permute-start.19 = (bf16[3,64,256]{2,1,0:T(8,128)(2,1)S(1)}, bf16[3,64,256]{2,1,0:T(8,128)(2,1)S(1)}, u32[]{:S(2)}, u32[]{:S(2)}) collective-permute-start(bf16[3,64,256]{2,1,0:T(8,128)(2,1)S(1)} %add_convert_fusion.refs_0_), channel_id=1, source_target_pairs={{0,12},{1,13},{2,14},{3,15},{4,0},{5,1},{6,2},{7,3},{8,4},{9,5},{1... | collective-permute-start | bytes 294920 | tf_op jit(solution)/shard_map/ppermute | solution.py:33
  60.5 1.2 %collective-permute-start.20 = (bf16[3,64,256]{2,1,0:T(8,128)(2,1)S(1)}, bf16[3,64,256]{2,1,0:T(8,128)(2,1)S(1)}, u32[]{:S(2)}, u32[]{:S(2)}) collective-permute-start(bf16[3,64,256]{2,1,0:T(8,128)(2,1)S(1)} %add_convert_fusion.refs_0_), channel_id=1, source_target_pairs={{0,14},{1,15},{2,0},{3,1},{4,2},{5,3},{6,4},{7,5},{8,6},{9,7},{10,... | collective-permute-start | bytes 294920 | tf_op jit(solution)/shard_map/ppermute | solution.py:33
  61.8 4.7 %collective-permute-done.17.refs_4_ = bf16[3,64,256]{2,1,0:T(8,128)(2,1)S(1)} collective-permute-done((bf16[3,64,256]{2,1,0:T(8,128)(2,1)S(1)}, bf16[3,64,256]{2,1,0:T(8,128)(2,1)S(1)}, u32[]{:S(2)}, u32[]{:S(2)}) %collective-permute-start.17) | collective-permute-done | bytes 98336 | tf_op jit(solution)/shard_map/ppermute | solution.py:33
  66.6 2.0 %collective-permute-start.21 = (bf16[3,64,256]{2,1,0:T(8,128)(2,1)S(1)}, bf16[3,64,256]{2,1,0:T(8,128)(2,1)S(1)}, u32[]{:S(2)}, u32[]{:S(2)}) collective-permute-start(bf16[3,64,256]{2,1,0:T(8,128)(2,1)S(1)} %add_convert_fusion.refs_0_), channel_id=1, source_target_pairs={{0,1},{1,0},{2,3},{3,2},{4,5},{5,4},{6,7},{7,6},{8,9},{9,8},{10,11... | collective-permute-start | bytes 294920 | tf_op jit(solution)/shard_map/ppermute | solution.py:33
  68.6 4.3 %collective-permute-done.19.refs_6_ = bf16[3,64,256]{2,1,0:T(8,128)(2,1)S(1)} collective-permute-done((bf16[3,64,256]{2,1,0:T(8,128)(2,1)S(1)}, bf16[3,64,256]{2,1,0:T(8,128)(2,1)S(1)}, u32[]{:S(2)}, u32[]{:S(2)}) %collective-permute-start.19) | collective-permute-done | bytes 98336 | tf_op jit(solution)/shard_map/ppermute | solution.py:33
  72.9 0.9 collective-permute-done.20.refs_7_
  73.8 0.5 collective-permute-start.32
  74.4 0.9 collective-permute-start.33
  75.3 0.5 collective-permute-start.34
  75.8 0.9 collective-permute-start.35
  76.8 0.5 collective-permute-start.36
  77.3 0.8 collective-permute-done.32.refs_19_
  78.1 3.9 %collective-permute-start.22 = (bf16[3,64,256]{2,1,0:T(8,128)(2,1)S(1)}, bf16[3,64,256]{2,1,0:T(8,128)(2,1)S(1)}, u32[]{:S(2)}, u32[]{:S(2)}) collective-permute-start(bf16[3,64,256]{2,1,0:T(8,128)(2,1)S(1)} %collective-permute-done.14.refs_1_), channel_id=1, source_target_pairs={{0,1},{1,0},{2,3},{3,2},{4,5},{5,4},{6,7},{7,6},{8,9},{9,8},{10,11... | collective-permute-start | bytes 294920 | tf_op jit(solution)/shard_map/ppermute | solution.py:33
  82.0 2.1 %collective-permute-start.23 = (bf16[3,64,256]{2,1,0:T(8,128)(2,1)S(1)}, bf16[3,64,256]{2,1,0:T(8,128)(2,1)S(1)}, u32[]{:S(2)}, u32[]{:S(2)}) collective-permute-start(bf16[3,64,256]{2,1,0:T(8,128)(2,1)S(1)} %collective-permute-done.15.refs_2_), channel_id=1, source_target_pairs={{0,1},{1,0},{2,3},{3,2},{4,5},{5,4},{6,7},{7,6},{8,9},{9,8},{10,11... | collective-permute-start | bytes 294920 | tf_op jit(solution)/shard_map/ppermute | solution.py:33
  84.2 2.1 %collective-permute-start.24 = (bf16[3,64,256]{2,1,0:T(8,128)(2,1)S(1)}, bf16[3,64,256]{2,1,0:T(8,128)(2,1)S(1)}, u32[]{:S(2)}, u32[]{:S(2)}) collective-permute-start(bf16[3,64,256]{2,1,0:T(8,128)(2,1)S(1)} %collective-permute-done.16.refs_3_), channel_id=1, source_target_pairs={{0,1},{1,0},{2,3},{3,2},{4,5},{5,4},{6,7},{7,6},{8,9},{9,8},{10,11... | collective-permute-start | bytes 294920 | tf_op jit(solution)/shard_map/ppermute | solution.py:33
  86.3 1.4 %collective-permute-start.25 = (bf16[3,64,256]{2,1,0:T(8,128)(2,1)S(1)}, bf16[3,64,256]{2,1,0:T(8,128)(2,1)S(1)}, u32[]{:S(2)}, u32[]{:S(2)}) collective-permute-start(bf16[3,64,256]{2,1,0:T(8,128)(2,1)S(1)} %collective-permute-done.17.refs_4_), channel_id=1, source_target_pairs={{0,1},{1,0},{2,3},{3,2},{4,5},{5,4},{6,7},{7,6},{8,9},{9,8},{10,11... | collective-permute-start | bytes 294920 | tf_op jit(solution)/shard_map/ppermute | solution.py:33
  87.6 1.1 collective-permute-start.26
  88.7 0.5 collective-permute-start.28
  89.3 0.4 collective-permute-start.38
  91.3 2.1 %fusion.9 = f32[64,2,1024]{2,0,1:T(8,128)S(1)} fusion(bf16[3,2,512,1024]{3,2,1,0:T(8,128)(2,1)} %refs_32_.1, bf16[8,2,8,512]{3,2,1,0:T(8,128)(2,1)S(1)} %bitcast.60), kind=kOutput, calls=%fused_computation.9 | convolution fusion | flops 134217728 | bytes 2752512 | tf_op jit(solution)/shard_map/thd,hdf->thf/dot_general | solution.py:224
  93.4 12.4 %renew_apply.1 = (bf16[64,512]{1,0:T(8,128)(2,1)S(1)}, bf16[64,512]{1,0:T(8,128)(2,1)S(1)}) custom-call(bf16[3,64,256]{2,1,0:T(8,128)(2,1)S(1)} %add_convert_fusion.refs_0_, bf16[3,64,256]{2,1,0:T(8,128)(2,1)S(1)} %collective-permute-done.14.refs_1_, bf16[3,64,256]{2,1,0:T(8,128)(2,1)S(1)} %collective-permute-done.15.refs_2_, ...), custom_call_target="tpu_custom_call" | custom-call | flops 6000000000 | bytes 7340032 | tf_op jit(solution)/shard_map/renew_apply/pallas_call | solution.py:202
  105.9 1.1 %collective-permute-start.46 = (bf16[64,512]{1,0:T(8,128)(2,1)S(1)}, bf16[64,512]{1,0:T(8,128)(2,1)S(1)}, u32[]{:S(2)}, u32[]{:S(2)}) collective-permute-start(bf16[64,512]{1,0:T(8,128)(2,1)S(1)} %get-tuple-element.54), channel_id=1, source_target_pairs={{0,48},{1,49},{2,50},{3,51},{4,52},{5,53},{6,54},{7,55},{8,56},{9,... | collective-permute-start | bytes 196616 | tf_op jit(solution)/shard_map/ppermute | solution.py:33
  107.0 3.4 %fusion.28 = bf16[64,2,512]{2,0,1:T(8,128)(2,1)S(1)} fusion(bf16[3,2,512,1024]{3,2,1,0:T(8,128)(2,1)} %refs_32_.1, f32[64,2,1024]{2,0,1:T(8,128)S(1)} %fusion.9, bf16[8,2,8,512]{3,2,1,0:T(8,128)(2,1)} %bitcast.61), kind=kOutput, calls=%fused_computation.14 | convolution fusion | flops 269287424 | bytes 4980736 | tf_op jit(solution)/shard_map/thf,hdf->thd/dot_general | solution.py:227
  110.7 0.7 pad_maximum_fusion
  (65 shorter events, 2.9 us)
Async XLA Ops:
  1.6 91.8 %copy-start.2 = (bf16[64,1024]{1,0:T(8,128)(2,1)}, bf16[64,1024]{1,0:T(8,128)(2,1)S(1)}, u32[]{:S(2)}) copy-start(bf16[64,1024]{1,0:T(8,128)(2,1)S(1)} %get-tuple-element.42) | copy-start | bytes 393220
  3.8 7.1 %collective-permute-start = (bf16[128,512]{1,0:T(8,128)(2,1)}, bf16[128,512]{1,0:T(8,128)(2,1)S(1)}, u32[]{:S(2)}, u32[]{:S(2)}) collective-permute-start(bf16[128,512]{1,0:T(8,128)(2,1)} %get-tuple-element.31), channel_id=1, source_target_pairs={{0,16},{1,17},{2,18},{3,19},{4,20},{5,21},{6,22},{7,23},{8,24},{9,... | collective-permute-start | bytes 393224 | tf_op jit(solution)/shard_map/ppermute | solution.py:33
  5.9 10.3 %collective-permute-start.1 = (bf16[128,512]{1,0:T(8,128)(2,1)}, bf16[128,512]{1,0:T(8,128)(2,1)S(1)}, u32[]{:S(2)}, u32[]{:S(2)}) collective-permute-start(bf16[128,512]{1,0:T(8,128)(2,1)} %get-tuple-element.32), channel_id=1, source_target_pairs={{0,32},{1,33},{2,34},{3,35},{4,36},{5,37},{6,38},{7,39},{8,40},{9,... | collective-permute-start | bytes 393224 | tf_op jit(solution)/shard_map/ppermute | solution.py:33
  8.3 7.8 %collective-permute-start.2 = (bf16[128,512]{1,0:T(8,128)(2,1)}, bf16[128,512]{1,0:T(8,128)(2,1)S(1)}, u32[]{:S(2)}, u32[]{:S(2)}) collective-permute-start(bf16[128,512]{1,0:T(8,128)(2,1)} %get-tuple-element.33), channel_id=1, source_target_pairs={{0,48},{1,49},{2,50},{3,51},{4,52},{5,53},{6,54},{7,55},{8,56},{9,... | collective-permute-start | bytes 393224 | tf_op jit(solution)/shard_map/ppermute | solution.py:33
  9.5 7.2 %collective-permute-start.3 = (bf16[128,512]{1,0:T(8,128)(2,1)}, bf16[128,512]{1,0:T(8,128)(2,1)S(1)}, u32[]{:S(2)}, u32[]{:S(2)}) collective-permute-start(bf16[128,512]{1,0:T(8,128)(2,1)} %get-tuple-element.30.refs_0_), channel_id=1, source_target_pairs={{0,1},{1,0},{2,3},{3,2},{4,5},{5,4},{6,7},{7,6},{8,9},{9,8},{10,11... | collective-permute-start | bytes 393224 | tf_op jit(solution)/shard_map/ppermute | solution.py:33
  11.0 6.2 %collective-permute-start.4 = (bf16[128,512]{1,0:T(8,128)(2,1)S(1)}, bf16[128,512]{1,0:T(8,128)(2,1)S(1)}, u32[]{:S(2)}, u32[]{:S(2)}) collective-permute-start(bf16[128,512]{1,0:T(8,128)(2,1)S(1)} %collective-permute-done.refs_1_), channel_id=1, source_target_pairs={{0,1},{1,0},{2,3},{3,2},{4,5},{5,4},{6,7},{7,6},{8,9},{9,8},{10,11... | collective-permute-start | bytes 393224 | tf_op jit(solution)/shard_map/ppermute | solution.py:33
  16.2 1.3 %collective-permute-start.5 = (bf16[128,512]{1,0:T(8,128)(2,1)S(1)}, bf16[128,512]{1,0:T(8,128)(2,1)S(1)}, u32[]{:S(2)}, u32[]{:S(2)}) collective-permute-start(bf16[128,512]{1,0:T(8,128)(2,1)S(1)} %collective-permute-done.1.refs_2_), channel_id=1, source_target_pairs={{0,1},{1,0},{2,3},{3,2},{4,5},{5,4},{6,7},{7,6},{8,9},{9,8},{10,11... | collective-permute-start | bytes 393224 | tf_op jit(solution)/shard_map/ppermute | solution.py:33
  16.2 1.5 %collective-permute-start.6 = (bf16[128,512]{1,0:T(8,128)(2,1)S(1)}, bf16[128,512]{1,0:T(8,128)(2,1)S(1)}, u32[]{:S(2)}, u32[]{:S(2)}) collective-permute-start(bf16[128,512]{1,0:T(8,128)(2,1)S(1)} %collective-permute-done.2.refs_3_), channel_id=1, source_target_pairs={{0,1},{1,0},{2,3},{3,2},{4,5},{5,4},{6,7},{7,6},{8,9},{9,8},{10,11... | collective-permute-start | bytes 393224 | tf_op jit(solution)/shard_map/ppermute | solution.py:33
  21.3 12.7 %collective-permute-start.10 = (bf16[3,64,256]{2,1,0:T(8,128)(2,1)S(1)}, bf16[3,64,256]{2,1,0:T(8,128)(2,1)S(1)}, u32[]{:S(2)}, u32[]{:S(2)}) collective-permute-start(bf16[3,64,256]{2,1,0:T(8,128)(2,1)S(1)} %get-tuple-element.47), channel_id=1, source_target_pairs={{0,4},{1,5},{2,6},{3,7},{4,8},{5,9},{6,10},{7,11},{8,12},{9,13},{1... | collective-permute-start | bytes 294920 | tf_op jit(solution)/shard_map/ppermute | solution.py:33
  23.8 10.2 %collective-permute-start.11 = (bf16[3,64,256]{2,1,0:T(8,128)(2,1)S(1)}, bf16[3,64,256]{2,1,0:T(8,128)(2,1)S(1)}, u32[]{:S(2)}, u32[]{:S(2)}) collective-permute-start(bf16[3,64,256]{2,1,0:T(8,128)(2,1)S(1)} %get-tuple-element.48), channel_id=1, source_target_pairs={{0,12},{1,13},{2,14},{3,15},{4,0},{5,1},{6,2},{7,3},{8,4},{9,5},{1... | collective-permute-start | bytes 294920 | tf_op jit(solution)/shard_map/ppermute | solution.py:33
  26.9 11.5 %collective-permute-start.12 = (bf16[3,64,256]{2,1,0:T(8,128)(2,1)S(1)}, bf16[3,64,256]{2,1,0:T(8,128)(2,1)S(1)}, u32[]{:S(2)}, u32[]{:S(2)}) collective-permute-start(bf16[3,64,256]{2,1,0:T(8,128)(2,1)S(1)} %get-tuple-element.49), channel_id=1, source_target_pairs={{0,2},{1,3},{2,4},{3,5},{4,6},{5,7},{6,8},{7,9},{8,10},{9,11},{10,... | collective-permute-start | bytes 294920 | tf_op jit(solution)/shard_map/ppermute | solution.py:33
  27.7 10.8 %collective-permute-start.13 = (bf16[3,64,256]{2,1,0:T(8,128)(2,1)S(1)}, bf16[3,64,256]{2,1,0:T(8,128)(2,1)S(1)}, u32[]{:S(2)}, u32[]{:S(2)}) collective-permute-start(bf16[3,64,256]{2,1,0:T(8,128)(2,1)S(1)} %get-tuple-element.50), channel_id=1, source_target_pairs={{0,14},{1,15},{2,0},{3,1},{4,2},{5,3},{6,4},{7,5},{8,6},{9,7},{10,... | collective-permute-start | bytes 294920 | tf_op jit(solution)/shard_map/ppermute | solution.py:33
  29.6 8.9 %collective-permute-start.7 = (bf16[3,64,256]{2,1,0:T(8,128)(2,1)S(1)}, bf16[3,64,256]{2,1,0:T(8,128)(2,1)S(1)}, u32[]{:S(2)}, u32[]{:S(2)}) collective-permute-start(bf16[3,64,256]{2,1,0:T(8,128)(2,1)S(1)} %get-tuple-element.44), channel_id=1, source_target_pairs={{0,8},{1,9},{2,10},{3,11},{4,12},{5,13},{6,14},{7,15},{8,0},{9,1},... | collective-permute-start | bytes 294920 | tf_op jit(solution)/shard_map/ppermute | solution.py:33
  34.0 10.5 %collective-permute-start.8 = (bf16[3,64,256]{2,1,0:T(8,128)(2,1)S(1)}, bf16[3,64,256]{2,1,0:T(8,128)(2,1)S(1)}, u32[]{:S(2)}, u32[]{:S(2)}) collective-permute-start(bf16[3,64,256]{2,1,0:T(8,128)(2,1)S(1)} %get-tuple-element.45), channel_id=1, source_target_pairs={{0,6},{1,7},{2,8},{3,9},{4,10},{5,11},{6,12},{7,13},{8,14},{9,15},... | collective-permute-start | bytes 294920 | tf_op jit(solution)/shard_map/ppermute | solution.py:33
  34.0 10.5 %collective-permute-start.9 = (bf16[3,64,256]{2,1,0:T(8,128)(2,1)S(1)}, bf16[3,64,256]{2,1,0:T(8,128)(2,1)S(1)}, u32[]{:S(2)}, u32[]{:S(2)}) collective-permute-start(bf16[3,64,256]{2,1,0:T(8,128)(2,1)S(1)} %get-tuple-element.46), channel_id=1, source_target_pairs={{0,10},{1,11},{2,12},{3,13},{4,14},{5,15},{6,0},{7,1},{8,2},{9,3},... | collective-permute-start | bytes 294920 | tf_op jit(solution)/shard_map/ppermute | solution.py:33
  44.6 14.0 %collective-permute-start.14 = (bf16[3,64,256]{2,1,0:T(8,128)(2,1)S(1)}, bf16[3,64,256]{2,1,0:T(8,128)(2,1)S(1)}, u32[]{:S(2)}, u32[]{:S(2)}) collective-permute-start(bf16[3,64,256]{2,1,0:T(8,128)(2,1)S(1)} %add_convert_fusion.refs_0_), channel_id=1, source_target_pairs={{0,2},{1,3},{2,4},{3,5},{4,6},{5,7},{6,8},{7,9},{8,10},{9,11},{10,... | collective-permute-start | bytes 294920 | tf_op jit(solution)/shard_map/ppermute | solution.py:33
  45.1 10.5 %collective-permute-start.45 = (bf16[64,512]{1,0:T(8,128)(2,1)S(1)}, bf16[64,512]{1,0:T(8,128)(2,1)S(1)}, u32[]{:S(2)}, u32[]{:S(2)}) collective-permute-start(bf16[64,512]{1,0:T(8,128)(2,1)S(1)} %copy-done.3), channel_id=1, source_target_pairs={{0,48},{1,49},{2,50},{3,51},{4,52},{5,53},{6,54},{7,55},{8,56},{9,... | collective-permute-start | bytes 196616 | tf_op jit(solution)/shard_map/ppermute | solution.py:33
  46.8 13.7 %collective-permute-start.15 = (bf16[3,64,256]{2,1,0:T(8,128)(2,1)S(1)}, bf16[3,64,256]{2,1,0:T(8,128)(2,1)S(1)}, u32[]{:S(2)}, u32[]{:S(2)}) collective-permute-start(bf16[3,64,256]{2,1,0:T(8,128)(2,1)S(1)} %add_convert_fusion.refs_0_), channel_id=1, source_target_pairs={{0,4},{1,5},{2,6},{3,7},{4,8},{5,9},{6,10},{7,11},{8,12},{9,13},{1... | collective-permute-start | bytes 294920 | tf_op jit(solution)/shard_map/ppermute | solution.py:33
  51.1 10.6 %collective-permute-start.16 = (bf16[3,64,256]{2,1,0:T(8,128)(2,1)S(1)}, bf16[3,64,256]{2,1,0:T(8,128)(2,1)S(1)}, u32[]{:S(2)}, u32[]{:S(2)}) collective-permute-start(bf16[3,64,256]{2,1,0:T(8,128)(2,1)S(1)} %add_convert_fusion.refs_0_), channel_id=1, source_target_pairs={{0,6},{1,7},{2,8},{3,9},{4,10},{5,11},{6,12},{7,13},{8,14},{9,15},... | collective-permute-start | bytes 294920 | tf_op jit(solution)/shard_map/ppermute | solution.py:33
  53.0 13.6 %collective-permute-start.17 = (bf16[3,64,256]{2,1,0:T(8,128)(2,1)S(1)}, bf16[3,64,256]{2,1,0:T(8,128)(2,1)S(1)}, u32[]{:S(2)}, u32[]{:S(2)}) collective-permute-start(bf16[3,64,256]{2,1,0:T(8,128)(2,1)S(1)} %add_convert_fusion.refs_0_), channel_id=1, source_target_pairs={{0,8},{1,9},{2,10},{3,11},{4,12},{5,13},{6,14},{7,15},{8,0},{9,1},... | collective-permute-start | bytes 294920 | tf_op jit(solution)/shard_map/ppermute | solution.py:33
  55.6 13.0 %collective-permute-start.18 = (bf16[3,64,256]{2,1,0:T(8,128)(2,1)S(1)}, bf16[3,64,256]{2,1,0:T(8,128)(2,1)S(1)}, u32[]{:S(2)}, u32[]{:S(2)}) collective-permute-start(bf16[3,64,256]{2,1,0:T(8,128)(2,1)S(1)} %add_convert_fusion.refs_0_), channel_id=1, source_target_pairs={{0,10},{1,11},{2,12},{3,13},{4,14},{5,15},{6,0},{7,1},{8,2},{9,3},... | collective-permute-start | bytes 294920 | tf_op jit(solution)/shard_map/ppermute | solution.py:33
  58.6 14.3 %collective-permute-start.19 = (bf16[3,64,256]{2,1,0:T(8,128)(2,1)S(1)}, bf16[3,64,256]{2,1,0:T(8,128)(2,1)S(1)}, u32[]{:S(2)}, u32[]{:S(2)}) collective-permute-start(bf16[3,64,256]{2,1,0:T(8,128)(2,1)S(1)} %add_convert_fusion.refs_0_), channel_id=1, source_target_pairs={{0,12},{1,13},{2,14},{3,15},{4,0},{5,1},{6,2},{7,3},{8,4},{9,5},{1... | collective-permute-start | bytes 294920 | tf_op jit(solution)/shard_map/ppermute | solution.py:33
  60.5 13.3 %collective-permute-start.20 = (bf16[3,64,256]{2,1,0:T(8,128)(2,1)S(1)}, bf16[3,64,256]{2,1,0:T(8,128)(2,1)S(1)}, u32[]{:S(2)}, u32[]{:S(2)}) collective-permute-start(bf16[3,64,256]{2,1,0:T(8,128)(2,1)S(1)} %add_convert_fusion.refs_0_), channel_id=1, source_target_pairs={{0,14},{1,15},{2,0},{3,1},{4,2},{5,3},{6,4},{7,5},{8,6},{9,7},{10,... | collective-permute-start | bytes 294920 | tf_op jit(solution)/shard_map/ppermute | solution.py:33
  61.7 12.7 %collective-permute-start.29 = (bf16[3,64,256]{2,1,0:T(8,128)(2,1)S(1)}, bf16[3,64,256]{2,1,0:T(8,128)(2,1)S(1)}, u32[]{:S(2)}, u32[]{:S(2)}) collective-permute-start(bf16[3,64,256]{2,1,0:T(8,128)(2,1)S(1)} %add_convert_fusion.refs_0_), channel_id=1, source_target_pairs={{0,16},{1,17},{2,18},{3,19},{4,20},{5,21},{6,22},{7,23},{8,24},{9,... | collective-permute-start | bytes 294920 | tf_op jit(solution)/shard_map/ppermute | solution.py:33
  66.6 8.7 %collective-permute-start.21 = (bf16[3,64,256]{2,1,0:T(8,128)(2,1)S(1)}, bf16[3,64,256]{2,1,0:T(8,128)(2,1)S(1)}, u32[]{:S(2)}, u32[]{:S(2)}) collective-permute-start(bf16[3,64,256]{2,1,0:T(8,128)(2,1)S(1)} %add_convert_fusion.refs_0_), channel_id=1, source_target_pairs={{0,1},{1,0},{2,3},{3,2},{4,5},{5,4},{6,7},{7,6},{8,9},{9,8},{10,11... | collective-permute-start | bytes 294920 | tf_op jit(solution)/shard_map/ppermute | solution.py:33
  68.6 7.2 %collective-permute-start.30 = (bf16[3,64,256]{2,1,0:T(8,128)(2,1)S(1)}, bf16[3,64,256]{2,1,0:T(8,128)(2,1)S(1)}, u32[]{:S(2)}, u32[]{:S(2)}) collective-permute-start(bf16[3,64,256]{2,1,0:T(8,128)(2,1)S(1)} %collective-permute-done.14.refs_1_), channel_id=1, source_target_pairs={{0,16},{1,17},{2,18},{3,19},{4,20},{5,21},{6,22},{7,23},{8,24},{9,... | collective-permute-start | bytes 294920 | tf_op jit(solution)/shard_map/ppermute | solution.py:33
  72.9 3.9 %collective-permute-start.31 = (bf16[3,64,256]{2,1,0:T(8,128)(2,1)S(1)}, bf16[3,64,256]{2,1,0:T(8,128)(2,1)S(1)}, u32[]{:S(2)}, u32[]{:S(2)}) collective-permute-start(bf16[3,64,256]{2,1,0:T(8,128)(2,1)S(1)} %collective-permute-done.15.refs_2_), channel_id=1, source_target_pairs={{0,16},{1,17},{2,18},{3,19},{4,20},{5,21},{6,22},{7,23},{8,24},{9,... | collective-permute-start | bytes 294920 | tf_op jit(solution)/shard_map/ppermute | solution.py:33
  73.8 4.3 %collective-permute-start.32 = (bf16[3,64,256]{2,1,0:T(8,128)(2,1)S(1)}, bf16[3,64,256]{2,1,0:T(8,128)(2,1)S(1)}, u32[]{:S(2)}, u32[]{:S(2)}) collective-permute-start(bf16[3,64,256]{2,1,0:T(8,128)(2,1)S(1)} %collective-permute-done.16.refs_3_), channel_id=1, source_target_pairs={{0,16},{1,17},{2,18},{3,19},{4,20},{5,21},{6,22},{7,23},{8,24},{9,... | collective-permute-start | bytes 294920 | tf_op jit(solution)/shard_map/ppermute | solution.py:33
  74.4 7.7 %collective-permute-start.33 = (bf16[3,64,256]{2,1,0:T(8,128)(2,1)S(1)}, bf16[3,64,256]{2,1,0:T(8,128)(2,1)S(1)}, u32[]{:S(2)}, u32[]{:S(2)}) collective-permute-start(bf16[3,64,256]{2,1,0:T(8,128)(2,1)S(1)} %collective-permute-done.17.refs_4_), channel_id=1, source_target_pairs={{0,16},{1,17},{2,18},{3,19},{4,20},{5,21},{6,22},{7,23},{8,24},{9,... | collective-permute-start | bytes 294920 | tf_op jit(solution)/shard_map/ppermute | solution.py:33
  75.3 8.9 %collective-permute-start.34 = (bf16[3,64,256]{2,1,0:T(8,128)(2,1)S(1)}, bf16[3,64,256]{2,1,0:T(8,128)(2,1)S(1)}, u32[]{:S(2)}, u32[]{:S(2)}) collective-permute-start(bf16[3,64,256]{2,1,0:T(8,128)(2,1)S(1)} %collective-permute-done.18.refs_5_), channel_id=1, source_target_pairs={{0,16},{1,17},{2,18},{3,19},{4,20},{5,21},{6,22},{7,23},{8,24},{9,... | collective-permute-start | bytes 294920 | tf_op jit(solution)/shard_map/ppermute | solution.py:33
  75.8 10.4 %collective-permute-start.35 = (bf16[3,64,256]{2,1,0:T(8,128)(2,1)S(1)}, bf16[3,64,256]{2,1,0:T(8,128)(2,1)S(1)}, u32[]{:S(2)}, u32[]{:S(2)}) collective-permute-start(bf16[3,64,256]{2,1,0:T(8,128)(2,1)S(1)} %collective-permute-done.19.refs_6_), channel_id=1, source_target_pairs={{0,16},{1,17},{2,18},{3,19},{4,20},{5,21},{6,22},{7,23},{8,24},{9,... | collective-permute-start | bytes 294920 | tf_op jit(solution)/shard_map/ppermute | solution.py:33
  76.8 10.9 %collective-permute-start.36 = (bf16[3,64,256]{2,1,0:T(8,128)(2,1)S(1)}, bf16[3,64,256]{2,1,0:T(8,128)(2,1)S(1)}, u32[]{:S(2)}, u32[]{:S(2)}) collective-permute-start(bf16[3,64,256]{2,1,0:T(8,128)(2,1)S(1)} %collective-permute-done.20.refs_7_), channel_id=1, source_target_pairs={{0,16},{1,17},{2,18},{3,19},{4,20},{5,21},{6,22},{7,23},{8,24},{9,... | collective-permute-start | bytes 294920 | tf_op jit(solution)/shard_map/ppermute | solution.py:33
  78.1 10.6 %collective-permute-start.22 = (bf16[3,64,256]{2,1,0:T(8,128)(2,1)S(1)}, bf16[3,64,256]{2,1,0:T(8,128)(2,1)S(1)}, u32[]{:S(2)}, u32[]{:S(2)}) collective-permute-start(bf16[3,64,256]{2,1,0:T(8,128)(2,1)S(1)} %collective-permute-done.14.refs_1_), channel_id=1, source_target_pairs={{0,1},{1,0},{2,3},{3,2},{4,5},{5,4},{6,7},{7,6},{8,9},{9,8},{10,11... | collective-permute-start | bytes 294920 | tf_op jit(solution)/shard_map/ppermute | solution.py:33
  82.0 6.7 %collective-permute-start.23 = (bf16[3,64,256]{2,1,0:T(8,128)(2,1)S(1)}, bf16[3,64,256]{2,1,0:T(8,128)(2,1)S(1)}, u32[]{:S(2)}, u32[]{:S(2)}) collective-permute-start(bf16[3,64,256]{2,1,0:T(8,128)(2,1)S(1)} %collective-permute-done.15.refs_2_), channel_id=1, source_target_pairs={{0,1},{1,0},{2,3},{3,2},{4,5},{5,4},{6,7},{7,6},{8,9},{9,8},{10,11... | collective-permute-start | bytes 294920 | tf_op jit(solution)/shard_map/ppermute | solution.py:33
  84.2 5.1 %collective-permute-start.24 = (bf16[3,64,256]{2,1,0:T(8,128)(2,1)S(1)}, bf16[3,64,256]{2,1,0:T(8,128)(2,1)S(1)}, u32[]{:S(2)}, u32[]{:S(2)}) collective-permute-start(bf16[3,64,256]{2,1,0:T(8,128)(2,1)S(1)} %collective-permute-done.16.refs_3_), channel_id=1, source_target_pairs={{0,1},{1,0},{2,3},{3,2},{4,5},{5,4},{6,7},{7,6},{8,9},{9,8},{10,11... | collective-permute-start | bytes 294920 | tf_op jit(solution)/shard_map/ppermute | solution.py:33
  86.3 3.1 %collective-permute-start.25 = (bf16[3,64,256]{2,1,0:T(8,128)(2,1)S(1)}, bf16[3,64,256]{2,1,0:T(8,128)(2,1)S(1)}, u32[]{:S(2)}, u32[]{:S(2)}) collective-permute-start(bf16[3,64,256]{2,1,0:T(8,128)(2,1)S(1)} %collective-permute-done.17.refs_4_), channel_id=1, source_target_pairs={{0,1},{1,0},{2,3},{3,2},{4,5},{5,4},{6,7},{7,6},{8,9},{9,8},{10,11... | collective-permute-start | bytes 294920 | tf_op jit(solution)/shard_map/ppermute | solution.py:33
  87.6 2.1 %collective-permute-start.26 = (bf16[3,64,256]{2,1,0:T(8,128)(2,1)S(1)}, bf16[3,64,256]{2,1,0:T(8,128)(2,1)S(1)}, u32[]{:S(2)}, u32[]{:S(2)}) collective-permute-start(bf16[3,64,256]{2,1,0:T(8,128)(2,1)S(1)} %collective-permute-done.18.refs_5_), channel_id=1, source_target_pairs={{0,1},{1,0},{2,3},{3,2},{4,5},{5,4},{6,7},{7,6},{8,9},{9,8},{10,11... | collective-permute-start | bytes 294920 | tf_op jit(solution)/shard_map/ppermute | solution.py:33
  88.7 1.3 %collective-permute-start.27 = (bf16[3,64,256]{2,1,0:T(8,128)(2,1)S(1)}, bf16[3,64,256]{2,1,0:T(8,128)(2,1)S(1)}, u32[]{:S(2)}, u32[]{:S(2)}) collective-permute-start(bf16[3,64,256]{2,1,0:T(8,128)(2,1)S(1)} %collective-permute-done.19.refs_6_), channel_id=1, source_target_pairs={{0,1},{1,0},{2,3},{3,2},{4,5},{5,4},{6,7},{7,6},{8,9},{9,8},{10,11... | collective-permute-start | bytes 294920 | tf_op jit(solution)/shard_map/ppermute | solution.py:33
  88.7 1.5 %collective-permute-start.28 = (bf16[3,64,256]{2,1,0:T(8,128)(2,1)S(1)}, bf16[3,64,256]{2,1,0:T(8,128)(2,1)S(1)}, u32[]{:S(2)}, u32[]{:S(2)}) collective-permute-start(bf16[3,64,256]{2,1,0:T(8,128)(2,1)S(1)} %collective-permute-done.20.refs_7_), channel_id=1, source_target_pairs={{0,1},{1,0},{2,3},{3,2},{4,5},{5,4},{6,7},{7,6},{8,9},{9,8},{10,11... | collective-permute-start | bytes 294920 | tf_op jit(solution)/shard_map/ppermute | solution.py:33
  89.2 1.3 %collective-permute-start.37 = (bf16[3,64,256]{2,1,0:T(8,128)(2,1)S(1)}, bf16[3,64,256]{2,1,0:T(8,128)(2,1)S(1)}, u32[]{:S(2)}, u32[]{:S(2)}) collective-permute-start(bf16[3,64,256]{2,1,0:T(8,128)(2,1)S(1)} %collective-permute-done.29.refs_16_), channel_id=1, source_target_pairs={{0,1},{1,0},{2,3},{3,2},{4,5},{5,4},{6,7},{7,6},{8,9},{9,8},{10,11... | collective-permute-start | bytes 294920 | tf_op jit(solution)/shard_map/ppermute | solution.py:33
  89.3 1.5 %collective-permute-start.38 = (bf16[3,64,256]{2,1,0:T(8,128)(2,1)S(1)}, bf16[3,64,256]{2,1,0:T(8,128)(2,1)S(1)}, u32[]{:S(2)}, u32[]{:S(2)}) collective-permute-start(bf16[3,64,256]{2,1,0:T(8,128)(2,1)S(1)} %collective-permute-done.30.refs_17_), channel_id=1, source_target_pairs={{0,1},{1,0},{2,3},{3,2},{4,5},{5,4},{6,7},{7,6},{8,9},{9,8},{10,11... | collective-permute-start | bytes 294920 | tf_op jit(solution)/shard_map/ppermute | solution.py:33
  89.7 1.3 %collective-permute-start.39 = (bf16[3,64,256]{2,1,0:T(8,128)(2,1)S(1)}, bf16[3,64,256]{2,1,0:T(8,128)(2,1)S(1)}, u32[]{:S(2)}, u32[]{:S(2)}) collective-permute-start(bf16[3,64,256]{2,1,0:T(8,128)(2,1)S(1)} %collective-permute-done.31.refs_18_), channel_id=1, source_target_pairs={{0,1},{1,0},{2,3},{3,2},{4,5},{5,4},{6,7},{7,6},{8,9},{9,8},{10,11... | collective-permute-start | bytes 294920 | tf_op jit(solution)/shard_map/ppermute | solution.py:33
  90.0 3.4 %collective-permute-start.40 = (bf16[3,64,256]{2,1,0:T(8,128)(2,1)S(1)}, bf16[3,64,256]{2,1,0:T(8,128)(2,1)S(1)}, u32[]{:S(2)}, u32[]{:S(2)}) collective-permute-start(bf16[3,64,256]{2,1,0:T(8,128)(2,1)S(1)} %collective-permute-done.32.refs_19_), channel_id=1, source_target_pairs={{0,1},{1,0},{2,3},{3,2},{4,5},{5,4},{6,7},{7,6},{8,9},{9,8},{10,11... | collective-permute-start | bytes 294920 | tf_op jit(solution)/shard_map/ppermute | solution.py:33
  90.3 3.1 %collective-permute-start.41 = (bf16[3,64,256]{2,1,0:T(8,128)(2,1)S(1)}, bf16[3,64,256]{2,1,0:T(8,128)(2,1)S(1)}, u32[]{:S(2)}, u32[]{:S(2)}) collective-permute-start(bf16[3,64,256]{2,1,0:T(8,128)(2,1)S(1)} %collective-permute-done.33.refs_20_), channel_id=1, source_target_pairs={{0,1},{1,0},{2,3},{3,2},{4,5},{5,4},{6,7},{7,6},{8,9},{9,8},{10,11... | collective-permute-start | bytes 294920 | tf_op jit(solution)/shard_map/ppermute | solution.py:33
  90.5 2.9 %collective-permute-start.42 = (bf16[3,64,256]{2,1,0:T(8,128)(2,1)S(1)}, bf16[3,64,256]{2,1,0:T(8,128)(2,1)S(1)}, u32[]{:S(2)}, u32[]{:S(2)}) collective-permute-start(bf16[3,64,256]{2,1,0:T(8,128)(2,1)S(1)} %collective-permute-done.34.refs_21_), channel_id=1, source_target_pairs={{0,1},{1,0},{2,3},{3,2},{4,5},{5,4},{6,7},{7,6},{8,9},{9,8},{10,11... | collective-permute-start | bytes 294920 | tf_op jit(solution)/shard_map/ppermute | solution.py:33
  90.8 2.6 %collective-permute-start.43 = (bf16[3,64,256]{2,1,0:T(8,128)(2,1)S(1)}, bf16[3,64,256]{2,1,0:T(8,128)(2,1)S(1)}, u32[]{:S(2)}, u32[]{:S(2)}) collective-permute-start(bf16[3,64,256]{2,1,0:T(8,128)(2,1)S(1)} %collective-permute-done.35.refs_22_), channel_id=1, source_target_pairs={{0,1},{1,0},{2,3},{3,2},{4,5},{5,4},{6,7},{7,6},{8,9},{9,8},{10,11... | collective-permute-start | bytes 294920 | tf_op jit(solution)/shard_map/ppermute | solution.py:33
  91.0 2.4 %collective-permute-start.44 = (bf16[3,64,256]{2,1,0:T(8,128)(2,1)S(1)}, bf16[3,64,256]{2,1,0:T(8,128)(2,1)S(1)}, u32[]{:S(2)}, u32[]{:S(2)}) collective-permute-start(bf16[3,64,256]{2,1,0:T(8,128)(2,1)S(1)} %collective-permute-done.36.refs_23_), channel_id=1, source_target_pairs={{0,1},{1,0},{2,3},{3,2},{4,5},{5,4},{6,7},{7,6},{8,9},{9,8},{10,11... | collective-permute-start | bytes 294920 | tf_op jit(solution)/shard_map/ppermute | solution.py:33
  105.9 4.7 %collective-permute-start.46 = (bf16[64,512]{1,0:T(8,128)(2,1)S(1)}, bf16[64,512]{1,0:T(8,128)(2,1)S(1)}, u32[]{:S(2)}, u32[]{:S(2)}) collective-permute-start(bf16[64,512]{1,0:T(8,128)(2,1)S(1)} %get-tuple-element.54), channel_id=1, source_target_pairs={{0,48},{1,49},{2,50},{3,51},{4,52},{5,53},{6,54},{7,55},{8,56},{9,... | collective-permute-start | bytes 196616 | tf_op jit(solution)/shard_map/ppermute | solution.py:33
  (3 other events, 102.3 us)

commit v2 on v1

v2 whole, which is shorter than its diff:
```python
import jax
import jax.numpy as jnp
from jax import lax
from jax.experimental import pallas as pl
from jax.experimental.pallas import tpu as pltpu
from jax.sharding import PartitionSpec as P

X, Z, C = 4, 8, 2
DIM, FF = 512, 1024
HALF, QUARTER = FF // 2, FF // 4
WIDE = HALF + QUARTER
ROWS = DIM // Z
BF, F32 = jnp.bfloat16, jnp.float32
VMEM_LIMIT = 48 * 1024 * 1024
upd_scale = 2.0
norm_eps = 1e-07
VMEM = pl.BlockSpec(memory_space=pltpu.VMEM)
ANY = pl.BlockSpec(memory_space=pl.ANY)


def place():
    index = lax.axis_index("ctx")
    return index // (Z * C), (index // C) % Z, index % C


def move(array, to):
    perm = []
    for x in range(X):
        for z in range(Z):
            for c in range(C):
                tx, tz, tc = to(x, z, c)
                perm.append(((x * Z + z) * C + c, (tx % X * Z + tz % Z) * C + tc % C))
    return lax.ppermute(array, "ctx", perm)


def along_x(array, distance):
    return move(array, lambda x, z, c: (x + distance, z, c))


def along_z(array, distance):
    return move(array, lambda x, z, c: (x, z + distance, c))


def pair_x(array):
    return move(array, lambda x, z, c: (x ^ 1, z, c))


def mirror_x(array):
    return move(array, lambda x, z, c: (X - 1 - x, z, c))


def mirror_x_core(array):
    return move(array, lambda x, z, c: (X - 1 - x, z, c + 1))


def other_core(array):
    return move(array, lambda x, z, c: (x, z, c + 1))


def dot(left, right, dims):
    return lax.dot_general(left, right, (dims, ((), ())), preferred_element_type=F32)


def shape(*dims, dtype=BF):
    return jax.ShapeDtypeStruct(dims, dtype)


def params():
    return pltpu.CompilerParams(vmem_limit_bytes=VMEM_LIMIT)


def cost(flops, size):
    return pl.CostEstimate(flops=flops, bytes_accessed=size, transcendentals=0)


def at_place(start, size):
    return pl.ds(pl.multiple_of(start, size), size)


def prepare_kernel(queries, keys, values, rates, own, far1, far2, far3, query_own, query_far):
    x, _, _ = place()
    tokens = keys.shape[1]
    diagonal = lax.broadcasted_iota(jnp.int32, (tokens, tokens), 0) == lax.broadcasted_iota(
        jnp.int32, (tokens, tokens), 1
    )
    for head in range(2):
        row = rates[0, head : head + 1, :]
        rate = jnp.sum(jnp.where(diagonal, row, 0.0), axis=1, keepdims=True)
        cols = slice(head * DIM, (head + 1) * DIM)
        scaled = (values[0, :, cols].astype(F32) * rate).astype(BF)
        for distance, ref in enumerate((own, far1, far2, far3)):

            @pl.when(lax.rem(x + distance, X) // 2 == head)
            def _():
                ref[:tokens, :] = keys[0, :, cols]
                ref[tokens:, :] = scaled

        @pl.when(x // 2 == head)
        def _():
            query_own[...] = queries[1, :, cols]

        @pl.when(x // 2 != head)
        def _():
            query_far[...] = queries[1, :, cols]


def prepare(queries, keys, values, rates):
    tokens = keys.shape[1]
    pair, half = shape(2 * tokens, DIM), shape(tokens, DIM)
    return pl.pallas_call(
        prepare_kernel,
        out_shape=(pair, pair, pair, pair, half, half),
        in_specs=[VMEM] * 4,
        out_specs=(VMEM,) * 6,
        name="prepare",
    )(queries, keys, values, rates)


def first_kernel(queries, weights, out, w, sem):
    copies = []
    for head in range(2):
        for m in range(3):
            copy = pltpu.make_async_copy(weights.at[m, head], w.at[head, m], sem.at[head, m])
            copy.start()
            copies.append(copy)
    for head in range(2):
        cols = slice(head * DIM, (head + 1) * DIM)
        query = queries[0, :, cols]
        copies[3 * head].wait()
        first_proj = dot(query, w[head, 0], ((1,), (0,)))
        copies[3 * head + 1].wait()
        third_proj = dot(query, w[head, 1], ((1,), (0,)))
        gated = (first_proj * jax.nn.sigmoid(first_proj) * third_proj).astype(BF)
        copies[3 * head + 2].wait()
        out[:, cols] = dot(gated, w[head, 2], ((1,), (1,))).astype(BF)


def first_block(queries, weights):
    tokens = queries.shape[1]
    return pl.pallas_call(
        first_kernel,
        out_shape=shape(tokens, 2 * DIM),
        in_specs=[VMEM, ANY],
        out_specs=VMEM,
        scratch_shapes=[pltpu.VMEM((2, 3, DIM, FF), BF), pltpu.SemaphoreType.DMA((2, 3))],
        compiler_params=params(),
        cost_estimate=cost(12 * tokens * DIM * FF, 7 << 20),
        name="first_block",
    )(queries, weights)


def gradient_kernel(*refs):
    pieces, weights = refs[:8], refs[8]
    own, near_up, near_down, keep_up, keep_down, send_up, send_down, far_up, far_down = refs[9:18]
    w, k, v, d, gated, total, sem = refs[18:]
    x, z, c = place()
    copies = []
    for m in range(3):
        copy = pltpu.make_async_copy(
            weights.at[m, x // 2, :, at_place(lax.rem(x, 2) * HALF, HALF)], w.at[m], sem.at[m]
        )
        copy.start()
        copies.append(copy)
    tokens = pieces[0].shape[0] // 2
    for i, piece in enumerate(pieces):
        k[i * tokens : (i + 1) * tokens, :] = piece[:tokens, :]
        v[i * tokens : (i + 1) * tokens, :] = piece[tokens:, :]
    for copy in copies:
        copy.wait()
    key_first = dot(k[...], w[0], ((1,), (0,)))
    key_third = dot(k[...], w[1], ((1,), (0,)))
    back_grad = -dot(v[...], w[2], ((1,), (0,)))
    sig = jax.nn.sigmoid(key_first)
    key_act = key_first * sig

    @pl.when(c == 0)
    def _():
        d[...] = (back_grad * key_third * sig * (1.0 + key_first * (1.0 - sig))).astype(BF)
        gated[...] = (key_act[:, :QUARTER] * key_third[:, :QUARTER]).astype(BF)

    @pl.when(c == 1)
    def _():
        d[...] = (back_grad * key_act).astype(BF)
        gated[...] = (key_act[:, QUARTER:] * key_third[:, QUARTER:]).astype(BF)

    total[:, :HALF] = dot(k[...], d[...], ((0,), (0,)))
    total[:, HALF:] = -dot(v[...], gated[...], ((0,), (0,)))

    def rows(distance):
        return total[at_place(lax.rem(z + distance + Z, Z) * ROWS, ROWS), :]

    own[...] = rows(0)
    near_up[...] = rows(1).astype(BF)
    near_down[...] = rows(-1).astype(BF)
    keep_up[...] = rows(2)
    keep_down[...] = rows(-2)
    send_up[...] = rows(3).astype(BF)
    send_down[...] = rows(-3).astype(BF)
    far = rows(4).astype(BF)
    far_up[...] = far[: ROWS // 2]
    far_down[...] = far[ROWS // 2 :]


def gradient(pieces, weights):
    tokens = 8 * pieces[0].shape[0] // 2
    kept, sent, half = shape(ROWS, WIDE, dtype=F32), shape(ROWS, WIDE), shape(ROWS // 2, WIDE)
    return pl.pallas_call(
        gradient_kernel,
        out_shape=(kept, sent, sent, kept, kept, sent, sent, half, half),
        in_specs=[VMEM] * 8 + [ANY],
        out_specs=(VMEM,) * 9,
        scratch_shapes=[
            pltpu.VMEM((3, DIM, HALF), BF),
            pltpu.VMEM((tokens, DIM), BF),
            pltpu.VMEM((tokens, DIM), BF),
            pltpu.VMEM((tokens, HALF), BF),
            pltpu.VMEM((tokens, QUARTER), BF),
            pltpu.VMEM((DIM, WIDE), F32),
            pltpu.SemaphoreType.DMA((3,)),
        ],
        compiler_params=params(),
        cost_estimate=cost(10 * tokens * DIM * HALF, 6 << 20),
        name="gradient",
    )(*pieces, weights)


def middle_kernel(keep_up, keep_down, got_up, got_down, far_up, far_down, up, down):
    half = ROWS // 2
    total = keep_up[...] + got_up[...].astype(F32)
    up[:half, :] = (total[:half] + far_up[...].astype(F32)).astype(BF)
    up[half:, :] = total[half:].astype(BF)
    total = keep_down[...] + got_down[...].astype(F32)
    down[:half, :] = total[:half].astype(BF)
    down[half:, :] = (total[half:] + far_down[...].astype(F32)).astype(BF)


def middle(*args):
    return pl.pallas_call(
        middle_kernel,
        out_shape=(shape(ROWS, WIDE), shape(ROWS, WIDE)),
        in_specs=[VMEM] * 6,
        out_specs=(VMEM, VMEM),
        name="middle",
    )(*args)


def total_kernel(own, a, b, c, d, out):
    total = own[...] + a[...].astype(F32) + b[...].astype(F32) + c[...].astype(F32)
    out[...] = (total + d[...].astype(F32)).astype(BF)


def add_up(*args):
    return pl.pallas_call(
        total_kernel,
        out_shape=shape(ROWS, WIDE),
        in_specs=[VMEM] * 5,
        out_specs=VMEM,
        name="add_up",
    )(*args)


def reduce_rows(parts):
    own, near_up, near_down, keep_up, keep_down, send_up, send_down, far_up, far_down = parts
    far_up, far_down = along_z(far_up, 2), along_z(far_down, -2)
    got_up, got_down = along_z(send_up, 1), along_z(send_down, -1)
    near_up, near_down = along_z(near_up, 1), along_z(near_down, -1)
    up, down = middle(keep_up, keep_down, got_up, got_down, far_up, far_down)
    up, down = along_z(up, 2), along_z(down, -2)
    return add_up(own, near_up, near_down, up, down)


ORIGINS = ((0, 0, ROWS), (-1, 0, ROWS), (1, 0, ROWS), (-2, 0, ROWS), (2, 0, ROWS)) + (
    (-3, 0, ROWS),
    (3, 0, ROWS),
    (-4, 0, ROWS // 2),
    (4, ROWS // 2, ROWS // 2),
)


def gather_rows(own):
    up1, down1 = along_z(own, 1), along_z(own, -1)
    up2, down2 = along_z(own, 2), along_z(own, -2)
    up3, down3 = along_z(up2, 1), along_z(down2, -1)
    up4, down4 = along_z(up2[: ROWS // 2], 2), along_z(down2[ROWS // 2 :], -2)
    pieces = [own, up1, down1, up2, down2, up3, down3, up4, down4]
    return pieces + [pair_x(piece) for piece in pieces]


def pack_kernel(*refs):
    pieces = refs[:18]
    matrix, shared, sem = refs[18:]
    x, z, _ = place()
    copies = []
    for i, piece in enumerate(pieces):
        side = lax.rem(x + i // 9, 2)
        step, first, count = ORIGINS[i % 9]
        start = lax.rem(z + step + Z, Z) * ROWS + first
        rows = at_place(start, count)
        for j, (target, size, offset) in enumerate(((matrix, HALF, 0), (shared, QUARTER, HALF))):
            copy = pltpu.make_async_copy(
                piece.at[:, pl.ds(offset, size)],
                target.at[rows, at_place(side * size, size)],
                sem.at[i, j],
            )
            copy.start()
            copies.append(copy)
    for copy in copies:
        copy.wait()


def pack(pieces):
    return pl.pallas_call(
        pack_kernel,
        out_shape=(shape(DIM, FF), shape(DIM, HALF)),
        in_specs=[ANY] * 18,
        out_specs=(VMEM, VMEM),
        scratch_shapes=[pltpu.SemaphoreType.DMA((18, 2))],
        compiler_params=params(),
        cost_estimate=cost(0, 3 << 20),
        name="pack",
    )(*pieces)


def gram_of(parts):
    gram = dot(parts[0], parts[0], ((1,), (1,)))
    for part in parts[1:]:
        gram += dot(part, part, ((1,), (1,)))
    gram = gram.astype(BF)
    gram_float = gram.astype(F32)
    level = jnp.sqrt(jnp.sum(gram_float * gram_float, keepdims=True)) + norm_eps
    half = 0.5 / level
    diagonal = lax.broadcasted_iota(jnp.int32, (DIM, DIM), 0) == lax.broadcasted_iota(
        jnp.int32, (DIM, DIM), 1
    )
    first_poly = (jnp.where(diagonal, 1.5, 0.0) - gram_float * half).astype(BF)
    return gram, first_poly, half, upd_scale / jnp.sqrt(level)


def combine(rows, offset, gram, first_poly, half):
    squared = dot(rows, first_poly, ((1,), (0,))).astype(BF)
    moved = dot(squared, gram, ((1,), (0,)))
    diagonal = lax.broadcasted_iota(jnp.int32, moved.shape, 0) + offset == lax.broadcasted_iota(
        jnp.int32, moved.shape, 1
    )
    second_poly = (jnp.where(diagonal, 1.5, 0.0) - moved * half).astype(BF)
    return dot(second_poly, first_poly, ((1,), (0,))).astype(BF)


def project_kernel(scaled, weights, query_own, query_core, query_far, query_far_core, out, w, q, sem):
    x, _, c = place()
    load = pltpu.make_async_copy(weights.at[c, x // 2], w, sem)
    load.start()
    tokens = query_own.shape[0]
    q[at_place(c * tokens, tokens), :] = query_own[...]
    q[at_place((1 - c) * tokens, tokens), :] = query_core[...]
    q[at_place((2 + c) * tokens, tokens), :] = query_far[...]
    q[at_place((3 - c) * tokens, tokens), :] = query_far_core[...]
    gram, first_poly, half, factor = gram_of([scaled[...]])
    combined = combine(first_poly, 0, gram, first_poly, half)
    update = dot(combined, scaled[...], ((1,), (0,))) * factor
    load.wait()
    renewed = (w[...].astype(F32) - update).astype(BF)
    out[...] = dot(q[...], renewed, ((1,), (0,)))


def project(scaled, weights, *queries):
    tokens = queries[0].shape[0]
    return pl.pallas_call(
        project_kernel,
        out_shape=shape(4 * tokens, FF, dtype=F32),
        in_specs=[VMEM, ANY] + [VMEM] * 4,
        out_specs=VMEM,
        scratch_shapes=[
            pltpu.VMEM((DIM, FF), BF),
            pltpu.VMEM((4 * tokens, DIM), BF),
            pltpu.SemaphoreType.DMA,
        ],
        compiler_params=params(),
        cost_estimate=cost(22 * 10**8, 5 << 20),
        name="project",
    )(scaled, weights, *queries)


def third_kernel(mine, other, weights, out, scaled, w, poly, sem):
    x, _, c = place()
    rows = DIM // 2
    load = pltpu.make_async_copy(weights.at[2, x // 2, at_place(c * rows, rows)], w, sem)
    load.start()
    for side in range(2):
        cols = slice(side * QUARTER, (side + 1) * QUARTER)
        scaled[:, at_place(side * HALF + c * QUARTER, QUARTER)] = mine[:, cols]
        scaled[:, at_place(side * HALF + (1 - c) * QUARTER, QUARTER)] = other[:, cols]
    gram, first_poly, half, factor = gram_of([scaled[...]])
    poly[...] = first_poly
    combined = combine(poly[at_place(c * rows, rows), :], c * rows, gram, first_poly, half)
    update = dot(combined, scaled[...], ((1,), (0,))) * factor
    load.wait()
    out[...] = (w[...].astype(F32) - update).astype(BF)


def renew_third(mine, other, weights):
    rows = DIM // 2
    return pl.pallas_call(
        third_kernel,
        out_shape=shape(rows, FF),
        in_specs=[VMEM, VMEM, ANY],
        out_specs=VMEM,
        scratch_shapes=[
            pltpu.VMEM((DIM, FF), BF),
            pltpu.VMEM((rows, FF), BF),
            pltpu.VMEM((DIM, DIM), BF),
            pltpu.SemaphoreType.DMA,
        ],
        compiler_params=params(),
        cost_estimate=cost(12 * 10**8, 4 << 20),
        name="renew_third",
    )(mine, other, weights)


def down_kernel(mine, other, rows, own, core, far, far_core, gated, result):
    _, _, c = place()

    @pl.when(c == 0)
    def _():
        first_proj = mine[...]
        gated[...] = (first_proj * jax.nn.sigmoid(first_proj) * other[...]).astype(BF)

    @pl.when(c == 1)
    def _():
        first_proj = other[...]
        gated[...] = (first_proj * jax.nn.sigmoid(first_proj) * mine[...]).astype(BF)

    result[...] = dot(gated[...], rows[...], ((1,), (1,))).astype(BF)
    tokens = own.shape[0]
    own[...] = result[at_place(c * tokens, tokens), :]
    core[...] = result[at_place((1 - c) * tokens, tokens), :]
    far[...] = result[at_place((2 + c) * tokens, tokens), :]
    far_core[...] = result[at_place((3 - c) * tokens, tokens), :]


def down(mine, other, rows):
    tokens = mine.shape[0] // 4
    part = shape(tokens, DIM // 2)
    return pl.pallas_call(
        down_kernel,
        out_shape=(part,) * 4,
        in_specs=[VMEM] * 3,
        out_specs=(VMEM,) * 4,
        scratch_shapes=[pltpu.VMEM((4 * tokens, FF), BF), pltpu.VMEM((4 * tokens, DIM // 2), BF)],
        compiler_params=params(),
        cost_estimate=cost(3 * 10**8, 3 << 20),
        name="down",
    )(mine, other, rows)


def finish_kernel(first_out, own, core, far, far_core, out):
    x, _, c = place()
    half = DIM // 2
    here, there = x // 2 * DIM, (1 - x // 2) * DIM
    out[0] = first_out[...]
    out[1, :, at_place(here + c * half, half)] = own[...]
    out[1, :, at_place(here + (1 - c) * half, half)] = core[...]
    out[1, :, at_place(there + c * half, half)] = far[...]
    out[1, :, at_place(there + (1 - c) * half, half)] = far_core[...]


def finish(first_out, *parts):
    return pl.pallas_call(
        finish_kernel,
        out_shape=shape(2, *first_out.shape),
        in_specs=[VMEM] * 5,
        out_specs=VMEM,
        name="finish",
    )(first_out, *parts)


def body(queries, keys, values, rates, weights):
    own, far1, far2, far3, query_own, query_far = prepare(queries, keys, values, rates)
    queries_late, own = lax.optimization_barrier((queries, own))
    first_out = first_block(queries_late, weights)
    got = [own, along_x(far1, 1), along_x(far2, 2), along_x(far3, 3)]
    got += [other_core(piece) for piece in got]
    got, first_out = lax.optimization_barrier((got, first_out))
    parts = gradient(got, weights)
    query_far, parts = lax.optimization_barrier((query_far, parts))
    query_far = mirror_x(query_far)
    query_core, query_far_core = other_core(query_own), other_core(query_far)
    pieces = gather_rows(reduce_rows(parts))
    matrix, shared = pack(pieces)
    shared_core = other_core(shared)
    projected = project(matrix, weights, query_own, query_core, query_far, query_far_core)
    projected_core = other_core(projected)
    rows = renew_third(shared, shared_core, weights)
    own, core, far, far_core = down(projected, projected_core, rows)
    return finish(first_out, own, other_core(core), mirror_x(far), mirror_x_core(far_core))


def solution(mesh):
    in_specs = (
        P(None, ("dp", "ctx"), None),
        P(None, ("dp", "ctx"), None),
        P(None, ("dp", "ctx"), None),
        P(None, None, ("dp", "ctx")),
        P(),
    )
    out_specs = P(None, ("dp", "ctx"), None)
    return jax.shard_map(body, mesh=mesh, in_specs=in_specs, out_specs=out_specs, check_vma=False)
```

time: 112 us -> 105 us (0.938)
  starting transfers between devices: 67 us -> 61.2 us
  matrix products: 5.45 us -> 0 us
  Pallas kernels: 17.3 us -> 22.4 us
  waiting for transfers between devices: 17.8 us -> 12.8 us
  local copies, waits for them, and re-layouts: 2.76 us -> 7.65 us
    unnamed x8 -> x42, local copies, waits for them, and re-layouts: 0.92 us -> 7.64 us
    ppermute x47 -> x40, starting transfers between devices: 67 us -> 61.2 us  [move(): return lax.ppermute(array, 'ctx', perm)]
    dot_general x2 -> x0, matrix products: 5.45 us -> none  [the longest x1 3.39 us: apply_block(): jnp.einsum('thf,hdf->thd', gated_hidden, weights[2], preferred_element_ty...]
    pallas_call x2 -> x9, Pallas kernels: 15.1 us -> 20.3 us  [the longest x1 4.21 us: project(): pl.pallas_call(project_kernel, out_shape=shape(4 * tokens, FF, dtype=F32)...]
    ppermute x47 -> x40, waiting for transfers between devices: 17.8 us -> 12.8 us  [move(): return lax.ppermute(array, 'ctx', perm)]
    squeeze x1 -> x0, local copies, waits for them, and re-layouts: 1.64 us -> none  [body(): queries[1]]
  transfers between devices with their start and end apart: 47 -> 40, of which waited for: 8 -> 10; matrix products, arithmetic and copies ran while one was open for 5% -> 0% of each run, Pallas kernels for 0% -> 10%
where the time goes in v2:
time: 105 us; the launch traced here: 104 us
  starting transfers between devices  61.2 us (58%)
  Pallas kernels  22.4 us (21%)
  waiting for transfers between devices  12.8 us (12%)
  local copies, waits for them, and re-layouts  7.65 us (7%)
    ppermute x40, starting transfers between devices, move(): return lax.ppermute(array, 'ctx', perm)  61.2 us
    ppermute x40, waiting for transfers between devices, move(): return lax.ppermute(array, 'ctx', perm)  12.8 us
    unnamed x42, local copies, waits for them, and re-layouts  7.64 us
    pallas_call x1, Pallas kernels, project(): pl.pallas_call(project_kernel, out_shape=shape(4 * tokens, FF, dtype=F32)...  4.21 us
    pallas_call x1, Pallas kernels, gradient(): pl.pallas_call(gradient_kernel, out_shape=(kept, sent, sent, kept, kept,...  3.52 us
    pallas_call x1, Pallas kernels, first_block(): pl.pallas_call(first_kernel, out_shape=shape(tokens, 2 * DIM), in_specs=[...  3.45 us
    pallas_call x1, Pallas kernels, renew_third(): pl.pallas_call(third_kernel, out_shape=shape(rows, FF), in_specs=[VMEM, V...  2.43 us
    pallas_call x1, Pallas kernels, prepare(): pl.pallas_call(prepare_kernel, out_shape=(pair, pair, pair, pair, half, h...  2.12 us
  transfers between devices with their start and end apart: 40, of which 10 were waited for; matrix products, arithmetic and copies ran while one was open for 0% of the time, Pallas kernels for 10%

profile of v2, /device:TPU:1, one launch (start us, length us, event | category | flops | bytes accessed | tf_op | source)
XLA Modules:
  0.0 104.3 jit_solution(12614831078628979484)
XLA Ops:
  0.0 2.1 %prepare.1 = (bf16[128,512]{1,0:T(8,128)(2,1)}, bf16[128,512]{1,0:T(8,128)(2,1)}, bf16[128,512]{1,0:T(8,128)(2,1)}, bf16[128,512]{1,0:T(8,128)(2,1)}, bf16[64,512]{1,0:T(8,128)(2,1)}, /*index=5*/bf16[64,512]{1,0:T(8,128)(2,1)}) custom-call(bf16[2,64,1024]{2,1,0:T(8,128)(2,1)} %queries.2, bf16[1,64,1024]{2,1,0:T(8,128)(2,1)} %keys.1, ...), custom_call_target="tpu_custom_call" | custom-call | tf_op jit(solution)/shard_map/prepare/pallas_call | solution.py:110
  2.1 2.0 %collective-permute-start = (bf16[128,512]{1,0:T(8,128)(2,1)}, bf16[128,512]{1,0:T(8,128)(2,1)S(1)}, u32[]{:S(2)}, u32[]{:S(2)}) collective-permute-start(bf16[128,512]{1,0:T(8,128)(2,1)} %get-tuple-element.51), channel_id=1, source_target_pairs={{0,16},{1,17},{2,18},{3,19},{4,20},{5,21},{6,22},{7,23},{8,24},{9,... | collective-permute-start | bytes 393224 | tf_op jit(solution)/shard_map/ppermute | solution.py:33
  4.2 2.4 %collective-permute-start.1 = (bf16[128,512]{1,0:T(8,128)(2,1)}, bf16[128,512]{1,0:T(8,128)(2,1)S(1)}, u32[]{:S(2)}, u32[]{:S(2)}) collective-permute-start(bf16[128,512]{1,0:T(8,128)(2,1)} %get-tuple-element.52), channel_id=1, source_target_pairs={{0,32},{1,33},{2,34},{3,35},{4,36},{5,37},{6,38},{7,39},{8,40},{9,... | collective-permute-start | bytes 393224 | tf_op jit(solution)/shard_map/ppermute | solution.py:33
  6.6 1.1 %collective-permute-start.2 = (bf16[128,512]{1,0:T(8,128)(2,1)}, bf16[128,512]{1,0:T(8,128)(2,1)S(1)}, u32[]{:S(2)}, u32[]{:S(2)}) collective-permute-start(bf16[128,512]{1,0:T(8,128)(2,1)} %get-tuple-element.53), channel_id=1, source_target_pairs={{0,48},{1,49},{2,50},{3,51},{4,52},{5,53},{6,54},{7,55},{8,56},{9,... | collective-permute-start | bytes 393224 | tf_op jit(solution)/shard_map/ppermute | solution.py:33
  7.7 1.5 %collective-permute-start.3 = (bf16[128,512]{1,0:T(8,128)(2,1)}, bf16[128,512]{1,0:T(8,128)(2,1)S(1)}, u32[]{:S(2)}, u32[]{:S(2)}) collective-permute-start(bf16[128,512]{1,0:T(8,128)(2,1)} %get-tuple-element.57.refs_0_), channel_id=1, source_target_pairs={{0,1},{1,0},{2,3},{3,2},{4,5},{5,4},{6,7},{7,6},{8,9},{9,8},{10,11... | collective-permute-start | bytes 393224 | tf_op jit(solution)/shard_map/ppermute | solution.py:33
  9.3 5.2 %collective-permute-start.4 = (bf16[128,512]{1,0:T(8,128)(2,1)S(1)}, bf16[128,512]{1,0:T(8,128)(2,1)S(1)}, u32[]{:S(2)}, u32[]{:S(2)}) collective-permute-start(bf16[128,512]{1,0:T(8,128)(2,1)S(1)} %collective-permute-done.refs_1_), channel_id=1, source_target_pairs={{0,1},{1,0},{2,3},{3,2},{4,5},{5,4},{6,7},{7,6},{8,9},{9,8},{10,11... | collective-permute-start | bytes 393224 | tf_op jit(solution)/shard_map/ppermute | solution.py:33
  15.0 0.9 copy-done
  15.9 3.4 %first_block.1.first_out = bf16[64,1024]{1,0:T(8,128)(2,1)S(1)} custom-call(bf16[2,64,1024]{2,1,0:T(8,128)(2,1)S(1)} %copy-done, bf16[3,2,512,1024]{3,2,1,0:T(8,128)(2,1)} %weights.5), custom_call_target="tpu_custom_call" | custom-call | flops 402653184 | bytes 7340032 | tf_op jit(solution)/shard_map/first_block/pallas_call | solution.py:140
  20.1 3.5 %gradient.1 = (f32[64,768]{1,0:T(8,128)S(1)}, bf16[64,768]{1,0:T(8,128)(2,1)S(1)}, bf16[64,768]{1,0:T(8,128)(2,1)S(1)}, f32[64,768]{1,0:T(8,128)S(1)}, f32[64,76...) custom-call(bf16[128,512]{1,0:T(8,128)(2,1)S(1)} %copy-done.6, ...), custom_call_target="tpu_custom_call" | custom-call | flops 1342177280 | bytes 6291456 | tf_op jit(solution)/shard_map/gradient/pallas_call | solution.py:207
  23.6 0.7 copy-done.3
  24.3 0.7 copy-done.4
  25.0 0.7 copy-done.5
  25.6 4.7 %collective-permute-start.10 = (bf16[64,768]{1,0:T(8,128)(2,1)S(1)}, bf16[64,768]{1,0:T(8,128)(2,1)S(1)}, u32[]{:S(2)}, u32[]{:S(2)}) collective-permute-start(bf16[64,768]{1,0:T(8,128)(2,1)S(1)} %get-tuple-element.80), channel_id=1, source_target_pairs={{0,14},{1,15},{2,0},{3,1},{4,2},{5,3},{6,4},{7,5},{8,6},{9,7},{10,... | collective-permute-start | bytes 294920 | tf_op jit(solution)/shard_map/ppermute | solution.py:33
  30.3 3.6 %collective-permute-start.12 = (bf16[32,768]{1,0:T(8,128)(2,1)S(1)}, bf16[32,768]{1,0:T(8,128)(2,1)S(1)}, u32[]{:S(2)}, u32[]{:S(2)}) collective-permute-start(bf16[32,768]{1,0:T(8,128)(2,1)S(1)} %get-tuple-element.82), channel_id=1, source_target_pairs={{0,12},{1,13},{2,14},{3,15},{4,0},{5,1},{6,2},{7,3},{8,4},{9,5},{1... | collective-permute-start | bytes 147464 | tf_op jit(solution)/shard_map/ppermute | solution.py:33
  34.2 1.7 %collective-permute-done.11.far_up = bf16[32,768]{1,0:T(8,128)(2,1)S(1)} collective-permute-done((bf16[32,768]{1,0:T(8,128)(2,1)S(1)}, bf16[32,768]{1,0:T(8,128)(2,1)S(1)}, u32[]{:S(2)}, u32[]{:S(2)}) %collective-permute-start.11) | collective-permute-done | bytes 49184 | tf_op jit(solution)/shard_map/ppermute | solution.py:33
  35.9 1.5 %collective-permute-start.8 = (bf16[64,768]{1,0:T(8,128)(2,1)S(1)}, bf16[64,768]{1,0:T(8,128)(2,1)S(1)}, u32[]{:S(2)}, u32[]{:S(2)}) collective-permute-start(bf16[64,768]{1,0:T(8,128)(2,1)S(1)} %get-tuple-element.76), channel_id=1, source_target_pairs={{0,14},{1,15},{2,0},{3,1},{4,2},{5,3},{6,4},{7,5},{8,6},{9,7},{10,... | collective-permute-start | bytes 294920 | tf_op jit(solution)/shard_map/ppermute | solution.py:33
  38.7 1.8 %middle.1 = (bf16[64,768]{1,0:T(8,128)(2,1)}, bf16[64,768]{1,0:T(8,128)(2,1)}) custom-call(f32[64,768]{1,0:T(8,128)} %copy-done.4, f32[64,768]{1,0:T(8,128)} %copy-done.5, bf16[64,768]{1,0:T(8,128)(2,1)} %copy-done.12, bf16[64,768]{1,0:T(8,128)(2,1)} %copy-done.11, bf16[32,768]{1,0:T(8,128)(2,1)} %copy-done.15, bf16[32,768]{1,0:T(8,128)(2,1)} %copy-done.16), custom_call_target="tpu_custom_call" | custom-call | tf_op jit(solution)/shard_map/middle/pallas_call | solution.py:238
  40.5 1.4 %collective-permute-start.13 = (bf16[64,768]{1,0:T(8,128)(2,1)}, bf16[64,768]{1,0:T(8,128)(2,1)S(1)}, u32[]{:S(2)}, u32[]{:S(2)}) collective-permute-start(bf16[64,768]{1,0:T(8,128)(2,1)} %get-tuple-element.83), channel_id=1, source_target_pairs={{0,4},{1,5},{2,6},{3,7},{4,8},{5,9},{6,10},{7,11},{8,12},{9,13},{1... | collective-permute-start | bytes 294920 | tf_op jit(solution)/shard_map/ppermute | solution.py:33
  41.9 2.2 %collective-permute-start.14 = (bf16[64,768]{1,0:T(8,128)(2,1)}, bf16[64,768]{1,0:T(8,128)(2,1)S(1)}, u32[]{:S(2)}, u32[]{:S(2)}) collective-permute-start(bf16[64,768]{1,0:T(8,128)(2,1)} %get-tuple-element.84), channel_id=1, source_target_pairs={{0,12},{1,13},{2,14},{3,15},{4,0},{5,1},{6,2},{7,3},{8,4},{9,5},{1... | collective-permute-start | bytes 294920 | tf_op jit(solution)/shard_map/ppermute | solution.py:33
  44.1 1.8 %collective-permute-start.33 = (bf16[64,512]{1,0:T(8,128)(2,1)S(1)}, bf16[64,512]{1,0:T(8,128)(2,1)S(1)}, u32[]{:S(2)}, u32[]{:S(2)}) collective-permute-start(bf16[64,512]{1,0:T(8,128)(2,1)S(1)} %copy-done.20), channel_id=1, source_target_pairs={{0,48},{1,49},{2,50},{3,51},{4,52},{5,53},{6,54},{7,55},{8,56},{9,... | collective-permute-start | bytes 196616 | tf_op jit(solution)/shard_map/ppermute | solution.py:33
  45.9 0.7 collective-permute-done.13.c
  46.6 1.0 collective-permute-done.14.d
  48.2 1.8 %add_up.1.refs_0_ = bf16[64,768]{1,0:T(8,128)(2,1)} custom-call(f32[64,768]{1,0:T(8,128)} %copy-done.3, bf16[64,768]{1,0:T(8,128)(2,1)} %copy-done.9, bf16[64,768]{1,0:T(8,128)(2,1)} %copy-done.10, bf16[64,768]{1,0:T(8,128)(2,1)} %copy-done.13, bf16[64,768]{1,0:T(8,128)(2,1)} %copy-done.14), custom_call_target="tpu_custom_call" | custom-call | tf_op jit(solution)/shard_map/add_up/pallas_call | solution.py:253
  50.0 2.0 %collective-permute-start.17 = (bf16[64,768]{1,0:T(8,128)(2,1)}, bf16[64,768]{1,0:T(8,128)(2,1)S(1)}, u32[]{:S(2)}, u32[]{:S(2)}) collective-permute-start(bf16[64,768]{1,0:T(8,128)(2,1)} %add_up.1.refs_0_), channel_id=1, source_target_pairs={{0,4},{1,5},{2,6},{3,7},{4,8},{5,9},{6,10},{7,11},{8,12},{9,13},{1... | collective-permute-start | bytes 294920 | tf_op jit(solution)/shard_map/ppermute | solution.py:33
  52.0 1.6 %collective-permute-start.18 = (bf16[64,768]{1,0:T(8,128)(2,1)}, bf16[64,768]{1,0:T(8,128)(2,1)S(1)}, u32[]{:S(2)}, u32[]{:S(2)}) collective-permute-start(bf16[64,768]{1,0:T(8,128)(2,1)} %add_up.1.refs_0_), channel_id=1, source_target_pairs={{0,12},{1,13},{2,14},{3,15},{4,0},{5,1},{6,2},{7,3},{8,4},{9,5},{1... | collective-permute-start | bytes 294920 | tf_op jit(solution)/shard_map/ppermute | solution.py:33
  53.9 2.4 %collective-permute-start.16 = (bf16[64,768]{1,0:T(8,128)(2,1)}, bf16[64,768]{1,0:T(8,128)(2,1)S(1)}, u32[]{:S(2)}, u32[]{:S(2)}) collective-permute-start(bf16[64,768]{1,0:T(8,128)(2,1)} %add_up.1.refs_0_), channel_id=1, source_target_pairs={{0,14},{1,15},{2,0},{3,1},{4,2},{5,3},{6,4},{7,5},{8,6},{9,7},{10,... | collective-permute-start | bytes 294920 | tf_op jit(solution)/shard_map/ppermute | solution.py:33
  56.3 1.4 %collective-permute-start.23 = (bf16[64,768]{1,0:T(8,128)(2,1)}, bf16[64,768]{1,0:T(8,128)(2,1)S(1)}, u32[]{:S(2)}, u32[]{:S(2)}) collective-permute-start(bf16[64,768]{1,0:T(8,128)(2,1)} %add_up.1.refs_0_), channel_id=1, source_target_pairs={{0,16},{1,17},{2,18},{3,19},{4,20},{5,21},{6,22},{7,23},{8,24},{9,... | collective-permute-start | bytes 294920 | tf_op jit(solution)/shard_map/ppermute | solution.py:33
  57.7 1.9 %collective-permute-start.21 = (bf16[32,768]{1,0:T(8,128)(2,1)S(1)}, bf16[32,768]{1,0:T(8,128)(2,1)S(1)}, u32[]{:S(2)}, u32[]{:S(2)}) collective-permute-start(bf16[32,768]{1,0:T(8,128)(2,1)S(1)} %slice.8), channel_id=1, source_target_pairs={{0,4},{1,5},{2,6},{3,7},{4,8},{5,9},{6,10},{7,11},{8,12},{9,13},{1... | collective-permute-start | bytes 147464 | tf_op jit(solution)/shard_map/ppermute | solution.py:33
  59.7 1.7 %collective-permute-start.22 = (bf16[32,768]{1,0:T(8,128)(2,1)S(1)}, bf16[32,768]{1,0:T(8,128)(2,1)S(1)}, u32[]{:S(2)}, u32[]{:S(2)}) collective-permute-start(bf16[32,768]{1,0:T(8,128)(2,1)S(1)} %slice.9), channel_id=1, source_target_pairs={{0,12},{1,13},{2,14},{3,15},{4,0},{5,1},{6,2},{7,3},{8,4},{9,5},{1... | collective-permute-start | bytes 147464 | tf_op jit(solution)/shard_map/ppermute | solution.py:33
  61.4 1.4 %collective-permute-start.20 = (bf16[64,768]{1,0:T(8,128)(2,1)S(1)}, bf16[64,768]{1,0:T(8,128)(2,1)S(1)}, u32[]{:S(2)}, u32[]{:S(2)}) collective-permute-start(bf16[64,768]{1,0:T(8,128)(2,1)S(1)} %collective-permute-done.18.refs_4_), channel_id=1, source_target_pairs={{0,14},{1,15},{2,0},{3,1},{4,2},{5,3},{6,4},{7,5},{8,6},{9,7},{10,... | collective-permute-start | bytes 294920 | tf_op jit(solution)/shard_map/ppermute | solution.py:33
  64.1 1.6 %collective-permute-start.25 = (bf16[64,768]{1,0:T(8,128)(2,1)S(1)}, bf16[64,768]{1,0:T(8,128)(2,1)S(1)}, u32[]{:S(2)}, u32[]{:S(2)}) collective-permute-start(bf16[64,768]{1,0:T(8,128)(2,1)S(1)} %collective-permute-done.16.refs_2_), channel_id=1, source_target_pairs={{0,16},{1,17},{2,18},{3,19},{4,20},{5,21},{6,22},{7,23},{8,24},{9,... | collective-permute-start | bytes 294920 | tf_op jit(solution)/shard_map/ppermute | solution.py:33
  65.7 1.4 %collective-permute-start.27 = (bf16[64,768]{1,0:T(8,128)(2,1)S(1)}, bf16[64,768]{1,0:T(8,128)(2,1)S(1)}, u32[]{:S(2)}, u32[]{:S(2)}) collective-permute-start(bf16[64,768]{1,0:T(8,128)(2,1)S(1)} %collective-permute-done.18.refs_4_), channel_id=1, source_target_pairs={{0,16},{1,17},{2,18},{3,19},{4,20},{5,21},{6,22},{7,23},{8,24},{9,... | collective-permute-start | bytes 294920 | tf_op jit(solution)/shard_map/ppermute | solution.py:33
  67.3 1.4 %collective-permute-start.28 = (bf16[64,768]{1,0:T(8,128)(2,1)S(1)}, bf16[64,768]{1,0:T(8,128)(2,1)S(1)}, u32[]{:S(2)}, u32[]{:S(2)}) collective-permute-start(bf16[64,768]{1,0:T(8,128)(2,1)S(1)} %collective-permute-done.19.refs_5_), channel_id=1, source_target_pairs={{0,16},{1,17},{2,18},{3,19},{4,20},{5,21},{6,22},{7,23},{8,24},{9,... | collective-permute-start | bytes 294920 | tf_op jit(solution)/shard_map/ppermute | solution.py:33
  69.4 7.6 %collective-permute-start.32 = (bf16[64,512]{1,0:T(8,128)(2,1)S(1)}, bf16[64,512]{1,0:T(8,128)(2,1)S(1)}, u32[]{:S(2)}, u32[]{:S(2)}) collective-permute-start(bf16[64,512]{1,0:T(8,128)(2,1)S(1)} %copy-done.7), channel_id=1, source_target_pairs={{0,1},{1,0},{2,3},{3,2},{4,5},{5,4},{6,7},{7,6},{8,9},{9,8},{10,11... | collective-permute-start | bytes 196616 | tf_op jit(solution)/shard_map/ppermute | solution.py:33
  77.0 0.8 collective-permute-start.34
  77.8 1.0 collective-permute-start.31
  78.8 1.9 %collective-permute-done.31.refs_17_ = bf16[32,768]{1,0:T(8,128)(2,1)S(1)} collective-permute-done((bf16[32,768]{1,0:T(8,128)(2,1)S(1)}, bf16[32,768]{1,0:T(8,128)(2,1)S(1)}, u32[]{:S(2)}, u32[]{:S(2)}) %collective-permute-start.31) | collective-permute-done | bytes 49184 | tf_op jit(solution)/shard_map/ppermute | solution.py:33
  80.7 0.9 copy-done.2
  81.6 0.8 pack.1
  82.4 4.2 %project.1.mine = f32[256,1024]{1,0:T(8,128)S(1)} custom-call(bf16[512,1024]{1,0:T(8,128)(2,1)S(1)} %get-tuple-element.85.scaled, bf16[3,2,512,1024]{3,2,1,0:T(8,128)(2,1)} %weights.5, bf16[64,512]{1,0:T(8,128)(2,1)S(1)} %copy-done.7, bf16[64,512]{1,0:T(8,128)(2,1)S(1)} %collective-permute-done.32.query_core, ...), custom_call_target="tpu_custom_call" | custom-call | flops 2200000000 | bytes 5242880 | tf_op jit(solution)/shard_map/project/pallas_call | solution.py:368
  86.6 1.8 %collective-permute-start.35 = (f32[256,1024]{1,0:T(8,128)S(1)}, f32[256,1024]{1,0:T(8,128)S(1)}, u32[]{:S(2)}, u32[]{:S(2)}) collective-permute-start(f32[256,1024]{1,0:T(8,128)S(1)} %project.1.mine), channel_id=1, source_target_pairs={{0,1},{1,0},{2,3},{3,2},{4,5},{5,4},{6,7},{7,6},{8,9},{9,8},{10,11... | collective-permute-start | bytes 3145736 | tf_op jit(solution)/shard_map/ppermute | solution.py:33
  88.5 2.9 %collective-permute-done.36.other = bf16[512,512]{1,0:T(8,128)(2,1)S(1)} collective-permute-done((bf16[512,512]{1,0:T(8,128)(2,1)S(1)}, bf16[512,512]{1,0:T(8,128)(2,1)S(1)}, u32[]{:S(2)}, u32[]{:S(2)}) %collective-permute-start.36) | collective-permute-done | bytes 524320 | tf_op jit(solution)/shard_map/ppermute | solution.py:33
  91.4 2.4 %renew_third.1.rows = bf16[256,1024]{1,0:T(8,128)(2,1)S(1)} custom-call(bf16[512,512]{1,0:T(8,128)(2,1)S(1)} %get-tuple-element.88.mine, bf16[512,512]{1,0:T(8,128)(2,1)S(1)} %collective-permute-done.36.other, bf16[3,2,512,1024]{3,2,1,0:T(8,128)(2,1)} %weights.5), custom_call_target="tpu_custom_call" | custom-call | flops 1200000000 | bytes 4194304 | tf_op jit(solution)/shard_map/renew_third/pallas_call | solution.py:403
  95.4 1.9 %collective-permute-start.38 = (bf16[64,256]{1,0:T(8,128)(2,1)S(1)}, bf16[64,256]{1,0:T(8,128)(2,1)S(1)}, u32[]{:S(2)}, u32[]{:S(2)}) collective-permute-start(bf16[64,256]{1,0:T(8,128)(2,1)S(1)} %get-tuple-element.91), channel_id=1, source_target_pairs={{0,48},{1,49},{2,50},{3,51},{4,52},{5,53},{6,54},{7,55},{8,56},{9,... | collective-permute-start | bytes 98312 | tf_op jit(solution)/shard_map/ppermute | solution.py:33
  97.3 1.1 %collective-permute-start.39 = (bf16[64,256]{1,0:T(8,128)(2,1)S(1)}, bf16[64,256]{1,0:T(8,128)(2,1)S(1)}, u32[]{:S(2)}, u32[]{:S(2)}) collective-permute-start(bf16[64,256]{1,0:T(8,128)(2,1)S(1)} %get-tuple-element.92), channel_id=1, source_target_pairs={{0,49},{1,48},{2,51},{3,50},{4,53},{5,52},{6,55},{7,54},{8,57},{9,... | collective-permute-start | bytes 98312 | tf_op jit(solution)/shard_map/ppermute | solution.py:33
  98.4 1.0 collective-permute-done.38.far
  99.4 2.6 %collective-permute-done.39.far_core = bf16[64,256]{1,0:T(8,128)(2,1)S(1)} collective-permute-done((bf16[64,256]{1,0:T(8,128)(2,1)S(1)}, bf16[64,256]{1,0:T(8,128)(2,1)S(1)}, u32[]{:S(2)}, u32[]{:S(2)}) %collective-permute-start.39) | collective-permute-done | bytes 32800 | tf_op jit(solution)/shard_map/ppermute | solution.py:33
  102.6 1.7 %finish.1 = bf16[2,64,1024]{2,1,0:T(8,128)(2,1)} custom-call(bf16[64,1024]{1,0:T(8,128)(2,1)} %copy-done.1, bf16[64,256]{1,0:T(8,128)(2,1)} %copy-done.8, bf16[64,256]{1,0:T(8,128)(2,1)} %copy-done.17, bf16[64,256]{1,0:T(8,128)(2,1)} %copy-done.18, bf16[64,256]{1,0:T(8,128)(2,1)} %copy-done.19), custom_call_target="tpu_custom_call" | custom-call | tf_op jit(solution)/shard_map/finish/pallas_call | solution.py:468
  (86 shorter events, 8.1 us)
Async XLA Ops:
  2.1 7.1 %collective-permute-start = (bf16[128,512]{1,0:T(8,128)(2,1)}, bf16[128,512]{1,0:T(8,128)(2,1)S(1)}, u32[]{:S(2)}, u32[]{:S(2)}) collective-permute-start(bf16[128,512]{1,0:T(8,128)(2,1)} %get-tuple-element.51), channel_id=1, source_target_pairs={{0,16},{1,17},{2,18},{3,19},{4,20},{5,21},{6,22},{7,23},{8,24},{9,... | collective-permute-start | bytes 393224 | tf_op jit(solution)/shard_map/ppermute | solution.py:33
  4.2 10.3 %collective-permute-start.1 = (bf16[128,512]{1,0:T(8,128)(2,1)}, bf16[128,512]{1,0:T(8,128)(2,1)S(1)}, u32[]{:S(2)}, u32[]{:S(2)}) collective-permute-start(bf16[128,512]{1,0:T(8,128)(2,1)} %get-tuple-element.52), channel_id=1, source_target_pairs={{0,32},{1,33},{2,34},{3,35},{4,36},{5,37},{6,38},{7,39},{8,40},{9,... | collective-permute-start | bytes 393224 | tf_op jit(solution)/shard_map/ppermute | solution.py:33
  6.6 7.8 %collective-permute-start.2 = (bf16[128,512]{1,0:T(8,128)(2,1)}, bf16[128,512]{1,0:T(8,128)(2,1)S(1)}, u32[]{:S(2)}, u32[]{:S(2)}) collective-permute-start(bf16[128,512]{1,0:T(8,128)(2,1)} %get-tuple-element.53), channel_id=1, source_target_pairs={{0,48},{1,49},{2,50},{3,51},{4,52},{5,53},{6,54},{7,55},{8,56},{9,... | collective-permute-start | bytes 393224 | tf_op jit(solution)/shard_map/ppermute | solution.py:33
  7.7 12.3 %collective-permute-start.3 = (bf16[128,512]{1,0:T(8,128)(2,1)}, bf16[128,512]{1,0:T(8,128)(2,1)S(1)}, u32[]{:S(2)}, u32[]{:S(2)}) collective-permute-start(bf16[128,512]{1,0:T(8,128)(2,1)} %get-tuple-element.57.refs_0_), channel_id=1, source_target_pairs={{0,1},{1,0},{2,3},{3,2},{4,5},{5,4},{6,7},{7,6},{8,9},{9,8},{10,11... | collective-permute-start | bytes 393224 | tf_op jit(solution)/shard_map/ppermute | solution.py:33
  9.3 10.8 %collective-permute-start.4 = (bf16[128,512]{1,0:T(8,128)(2,1)S(1)}, bf16[128,512]{1,0:T(8,128)(2,1)S(1)}, u32[]{:S(2)}, u32[]{:S(2)}) collective-permute-start(bf16[128,512]{1,0:T(8,128)(2,1)S(1)} %collective-permute-done.refs_1_), channel_id=1, source_target_pairs={{0,1},{1,0},{2,3},{3,2},{4,5},{5,4},{6,7},{7,6},{8,9},{9,8},{10,11... | collective-permute-start | bytes 393224 | tf_op jit(solution)/shard_map/ppermute | solution.py:33
  14.4 5.6 %collective-permute-start.5 = (bf16[128,512]{1,0:T(8,128)(2,1)S(1)}, bf16[128,512]{1,0:T(8,128)(2,1)S(1)}, u32[]{:S(2)}, u32[]{:S(2)}) collective-permute-start(bf16[128,512]{1,0:T(8,128)(2,1)S(1)} %collective-permute-done.1.refs_2_), channel_id=1, source_target_pairs={{0,1},{1,0},{2,3},{3,2},{4,5},{5,4},{6,7},{7,6},{8,9},{9,8},{10,11... | collective-permute-start | bytes 393224 | tf_op jit(solution)/shard_map/ppermute | solution.py:33
  14.5 5.6 %collective-permute-start.6 = (bf16[128,512]{1,0:T(8,128)(2,1)S(1)}, bf16[128,512]{1,0:T(8,128)(2,1)S(1)}, u32[]{:S(2)}, u32[]{:S(2)}) collective-permute-start(bf16[128,512]{1,0:T(8,128)(2,1)S(1)} %collective-permute-done.2.refs_3_), channel_id=1, source_target_pairs={{0,1},{1,0},{2,3},{3,2},{4,5},{5,4},{6,7},{7,6},{8,9},{9,8},{10,11... | collective-permute-start | bytes 393224 | tf_op jit(solution)/shard_map/ppermute | solution.py:33
  15.9 4.1 %copy-start.6 = (bf16[128,512]{1,0:T(8,128)(2,1)S(1)}, bf16[128,512]{1,0:T(8,128)(2,1)}, u32[]{:S(2)}) copy-start(bf16[128,512]{1,0:T(8,128)(2,1)} %get-tuple-element.57.refs_0_) | copy-start | bytes 393220
  15.9 28.2 %copy-start.20 = (bf16[64,512]{1,0:T(8,128)(2,1)S(1)}, bf16[64,512]{1,0:T(8,128)(2,1)}, u32[]{:S(2)}) copy-start(bf16[64,512]{1,0:T(8,128)(2,1)} %get-tuple-element.87) | copy-start | bytes 196612
  15.9 53.4 %copy-start.7 = (bf16[64,512]{1,0:T(8,128)(2,1)S(1)}, bf16[64,512]{1,0:T(8,128)(2,1)}, u32[]{:S(2)}) copy-start(bf16[64,512]{1,0:T(8,128)(2,1)} %get-tuple-element.86.query_own) | copy-start | bytes 196612
  25.6 11.8 %collective-permute-start.10 = (bf16[64,768]{1,0:T(8,128)(2,1)S(1)}, bf16[64,768]{1,0:T(8,128)(2,1)S(1)}, u32[]{:S(2)}, u32[]{:S(2)}) collective-permute-start(bf16[64,768]{1,0:T(8,128)(2,1)S(1)} %get-tuple-element.80), channel_id=1, source_target_pairs={{0,14},{1,15},{2,0},{3,1},{4,2},{5,3},{6,4},{7,5},{8,6},{9,7},{10,... | collective-permute-start | bytes 294920 | tf_op jit(solution)/shard_map/ppermute | solution.py:33
  30.3 7.1 %collective-permute-start.9 = (bf16[64,768]{1,0:T(8,128)(2,1)S(1)}, bf16[64,768]{1,0:T(8,128)(2,1)S(1)}, u32[]{:S(2)}, u32[]{:S(2)}) collective-permute-start(bf16[64,768]{1,0:T(8,128)(2,1)S(1)} %get-tuple-element.79), channel_id=1, source_target_pairs={{0,2},{1,3},{2,4},{3,5},{4,6},{5,7},{6,8},{7,9},{8,10},{9,11},{10,... | collective-permute-start | bytes 294920 | tf_op jit(solution)/shard_map/ppermute | solution.py:33
  30.3 5.6 %collective-permute-start.11 = (bf16[32,768]{1,0:T(8,128)(2,1)S(1)}, bf16[32,768]{1,0:T(8,128)(2,1)S(1)}, u32[]{:S(2)}, u32[]{:S(2)}) collective-permute-start(bf16[32,768]{1,0:T(8,128)(2,1)S(1)} %get-tuple-element.81), channel_id=1, source_target_pairs={{0,4},{1,5},{2,6},{3,7},{4,8},{5,9},{6,10},{7,11},{8,12},{9,13},{1... | collective-permute-start | bytes 147464 | tf_op jit(solution)/shard_map/ppermute | solution.py:33
  30.3 7.1 %collective-permute-start.12 = (bf16[32,768]{1,0:T(8,128)(2,1)S(1)}, bf16[32,768]{1,0:T(8,128)(2,1)S(1)}, u32[]{:S(2)}, u32[]{:S(2)}) collective-permute-start(bf16[32,768]{1,0:T(8,128)(2,1)S(1)} %get-tuple-element.82), channel_id=1, source_target_pairs={{0,12},{1,13},{2,14},{3,15},{4,0},{5,1},{6,2},{7,3},{8,4},{9,5},{1... | collective-permute-start | bytes 147464 | tf_op jit(solution)/shard_map/ppermute | solution.py:33
  33.9 12.0 %collective-permute-start.7 = (bf16[64,768]{1,0:T(8,128)(2,1)S(1)}, bf16[64,768]{1,0:T(8,128)(2,1)S(1)}, u32[]{:S(2)}, u32[]{:S(2)}) collective-permute-start(bf16[64,768]{1,0:T(8,128)(2,1)S(1)} %get-tuple-element.75), channel_id=1, source_target_pairs={{0,2},{1,3},{2,4},{3,5},{4,6},{5,7},{6,8},{7,9},{8,10},{9,11},{10,... | collective-permute-start | bytes 294920 | tf_op jit(solution)/shard_map/ppermute | solution.py:33
  35.9 1.5 %copy-start.15 = (bf16[32,768]{1,0:T(8,128)(2,1)}, bf16[32,768]{1,0:T(8,128)(2,1)S(1)}, u32[]{:S(2)}) copy-start(bf16[32,768]{1,0:T(8,128)(2,1)S(1)} %collective-permute-done.11.far_up) | copy-start | bytes 147460
  35.9 10.0 %collective-permute-start.8 = (bf16[64,768]{1,0:T(8,128)(2,1)S(1)}, bf16[64,768]{1,0:T(8,128)(2,1)S(1)}, u32[]{:S(2)}, u32[]{:S(2)}) collective-permute-start(bf16[64,768]{1,0:T(8,128)(2,1)S(1)} %get-tuple-element.76), channel_id=1, source_target_pairs={{0,14},{1,15},{2,0},{3,1},{4,2},{5,3},{6,4},{7,5},{8,6},{9,7},{10,... | collective-permute-start | bytes 294920 | tf_op jit(solution)/shard_map/ppermute | solution.py:33
  40.5 6.1 %collective-permute-start.13 = (bf16[64,768]{1,0:T(8,128)(2,1)}, bf16[64,768]{1,0:T(8,128)(2,1)S(1)}, u32[]{:S(2)}, u32[]{:S(2)}) collective-permute-start(bf16[64,768]{1,0:T(8,128)(2,1)} %get-tuple-element.83), channel_id=1, source_target_pairs={{0,4},{1,5},{2,6},{3,7},{4,8},{5,9},{6,10},{7,11},{8,12},{9,13},{1... | collective-permute-start | bytes 294920 | tf_op jit(solution)/shard_map/ppermute | solution.py:33
  41.9 5.7 %collective-permute-start.14 = (bf16[64,768]{1,0:T(8,128)(2,1)}, bf16[64,768]{1,0:T(8,128)(2,1)S(1)}, u32[]{:S(2)}, u32[]{:S(2)}) collective-permute-start(bf16[64,768]{1,0:T(8,128)(2,1)} %get-tuple-element.84), channel_id=1, source_target_pairs={{0,12},{1,13},{2,14},{3,15},{4,0},{5,1},{6,2},{7,3},{8,4},{9,5},{1... | collective-permute-start | bytes 294920 | tf_op jit(solution)/shard_map/ppermute | solution.py:33
  44.1 12.2 %collective-permute-start.33 = (bf16[64,512]{1,0:T(8,128)(2,1)S(1)}, bf16[64,512]{1,0:T(8,128)(2,1)S(1)}, u32[]{:S(2)}, u32[]{:S(2)}) collective-permute-start(bf16[64,512]{1,0:T(8,128)(2,1)S(1)} %copy-done.20), channel_id=1, source_target_pairs={{0,48},{1,49},{2,50},{3,51},{4,52},{5,53},{6,54},{7,55},{8,56},{9,... | collective-permute-start | bytes 196616 | tf_op jit(solution)/shard_map/ppermute | solution.py:33
  45.9 1.7 %copy-start.9 = (bf16[64,768]{1,0:T(8,128)(2,1)}, bf16[64,768]{1,0:T(8,128)(2,1)S(1)}, u32[]{:S(2)}) copy-start(bf16[64,768]{1,0:T(8,128)(2,1)S(1)} %collective-permute-done.7.a) | copy-start | bytes 294916
  45.9 1.7 %copy-start.10 = (bf16[64,768]{1,0:T(8,128)(2,1)}, bf16[64,768]{1,0:T(8,128)(2,1)S(1)}, u32[]{:S(2)}) copy-start(bf16[64,768]{1,0:T(8,128)(2,1)S(1)} %collective-permute-done.8.b) | copy-start | bytes 294916
  50.0 7.6 %collective-permute-start.17 = (bf16[64,768]{1,0:T(8,128)(2,1)}, bf16[64,768]{1,0:T(8,128)(2,1)S(1)}, u32[]{:S(2)}, u32[]{:S(2)}) collective-permute-start(bf16[64,768]{1,0:T(8,128)(2,1)} %add_up.1.refs_0_), channel_id=1, source_target_pairs={{0,4},{1,5},{2,6},{3,7},{4,8},{5,9},{6,10},{7,11},{8,12},{9,13},{1... | collective-permute-start | bytes 294920 | tf_op jit(solution)/shard_map/ppermute | solution.py:33
  52.0 5.7 %collective-permute-start.18 = (bf16[64,768]{1,0:T(8,128)(2,1)}, bf16[64,768]{1,0:T(8,128)(2,1)S(1)}, u32[]{:S(2)}, u32[]{:S(2)}) collective-permute-start(bf16[64,768]{1,0:T(8,128)(2,1)} %add_up.1.refs_0_), channel_id=1, source_target_pairs={{0,12},{1,13},{2,14},{3,15},{4,0},{5,1},{6,2},{7,3},{8,4},{9,5},{1... | collective-permute-start | bytes 294920 | tf_op jit(solution)/shard_map/ppermute | solution.py:33
  53.6 6.1 %collective-permute-start.15 = (bf16[64,768]{1,0:T(8,128)(2,1)}, bf16[64,768]{1,0:T(8,128)(2,1)S(1)}, u32[]{:S(2)}, u32[]{:S(2)}) collective-permute-start(bf16[64,768]{1,0:T(8,128)(2,1)} %add_up.1.refs_0_), channel_id=1, source_target_pairs={{0,2},{1,3},{2,4},{3,5},{4,6},{5,7},{6,8},{7,9},{8,10},{9,11},{10,... | collective-permute-start | bytes 294920 | tf_op jit(solution)/shard_map/ppermute | solution.py:33
  53.9 7.5 %collective-permute-start.16 = (bf16[64,768]{1,0:T(8,128)(2,1)}, bf16[64,768]{1,0:T(8,128)(2,1)S(1)}, u32[]{:S(2)}, u32[]{:S(2)}) collective-permute-start(bf16[64,768]{1,0:T(8,128)(2,1)} %add_up.1.refs_0_), channel_id=1, source_target_pairs={{0,14},{1,15},{2,0},{3,1},{4,2},{5,3},{6,4},{7,5},{8,6},{9,7},{10,... | collective-permute-start | bytes 294920 | tf_op jit(solution)/shard_map/ppermute | solution.py:33
  56.3 6.6 %collective-permute-start.23 = (bf16[64,768]{1,0:T(8,128)(2,1)}, bf16[64,768]{1,0:T(8,128)(2,1)S(1)}, u32[]{:S(2)}, u32[]{:S(2)}) collective-permute-start(bf16[64,768]{1,0:T(8,128)(2,1)} %add_up.1.refs_0_), channel_id=1, source_target_pairs={{0,16},{1,17},{2,18},{3,19},{4,20},{5,21},{6,22},{7,23},{8,24},{9,... | collective-permute-start | bytes 294920 | tf_op jit(solution)/shard_map/ppermute | solution.py:33
  57.6 8.1 %collective-permute-start.19 = (bf16[64,768]{1,0:T(8,128)(2,1)S(1)}, bf16[64,768]{1,0:T(8,128)(2,1)S(1)}, u32[]{:S(2)}, u32[]{:S(2)}) collective-permute-start(bf16[64,768]{1,0:T(8,128)(2,1)S(1)} %collective-permute-done.17.refs_3_), channel_id=1, source_target_pairs={{0,2},{1,3},{2,4},{3,5},{4,6},{5,7},{6,8},{7,9},{8,10},{9,11},{10,... | collective-permute-start | bytes 294920 | tf_op jit(solution)/shard_map/ppermute | solution.py:33
  57.7 6.4 %collective-permute-start.21 = (bf16[32,768]{1,0:T(8,128)(2,1)S(1)}, bf16[32,768]{1,0:T(8,128)(2,1)S(1)}, u32[]{:S(2)}, u32[]{:S(2)}) collective-permute-start(bf16[32,768]{1,0:T(8,128)(2,1)S(1)} %slice.8), channel_id=1, source_target_pairs={{0,4},{1,5},{2,6},{3,7},{4,8},{5,9},{6,10},{7,11},{8,12},{9,13},{1... | collective-permute-start | bytes 147464 | tf_op jit(solution)/shard_map/ppermute | solution.py:33
  59.7 6.0 %collective-permute-start.22 = (bf16[32,768]{1,0:T(8,128)(2,1)S(1)}, bf16[32,768]{1,0:T(8,128)(2,1)S(1)}, u32[]{:S(2)}, u32[]{:S(2)}) collective-permute-start(bf16[32,768]{1,0:T(8,128)(2,1)S(1)} %slice.9), channel_id=1, source_target_pairs={{0,12},{1,13},{2,14},{3,15},{4,0},{5,1},{6,2},{7,3},{8,4},{9,5},{1... | collective-permute-start | bytes 147464 | tf_op jit(solution)/shard_map/ppermute | solution.py:33
  61.4 5.8 %collective-permute-start.20 = (bf16[64,768]{1,0:T(8,128)(2,1)S(1)}, bf16[64,768]{1,0:T(8,128)(2,1)S(1)}, u32[]{:S(2)}, u32[]{:S(2)}) collective-permute-start(bf16[64,768]{1,0:T(8,128)(2,1)S(1)} %collective-permute-done.18.refs_4_), channel_id=1, source_target_pairs={{0,14},{1,15},{2,0},{3,1},{4,2},{5,3},{6,4},{7,5},{8,6},{9,7},{10,... | collective-permute-start | bytes 294920 | tf_op jit(solution)/shard_map/ppermute | solution.py:33
  62.9 4.4 %collective-permute-start.24 = (bf16[64,768]{1,0:T(8,128)(2,1)S(1)}, bf16[64,768]{1,0:T(8,128)(2,1)S(1)}, u32[]{:S(2)}, u32[]{:S(2)}) collective-permute-start(bf16[64,768]{1,0:T(8,128)(2,1)S(1)} %collective-permute-done.15.refs_1_), channel_id=1, source_target_pairs={{0,16},{1,17},{2,18},{3,19},{4,20},{5,21},{6,22},{7,23},{8,24},{9,... | collective-permute-start | bytes 294920 | tf_op jit(solution)/shard_map/ppermute | solution.py:33
  64.1 4.5 %collective-permute-start.25 = (bf16[64,768]{1,0:T(8,128)(2,1)S(1)}, bf16[64,768]{1,0:T(8,128)(2,1)S(1)}, u32[]{:S(2)}, u32[]{:S(2)}) collective-permute-start(bf16[64,768]{1,0:T(8,128)(2,1)S(1)} %collective-permute-done.16.refs_2_), channel_id=1, source_target_pairs={{0,16},{1,17},{2,18},{3,19},{4,20},{5,21},{6,22},{7,23},{8,24},{9,... | collective-permute-start | bytes 294920 | tf_op jit(solution)/shard_map/ppermute | solution.py:33
  65.7 3.7 %collective-permute-start.26 = (bf16[64,768]{1,0:T(8,128)(2,1)S(1)}, bf16[64,768]{1,0:T(8,128)(2,1)S(1)}, u32[]{:S(2)}, u32[]{:S(2)}) collective-permute-start(bf16[64,768]{1,0:T(8,128)(2,1)S(1)} %collective-permute-done.17.refs_3_), channel_id=1, source_target_pairs={{0,16},{1,17},{2,18},{3,19},{4,20},{5,21},{6,22},{7,23},{8,24},{9,... | collective-permute-start | bytes 294920 | tf_op jit(solution)/shard_map/ppermute | solution.py:33
  65.7 11.3 %collective-permute-start.27 = (bf16[64,768]{1,0:T(8,128)(2,1)S(1)}, bf16[64,768]{1,0:T(8,128)(2,1)S(1)}, u32[]{:S(2)}, u32[]{:S(2)}) collective-permute-start(bf16[64,768]{1,0:T(8,128)(2,1)S(1)} %collective-permute-done.18.refs_4_), channel_id=1, source_target_pairs={{0,16},{1,17},{2,18},{3,19},{4,20},{5,21},{6,22},{7,23},{8,24},{9,... | collective-permute-start | bytes 294920 | tf_op jit(solution)/shard_map/ppermute | solution.py:33
  67.2 10.6 %collective-permute-start.30 = (bf16[32,768]{1,0:T(8,128)(2,1)S(1)}, bf16[32,768]{1,0:T(8,128)(2,1)S(1)}, u32[]{:S(2)}, u32[]{:S(2)}) collective-permute-start(bf16[32,768]{1,0:T(8,128)(2,1)S(1)} %collective-permute-done.21.refs_7_), channel_id=1, source_target_pairs={{0,16},{1,17},{2,18},{3,19},{4,20},{5,21},{6,22},{7,23},{8,24},{9,... | collective-permute-start | bytes 147464 | tf_op jit(solution)/shard_map/ppermute | solution.py:33
  67.3 13.5 %collective-permute-start.28 = (bf16[64,768]{1,0:T(8,128)(2,1)S(1)}, bf16[64,768]{1,0:T(8,128)(2,1)S(1)}, u32[]{:S(2)}, u32[]{:S(2)}) collective-permute-start(bf16[64,768]{1,0:T(8,128)(2,1)S(1)} %collective-permute-done.19.refs_5_), channel_id=1, source_target_pairs={{0,16},{1,17},{2,18},{3,19},{4,20},{5,21},{6,22},{7,23},{8,24},{9,... | collective-permute-start | bytes 294920 | tf_op jit(solution)/shard_map/ppermute | solution.py:33
  68.6 12.1 %collective-permute-start.29 = (bf16[64,768]{1,0:T(8,128)(2,1)S(1)}, bf16[64,768]{1,0:T(8,128)(2,1)S(1)}, u32[]{:S(2)}, u32[]{:S(2)}) collective-permute-start(bf16[64,768]{1,0:T(8,128)(2,1)S(1)} %collective-permute-done.20.refs_6_), channel_id=1, source_target_pairs={{0,16},{1,17},{2,18},{3,19},{4,20},{5,21},{6,22},{7,23},{8,24},{9,... | collective-permute-start | bytes 294920 | tf_op jit(solution)/shard_map/ppermute | solution.py:33
  69.4 13.1 %collective-permute-start.32 = (bf16[64,512]{1,0:T(8,128)(2,1)S(1)}, bf16[64,512]{1,0:T(8,128)(2,1)S(1)}, u32[]{:S(2)}, u32[]{:S(2)}) collective-permute-start(bf16[64,512]{1,0:T(8,128)(2,1)S(1)} %copy-done.7), channel_id=1, source_target_pairs={{0,1},{1,0},{2,3},{3,2},{4,5},{5,4},{6,7},{7,6},{8,9},{9,8},{10,11... | collective-permute-start | bytes 196616 | tf_op jit(solution)/shard_map/ppermute | solution.py:33
  77.0 5.4 %collective-permute-start.34 = (bf16[64,512]{1,0:T(8,128)(2,1)S(1)}, bf16[64,512]{1,0:T(8,128)(2,1)S(1)}, u32[]{:S(2)}, u32[]{:S(2)}) collective-permute-start(bf16[64,512]{1,0:T(8,128)(2,1)S(1)} %collective-permute-done.33.query_far), channel_id=1, source_target_pairs={{0,1},{1,0},{2,3},{3,2},{4,5},{5,4},{6,7},{7,6},{8,9},{9,8},{10,11... | collective-permute-start | bytes 196616 | tf_op jit(solution)/shard_map/ppermute | solution.py:33
  77.8 2.9 %collective-permute-start.31 = (bf16[32,768]{1,0:T(8,128)(2,1)S(1)}, bf16[32,768]{1,0:T(8,128)(2,1)S(1)}, u32[]{:S(2)}, u32[]{:S(2)}) collective-permute-start(bf16[32,768]{1,0:T(8,128)(2,1)S(1)} %collective-permute-done.22.refs_8_), channel_id=1, source_target_pairs={{0,16},{1,17},{2,18},{3,19},{4,20},{5,21},{6,22},{7,23},{8,24},{9,... | collective-permute-start | bytes 147464 | tf_op jit(solution)/shard_map/ppermute | solution.py:33
  86.6 7.2 %collective-permute-start.35 = (f32[256,1024]{1,0:T(8,128)S(1)}, f32[256,1024]{1,0:T(8,128)S(1)}, u32[]{:S(2)}, u32[]{:S(2)}) collective-permute-start(f32[256,1024]{1,0:T(8,128)S(1)} %project.1.mine), channel_id=1, source_target_pairs={{0,1},{1,0},{2,3},{3,2},{4,5},{5,4},{6,7},{7,6},{8,9},{9,8},{10,11... | collective-permute-start | bytes 3145736 | tf_op jit(solution)/shard_map/ppermute | solution.py:33
  88.4 3.0 %collective-permute-start.36 = (bf16[512,512]{1,0:T(8,128)(2,1)S(1)}, bf16[512,512]{1,0:T(8,128)(2,1)S(1)}, u32[]{:S(2)}, u32[]{:S(2)}) collective-permute-start(bf16[512,512]{1,0:T(8,128)(2,1)S(1)} %get-tuple-element.88.mine), channel_id=1, source_target_pairs={{0,1},{1,0},{2,3},{3,2},{4,5},{5,4},{6,7},{7,6},{8,9},{9,8},{10,11... | collective-permute-start | bytes 1572872 | tf_op jit(solution)/shard_map/ppermute | solution.py:33
  95.1 3.4 %collective-permute-start.37 = (bf16[64,256]{1,0:T(8,128)(2,1)S(1)}, bf16[64,256]{1,0:T(8,128)(2,1)S(1)}, u32[]{:S(2)}, u32[]{:S(2)}) collective-permute-start(bf16[64,256]{1,0:T(8,128)(2,1)S(1)} %get-tuple-element.90), channel_id=1, source_target_pairs={{0,1},{1,0},{2,3},{3,2},{4,5},{5,4},{6,7},{7,6},{8,9},{9,8},{10,11... | collective-permute-start | bytes 98312 | tf_op jit(solution)/shard_map/ppermute | solution.py:33
  95.4 4.0 %collective-permute-start.38 = (bf16[64,256]{1,0:T(8,128)(2,1)S(1)}, bf16[64,256]{1,0:T(8,128)(2,1)S(1)}, u32[]{:S(2)}, u32[]{:S(2)}) collective-permute-start(bf16[64,256]{1,0:T(8,128)(2,1)S(1)} %get-tuple-element.91), channel_id=1, source_target_pairs={{0,48},{1,49},{2,50},{3,51},{4,52},{5,53},{6,54},{7,55},{8,56},{9,... | collective-permute-start | bytes 98312 | tf_op jit(solution)/shard_map/ppermute | solution.py:33
  97.3 4.7 %collective-permute-start.39 = (bf16[64,256]{1,0:T(8,128)(2,1)S(1)}, bf16[64,256]{1,0:T(8,128)(2,1)S(1)}, u32[]{:S(2)}, u32[]{:S(2)}) collective-permute-start(bf16[64,256]{1,0:T(8,128)(2,1)S(1)} %get-tuple-element.92), channel_id=1, source_target_pairs={{0,49},{1,48},{2,51},{3,50},{4,53},{5,52},{6,55},{7,54},{8,57},{9,... | collective-permute-start | bytes 98312 | tf_op jit(solution)/shard_map/ppermute | solution.py:33
  98.4 3.6 %copy-start.17 = (bf16[64,256]{1,0:T(8,128)(2,1)}, bf16[64,256]{1,0:T(8,128)(2,1)S(1)}, u32[]{:S(2)}) copy-start(bf16[64,256]{1,0:T(8,128)(2,1)S(1)} %collective-permute-done.37.core) | copy-start | bytes 98308
  99.4 2.6 %copy-start.18 = (bf16[64,256]{1,0:T(8,128)(2,1)}, bf16[64,256]{1,0:T(8,128)(2,1)S(1)}, u32[]{:S(2)}) copy-start(bf16[64,256]{1,0:T(8,128)(2,1)S(1)} %collective-permute-done.38.far) | copy-start | bytes 98308
  (13 other events, 9.3 us)

commit v3 on v2

--- a/solution.py
+++ b/solution.py
@@ -11,7 +11,6 @@
 WIDE = HALF + QUARTER
 ROWS = DIM // Z
 BF, F32 = jnp.bfloat16, jnp.float32
-VMEM_LIMIT = 48 * 1024 * 1024
 upd_scale = 2.0
 norm_eps = 1e-07
 VMEM = pl.BlockSpec(memory_space=pltpu.VMEM)
@@ -65,8 +64,8 @@
     return jax.ShapeDtypeStruct(dims, dtype)
 
 
-def params():
-    return pltpu.CompilerParams(vmem_limit_bytes=VMEM_LIMIT)
+def params(mib):
+    return pltpu.CompilerParams(vmem_limit_bytes=mib << 20)
 
 
 def cost(flops, size):
@@ -112,6 +111,7 @@
         out_shape=(pair, pair, pair, pair, half, half),
         in_specs=[VMEM] * 4,
         out_specs=(VMEM,) * 6,
+        compiler_params=params(3),
         name="prepare",
     )(queries, keys, values, rates)
 
@@ -143,7 +143,7 @@
         in_specs=[VMEM, ANY],
         out_specs=VMEM,
         scratch_shapes=[pltpu.VMEM((2, 3, DIM, FF), BF), pltpu.SemaphoreType.DMA((2, 3))],
-        compiler_params=params(),
+        compiler_params=params(12),
         cost_estimate=cost(12 * tokens * DIM * FF, 7 << 20),
         name="first_block",
     )(queries, weights)
@@ -218,7 +218,7 @@
             pltpu.VMEM((DIM, WIDE), F32),
             pltpu.SemaphoreType.DMA((3,)),
         ],
-        compiler_params=params(),
+        compiler_params=params(16),
         cost_estimate=cost(10 * tokens * DIM * HALF, 6 << 20),
         name="gradient",
     )(*pieces, weights)
@@ -240,6 +240,7 @@
         out_shape=(shape(ROWS, WIDE), shape(ROWS, WIDE)),
         in_specs=[VMEM] * 6,
         out_specs=(VMEM, VMEM),
+        compiler_params=params(3),
         name="middle",
     )(*args)
 
@@ -255,6 +256,7 @@
         out_shape=shape(ROWS, WIDE),
         in_specs=[VMEM] * 5,
         out_specs=VMEM,
+        compiler_params=params(3),
         name="add_up",
     )(*args)
 
@@ -278,27 +280,27 @@
 
 
 def gather_rows(own):
+    own = jnp.concatenate([own, pair_x(own)], axis=1)
     up1, down1 = along_z(own, 1), along_z(own, -1)
     up2, down2 = along_z(own, 2), along_z(own, -2)
     up3, down3 = along_z(up2, 1), along_z(down2, -1)
     up4, down4 = along_z(up2[: ROWS // 2], 2), along_z(down2[ROWS // 2 :], -2)
-    pieces = [own, up1, down1, up2, down2, up3, down3, up4, down4]
-    return pieces + [pair_x(piece) for piece in pieces]
+    return [own, up1, down1, up2, down2, up3, down3, up4, down4]
 
 
 def pack_kernel(*refs):
-    pieces = refs[:18]
-    matrix, shared, sem = refs[18:]
+    pieces = refs[:9]
+    matrix, shared, sem = refs[9:]
     x, z, _ = place()
     copies = []
     for i, piece in enumerate(pieces):
-        side = lax.rem(x + i // 9, 2)
-        step, first, count = ORIGINS[i % 9]
-        start = lax.rem(z + step + Z, Z) * ROWS + first
-        rows = at_place(start, count)
-        for j, (target, size, offset) in enumerate(((matrix, HALF, 0), (shared, QUARTER, HALF))):
+        step, first, count = ORIGINS[i]
+        rows = at_place(lax.rem(z + step + Z, Z) * ROWS + first, count)
+        for j in range(4):
+            side = lax.rem(x + j // 2, 2)
+            target, size, offset = ((matrix, HALF, 0), (shared, QUARTER, HALF))[j % 2]
             copy = pltpu.make_async_copy(
-                piece.at[:, pl.ds(offset, size)],
+                piece.at[:, pl.ds(j // 2 * WIDE + offset, size)],
                 target.at[rows, at_place(side * size, size)],
                 sem.at[i, j],
             )
@@ -312,10 +314,10 @@
     return pl.pallas_call(
         pack_kernel,
         out_shape=(shape(DIM, FF), shape(DIM, HALF)),
-        in_specs=[ANY] * 18,
+        in_specs=[ANY] * 9,
         out_specs=(VMEM, VMEM),
-        scratch_shapes=[pltpu.SemaphoreType.DMA((18, 2))],
-        compiler_params=params(),
+        scratch_shapes=[pltpu.SemaphoreType.DMA((9, 4))],
+        compiler_params=params(4),
         cost_estimate=cost(0, 3 << 20),
         name="pack",
     )(*pieces)
@@ -375,7 +377,7 @@
             pltpu.VMEM((4 * tokens, DIM), BF),
             pltpu.SemaphoreType.DMA,
         ],
-        compiler_params=params(),
+        compiler_params=params(16),
         cost_estimate=cost(22 * 10**8, 5 << 20),
         name="project",
     )(scaled, weights, *queries)
@@ -411,7 +413,7 @@
             pltpu.VMEM((DIM, DIM), BF),
             pltpu.SemaphoreType.DMA,
         ],
-        compiler_params=params(),
+        compiler_params=params(14),
         cost_estimate=cost(12 * 10**8, 4 << 20),
         name="renew_third",
     )(mine, other, weights)
@@ -447,7 +449,7 @@
         in_specs=[VMEM] * 3,
         out_specs=(VMEM,) * 4,
         scratch_shapes=[pltpu.VMEM((4 * tokens, FF), BF), pltpu.VMEM((4 * tokens, DIM // 2), BF)],
-        compiler_params=params(),
+        compiler_params=params(8),
         cost_estimate=cost(3 * 10**8, 3 << 20),
         name="down",
     )(mine, other, rows)
@@ -470,6 +472,7 @@
         out_shape=shape(2, *first_out.shape),
         in_specs=[VMEM] * 5,
         out_specs=VMEM,
+        compiler_params=params(2),
         name="finish",
     )(first_out, *parts)
 
@@ -479,8 +482,8 @@
     queries_late, own = lax.optimization_barrier((queries, own))
     first_out = first_block(queries_late, weights)
     got = [own, along_x(far1, 1), along_x(far2, 2), along_x(far3, 3)]
+    got, first_out = lax.optimization_barrier((got, first_out))
     got += [other_core(piece) for piece in got]
-    got, first_out = lax.optimization_barrier((got, first_out))
     parts = gradient(got, weights)
     query_far, parts = lax.optimization_barrier((query_far, parts))
     query_far = mirror_x(query_far)
@@ -489,6 +492,7 @@
     matrix, shared = pack(pieces)
     shared_core = other_core(shared)
     projected = project(matrix, weights, query_own, query_core, query_far, query_far_core)
+    projected, shared_core = lax.optimization_barrier((projected, shared_core))
     projected_core = other_core(projected)
     rows = renew_third(shared, shared_core, weights)
     own, core, far, far_core = down(projected, projected_core, rows)

time: 105 us -> 94.4 us (0.90)
  starting transfers between devices: 61.2 us -> 44.6 us
  waiting for transfers between devices: 12.8 us -> 29.3 us
  Pallas kernels: 22.4 us -> 13 us
    ppermute x40 -> x32, starting transfers between devices: 61.2 us -> 44.6 us  [move(): return lax.ppermute(array, 'ctx', perm)]
    ppermute x40 -> x32, waiting for transfers between devices: 12.8 us -> 29.3 us  [move(): return lax.ppermute(array, 'ctx', perm)]
    pallas_call x1, Pallas kernels: 2.12 us -> 0.26 us  [prepare(): pl.pallas_call(prepare_kernel, out_shape=(pair, pair, pair, pair, half, h...]
    pallas_call x1, Pallas kernels: 1.84 us -> 0.05 us  [middle(): pl.pallas_call(middle_kernel, out_shape=(shape(ROWS, WIDE), shape(ROWS, W...]
    pallas_call x1, Pallas kernels: 1.82 us -> 0.06 us  [add_up(): pl.pallas_call(total_kernel, out_shape=shape(ROWS, WIDE), in_specs=[VMEM]...]
    pallas_call x1, Pallas kernels: 3.52 us -> 2.4 us  [gradient(): pl.pallas_call(gradient_kernel, out_shape=(kept, sent, sent, kept, kept,...]
    pallas_call x1, Pallas kernels: 4.21 us -> 3.11 us  [project(): pl.pallas_call(project_kernel, out_shape=shape(4 * tokens, FF, dtype=F32)...]
    unnamed x42 -> x14, local copies, waits for them, and re-layouts: 7.64 us -> 7.17 us
  transfers between devices with their start and end apart: 40 -> 32, of which waited for: 10 -> 15; matrix products, arithmetic and copies ran while one was open for 0% -> 0% of each run, Pallas kernels for 10% -> 9%
where the time goes in v3:
time: 94.4 us; the launch traced here: 94.2 us
  starting transfers between devices  44.6 us (47%)
  waiting for transfers between devices  29.3 us (31%)
  Pallas kernels  13 us (14%)
  local copies, waits for them, and re-layouts  7.19 us (8%)
    ppermute x32, starting transfers between devices, move(): return lax.ppermute(array, 'ctx', perm)  44.6 us
    ppermute x32, waiting for transfers between devices, move(): return lax.ppermute(array, 'ctx', perm)  29.3 us
    unnamed x14, local copies, waits for them, and re-layouts  7.17 us
    pallas_call x1, Pallas kernels, project(): pl.pallas_call(project_kernel, out_shape=shape(4 * tokens, FF, dtype=F32)...  3.11 us
    pallas_call x1, Pallas kernels, first_block(): pl.pallas_call(first_kernel, out_shape=shape(tokens, 2 * DIM), in_specs=[...  2.58 us
    pallas_call x1, Pallas kernels, renew_third(): pl.pallas_call(third_kernel, out_shape=shape(rows, FF), in_specs=[VMEM, V...  2.46 us
    pallas_call x1, Pallas kernels, gradient(): pl.pallas_call(gradient_kernel, out_shape=(kept, sent, sent, kept, kept,...  2.4 us
  transfers between devices with their start and end apart: 32, of which 15 were waited for; matrix products, arithmetic and copies ran while one was open for 0% of the time, Pallas kernels for 9%

profile of v3, /device:TPU:1, one launch (start us, length us, event | category | flops | bytes accessed | tf_op | source)
XLA Modules:
  0.0 94.2 jit_solution(10169044342307706003)
XLA Ops:
  0.0 0.9 %copy-done.2 = bf16[2,64,1024]{2,1,0:T(8,128)(2,1)S(1)} copy-done((bf16[2,64,1024]{2,1,0:T(8,128)(2,1)S(1)}, bf16[2,64,1024]{2,1,0:T(8,128)(2,1)}, u32[]{:S(2)}) %copy-start.2) | copy-done | bytes 262168
  1.0 0.9 copy-done.4
  1.9 0.9 copy-done.5
  2.8 0.7 copy-done.6
  3.7 2.1 %collective-permute-start = (bf16[128,512]{1,0:T(8,128)(2,1)S(1)}, bf16[128,512]{1,0:T(8,128)(2,1)S(1)}, u32[]{:S(2)}, u32[]{:S(2)}) collective-permute-start(bf16[128,512]{1,0:T(8,128)(2,1)S(1)} %get-tuple-element.49), channel_id=1, source_target_pairs={{0,16},{1,17},{2,18},{3,19},{4,20},{5,21},{6,22},{7,23},{8,24},{9,... | collective-permute-start | bytes 393224 | tf_op jit(solution)/shard_map/ppermute | solution.py:32
  5.8 2.4 %collective-permute-start.1 = (bf16[128,512]{1,0:T(8,128)(2,1)S(1)}, bf16[128,512]{1,0:T(8,128)(2,1)S(1)}, u32[]{:S(2)}, u32[]{:S(2)}) collective-permute-start(bf16[128,512]{1,0:T(8,128)(2,1)S(1)} %get-tuple-element.50), channel_id=1, source_target_pairs={{0,32},{1,33},{2,34},{3,35},{4,36},{5,37},{6,38},{7,39},{8,40},{9,... | collective-permute-start | bytes 393224 | tf_op jit(solution)/shard_map/ppermute | solution.py:32
  8.3 1.1 %collective-permute-start.2 = (bf16[128,512]{1,0:T(8,128)(2,1)S(1)}, bf16[128,512]{1,0:T(8,128)(2,1)S(1)}, u32[]{:S(2)}, u32[]{:S(2)}) collective-permute-start(bf16[128,512]{1,0:T(8,128)(2,1)S(1)} %get-tuple-element.51), channel_id=1, source_target_pairs={{0,48},{1,49},{2,50},{3,51},{4,52},{5,53},{6,54},{7,55},{8,56},{9,... | collective-permute-start | bytes 393224 | tf_op jit(solution)/shard_map/ppermute | solution.py:32
  9.4 2.8 %copy-done = bf16[3,2,512,1024]{3,2,1,0:T(8,128)(2,1)S(1)} copy-done((bf16[3,2,512,1024]{3,2,1,0:T(8,128)(2,1)S(1)}, bf16[3,2,512,1024]{3,2,1,0:T(8,128)(2,1)}, u32[]{:S(2)}) %copy-start) | copy-done | bytes 6291480
  12.2 0.9 %copy-done.3 = bf16[2,64,1024]{2,1,0:T(8,128)(2,1)S(1)} copy-done((bf16[2,64,1024]{2,1,0:T(8,128)(2,1)S(1)}, bf16[2,64,1024]{2,1,0:T(8,128)(2,1)}, u32[]{:S(2)}) %copy-start.3) | copy-done | bytes 262168
  13.1 2.6 %first_block.1.first_out = bf16[64,1024]{1,0:T(8,128)(2,1)S(1)} custom-call(bf16[2,64,1024]{2,1,0:T(8,128)(2,1)S(1)} %copy-done.3, bf16[3,2,512,1024]{3,2,1,0:T(8,128)(2,1)S(1)} %copy-done), custom_call_target="tpu_custom_call" | custom-call | flops 402653184 | bytes 7340032 | tf_op jit(solution)/shard_map/first_block/pallas_call | solution.py:140
  15.8 1.6 %collective-permute-start.3 = (bf16[128,512]{1,0:T(8,128)(2,1)S(1)}, bf16[128,512]{1,0:T(8,128)(2,1)S(1)}, u32[]{:S(2)}, u32[]{:S(2)}) collective-permute-start(bf16[128,512]{1,0:T(8,128)(2,1)S(1)} %get-tuple-element.55.refs_0_), channel_id=1, source_target_pairs={{0,1},{1,0},{2,3},{3,2},{4,5},{5,4},{6,7},{7,6},{8,9},{9,8},{10,11... | collective-permute-start | bytes 393224 | tf_op jit(solution)/shard_map/ppermute | solution.py:32
  17.5 0.4 collective-permute-start.5
  18.0 0.4 collective-permute-done.3.refs_4_
  18.4 0.4 collective-permute-done.4.refs_5_
  18.9 0.3 collective-permute-done.6.refs_7_
  19.2 2.4 %gradient.1 = (f32[64,768]{1,0:T(8,128)S(1)}, bf16[64,768]{1,0:T(8,128)(2,1)S(1)}, bf16[64,768]{1,0:T(8,128)(2,1)S(1)}, f32[64,768]{1,0:T(8,128)S(1)}, f32[64,76...) custom-call(bf16[128,512]{1,0:T(8,128)(2,1)S(1)} %get-tuple-element., ...), custom_call_target="tpu_custom_call" | custom-call | flops 1342177280 | bytes 6291456 | tf_op jit(solution)/shard_map/gradient/pallas_call | solution.py:207
  21.6 5.6 %collective-permute-start.10 = (bf16[64,768]{1,0:T(8,128)(2,1)S(1)}, bf16[64,768]{1,0:T(8,128)(2,1)S(1)}, u32[]{:S(2)}, u32[]{:S(2)}) collective-permute-start(bf16[64,768]{1,0:T(8,128)(2,1)S(1)} %get-tuple-element.74), channel_id=1, source_target_pairs={{0,14},{1,15},{2,0},{3,1},{4,2},{5,3},{6,4},{7,5},{8,6},{9,7},{10,... | collective-permute-start | bytes 294920 | tf_op jit(solution)/shard_map/ppermute | solution.py:32
  27.3 3.6 %collective-permute-start.12 = (bf16[32,768]{1,0:T(8,128)(2,1)S(1)}, bf16[32,768]{1,0:T(8,128)(2,1)S(1)}, u32[]{:S(2)}, u32[]{:S(2)}) collective-permute-start(bf16[32,768]{1,0:T(8,128)(2,1)S(1)} %get-tuple-element.76), channel_id=1, source_target_pairs={{0,12},{1,13},{2,14},{3,15},{4,0},{5,1},{6,2},{7,3},{8,4},{9,5},{1... | collective-permute-start | bytes 147464 | tf_op jit(solution)/shard_map/ppermute | solution.py:32
  31.2 1.6 %collective-permute-done.11.far_up = bf16[32,768]{1,0:T(8,128)(2,1)S(1)} collective-permute-done((bf16[32,768]{1,0:T(8,128)(2,1)S(1)}, bf16[32,768]{1,0:T(8,128)(2,1)S(1)}, u32[]{:S(2)}, u32[]{:S(2)}) %collective-permute-start.11) | collective-permute-done | bytes 49184 | tf_op jit(solution)/shard_map/ppermute | solution.py:32
  32.8 1.5 %collective-permute-start.8 = (bf16[64,768]{1,0:T(8,128)(2,1)S(1)}, bf16[64,768]{1,0:T(8,128)(2,1)S(1)}, u32[]{:S(2)}, u32[]{:S(2)}) collective-permute-start(bf16[64,768]{1,0:T(8,128)(2,1)S(1)} %get-tuple-element.70), channel_id=1, source_target_pairs={{0,14},{1,15},{2,0},{3,1},{4,2},{5,3},{6,4},{7,5},{8,6},{9,7},{10,... | collective-permute-start | bytes 294920 | tf_op jit(solution)/shard_map/ppermute | solution.py:32
  34.3 2.3 %collective-permute-start.13 = (bf16[64,768]{1,0:T(8,128)(2,1)S(1)}, bf16[64,768]{1,0:T(8,128)(2,1)S(1)}, u32[]{:S(2)}, u32[]{:S(2)}) collective-permute-start(bf16[64,768]{1,0:T(8,128)(2,1)S(1)} %get-tuple-element.77), channel_id=1, source_target_pairs={{0,4},{1,5},{2,6},{3,7},{4,8},{5,9},{6,10},{7,11},{8,12},{9,13},{1... | collective-permute-start | bytes 294920 | tf_op jit(solution)/shard_map/ppermute | solution.py:32
  36.6 1.4 %collective-permute-start.14 = (bf16[64,768]{1,0:T(8,128)(2,1)S(1)}, bf16[64,768]{1,0:T(8,128)(2,1)S(1)}, u32[]{:S(2)}, u32[]{:S(2)}) collective-permute-start(bf16[64,768]{1,0:T(8,128)(2,1)S(1)} %get-tuple-element.78), channel_id=1, source_target_pairs={{0,12},{1,13},{2,14},{3,15},{4,0},{5,1},{6,2},{7,3},{8,4},{9,5},{1... | collective-permute-start | bytes 294920 | tf_op jit(solution)/shard_map/ppermute | solution.py:32
  38.0 2.5 %collective-permute-done.13.c = bf16[64,768]{1,0:T(8,128)(2,1)S(1)} collective-permute-done((bf16[64,768]{1,0:T(8,128)(2,1)S(1)}, bf16[64,768]{1,0:T(8,128)(2,1)S(1)}, u32[]{:S(2)}, u32[]{:S(2)}) %collective-permute-start.13) | collective-permute-done | bytes 98336 | tf_op jit(solution)/shard_map/ppermute | solution.py:32
  40.5 2.4 %collective-permute-done.14.d = bf16[64,768]{1,0:T(8,128)(2,1)S(1)} collective-permute-done((bf16[64,768]{1,0:T(8,128)(2,1)S(1)}, bf16[64,768]{1,0:T(8,128)(2,1)S(1)}, u32[]{:S(2)}, u32[]{:S(2)}) %collective-permute-start.14) | collective-permute-done | bytes 98336 | tf_op jit(solution)/shard_map/ppermute | solution.py:32
  42.9 0.4 collective-permute-start.15
  43.3 3.1 %collective-permute-done.15 = bf16[64,768]{1,0:T(8,128)(2,1)S(1)} collective-permute-done((bf16[64,768]{1,0:T(8,128)(2,1)S(1)}, bf16[64,768]{1,0:T(8,128)(2,1)S(1)}, u32[]{:S(2)}, u32[]{:S(2)}) %collective-permute-start.15) | collective-permute-done | bytes 98336 | tf_op jit(solution)/shard_map/ppermute | solution.py:32
  46.5 0.6 collective-permute-start.18
  47.1 3.1 %collective-permute-start.19 = (bf16[64,1536]{1,0:T(8,128)(2,1)S(1)}, bf16[64,1536]{1,0:T(8,128)(2,1)S(1)}, u32[]{:S(2)}, u32[]{:S(2)}) collective-permute-start(bf16[64,1536]{1,0:T(8,128)(2,1)S(1)} %pad_maximum_fusion.refs_0_), channel_id=1, source_target_pairs={{0,12},{1,13},{2,14},{3,15},{4,0},{5,1},{6,2},{7,3},{8,4},{9,5},{1... | collective-permute-start | bytes 589832 | tf_op jit(solution)/shard_map/ppermute | solution.py:32
  50.1 2.7 %collective-permute-start.17 = (bf16[64,1536]{1,0:T(8,128)(2,1)S(1)}, bf16[64,1536]{1,0:T(8,128)(2,1)S(1)}, u32[]{:S(2)}, u32[]{:S(2)}) collective-permute-start(bf16[64,1536]{1,0:T(8,128)(2,1)S(1)} %pad_maximum_fusion.refs_0_), channel_id=1, source_target_pairs={{0,14},{1,15},{2,0},{3,1},{4,2},{5,3},{6,4},{7,5},{8,6},{9,7},{10,... | collective-permute-start | bytes 589832 | tf_op jit(solution)/shard_map/ppermute | solution.py:32
  52.8 2.1 %collective-permute-done.18.refs_3_ = bf16[64,1536]{1,0:T(8,128)(2,1)S(1)} collective-permute-done((bf16[64,1536]{1,0:T(8,128)(2,1)S(1)}, bf16[64,1536]{1,0:T(8,128)(2,1)S(1)}, u32[]{:S(2)}, u32[]{:S(2)}) %collective-permute-start.18) | collective-permute-done | bytes 196640 | tf_op jit(solution)/shard_map/ppermute | solution.py:32
  54.9 2.7 %collective-permute-start.21 = (bf16[64,1536]{1,0:T(8,128)(2,1)S(1)}, bf16[64,1536]{1,0:T(8,128)(2,1)S(1)}, u32[]{:S(2)}, u32[]{:S(2)}) collective-permute-start(bf16[64,1536]{1,0:T(8,128)(2,1)S(1)} %collective-permute-done.19.refs_4_), channel_id=1, source_target_pairs={{0,14},{1,15},{2,0},{3,1},{4,2},{5,3},{6,4},{7,5},{8,6},{9,7},{10,... | collective-permute-start | bytes 589832 | tf_op jit(solution)/shard_map/ppermute | solution.py:32
  57.7 2.5 %collective-permute-done.16.refs_1_ = bf16[64,1536]{1,0:T(8,128)(2,1)S(1)} collective-permute-done((bf16[64,1536]{1,0:T(8,128)(2,1)S(1)}, bf16[64,1536]{1,0:T(8,128)(2,1)S(1)}, u32[]{:S(2)}, u32[]{:S(2)}) %collective-permute-start.16) | collective-permute-done | bytes 196640 | tf_op jit(solution)/shard_map/ppermute | solution.py:32
  60.2 1.2 %collective-permute-start.23 = (bf16[32,1536]{1,0:T(8,128)(2,1)S(1)}, bf16[32,1536]{1,0:T(8,128)(2,1)S(1)}, u32[]{:S(2)}, u32[]{:S(2)}) collective-permute-start(bf16[32,1536]{1,0:T(8,128)(2,1)S(1)} %slice.9), channel_id=1, source_target_pairs={{0,12},{1,13},{2,14},{3,15},{4,0},{5,1},{6,2},{7,3},{8,4},{9,5},{1... | collective-permute-start | bytes 294920 | tf_op jit(solution)/shard_map/ppermute | solution.py:32
  61.4 6.4 %collective-permute-done.22.refs_7_ = bf16[32,1536]{1,0:T(8,128)(2,1)S(1)} collective-permute-done((bf16[32,1536]{1,0:T(8,128)(2,1)S(1)}, bf16[32,1536]{1,0:T(8,128)(2,1)S(1)}, u32[]{:S(2)}, u32[]{:S(2)}) %collective-permute-start.22) | collective-permute-done | bytes 98336 | tf_op jit(solution)/shard_map/ppermute | solution.py:32
  67.8 0.8 pack.1
  68.6 6.1 %collective-permute-start.27 = (bf16[512,512]{1,0:T(8,128)(2,1)S(1)}, bf16[512,512]{1,0:T(8,128)(2,1)S(1)}, u32[]{:S(2)}, u32[]{:S(2)}) collective-permute-start(bf16[512,512]{1,0:T(8,128)(2,1)S(1)} %get-tuple-element.82.mine), channel_id=1, source_target_pairs={{0,1},{1,0},{2,3},{3,2},{4,5},{5,4},{6,7},{7,6},{8,9},{9,8},{10,11... | collective-permute-start | bytes 1572872 | tf_op jit(solution)/shard_map/ppermute | solution.py:32
  74.8 0.4 collective-permute-start.24
  75.2 4.3 %collective-permute-done.25.query_far = bf16[64,512]{1,0:T(8,128)(2,1)S(1)} collective-permute-done((bf16[64,512]{1,0:T(8,128)(2,1)S(1)}, bf16[64,512]{1,0:T(8,128)(2,1)S(1)}, u32[]{:S(2)}, u32[]{:S(2)}) %collective-permute-start.25) | collective-permute-done | bytes 65568 | tf_op jit(solution)/shard_map/ppermute | solution.py:32
  79.5 0.9 collective-permute-start.26
  80.4 0.9 collective-permute-done.26.query_far_core
  81.3 3.1 %project.1.mine = f32[256,1024]{1,0:T(8,128)S(1)} custom-call(bf16[512,1024]{1,0:T(8,128)(2,1)S(1)} %get-tuple-element.79.scaled, bf16[3,2,512,1024]{3,2,1,0:T(8,128)(2,1)S(1)} %copy-done.1, bf16[64,512]{1,0:T(8,128)(2,1)S(1)} %get-tuple-element.80.query_own, bf16[64,512]{1,0:T(8,128)(2,1)S(1)} %collective-permute-done.24.query_core, ...), custom_call_target="tpu_custom_call" | custom-call | flops 2200000000 | bytes 5242880 | tf_op jit(solution)/shard_map/project/pallas_call | solution.py:370
  84.4 0.4 collective-permute-start.28
  84.9 2.5 %renew_third.1.rows = bf16[256,1024]{1,0:T(8,128)(2,1)S(1)} custom-call(bf16[512,512]{1,0:T(8,128)(2,1)S(1)} %get-tuple-element.82.mine, bf16[512,512]{1,0:T(8,128)(2,1)S(1)} %collective-permute-done.27.other, bf16[3,2,512,1024]{3,2,1,0:T(8,128)(2,1)S(1)} %copy-done.1), custom_call_target="tpu_custom_call" | custom-call | flops 1200000000 | bytes 4194304 | tf_op jit(solution)/shard_map/renew_third/pallas_call | solution.py:405
  87.3 0.6 down.1
  88.3 3.0 %collective-permute-start.31 = (bf16[64,256]{1,0:T(8,128)(2,1)S(1)}, bf16[64,256]{1,0:T(8,128)(2,1)S(1)}, u32[]{:S(2)}, u32[]{:S(2)}) collective-permute-start(bf16[64,256]{1,0:T(8,128)(2,1)S(1)} %get-tuple-element.88), channel_id=1, source_target_pairs={{0,49},{1,48},{2,51},{3,50},{4,53},{5,52},{6,55},{7,54},{8,57},{9,... | collective-permute-start | bytes 98312 | tf_op jit(solution)/shard_map/ppermute | solution.py:32
  91.3 0.8 collective-permute-done.30.far
  92.1 1.4 %collective-permute-done.31.far_core = bf16[64,256]{1,0:T(8,128)(2,1)S(1)} collective-permute-done((bf16[64,256]{1,0:T(8,128)(2,1)S(1)}, bf16[64,256]{1,0:T(8,128)(2,1)S(1)}, u32[]{:S(2)}, u32[]{:S(2)}) %collective-permute-start.31) | collective-permute-done | bytes 32800 | tf_op jit(solution)/shard_map/ppermute | solution.py:32
  93.5 0.7 finish.1
  (43 shorter events, 1.8 us)
Async XLA Ops:
  0.0 0.9 %copy-start.2 = (bf16[2,64,1024]{2,1,0:T(8,128)(2,1)S(1)}, bf16[2,64,1024]{2,1,0:T(8,128)(2,1)}, u32[]{:S(2)}) copy-start(bf16[2,64,1024]{2,1,0:T(8,128)(2,1)} %queries.2) | copy-start | bytes 786436
  1.0 0.9 copy-start.4
  1.9 0.9 copy-start.5
  2.8 0.7 copy-start.6
  3.7 12.0 %collective-permute-start = (bf16[128,512]{1,0:T(8,128)(2,1)S(1)}, bf16[128,512]{1,0:T(8,128)(2,1)S(1)}, u32[]{:S(2)}, u32[]{:S(2)}) collective-permute-start(bf16[128,512]{1,0:T(8,128)(2,1)S(1)} %get-tuple-element.49), channel_id=1, source_target_pairs={{0,16},{1,17},{2,18},{3,19},{4,20},{5,21},{6,22},{7,23},{8,24},{9,... | collective-permute-start | bytes 393224 | tf_op jit(solution)/shard_map/ppermute | solution.py:32
  5.8 9.9 %collective-permute-start.1 = (bf16[128,512]{1,0:T(8,128)(2,1)S(1)}, bf16[128,512]{1,0:T(8,128)(2,1)S(1)}, u32[]{:S(2)}, u32[]{:S(2)}) collective-permute-start(bf16[128,512]{1,0:T(8,128)(2,1)S(1)} %get-tuple-element.50), channel_id=1, source_target_pairs={{0,32},{1,33},{2,34},{3,35},{4,36},{5,37},{6,38},{7,39},{8,40},{9,... | collective-permute-start | bytes 393224 | tf_op jit(solution)/shard_map/ppermute | solution.py:32
  8.3 7.5 %collective-permute-start.2 = (bf16[128,512]{1,0:T(8,128)(2,1)S(1)}, bf16[128,512]{1,0:T(8,128)(2,1)S(1)}, u32[]{:S(2)}, u32[]{:S(2)}) collective-permute-start(bf16[128,512]{1,0:T(8,128)(2,1)S(1)} %get-tuple-element.51), channel_id=1, source_target_pairs={{0,48},{1,49},{2,50},{3,51},{4,52},{5,53},{6,54},{7,55},{8,56},{9,... | collective-permute-start | bytes 393224 | tf_op jit(solution)/shard_map/ppermute | solution.py:32
  9.4 2.8 %copy-start = (bf16[3,2,512,1024]{3,2,1,0:T(8,128)(2,1)S(1)}, bf16[3,2,512,1024]{3,2,1,0:T(8,128)(2,1)}, u32[]{:S(2)}) copy-start(bf16[3,2,512,1024]{3,2,1,0:T(8,128)(2,1)} %weights.5) | copy-start | bytes 18874372
  12.2 0.9 %copy-start.3 = (bf16[2,64,1024]{2,1,0:T(8,128)(2,1)S(1)}, bf16[2,64,1024]{2,1,0:T(8,128)(2,1)}, u32[]{:S(2)}) copy-start(bf16[2,64,1024]{2,1,0:T(8,128)(2,1)} %queries.2) | copy-start | bytes 786436
  13.1 6.1 %copy-start.1 = (bf16[3,2,512,1024]{3,2,1,0:T(8,128)(2,1)S(1)}, bf16[3,2,512,1024]{3,2,1,0:T(8,128)(2,1)}, u32[]{:S(2)}) copy-start(bf16[3,2,512,1024]{3,2,1,0:T(8,128)(2,1)} %weights.5) | copy-start | bytes 18874372
  15.8 2.6 %collective-permute-start.3 = (bf16[128,512]{1,0:T(8,128)(2,1)S(1)}, bf16[128,512]{1,0:T(8,128)(2,1)S(1)}, u32[]{:S(2)}, u32[]{:S(2)}) collective-permute-start(bf16[128,512]{1,0:T(8,128)(2,1)S(1)} %get-tuple-element.55.refs_0_), channel_id=1, source_target_pairs={{0,1},{1,0},{2,3},{3,2},{4,5},{5,4},{6,7},{7,6},{8,9},{9,8},{10,11... | collective-permute-start | bytes 393224 | tf_op jit(solution)/shard_map/ppermute | solution.py:32
  17.4 1.3 %collective-permute-start.4 = (bf16[128,512]{1,0:T(8,128)(2,1)S(1)}, bf16[128,512]{1,0:T(8,128)(2,1)S(1)}, u32[]{:S(2)}, u32[]{:S(2)}) collective-permute-start(bf16[128,512]{1,0:T(8,128)(2,1)S(1)} %collective-permute-done.refs_1_), channel_id=1, source_target_pairs={{0,1},{1,0},{2,3},{3,2},{4,5},{5,4},{6,7},{7,6},{8,9},{9,8},{10,11... | collective-permute-start | bytes 393224 | tf_op jit(solution)/shard_map/ppermute | solution.py:32
  17.5 1.4 %collective-permute-start.5 = (bf16[128,512]{1,0:T(8,128)(2,1)S(1)}, bf16[128,512]{1,0:T(8,128)(2,1)S(1)}, u32[]{:S(2)}, u32[]{:S(2)}) collective-permute-start(bf16[128,512]{1,0:T(8,128)(2,1)S(1)} %collective-permute-done.1.refs_2_), channel_id=1, source_target_pairs={{0,1},{1,0},{2,3},{3,2},{4,5},{5,4},{6,7},{7,6},{8,9},{9,8},{10,11... | collective-permute-start | bytes 393224 | tf_op jit(solution)/shard_map/ppermute | solution.py:32
  17.9 1.3 %collective-permute-start.6 = (bf16[128,512]{1,0:T(8,128)(2,1)S(1)}, bf16[128,512]{1,0:T(8,128)(2,1)S(1)}, u32[]{:S(2)}, u32[]{:S(2)}) collective-permute-start(bf16[128,512]{1,0:T(8,128)(2,1)S(1)} %collective-permute-done.2.refs_3_), channel_id=1, source_target_pairs={{0,1},{1,0},{2,3},{3,2},{4,5},{5,4},{6,7},{7,6},{8,9},{9,8},{10,11... | collective-permute-start | bytes 393224 | tf_op jit(solution)/shard_map/ppermute | solution.py:32
  21.6 12.6 %collective-permute-start.10 = (bf16[64,768]{1,0:T(8,128)(2,1)S(1)}, bf16[64,768]{1,0:T(8,128)(2,1)S(1)}, u32[]{:S(2)}, u32[]{:S(2)}) collective-permute-start(bf16[64,768]{1,0:T(8,128)(2,1)S(1)} %get-tuple-element.74), channel_id=1, source_target_pairs={{0,14},{1,15},{2,0},{3,1},{4,2},{5,3},{6,4},{7,5},{8,6},{9,7},{10,... | collective-permute-start | bytes 294920 | tf_op jit(solution)/shard_map/ppermute | solution.py:32
  27.3 7.0 %collective-permute-start.9 = (bf16[64,768]{1,0:T(8,128)(2,1)S(1)}, bf16[64,768]{1,0:T(8,128)(2,1)S(1)}, u32[]{:S(2)}, u32[]{:S(2)}) collective-permute-start(bf16[64,768]{1,0:T(8,128)(2,1)S(1)} %get-tuple-element.73), channel_id=1, source_target_pairs={{0,2},{1,3},{2,4},{3,5},{4,6},{5,7},{6,8},{7,9},{8,10},{9,11},{10,... | collective-permute-start | bytes 294920 | tf_op jit(solution)/shard_map/ppermute | solution.py:32
  27.3 5.5 %collective-permute-start.11 = (bf16[32,768]{1,0:T(8,128)(2,1)S(1)}, bf16[32,768]{1,0:T(8,128)(2,1)S(1)}, u32[]{:S(2)}, u32[]{:S(2)}) collective-permute-start(bf16[32,768]{1,0:T(8,128)(2,1)S(1)} %get-tuple-element.75), channel_id=1, source_target_pairs={{0,4},{1,5},{2,6},{3,7},{4,8},{5,9},{6,10},{7,11},{8,12},{9,13},{1... | collective-permute-start | bytes 147464 | tf_op jit(solution)/shard_map/ppermute | solution.py:32
  27.3 7.0 %collective-permute-start.12 = (bf16[32,768]{1,0:T(8,128)(2,1)S(1)}, bf16[32,768]{1,0:T(8,128)(2,1)S(1)}, u32[]{:S(2)}, u32[]{:S(2)}) collective-permute-start(bf16[32,768]{1,0:T(8,128)(2,1)S(1)} %get-tuple-element.76), channel_id=1, source_target_pairs={{0,12},{1,13},{2,14},{3,15},{4,0},{5,1},{6,2},{7,3},{8,4},{9,5},{1... | collective-permute-start | bytes 147464 | tf_op jit(solution)/shard_map/ppermute | solution.py:32
  30.9 7.1 %collective-permute-start.7 = (bf16[64,768]{1,0:T(8,128)(2,1)S(1)}, bf16[64,768]{1,0:T(8,128)(2,1)S(1)}, u32[]{:S(2)}, u32[]{:S(2)}) collective-permute-start(bf16[64,768]{1,0:T(8,128)(2,1)S(1)} %get-tuple-element.69), channel_id=1, source_target_pairs={{0,2},{1,3},{2,4},{3,5},{4,6},{5,7},{6,8},{7,9},{8,10},{9,11},{10,... | collective-permute-start | bytes 294920 | tf_op jit(solution)/shard_map/ppermute | solution.py:32
  32.8 5.2 %collective-permute-start.8 = (bf16[64,768]{1,0:T(8,128)(2,1)S(1)}, bf16[64,768]{1,0:T(8,128)(2,1)S(1)}, u32[]{:S(2)}, u32[]{:S(2)}) collective-permute-start(bf16[64,768]{1,0:T(8,128)(2,1)S(1)} %get-tuple-element.70), channel_id=1, source_target_pairs={{0,14},{1,15},{2,0},{3,1},{4,2},{5,3},{6,4},{7,5},{8,6},{9,7},{10,... | collective-permute-start | bytes 294920 | tf_op jit(solution)/shard_map/ppermute | solution.py:32
  34.3 6.1 %collective-permute-start.13 = (bf16[64,768]{1,0:T(8,128)(2,1)S(1)}, bf16[64,768]{1,0:T(8,128)(2,1)S(1)}, u32[]{:S(2)}, u32[]{:S(2)}) collective-permute-start(bf16[64,768]{1,0:T(8,128)(2,1)S(1)} %get-tuple-element.77), channel_id=1, source_target_pairs={{0,4},{1,5},{2,6},{3,7},{4,8},{5,9},{6,10},{7,11},{8,12},{9,13},{1... | collective-permute-start | bytes 294920 | tf_op jit(solution)/shard_map/ppermute | solution.py:32
  36.6 6.2 %collective-permute-start.14 = (bf16[64,768]{1,0:T(8,128)(2,1)S(1)}, bf16[64,768]{1,0:T(8,128)(2,1)S(1)}, u32[]{:S(2)}, u32[]{:S(2)}) collective-permute-start(bf16[64,768]{1,0:T(8,128)(2,1)S(1)} %get-tuple-element.78), channel_id=1, source_target_pairs={{0,12},{1,13},{2,14},{3,15},{4,0},{5,1},{6,2},{7,3},{8,4},{9,5},{1... | collective-permute-start | bytes 294920 | tf_op jit(solution)/shard_map/ppermute | solution.py:32
  42.9 3.6 %collective-permute-start.15 = (bf16[64,768]{1,0:T(8,128)(2,1)S(1)}, bf16[64,768]{1,0:T(8,128)(2,1)S(1)}, u32[]{:S(2)}, u32[]{:S(2)}) collective-permute-start(bf16[64,768]{1,0:T(8,128)(2,1)S(1)} %add_up.1), channel_id=1, source_target_pairs={{0,16},{1,17},{2,18},{3,19},{4,20},{5,21},{6,22},{7,23},{8,24},{9,... | collective-permute-start | bytes 294920 | tf_op jit(solution)/shard_map/ppermute | solution.py:32
  46.5 8.5 %collective-permute-start.18 = (bf16[64,1536]{1,0:T(8,128)(2,1)S(1)}, bf16[64,1536]{1,0:T(8,128)(2,1)S(1)}, u32[]{:S(2)}, u32[]{:S(2)}) collective-permute-start(bf16[64,1536]{1,0:T(8,128)(2,1)S(1)} %pad_maximum_fusion.refs_0_), channel_id=1, source_target_pairs={{0,4},{1,5},{2,6},{3,7},{4,8},{5,9},{6,10},{7,11},{8,12},{9,13},{1... | collective-permute-start | bytes 589832 | tf_op jit(solution)/shard_map/ppermute | solution.py:32
  47.1 7.9 %collective-permute-start.19 = (bf16[64,1536]{1,0:T(8,128)(2,1)S(1)}, bf16[64,1536]{1,0:T(8,128)(2,1)S(1)}, u32[]{:S(2)}, u32[]{:S(2)}) collective-permute-start(bf16[64,1536]{1,0:T(8,128)(2,1)S(1)} %pad_maximum_fusion.refs_0_), channel_id=1, source_target_pairs={{0,12},{1,13},{2,14},{3,15},{4,0},{5,1},{6,2},{7,3},{8,4},{9,5},{1... | collective-permute-start | bytes 589832 | tf_op jit(solution)/shard_map/ppermute | solution.py:32
  50.1 10.1 %collective-permute-start.16 = (bf16[64,1536]{1,0:T(8,128)(2,1)S(1)}, bf16[64,1536]{1,0:T(8,128)(2,1)S(1)}, u32[]{:S(2)}, u32[]{:S(2)}) collective-permute-start(bf16[64,1536]{1,0:T(8,128)(2,1)S(1)} %pad_maximum_fusion.refs_0_), channel_id=1, source_target_pairs={{0,2},{1,3},{2,4},{3,5},{4,6},{5,7},{6,8},{7,9},{8,10},{9,11},{10,... | collective-permute-start | bytes 589832 | tf_op jit(solution)/shard_map/ppermute | solution.py:32
  50.1 11.2 %collective-permute-start.17 = (bf16[64,1536]{1,0:T(8,128)(2,1)S(1)}, bf16[64,1536]{1,0:T(8,128)(2,1)S(1)}, u32[]{:S(2)}, u32[]{:S(2)}) collective-permute-start(bf16[64,1536]{1,0:T(8,128)(2,1)S(1)} %pad_maximum_fusion.refs_0_), channel_id=1, source_target_pairs={{0,14},{1,15},{2,0},{3,1},{4,2},{5,3},{6,4},{7,5},{8,6},{9,7},{10,... | collective-permute-start | bytes 589832 | tf_op jit(solution)/shard_map/ppermute | solution.py:32
  54.9 12.9 %collective-permute-start.20 = (bf16[64,1536]{1,0:T(8,128)(2,1)S(1)}, bf16[64,1536]{1,0:T(8,128)(2,1)S(1)}, u32[]{:S(2)}, u32[]{:S(2)}) collective-permute-start(bf16[64,1536]{1,0:T(8,128)(2,1)S(1)} %collective-permute-done.18.refs_3_), channel_id=1, source_target_pairs={{0,2},{1,3},{2,4},{3,5},{4,6},{5,7},{6,8},{7,9},{8,10},{9,11},{10,... | collective-permute-start | bytes 589832 | tf_op jit(solution)/shard_map/ppermute | solution.py:32
  54.9 12.9 %collective-permute-start.21 = (bf16[64,1536]{1,0:T(8,128)(2,1)S(1)}, bf16[64,1536]{1,0:T(8,128)(2,1)S(1)}, u32[]{:S(2)}, u32[]{:S(2)}) collective-permute-start(bf16[64,1536]{1,0:T(8,128)(2,1)S(1)} %collective-permute-done.19.refs_4_), channel_id=1, source_target_pairs={{0,14},{1,15},{2,0},{3,1},{4,2},{5,3},{6,4},{7,5},{8,6},{9,7},{10,... | collective-permute-start | bytes 589832 | tf_op jit(solution)/shard_map/ppermute | solution.py:32
  57.6 10.2 %collective-permute-start.22 = (bf16[32,1536]{1,0:T(8,128)(2,1)S(1)}, bf16[32,1536]{1,0:T(8,128)(2,1)S(1)}, u32[]{:S(2)}, u32[]{:S(2)}) collective-permute-start(bf16[32,1536]{1,0:T(8,128)(2,1)S(1)} %slice.8), channel_id=1, source_target_pairs={{0,4},{1,5},{2,6},{3,7},{4,8},{5,9},{6,10},{7,11},{8,12},{9,13},{1... | collective-permute-start | bytes 294920 | tf_op jit(solution)/shard_map/ppermute | solution.py:32
  60.2 7.6 %collective-permute-start.23 = (bf16[32,1536]{1,0:T(8,128)(2,1)S(1)}, bf16[32,1536]{1,0:T(8,128)(2,1)S(1)}, u32[]{:S(2)}, u32[]{:S(2)}) collective-permute-start(bf16[32,1536]{1,0:T(8,128)(2,1)S(1)} %slice.9), channel_id=1, source_target_pairs={{0,12},{1,13},{2,14},{3,15},{4,0},{5,1},{6,2},{7,3},{8,4},{9,5},{1... | collective-permute-start | bytes 294920 | tf_op jit(solution)/shard_map/ppermute | solution.py:32
  68.6 15.8 %collective-permute-start.27 = (bf16[512,512]{1,0:T(8,128)(2,1)S(1)}, bf16[512,512]{1,0:T(8,128)(2,1)S(1)}, u32[]{:S(2)}, u32[]{:S(2)}) collective-permute-start(bf16[512,512]{1,0:T(8,128)(2,1)S(1)} %get-tuple-element.82.mine), channel_id=1, source_target_pairs={{0,1},{1,0},{2,3},{3,2},{4,5},{5,4},{6,7},{7,6},{8,9},{9,8},{10,11... | collective-permute-start | bytes 1572872 | tf_op jit(solution)/shard_map/ppermute | solution.py:32
  74.6 4.9 %collective-permute-start.25 = (bf16[64,512]{1,0:T(8,128)(2,1)S(1)}, bf16[64,512]{1,0:T(8,128)(2,1)S(1)}, u32[]{:S(2)}, u32[]{:S(2)}) collective-permute-start(bf16[64,512]{1,0:T(8,128)(2,1)S(1)} %get-tuple-element.81), channel_id=1, source_target_pairs={{0,48},{1,49},{2,50},{3,51},{4,52},{5,53},{6,54},{7,55},{8,56},{9,... | collective-permute-start | bytes 196616 | tf_op jit(solution)/shard_map/ppermute | solution.py:32
  74.8 5.6 %collective-permute-start.24 = (bf16[64,512]{1,0:T(8,128)(2,1)S(1)}, bf16[64,512]{1,0:T(8,128)(2,1)S(1)}, u32[]{:S(2)}, u32[]{:S(2)}) collective-permute-start(bf16[64,512]{1,0:T(8,128)(2,1)S(1)} %get-tuple-element.80.query_own), channel_id=1, source_target_pairs={{0,1},{1,0},{2,3},{3,2},{4,5},{5,4},{6,7},{7,6},{8,9},{9,8},{10,11... | collective-permute-start | bytes 196616 | tf_op jit(solution)/shard_map/ppermute | solution.py:32
  79.5 1.8 %collective-permute-start.26 = (bf16[64,512]{1,0:T(8,128)(2,1)S(1)}, bf16[64,512]{1,0:T(8,128)(2,1)S(1)}, u32[]{:S(2)}, u32[]{:S(2)}) collective-permute-start(bf16[64,512]{1,0:T(8,128)(2,1)S(1)} %collective-permute-done.25.query_far), channel_id=1, source_target_pairs={{0,1},{1,0},{2,3},{3,2},{4,5},{5,4},{6,7},{7,6},{8,9},{9,8},{10,11... | collective-permute-start | bytes 196616 | tf_op jit(solution)/shard_map/ppermute | solution.py:32
  84.4 2.9 %collective-permute-start.28 = (f32[256,1024]{1,0:T(8,128)S(1)}, f32[256,1024]{1,0:T(8,128)S(1)}, u32[]{:S(2)}, u32[]{:S(2)}) collective-permute-start(f32[256,1024]{1,0:T(8,128)S(1)} %project.1.mine), channel_id=1, source_target_pairs={{0,1},{1,0},{2,3},{3,2},{4,5},{5,4},{6,7},{7,6},{8,9},{9,8},{10,11... | collective-permute-start | bytes 3145736 | tf_op jit(solution)/shard_map/ppermute | solution.py:32
  87.9 3.4 %collective-permute-start.29 = (bf16[64,256]{1,0:T(8,128)(2,1)S(1)}, bf16[64,256]{1,0:T(8,128)(2,1)S(1)}, u32[]{:S(2)}, u32[]{:S(2)}) collective-permute-start(bf16[64,256]{1,0:T(8,128)(2,1)S(1)} %get-tuple-element.86), channel_id=1, source_target_pairs={{0,1},{1,0},{2,3},{3,2},{4,5},{5,4},{6,7},{7,6},{8,9},{9,8},{10,11... | collective-permute-start | bytes 98312 | tf_op jit(solution)/shard_map/ppermute | solution.py:32
  88.2 4.0 %collective-permute-start.30 = (bf16[64,256]{1,0:T(8,128)(2,1)S(1)}, bf16[64,256]{1,0:T(8,128)(2,1)S(1)}, u32[]{:S(2)}, u32[]{:S(2)}) collective-permute-start(bf16[64,256]{1,0:T(8,128)(2,1)S(1)} %get-tuple-element.87), channel_id=1, source_target_pairs={{0,48},{1,49},{2,50},{3,51},{4,52},{5,53},{6,54},{7,55},{8,56},{9,... | collective-permute-start | bytes 98312 | tf_op jit(solution)/shard_map/ppermute | solution.py:32
  88.3 5.2 %collective-permute-start.31 = (bf16[64,256]{1,0:T(8,128)(2,1)S(1)}, bf16[64,256]{1,0:T(8,128)(2,1)S(1)}, u32[]{:S(2)}, u32[]{:S(2)}) collective-permute-start(bf16[64,256]{1,0:T(8,128)(2,1)S(1)} %get-tuple-element.88), channel_id=1, source_target_pairs={{0,49},{1,48},{2,51},{3,50},{4,53},{5,52},{6,55},{7,54},{8,57},{9,... | collective-permute-start | bytes 98312 | tf_op jit(solution)/shard_map/ppermute | solution.py:32

commit v4 on v3

--- a/solution.py
+++ b/solution.py
@@ -15,6 +15,7 @@
 norm_eps = 1e-07
 VMEM = pl.BlockSpec(memory_space=pltpu.VMEM)
 ANY = pl.BlockSpec(memory_space=pl.ANY)
+HBM = pl.BlockSpec(memory_space=pltpu.HBM)
 
 
 def place():
@@ -76,56 +77,76 @@
     return pl.ds(pl.multiple_of(start, size), size)
 
 
-def prepare_kernel(queries, keys, values, rates, own, far1, far2, far3, query_own, query_far):
+def prepare_kernel(queries, keys, values, rates, *refs):
+    own, far1, far2, far3, query_own, query_far, q, k, v, r, sem = refs
+    copies = []
+    for i, (source, target) in enumerate(
+        ((rates, r), (values.at[0], v), (keys.at[0], k), (queries.at[1], q))
+    ):
+        copy = pltpu.make_async_copy(source, target, sem.at[i])
+        copy.start()
+        copies.append(copy)
     x, _, _ = place()
-    tokens = keys.shape[1]
+    tokens = k.shape[0]
     diagonal = lax.broadcasted_iota(jnp.int32, (tokens, tokens), 0) == lax.broadcasted_iota(
         jnp.int32, (tokens, tokens), 1
     )
+    for copy in copies:
+        copy.wait()
     for head in range(2):
-        row = rates[0, head : head + 1, :]
+        row = r[0, head : head + 1, :]
         rate = jnp.sum(jnp.where(diagonal, row, 0.0), axis=1, keepdims=True)
         cols = slice(head * DIM, (head + 1) * DIM)
-        scaled = (values[0, :, cols].astype(F32) * rate).astype(BF)
+        scaled = (v[:, cols].astype(F32) * rate).astype(BF)
         for distance, ref in enumerate((own, far1, far2, far3)):
 
             @pl.when(lax.rem(x + distance, X) // 2 == head)
             def _():
-                ref[:tokens, :] = keys[0, :, cols]
+                ref[:tokens, :] = k[:, cols]
                 ref[tokens:, :] = scaled
 
         @pl.when(x // 2 == head)
         def _():
-            query_own[...] = queries[1, :, cols]
+            query_own[...] = q[:, cols]
 
         @pl.when(x // 2 != head)
         def _():
-            query_far[...] = queries[1, :, cols]
+            query_far[...] = q[:, cols]
 
 
 def prepare(queries, keys, values, rates):
     tokens = keys.shape[1]
     pair, half = shape(2 * tokens, DIM), shape(tokens, DIM)
+    wide = pltpu.VMEM((tokens, 2 * DIM), BF)
     return pl.pallas_call(
         prepare_kernel,
         out_shape=(pair, pair, pair, pair, half, half),
-        in_specs=[VMEM] * 4,
+        in_specs=[HBM] * 4,
         out_specs=(VMEM,) * 6,
-        compiler_params=params(3),
+        scratch_shapes=[
+            wide,
+            wide,
+            wide,
+            pltpu.VMEM(rates.shape, F32),
+            pltpu.SemaphoreType.DMA((4,)),
+        ],
         name="prepare",
     )(queries, keys, values, rates)
 
 
-def first_kernel(queries, weights, out, w, sem):
+def first_kernel(queries, weights, out, q, w, sem, query_sem):
+    load_query = pltpu.make_async_copy(queries.at[0], q, query_sem)
+    load_query.start()
     copies = []
     for head in range(2):
         for m in range(3):
             copy = pltpu.make_async_copy(weights.at[m, head], w.at[head, m], sem.at[head, m])
             copy.start()
             copies.append(copy)
+    load_query.wait()
     for head in range(2):
         cols = slice(head * DIM, (head + 1) * DIM)
-        query = queries[0, :, cols]
+        query = q[:, cols]
         copies[3 * head].wait()
         first_proj = dot(query, w[head, 0], ((1,), (0,)))
         copies[3 * head + 1].wait()
@@ -140,33 +161,55 @@
     return pl.pallas_call(
         first_kernel,
         out_shape=shape(tokens, 2 * DIM),
-        in_specs=[VMEM, ANY],
+        in_specs=[HBM, HBM],
         out_specs=VMEM,
-        scratch_shapes=[pltpu.VMEM((2, 3, DIM, FF), BF), pltpu.SemaphoreType.DMA((2, 3))],
+        scratch_shapes=[
+            pltpu.VMEM((tokens, 2 * DIM), BF),
+            pltpu.VMEM((2, 3, DIM, FF), BF),
+            pltpu.SemaphoreType.DMA((2, 3)),
+            pltpu.SemaphoreType.DMA,
+        ],
         compiler_params=params(12),
         cost_estimate=cost(12 * tokens * DIM * FF, 7 << 20),
         name="first_block",
     )(queries, weights)
 
 
-def gradient_kernel(*refs):
-    pieces, weights = refs[:8], refs[8]
-    own, near_up, near_down, keep_up, keep_down, send_up, send_down, far_up, far_down = refs[9:18]
-    w, k, v, d, gated, total, sem = refs[18:]
-    x, z, c = place()
+def load_kernel(weights, out, sem):
+    x, _, _ = place()
     copies = []
     for m in range(3):
         copy = pltpu.make_async_copy(
-            weights.at[m, x // 2, :, at_place(lax.rem(x, 2) * HALF, HALF)], w.at[m], sem.at[m]
+            weights.at[m, x // 2, :, at_place(lax.rem(x, 2) * HALF, HALF)], out.at[m], sem.at[m]
         )
         copy.start()
         copies.append(copy)
+    for copy in copies:
+        copy.wait()
+
+
+def load(weights):
+    return pl.pallas_call(
+        load_kernel,
+        out_shape=shape(3, DIM, HALF),
+        in_specs=[HBM],
+        out_specs=VMEM,
+        scratch_shapes=[pltpu.SemaphoreType.DMA((3,))],
+        compiler_params=params(2),
+        cost_estimate=cost(0, 3 << 20),
+        name="load",
+    )(weights)
+
+
+def gradient_kernel(*refs):
+    pieces, w = refs[:8], refs[8]
+    own, near_up, near_down, keep_up, keep_down, send_up, send_down, far_up, far_down = refs[9:18]
+    k, v, d, gated, total = refs[18:]
+    _, z, c = place()
     tokens = pieces[0].shape[0] // 2
     for i, piece in enumerate(pieces):
         k[i * tokens : (i + 1) * tokens, :] = piece[:tokens, :]
         v[i * tokens : (i + 1) * tokens, :] = piece[tokens:, :]
-    for copy in copies:
-        copy.wait()
     key_first = dot(k[...], w[0], ((1,), (0,)))
     key_third = dot(k[...], w[1], ((1,), (0,)))
     back_grad = -dot(v[...], w[2], ((1,), (0,)))
@@ -207,16 +250,14 @@
     return pl.pallas_call(
         gradient_kernel,
         out_shape=(kept, sent, sent, kept, kept, sent, sent, half, half),
-        in_specs=[VMEM] * 8 + [ANY],
+        in_specs=[VMEM] * 9,
         out_specs=(VMEM,) * 9,
         scratch_shapes=[
-            pltpu.VMEM((3, DIM, HALF), BF),
             pltpu.VMEM((tokens, DIM), BF),
             pltpu.VMEM((tokens, DIM), BF),
             pltpu.VMEM((tokens, HALF), BF),
             pltpu.VMEM((tokens, QUARTER), BF),
             pltpu.VMEM((DIM, WIDE), F32),
-            pltpu.SemaphoreType.DMA((3,)),
         ],
         compiler_params=params(16),
         cost_estimate=cost(10 * tokens * DIM * HALF, 6 << 20),
@@ -280,7 +321,6 @@
 
 
 def gather_rows(own):
-    own = jnp.concatenate([own, pair_x(own)], axis=1)
     up1, down1 = along_z(own, 1), along_z(own, -1)
     up2, down2 = along_z(own, 2), along_z(own, -2)
     up3, down3 = along_z(up2, 1), along_z(down2, -1)
@@ -370,7 +410,7 @@
     return pl.pallas_call(
         project_kernel,
         out_shape=shape(4 * tokens, FF, dtype=F32),
-        in_specs=[VMEM, ANY] + [VMEM] * 4,
+        in_specs=[VMEM, HBM] + [VMEM] * 4,
         out_specs=VMEM,
         scratch_shapes=[
             pltpu.VMEM((DIM, FF), BF),
@@ -405,7 +445,7 @@
     return pl.pallas_call(
         third_kernel,
         out_shape=shape(rows, FF),
-        in_specs=[VMEM, VMEM, ANY],
+        in_specs=[VMEM, VMEM, HBM],
         out_specs=VMEM,
         scratch_shapes=[
             pltpu.VMEM((DIM, FF), BF),
@@ -478,17 +518,23 @@
 
 
 def body(queries, keys, values, rates, weights):
+    barrier = lax.optimization_barrier
     own, far1, far2, far3, query_own, query_far = prepare(queries, keys, values, rates)
-    queries_late, own = lax.optimization_barrier((queries, own))
-    first_out = first_block(queries_late, weights)
+    own, weights = barrier((own, weights))
     got = [own, along_x(far1, 1), along_x(far2, 2), along_x(far3, 3)]
-    got, first_out = lax.optimization_barrier((got, first_out))
+    got, query_far, part = barrier((got, query_far, load(weights)))
+    query_far = mirror_x(query_far)
     got += [other_core(piece) for piece in got]
-    parts = gradient(got, weights)
-    query_far, parts = lax.optimization_barrier((query_far, parts))
-    query_far = mirror_x(query_far)
+    parts, query_far = barrier((gradient(got, part), query_far))
+    own, queries, query_own, query_far = barrier(
+        (reduce_rows(parts), queries, query_own, query_far)
+    )
+    first_out = first_block(queries, weights)
     query_core, query_far_core = other_core(query_own), other_core(query_far)
-    pieces = gather_rows(reduce_rows(parts))
+    own, near, first_out, query_core, query_far_core = barrier(
+        (own, pair_x(own), first_out, query_core, query_far_core)
+    )
+    pieces = gather_rows(jnp.concatenate([own, near], axis=1))
     matrix, shared = pack(pieces)
     shared_core = other_core(shared)
     projected = project(matrix, weights, query_own, query_core, query_far, query_far_core)

time: 94.4 us -> 90.7 us (0.961)
  local copies, waits for them, and re-layouts: 7.19 us -> 2.84 us
  Pallas kernels: 13 us -> 15 us
  starting transfers between devices: 44.6 us -> 43.4 us
    unnamed x14 -> x13, local copies, waits for them, and re-layouts: 7.17 us -> 2.81 us
    pallas_call x1, Pallas kernels: 0.26 us -> 2.15 us  [prepare(): pl.pallas_call(prepare_kernel, out_shape=(pair, pair, pair, pair, half, h...]
    ppermute x32, starting transfers between devices: 44.6 us -> 43.4 us  [move(): return lax.ppermute(array, 'ctx', perm)]
  transfers between devices with their start and end apart: 32 -> 32, of which waited for: 15 -> 11; matrix products, arithmetic and copies ran while one was open for 0% -> 0% of each run, Pallas kernels for 9% -> 12%
where the time goes in v4:
time: 90.7 us; the launch traced here: 90.5 us
  starting transfers between devices  43.4 us (48%)
  waiting for transfers between devices  29.1 us (32%)
  Pallas kernels  15 us (17%)
  local copies, waits for them, and re-layouts  2.84 us (3%)
    ppermute x32, starting transfers between devices, move(): return lax.ppermute(array, 'ctx', perm)  43.4 us
    ppermute x32, waiting for transfers between devices, move(): return lax.ppermute(array, 'ctx', perm)  29.1 us
    pallas_call x1, Pallas kernels, project(): pl.pallas_call(project_kernel, out_shape=shape(4 * tokens, FF, dtype=F32)...  3.11 us
    unnamed x13, local copies, waits for them, and re-layouts  2.81 us
    pallas_call x1, Pallas kernels, first_block(): pl.pallas_call(first_kernel, out_shape=shape(tokens, 2 * DIM), in_specs=[...  2.76 us
    pallas_call x1, Pallas kernels, renew_third(): pl.pallas_call(third_kernel, out_shape=shape(rows, FF), in_specs=[VMEM, V...  2.45 us
    pallas_call x1, Pallas kernels, prepare(): pl.pallas_call(prepare_kernel, out_shape=(pair, pair, pair, pair, half, h...  2.15 us
    pallas_call x1, Pallas kernels, gradient(): pl.pallas_call(gradient_kernel, out_shape=(kept, sent, sent, kept, kept,...  2.12 us
  transfers between devices with their start and end apart: 32, of which 11 were waited for; matrix products, arithmetic and copies ran while one was open for 0% of the time, Pallas kernels for 12%

profile of v4, /device:TPU:1, one launch (start us, length us, event | category | flops | bytes accessed | tf_op | source)
XLA Modules:
  0.0 90.5 jit_solution(12152781686844201459)
XLA Ops:
  0.0 2.1 %prepare.1 = (bf16[128,512]{1,0:T(8,128)(2,1)}, bf16[128,512]{1,0:T(8,128)(2,1)}, bf16[128,512]{1,0:T(8,128)(2,1)}, bf16[128,512]{1,0:T(8,128)(2,1)}, bf16[64,512]{1,0:T(8,128)(2,1)}, /*index=5*/bf16[64,512]{1,0:T(8,128)(2,1)}) custom-call(bf16[2,64,1024]{2,1,0:T(8,128)(2,1)} %queries.2, bf16[1,64,1024]{2,1,0:T(8,128)(2,1)} %keys.1, ...), custom_call_target="tpu_custom_call" | custom-call | tf_op jit(solution)/shard_map/prepare/pallas_call | solution.py:121
  2.2 2.1 %collective-permute-start = (bf16[128,512]{1,0:T(8,128)(2,1)}, bf16[128,512]{1,0:T(8,128)(2,1)S(1)}, u32[]{:S(2)}, u32[]{:S(2)}) collective-permute-start(bf16[128,512]{1,0:T(8,128)(2,1)} %get-tuple-element.59), channel_id=1, source_target_pairs={{0,16},{1,17},{2,18},{3,19},{4,20},{5,21},{6,22},{7,23},{8,24},{9,... | collective-permute-start | bytes 393224 | tf_op jit(solution)/shard_map/ppermute | solution.py:33
  4.3 2.4 %collective-permute-start.1 = (bf16[128,512]{1,0:T(8,128)(2,1)}, bf16[128,512]{1,0:T(8,128)(2,1)S(1)}, u32[]{:S(2)}, u32[]{:S(2)}) collective-permute-start(bf16[128,512]{1,0:T(8,128)(2,1)} %get-tuple-element.60), channel_id=1, source_target_pairs={{0,32},{1,33},{2,34},{3,35},{4,36},{5,37},{6,38},{7,39},{8,40},{9,... | collective-permute-start | bytes 393224 | tf_op jit(solution)/shard_map/ppermute | solution.py:33
  6.7 1.1 %collective-permute-start.2 = (bf16[128,512]{1,0:T(8,128)(2,1)}, bf16[128,512]{1,0:T(8,128)(2,1)S(1)}, u32[]{:S(2)}, u32[]{:S(2)}) collective-permute-start(bf16[128,512]{1,0:T(8,128)(2,1)} %get-tuple-element.61), channel_id=1, source_target_pairs={{0,48},{1,49},{2,50},{3,51},{4,52},{5,53},{6,54},{7,55},{8,56},{9,... | collective-permute-start | bytes 393224 | tf_op jit(solution)/shard_map/ppermute | solution.py:33
  7.9 2.8 %copy-done = bf16[3,2,512,1024]{3,2,1,0:T(8,128)(2,1)S(1)} copy-done((bf16[3,2,512,1024]{3,2,1,0:T(8,128)(2,1)S(1)}, bf16[3,2,512,1024]{3,2,1,0:T(8,128)(2,1)}, u32[]{:S(2)}) %copy-start) | copy-done | bytes 6291480
  10.7 0.3 load.1.refs_8_
  11.0 1.7 %collective-permute-done.1.refs_2_ = bf16[128,512]{1,0:T(8,128)(2,1)S(1)} collective-permute-done((bf16[128,512]{1,0:T(8,128)(2,1)}, bf16[128,512]{1,0:T(8,128)(2,1)S(1)}, u32[]{:S(2)}, u32[]{:S(2)}) %collective-permute-start.1) | collective-permute-done | bytes 131104 | tf_op jit(solution)/shard_map/ppermute | solution.py:33
  12.6 2.0 %collective-permute-start.3 = (bf16[128,512]{1,0:T(8,128)(2,1)S(1)}, bf16[128,512]{1,0:T(8,128)(2,1)S(1)}, u32[]{:S(2)}, u32[]{:S(2)}) collective-permute-start(bf16[128,512]{1,0:T(8,128)(2,1)S(1)} %copy-done.4), channel_id=1, source_target_pairs={{0,1},{1,0},{2,3},{3,2},{4,5},{5,4},{6,7},{7,6},{8,9},{9,8},{10,11... | collective-permute-start | bytes 393224 | tf_op jit(solution)/shard_map/ppermute | solution.py:33
  14.7 0.1 collective-permute-start.4
  14.8 0.4 collective-permute-start.5
  15.2 0.1 collective-permute-start.6
  15.3 1.9 %collective-permute-start.7 = (bf16[64,512]{1,0:T(8,128)(2,1)S(1)}, bf16[64,512]{1,0:T(8,128)(2,1)S(1)}, u32[]{:S(2)}, u32[]{:S(2)}) collective-permute-start(bf16[64,512]{1,0:T(8,128)(2,1)S(1)} %copy-done.5), channel_id=1, source_target_pairs={{0,48},{1,49},{2,50},{3,51},{4,52},{5,53},{6,54},{7,55},{8,56},{9,... | collective-permute-start | bytes 196616 | tf_op jit(solution)/shard_map/ppermute | solution.py:33
  17.2 2.1 %gradient.1 = (f32[64,768]{1,0:T(8,128)S(1)}, bf16[64,768]{1,0:T(8,128)(2,1)S(1)}, bf16[64,768]{1,0:T(8,128)(2,1)S(1)}, f32[64,768]{1,0:T(8,128)S(1)}, f32[64,76...) custom-call(bf16[128,512]{1,0:T(8,128)(2,1)S(1)} %copy-done.4, ...), custom_call_target="tpu_custom_call" | custom-call | flops 1342177280 | bytes 6291456 | tf_op jit(solution)/shard_map/gradient/pallas_call | solution.py:250
  19.3 0.3 collective-permute-done.7.query_far
  19.6 1.2 %collective-permute-start.10 = (bf16[64,768]{1,0:T(8,128)(2,1)S(1)}, bf16[64,768]{1,0:T(8,128)(2,1)S(1)}, u32[]{:S(2)}, u32[]{:S(2)}) collective-permute-start(bf16[64,768]{1,0:T(8,128)(2,1)S(1)} %get-tuple-element.84), channel_id=1, source_target_pairs={{0,2},{1,3},{2,4},{3,5},{4,6},{5,7},{6,8},{7,9},{8,10},{9,11},{10,... | collective-permute-start | bytes 294920 | tf_op jit(solution)/shard_map/ppermute | solution.py:33
  20.8 3.9 %collective-permute-start.11 = (bf16[64,768]{1,0:T(8,128)(2,1)S(1)}, bf16[64,768]{1,0:T(8,128)(2,1)S(1)}, u32[]{:S(2)}, u32[]{:S(2)}) collective-permute-start(bf16[64,768]{1,0:T(8,128)(2,1)S(1)} %get-tuple-element.85), channel_id=1, source_target_pairs={{0,14},{1,15},{2,0},{3,1},{4,2},{5,3},{6,4},{7,5},{8,6},{9,7},{10,... | collective-permute-start | bytes 294920 | tf_op jit(solution)/shard_map/ppermute | solution.py:33
  24.7 3.6 %collective-permute-start.13 = (bf16[32,768]{1,0:T(8,128)(2,1)S(1)}, bf16[32,768]{1,0:T(8,128)(2,1)S(1)}, u32[]{:S(2)}, u32[]{:S(2)}) collective-permute-start(bf16[32,768]{1,0:T(8,128)(2,1)S(1)} %get-tuple-element.87), channel_id=1, source_target_pairs={{0,12},{1,13},{2,14},{3,15},{4,0},{5,1},{6,2},{7,3},{8,4},{9,5},{1... | collective-permute-start | bytes 147464 | tf_op jit(solution)/shard_map/ppermute | solution.py:33
  28.3 2.4 %collective-permute-done.12.far_up = bf16[32,768]{1,0:T(8,128)(2,1)S(1)} collective-permute-done((bf16[32,768]{1,0:T(8,128)(2,1)S(1)}, bf16[32,768]{1,0:T(8,128)(2,1)S(1)}, u32[]{:S(2)}, u32[]{:S(2)}) %collective-permute-start.12) | collective-permute-done | bytes 49184 | tf_op jit(solution)/shard_map/ppermute | solution.py:33
  30.7 0.5 collective-permute-start.9
  31.3 3.5 %collective-permute-start.14 = (bf16[64,768]{1,0:T(8,128)(2,1)S(1)}, bf16[64,768]{1,0:T(8,128)(2,1)S(1)}, u32[]{:S(2)}, u32[]{:S(2)}) collective-permute-start(bf16[64,768]{1,0:T(8,128)(2,1)S(1)} %get-tuple-element.88), channel_id=1, source_target_pairs={{0,4},{1,5},{2,6},{3,7},{4,8},{5,9},{6,10},{7,11},{8,12},{9,13},{1... | collective-permute-start | bytes 294920 | tf_op jit(solution)/shard_map/ppermute | solution.py:33
  34.8 0.4 collective-permute-start.15
  35.2 2.6 %collective-permute-done.14.c = bf16[64,768]{1,0:T(8,128)(2,1)S(1)} collective-permute-done((bf16[64,768]{1,0:T(8,128)(2,1)S(1)}, bf16[64,768]{1,0:T(8,128)(2,1)S(1)}, u32[]{:S(2)}, u32[]{:S(2)}) %collective-permute-start.14) | collective-permute-done | bytes 98336 | tf_op jit(solution)/shard_map/ppermute | solution.py:33
  37.7 2.1 %collective-permute-done.15.d = bf16[64,768]{1,0:T(8,128)(2,1)S(1)} collective-permute-done((bf16[64,768]{1,0:T(8,128)(2,1)S(1)}, bf16[64,768]{1,0:T(8,128)(2,1)S(1)}, u32[]{:S(2)}, u32[]{:S(2)}) %collective-permute-start.15) | collective-permute-done | bytes 98336 | tf_op jit(solution)/shard_map/ppermute | solution.py:33
  39.8 0.1 collective-permute-start.16
  39.9 5.0 %collective-permute-start.17 = (bf16[64,512]{1,0:T(8,128)(2,1)S(1)}, bf16[64,512]{1,0:T(8,128)(2,1)S(1)}, u32[]{:S(2)}, u32[]{:S(2)}) collective-permute-start(bf16[64,512]{1,0:T(8,128)(2,1)S(1)} %copy-done.3), channel_id=1, source_target_pairs={{0,1},{1,0},{2,3},{3,2},{4,5},{5,4},{6,7},{7,6},{8,9},{9,8},{10,11... | collective-permute-start | bytes 196616 | tf_op jit(solution)/shard_map/ppermute | solution.py:33
  44.9 2.8 %first_block.1.first_out = bf16[64,1024]{1,0:T(8,128)(2,1)S(1)} custom-call(bf16[2,64,1024]{2,1,0:T(8,128)(2,1)S(1)} %copy-done.2, bf16[3,2,512,1024]{3,2,1,0:T(8,128)(2,1)S(1)} %copy-done.1), custom_call_target="tpu_custom_call" | custom-call | flops 402653184 | bytes 7340032 | tf_op jit(solution)/shard_map/first_block/pallas_call | solution.py:161
  47.8 2.1 %collective-permute-start.22 = (bf16[64,1536]{1,0:T(8,128)(2,1)S(1)}, bf16[64,1536]{1,0:T(8,128)(2,1)S(1)}, u32[]{:S(2)}, u32[]{:S(2)}) collective-permute-start(bf16[64,1536]{1,0:T(8,128)(2,1)S(1)} %constant_dynamic-update-slice_fusion.refs_0_), channel_id=1, source_target_pairs={{0,12},{1,13},{2,14},{3,15},{4,0},{5,1},{6,2},{7,3},{8,4},{9,5},{1... | collective-permute-start | bytes 589832 | tf_op jit(solution)/shard_map/ppermute | solution.py:33
  49.8 0.4 collective-permute-start.21
  50.2 1.8 %collective-permute-start.20 = (bf16[64,1536]{1,0:T(8,128)(2,1)S(1)}, bf16[64,1536]{1,0:T(8,128)(2,1)S(1)}, u32[]{:S(2)}, u32[]{:S(2)}) collective-permute-start(bf16[64,1536]{1,0:T(8,128)(2,1)S(1)} %constant_dynamic-update-slice_fusion.refs_0_), channel_id=1, source_target_pairs={{0,14},{1,15},{2,0},{3,1},{4,2},{5,3},{6,4},{7,5},{8,6},{9,7},{10,... | collective-permute-start | bytes 589832 | tf_op jit(solution)/shard_map/ppermute | solution.py:33
  52.0 7.7 %collective-permute-done.22.refs_4_ = bf16[64,1536]{1,0:T(8,128)(2,1)S(1)} collective-permute-done((bf16[64,1536]{1,0:T(8,128)(2,1)S(1)}, bf16[64,1536]{1,0:T(8,128)(2,1)S(1)}, u32[]{:S(2)}, u32[]{:S(2)}) %collective-permute-start.22) | collective-permute-done | bytes 196640 | tf_op jit(solution)/shard_map/ppermute | solution.py:33
  59.7 1.5 %collective-permute-start.23 = (bf16[64,1536]{1,0:T(8,128)(2,1)S(1)}, bf16[64,1536]{1,0:T(8,128)(2,1)S(1)}, u32[]{:S(2)}, u32[]{:S(2)}) collective-permute-start(bf16[64,1536]{1,0:T(8,128)(2,1)S(1)} %collective-permute-done.21.refs_3_), channel_id=1, source_target_pairs={{0,2},{1,3},{2,4},{3,5},{4,6},{5,7},{6,8},{7,9},{8,10},{9,11},{10,... | collective-permute-start | bytes 589832 | tf_op jit(solution)/shard_map/ppermute | solution.py:33
  61.2 2.0 %collective-permute-start.26 = (bf16[32,1536]{1,0:T(8,128)(2,1)S(1)}, bf16[32,1536]{1,0:T(8,128)(2,1)S(1)}, u32[]{:S(2)}, u32[]{:S(2)}) collective-permute-start(bf16[32,1536]{1,0:T(8,128)(2,1)S(1)} %slice.9), channel_id=1, source_target_pairs={{0,12},{1,13},{2,14},{3,15},{4,0},{5,1},{6,2},{7,3},{8,4},{9,5},{1... | collective-permute-start | bytes 294920 | tf_op jit(solution)/shard_map/ppermute | solution.py:33
  63.2 0.7 collective-permute-start.25
  63.9 0.3 collective-permute-done.19.refs_1_
  64.2 8.2 %collective-permute-done.26.refs_8_ = bf16[32,1536]{1,0:T(8,128)(2,1)S(1)} collective-permute-done((bf16[32,1536]{1,0:T(8,128)(2,1)S(1)}, bf16[32,1536]{1,0:T(8,128)(2,1)S(1)}, u32[]{:S(2)}, u32[]{:S(2)}) %collective-permute-start.26) | collective-permute-done | bytes 98336 | tf_op jit(solution)/shard_map/ppermute | solution.py:33
  72.4 0.8 pack.1
  73.2 3.1 %collective-permute-start.27 = (bf16[512,512]{1,0:T(8,128)(2,1)S(1)}, bf16[512,512]{1,0:T(8,128)(2,1)S(1)}, u32[]{:S(2)}, u32[]{:S(2)}) collective-permute-start(bf16[512,512]{1,0:T(8,128)(2,1)S(1)} %get-tuple-element.102.mine), channel_id=1, source_target_pairs={{0,1},{1,0},{2,3},{3,2},{4,5},{5,4},{6,7},{7,6},{8,9},{9,8},{10,11... | collective-permute-start | bytes 1572872 | tf_op jit(solution)/shard_map/ppermute | solution.py:33
  76.2 3.1 %project.1.mine = f32[256,1024]{1,0:T(8,128)S(1)} custom-call(bf16[512,1024]{1,0:T(8,128)(2,1)S(1)} %get-tuple-element.99.scaled, bf16[3,2,512,1024]{3,2,1,0:T(8,128)(2,1)S(1)} %copy-done.1, bf16[64,512]{1,0:T(8,128)(2,1)S(1)} %copy-done.3, bf16[64,512]{1,0:T(8,128)(2,1)S(1)} %collective-permute-done.17.query_core, ...), custom_call_target="tpu_custom_call" | custom-call | flops 2200000000 | bytes 5242880 | tf_op jit(solution)/shard_map/project/pallas_call | solution.py:410
  79.4 0.1 collective-permute-start.28
  79.5 2.5 %renew_third.1.rows = bf16[256,1024]{1,0:T(8,128)(2,1)S(1)} custom-call(bf16[512,512]{1,0:T(8,128)(2,1)S(1)} %get-tuple-element.102.mine, bf16[512,512]{1,0:T(8,128)(2,1)S(1)} %collective-permute-done.27.other, bf16[3,2,512,1024]{3,2,1,0:T(8,128)(2,1)S(1)} %copy-done.1), custom_call_target="tpu_custom_call" | custom-call | flops 1200000000 | bytes 4194304 | tf_op jit(solution)/shard_map/renew_third/pallas_call | solution.py:445
  81.9 0.2 collective-permute-done.28.other
  82.1 0.5 down.1
  82.6 0.4 collective-permute-start.29
  83.1 2.0 %collective-permute-start.30 = (bf16[64,256]{1,0:T(8,128)(2,1)S(1)}, bf16[64,256]{1,0:T(8,128)(2,1)S(1)}, u32[]{:S(2)}, u32[]{:S(2)}) collective-permute-start(bf16[64,256]{1,0:T(8,128)(2,1)S(1)} %get-tuple-element.107), channel_id=1, source_target_pairs={{0,48},{1,49},{2,50},{3,51},{4,52},{5,53},{6,54},{7,55},{8,56},{9,... | collective-permute-start | bytes 98312 | tf_op jit(solution)/shard_map/ppermute | solution.py:33
  85.1 1.0 %collective-permute-start.31 = (bf16[64,256]{1,0:T(8,128)(2,1)S(1)}, bf16[64,256]{1,0:T(8,128)(2,1)S(1)}, u32[]{:S(2)}, u32[]{:S(2)}) collective-permute-start(bf16[64,256]{1,0:T(8,128)(2,1)S(1)} %get-tuple-element.108), channel_id=1, source_target_pairs={{0,49},{1,48},{2,51},{3,50},{4,53},{5,52},{6,55},{7,54},{8,57},{9,... | collective-permute-start | bytes 98312 | tf_op jit(solution)/shard_map/ppermute | solution.py:33
  86.1 0.9 %collective-permute-done.30.far = bf16[64,256]{1,0:T(8,128)(2,1)S(1)} collective-permute-done((bf16[64,256]{1,0:T(8,128)(2,1)S(1)}, bf16[64,256]{1,0:T(8,128)(2,1)S(1)}, u32[]{:S(2)}, u32[]{:S(2)}) %collective-permute-start.30) | collective-permute-done | bytes 32800 | tf_op jit(solution)/shard_map/ppermute | solution.py:33
  87.0 2.8 %collective-permute-done.31.far_core = bf16[64,256]{1,0:T(8,128)(2,1)S(1)} collective-permute-done((bf16[64,256]{1,0:T(8,128)(2,1)S(1)}, bf16[64,256]{1,0:T(8,128)(2,1)S(1)}, u32[]{:S(2)}, u32[]{:S(2)}) %collective-permute-start.31) | collective-permute-done | bytes 32800 | tf_op jit(solution)/shard_map/ppermute | solution.py:33
  89.8 0.7 finish.1
  (43 shorter events, 0.2 us)
Async XLA Ops:
  2.2 8.8 %collective-permute-start = (bf16[128,512]{1,0:T(8,128)(2,1)}, bf16[128,512]{1,0:T(8,128)(2,1)S(1)}, u32[]{:S(2)}, u32[]{:S(2)}) collective-permute-start(bf16[128,512]{1,0:T(8,128)(2,1)} %get-tuple-element.59), channel_id=1, source_target_pairs={{0,16},{1,17},{2,18},{3,19},{4,20},{5,21},{6,22},{7,23},{8,24},{9,... | collective-permute-start | bytes 393224 | tf_op jit(solution)/shard_map/ppermute | solution.py:33
  4.3 8.4 %collective-permute-start.1 = (bf16[128,512]{1,0:T(8,128)(2,1)}, bf16[128,512]{1,0:T(8,128)(2,1)S(1)}, u32[]{:S(2)}, u32[]{:S(2)}) collective-permute-start(bf16[128,512]{1,0:T(8,128)(2,1)} %get-tuple-element.60), channel_id=1, source_target_pairs={{0,32},{1,33},{2,34},{3,35},{4,36},{5,37},{6,38},{7,39},{8,40},{9,... | collective-permute-start | bytes 393224 | tf_op jit(solution)/shard_map/ppermute | solution.py:33
  6.7 5.9 %collective-permute-start.2 = (bf16[128,512]{1,0:T(8,128)(2,1)}, bf16[128,512]{1,0:T(8,128)(2,1)S(1)}, u32[]{:S(2)}, u32[]{:S(2)}) collective-permute-start(bf16[128,512]{1,0:T(8,128)(2,1)} %get-tuple-element.61), channel_id=1, source_target_pairs={{0,48},{1,49},{2,50},{3,51},{4,52},{5,53},{6,54},{7,55},{8,56},{9,... | collective-permute-start | bytes 393224 | tf_op jit(solution)/shard_map/ppermute | solution.py:33
  7.9 2.8 %copy-start = (bf16[3,2,512,1024]{3,2,1,0:T(8,128)(2,1)S(1)}, bf16[3,2,512,1024]{3,2,1,0:T(8,128)(2,1)}, u32[]{:S(2)}) copy-start(bf16[3,2,512,1024]{3,2,1,0:T(8,128)(2,1)} %weights.3) | copy-start | bytes 18874372
  10.6 2.0 %copy-start.4 = (bf16[128,512]{1,0:T(8,128)(2,1)S(1)}, bf16[128,512]{1,0:T(8,128)(2,1)}, u32[]{:S(2)}) copy-start(bf16[128,512]{1,0:T(8,128)(2,1)} %get-tuple-element.64.refs_0_) | copy-start | bytes 393220
  10.7 4.6 %copy-start.5 = (bf16[64,512]{1,0:T(8,128)(2,1)S(1)}, bf16[64,512]{1,0:T(8,128)(2,1)}, u32[]{:S(2)}) copy-start(bf16[64,512]{1,0:T(8,128)(2,1)} %get-tuple-element.78) | copy-start | bytes 196612
  10.7 29.3 %copy-start.3 = (bf16[64,512]{1,0:T(8,128)(2,1)S(1)}, bf16[64,512]{1,0:T(8,128)(2,1)}, u32[]{:S(2)}) copy-start(bf16[64,512]{1,0:T(8,128)(2,1)} %get-tuple-element.94.query_own) | copy-start | bytes 196612
  10.7 34.3 %copy-start.1 = (bf16[3,2,512,1024]{3,2,1,0:T(8,128)(2,1)S(1)}, bf16[3,2,512,1024]{3,2,1,0:T(8,128)(2,1)}, u32[]{:S(2)}) copy-start(bf16[3,2,512,1024]{3,2,1,0:T(8,128)(2,1)} %weights.3) | copy-start | bytes 18874372
  10.7 34.3 %copy-start.2 = (bf16[2,64,1024]{2,1,0:T(8,128)(2,1)S(1)}, bf16[2,64,1024]{2,1,0:T(8,128)(2,1)}, u32[]{:S(2)}) copy-start(bf16[2,64,1024]{2,1,0:T(8,128)(2,1)} %queries.2) | copy-start | bytes 786436
  12.6 4.5 %collective-permute-start.3 = (bf16[128,512]{1,0:T(8,128)(2,1)S(1)}, bf16[128,512]{1,0:T(8,128)(2,1)S(1)}, u32[]{:S(2)}, u32[]{:S(2)}) collective-permute-start(bf16[128,512]{1,0:T(8,128)(2,1)S(1)} %copy-done.4), channel_id=1, source_target_pairs={{0,1},{1,0},{2,3},{3,2},{4,5},{5,4},{6,7},{7,6},{8,9},{9,8},{10,11... | collective-permute-start | bytes 393224 | tf_op jit(solution)/shard_map/ppermute | solution.py:33
  14.7 2.5 %collective-permute-start.4 = (bf16[128,512]{1,0:T(8,128)(2,1)S(1)}, bf16[128,512]{1,0:T(8,128)(2,1)S(1)}, u32[]{:S(2)}, u32[]{:S(2)}) collective-permute-start(bf16[128,512]{1,0:T(8,128)(2,1)S(1)} %collective-permute-done.refs_1_), channel_id=1, source_target_pairs={{0,1},{1,0},{2,3},{3,2},{4,5},{5,4},{6,7},{7,6},{8,9},{9,8},{10,11... | collective-permute-start | bytes 393224 | tf_op jit(solution)/shard_map/ppermute | solution.py:33
  14.8 2.4 %collective-permute-start.5 = (bf16[128,512]{1,0:T(8,128)(2,1)S(1)}, bf16[128,512]{1,0:T(8,128)(2,1)S(1)}, u32[]{:S(2)}, u32[]{:S(2)}) collective-permute-start(bf16[128,512]{1,0:T(8,128)(2,1)S(1)} %collective-permute-done.1.refs_2_), channel_id=1, source_target_pairs={{0,1},{1,0},{2,3},{3,2},{4,5},{5,4},{6,7},{7,6},{8,9},{9,8},{10,11... | collective-permute-start | bytes 393224 | tf_op jit(solution)/shard_map/ppermute | solution.py:33
  15.2 2.0 %collective-permute-start.6 = (bf16[128,512]{1,0:T(8,128)(2,1)S(1)}, bf16[128,512]{1,0:T(8,128)(2,1)S(1)}, u32[]{:S(2)}, u32[]{:S(2)}) collective-permute-start(bf16[128,512]{1,0:T(8,128)(2,1)S(1)} %collective-permute-done.2.refs_3_), channel_id=1, source_target_pairs={{0,1},{1,0},{2,3},{3,2},{4,5},{5,4},{6,7},{7,6},{8,9},{9,8},{10,11... | collective-permute-start | bytes 393224 | tf_op jit(solution)/shard_map/ppermute | solution.py:33
  15.3 4.3 %collective-permute-start.7 = (bf16[64,512]{1,0:T(8,128)(2,1)S(1)}, bf16[64,512]{1,0:T(8,128)(2,1)S(1)}, u32[]{:S(2)}, u32[]{:S(2)}) collective-permute-start(bf16[64,512]{1,0:T(8,128)(2,1)S(1)} %copy-done.5), channel_id=1, source_target_pairs={{0,48},{1,49},{2,50},{3,51},{4,52},{5,53},{6,54},{7,55},{8,56},{9,... | collective-permute-start | bytes 196616 | tf_op jit(solution)/shard_map/ppermute | solution.py:33
  19.6 11.7 %collective-permute-start.10 = (bf16[64,768]{1,0:T(8,128)(2,1)S(1)}, bf16[64,768]{1,0:T(8,128)(2,1)S(1)}, u32[]{:S(2)}, u32[]{:S(2)}) collective-permute-start(bf16[64,768]{1,0:T(8,128)(2,1)S(1)} %get-tuple-element.84), channel_id=1, source_target_pairs={{0,2},{1,3},{2,4},{3,5},{4,6},{5,7},{6,8},{7,9},{8,10},{9,11},{10,... | collective-permute-start | bytes 294920 | tf_op jit(solution)/shard_map/ppermute | solution.py:33
  20.8 10.5 %collective-permute-start.11 = (bf16[64,768]{1,0:T(8,128)(2,1)S(1)}, bf16[64,768]{1,0:T(8,128)(2,1)S(1)}, u32[]{:S(2)}, u32[]{:S(2)}) collective-permute-start(bf16[64,768]{1,0:T(8,128)(2,1)S(1)} %get-tuple-element.85), channel_id=1, source_target_pairs={{0,14},{1,15},{2,0},{3,1},{4,2},{5,3},{6,4},{7,5},{8,6},{9,7},{10,... | collective-permute-start | bytes 294920 | tf_op jit(solution)/shard_map/ppermute | solution.py:33
  24.7 6.0 %collective-permute-start.12 = (bf16[32,768]{1,0:T(8,128)(2,1)S(1)}, bf16[32,768]{1,0:T(8,128)(2,1)S(1)}, u32[]{:S(2)}, u32[]{:S(2)}) collective-permute-start(bf16[32,768]{1,0:T(8,128)(2,1)S(1)} %get-tuple-element.86), channel_id=1, source_target_pairs={{0,4},{1,5},{2,6},{3,7},{4,8},{5,9},{6,10},{7,11},{8,12},{9,13},{1... | collective-permute-start | bytes 147464 | tf_op jit(solution)/shard_map/ppermute | solution.py:33
  24.7 6.5 %collective-permute-start.13 = (bf16[32,768]{1,0:T(8,128)(2,1)S(1)}, bf16[32,768]{1,0:T(8,128)(2,1)S(1)}, u32[]{:S(2)}, u32[]{:S(2)}) collective-permute-start(bf16[32,768]{1,0:T(8,128)(2,1)S(1)} %get-tuple-element.87), channel_id=1, source_target_pairs={{0,12},{1,13},{2,14},{3,15},{4,0},{5,1},{6,2},{7,3},{8,4},{9,5},{1... | collective-permute-start | bytes 147464 | tf_op jit(solution)/shard_map/ppermute | solution.py:33
  28.3 6.9 %collective-permute-start.8 = (bf16[64,768]{1,0:T(8,128)(2,1)S(1)}, bf16[64,768]{1,0:T(8,128)(2,1)S(1)}, u32[]{:S(2)}, u32[]{:S(2)}) collective-permute-start(bf16[64,768]{1,0:T(8,128)(2,1)S(1)} %get-tuple-element.80), channel_id=1, source_target_pairs={{0,2},{1,3},{2,4},{3,5},{4,6},{5,7},{6,8},{7,9},{8,10},{9,11},{10,... | collective-permute-start | bytes 294920 | tf_op jit(solution)/shard_map/ppermute | solution.py:33
  30.7 4.5 %collective-permute-start.9 = (bf16[64,768]{1,0:T(8,128)(2,1)S(1)}, bf16[64,768]{1,0:T(8,128)(2,1)S(1)}, u32[]{:S(2)}, u32[]{:S(2)}) collective-permute-start(bf16[64,768]{1,0:T(8,128)(2,1)S(1)} %get-tuple-element.81), channel_id=1, source_target_pairs={{0,14},{1,15},{2,0},{3,1},{4,2},{5,3},{6,4},{7,5},{8,6},{9,7},{10,... | collective-permute-start | bytes 294920 | tf_op jit(solution)/shard_map/ppermute | solution.py:33
  31.3 6.4 %collective-permute-start.14 = (bf16[64,768]{1,0:T(8,128)(2,1)S(1)}, bf16[64,768]{1,0:T(8,128)(2,1)S(1)}, u32[]{:S(2)}, u32[]{:S(2)}) collective-permute-start(bf16[64,768]{1,0:T(8,128)(2,1)S(1)} %get-tuple-element.88), channel_id=1, source_target_pairs={{0,4},{1,5},{2,6},{3,7},{4,8},{5,9},{6,10},{7,11},{8,12},{9,13},{1... | collective-permute-start | bytes 294920 | tf_op jit(solution)/shard_map/ppermute | solution.py:33
  34.8 5.0 %collective-permute-start.15 = (bf16[64,768]{1,0:T(8,128)(2,1)S(1)}, bf16[64,768]{1,0:T(8,128)(2,1)S(1)}, u32[]{:S(2)}, u32[]{:S(2)}) collective-permute-start(bf16[64,768]{1,0:T(8,128)(2,1)S(1)} %get-tuple-element.89), channel_id=1, source_target_pairs={{0,12},{1,13},{2,14},{3,15},{4,0},{5,1},{6,2},{7,3},{8,4},{9,5},{1... | collective-permute-start | bytes 294920 | tf_op jit(solution)/shard_map/ppermute | solution.py:33
  39.8 7.9 %collective-permute-start.16 = (bf16[64,768]{1,0:T(8,128)(2,1)S(1)}, bf16[64,768]{1,0:T(8,128)(2,1)S(1)}, u32[]{:S(2)}, u32[]{:S(2)}) collective-permute-start(bf16[64,768]{1,0:T(8,128)(2,1)S(1)} %add_up.1), channel_id=1, source_target_pairs={{0,16},{1,17},{2,18},{3,19},{4,20},{5,21},{6,22},{7,23},{8,24},{9,... | collective-permute-start | bytes 294920 | tf_op jit(solution)/shard_map/ppermute | solution.py:33
  39.9 7.8 %collective-permute-start.17 = (bf16[64,512]{1,0:T(8,128)(2,1)S(1)}, bf16[64,512]{1,0:T(8,128)(2,1)S(1)}, u32[]{:S(2)}, u32[]{:S(2)}) collective-permute-start(bf16[64,512]{1,0:T(8,128)(2,1)S(1)} %copy-done.3), channel_id=1, source_target_pairs={{0,1},{1,0},{2,3},{3,2},{4,5},{5,4},{6,7},{7,6},{8,9},{9,8},{10,11... | collective-permute-start | bytes 196616 | tf_op jit(solution)/shard_map/ppermute | solution.py:33
  44.9 2.8 %collective-permute-start.18 = (bf16[64,512]{1,0:T(8,128)(2,1)S(1)}, bf16[64,512]{1,0:T(8,128)(2,1)S(1)}, u32[]{:S(2)}, u32[]{:S(2)}) collective-permute-start(bf16[64,512]{1,0:T(8,128)(2,1)S(1)} %collective-permute-done.7.query_far), channel_id=1, source_target_pairs={{0,1},{1,0},{2,3},{3,2},{4,5},{5,4},{6,7},{7,6},{8,9},{9,8},{10,11... | collective-permute-start | bytes 196616 | tf_op jit(solution)/shard_map/ppermute | solution.py:33
  47.8 12.0 %collective-permute-start.22 = (bf16[64,1536]{1,0:T(8,128)(2,1)S(1)}, bf16[64,1536]{1,0:T(8,128)(2,1)S(1)}, u32[]{:S(2)}, u32[]{:S(2)}) collective-permute-start(bf16[64,1536]{1,0:T(8,128)(2,1)S(1)} %constant_dynamic-update-slice_fusion.refs_0_), channel_id=1, source_target_pairs={{0,12},{1,13},{2,14},{3,15},{4,0},{5,1},{6,2},{7,3},{8,4},{9,5},{1... | collective-permute-start | bytes 589832 | tf_op jit(solution)/shard_map/ppermute | solution.py:33
  49.8 9.9 %collective-permute-start.21 = (bf16[64,1536]{1,0:T(8,128)(2,1)S(1)}, bf16[64,1536]{1,0:T(8,128)(2,1)S(1)}, u32[]{:S(2)}, u32[]{:S(2)}) collective-permute-start(bf16[64,1536]{1,0:T(8,128)(2,1)S(1)} %constant_dynamic-update-slice_fusion.refs_0_), channel_id=1, source_target_pairs={{0,4},{1,5},{2,6},{3,7},{4,8},{5,9},{6,10},{7,11},{8,12},{9,13},{1... | collective-permute-start | bytes 589832 | tf_op jit(solution)/shard_map/ppermute | solution.py:33
  50.2 12.9 %collective-permute-start.20 = (bf16[64,1536]{1,0:T(8,128)(2,1)S(1)}, bf16[64,1536]{1,0:T(8,128)(2,1)S(1)}, u32[]{:S(2)}, u32[]{:S(2)}) collective-permute-start(bf16[64,1536]{1,0:T(8,128)(2,1)S(1)} %constant_dynamic-update-slice_fusion.refs_0_), channel_id=1, source_target_pairs={{0,14},{1,15},{2,0},{3,1},{4,2},{5,3},{6,4},{7,5},{8,6},{9,7},{10,... | collective-permute-start | bytes 589832 | tf_op jit(solution)/shard_map/ppermute | solution.py:33
  52.0 12.1 %collective-permute-start.19 = (bf16[64,1536]{1,0:T(8,128)(2,1)S(1)}, bf16[64,1536]{1,0:T(8,128)(2,1)S(1)}, u32[]{:S(2)}, u32[]{:S(2)}) collective-permute-start(bf16[64,1536]{1,0:T(8,128)(2,1)S(1)} %constant_dynamic-update-slice_fusion.refs_0_), channel_id=1, source_target_pairs={{0,2},{1,3},{2,4},{3,5},{4,6},{5,7},{6,8},{7,9},{8,10},{9,11},{10,... | collective-permute-start | bytes 589832 | tf_op jit(solution)/shard_map/ppermute | solution.py:33
  59.7 12.6 %collective-permute-start.24 = (bf16[64,1536]{1,0:T(8,128)(2,1)S(1)}, bf16[64,1536]{1,0:T(8,128)(2,1)S(1)}, u32[]{:S(2)}, u32[]{:S(2)}) collective-permute-start(bf16[64,1536]{1,0:T(8,128)(2,1)S(1)} %collective-permute-done.22.refs_4_), channel_id=1, source_target_pairs={{0,14},{1,15},{2,0},{3,1},{4,2},{5,3},{6,4},{7,5},{8,6},{9,7},{10,... | collective-permute-start | bytes 589832 | tf_op jit(solution)/shard_map/ppermute | solution.py:33
  59.7 12.6 %collective-permute-start.23 = (bf16[64,1536]{1,0:T(8,128)(2,1)S(1)}, bf16[64,1536]{1,0:T(8,128)(2,1)S(1)}, u32[]{:S(2)}, u32[]{:S(2)}) collective-permute-start(bf16[64,1536]{1,0:T(8,128)(2,1)S(1)} %collective-permute-done.21.refs_3_), channel_id=1, source_target_pairs={{0,2},{1,3},{2,4},{3,5},{4,6},{5,7},{6,8},{7,9},{8,10},{9,11},{10,... | collective-permute-start | bytes 589832 | tf_op jit(solution)/shard_map/ppermute | solution.py:33
  61.2 11.2 %collective-permute-start.26 = (bf16[32,1536]{1,0:T(8,128)(2,1)S(1)}, bf16[32,1536]{1,0:T(8,128)(2,1)S(1)}, u32[]{:S(2)}, u32[]{:S(2)}) collective-permute-start(bf16[32,1536]{1,0:T(8,128)(2,1)S(1)} %slice.9), channel_id=1, source_target_pairs={{0,12},{1,13},{2,14},{3,15},{4,0},{5,1},{6,2},{7,3},{8,4},{9,5},{1... | collective-permute-start | bytes 294920 | tf_op jit(solution)/shard_map/ppermute | solution.py:33
  63.2 9.2 %collective-permute-start.25 = (bf16[32,1536]{1,0:T(8,128)(2,1)S(1)}, bf16[32,1536]{1,0:T(8,128)(2,1)S(1)}, u32[]{:S(2)}, u32[]{:S(2)}) collective-permute-start(bf16[32,1536]{1,0:T(8,128)(2,1)S(1)} %slice.8), channel_id=1, source_target_pairs={{0,4},{1,5},{2,6},{3,7},{4,8},{5,9},{6,10},{7,11},{8,12},{9,13},{1... | collective-permute-start | bytes 294920 | tf_op jit(solution)/shard_map/ppermute | solution.py:33
  73.2 6.2 %collective-permute-start.27 = (bf16[512,512]{1,0:T(8,128)(2,1)S(1)}, bf16[512,512]{1,0:T(8,128)(2,1)S(1)}, u32[]{:S(2)}, u32[]{:S(2)}) collective-permute-start(bf16[512,512]{1,0:T(8,128)(2,1)S(1)} %get-tuple-element.102.mine), channel_id=1, source_target_pairs={{0,1},{1,0},{2,3},{3,2},{4,5},{5,4},{6,7},{7,6},{8,9},{9,8},{10,11... | collective-permute-start | bytes 1572872 | tf_op jit(solution)/shard_map/ppermute | solution.py:33
  79.4 2.7 %collective-permute-start.28 = (f32[256,1024]{1,0:T(8,128)S(1)}, f32[256,1024]{1,0:T(8,128)S(1)}, u32[]{:S(2)}, u32[]{:S(2)}) collective-permute-start(f32[256,1024]{1,0:T(8,128)S(1)} %project.1.mine), channel_id=1, source_target_pairs={{0,1},{1,0},{2,3},{3,2},{4,5},{5,4},{6,7},{7,6},{8,9},{9,8},{10,11... | collective-permute-start | bytes 3145736 | tf_op jit(solution)/shard_map/ppermute | solution.py:33
  82.6 3.4 %collective-permute-start.29 = (bf16[64,256]{1,0:T(8,128)(2,1)S(1)}, bf16[64,256]{1,0:T(8,128)(2,1)S(1)}, u32[]{:S(2)}, u32[]{:S(2)}) collective-permute-start(bf16[64,256]{1,0:T(8,128)(2,1)S(1)} %get-tuple-element.106), channel_id=1, source_target_pairs={{0,1},{1,0},{2,3},{3,2},{4,5},{5,4},{6,7},{7,6},{8,9},{9,8},{10,11... | collective-permute-start | bytes 98312 | tf_op jit(solution)/shard_map/ppermute | solution.py:33
  83.1 4.0 %collective-permute-start.30 = (bf16[64,256]{1,0:T(8,128)(2,1)S(1)}, bf16[64,256]{1,0:T(8,128)(2,1)S(1)}, u32[]{:S(2)}, u32[]{:S(2)}) collective-permute-start(bf16[64,256]{1,0:T(8,128)(2,1)S(1)} %get-tuple-element.107), channel_id=1, source_target_pairs={{0,48},{1,49},{2,50},{3,51},{4,52},{5,53},{6,54},{7,55},{8,56},{9,... | collective-permute-start | bytes 98312 | tf_op jit(solution)/shard_map/ppermute | solution.py:33
  85.1 4.7 %collective-permute-start.31 = (bf16[64,256]{1,0:T(8,128)(2,1)S(1)}, bf16[64,256]{1,0:T(8,128)(2,1)S(1)}, u32[]{:S(2)}, u32[]{:S(2)}) collective-permute-start(bf16[64,256]{1,0:T(8,128)(2,1)S(1)} %get-tuple-element.108), channel_id=1, source_target_pairs={{0,49},{1,48},{2,51},{3,50},{4,53},{5,52},{6,55},{7,54},{8,57},{9,... | collective-permute-start | bytes 98312 | tf_op jit(solution)/shard_map/ppermute | solution.py:33

commit v5 on v4

--- a/solution.py
+++ b/solution.py
@@ -16,6 +16,9 @@
 VMEM = pl.BlockSpec(memory_space=pltpu.VMEM)
 ANY = pl.BlockSpec(memory_space=pl.ANY)
 HBM = pl.BlockSpec(memory_space=pltpu.HBM)
+
+
+barrier = lax.optimization_barrier
 
 
 def place():
@@ -203,8 +206,8 @@
 
 def gradient_kernel(*refs):
     pieces, w = refs[:8], refs[8]
-    own, near_up, near_down, keep_up, keep_down, send_up, send_down, far_up, far_down = refs[9:18]
-    k, v, d, gated, total = refs[18:]
+    own, up, down, keep_up, keep_down, far_up, far_down = refs[9:16]
+    k, v, d, gated, total = refs[16:]
     _, z, c = place()
     tokens = pieces[0].shape[0] // 2
     for i, piece in enumerate(pieces):
@@ -233,12 +236,12 @@
         return total[at_place(lax.rem(z + distance + Z, Z) * ROWS, ROWS), :]
 
     own[...] = rows(0)
-    near_up[...] = rows(1).astype(BF)
-    near_down[...] = rows(-1).astype(BF)
+    up[:ROWS, :] = rows(1).astype(BF)
+    up[ROWS:, :] = rows(3).astype(BF)
+    down[:ROWS, :] = rows(-1).astype(BF)
+    down[ROWS:, :] = rows(-3).astype(BF)
     keep_up[...] = rows(2)
     keep_down[...] = rows(-2)
-    send_up[...] = rows(3).astype(BF)
-    send_down[...] = rows(-3).astype(BF)
     far = rows(4).astype(BF)
     far_up[...] = far[: ROWS // 2]
     far_down[...] = far[ROWS // 2 :]
@@ -246,12 +249,12 @@
 
 def gradient(pieces, weights):
     tokens = 8 * pieces[0].shape[0] // 2
-    kept, sent, half = shape(ROWS, WIDE, dtype=F32), shape(ROWS, WIDE), shape(ROWS // 2, WIDE)
+    kept, sent, half = shape(ROWS, WIDE, dtype=F32), shape(2 * ROWS, WIDE), shape(ROWS // 2, WIDE)
     return pl.pallas_call(
         gradient_kernel,
-        out_shape=(kept, sent, sent, kept, kept, sent, sent, half, half),
+        out_shape=(kept, sent, sent, kept, kept, half, half),
         in_specs=[VMEM] * 9,
-        out_specs=(VMEM,) * 9,
+        out_specs=(VMEM,) * 7,
         scratch_shapes=[
             pltpu.VMEM((tokens, DIM), BF),
             pltpu.VMEM((tokens, DIM), BF),
@@ -267,10 +270,10 @@
 
 def middle_kernel(keep_up, keep_down, got_up, got_down, far_up, far_down, up, down):
     half = ROWS // 2
-    total = keep_up[...] + got_up[...].astype(F32)
+    total = keep_up[...] + got_up[ROWS:, :].astype(F32)
     up[:half, :] = (total[:half] + far_up[...].astype(F32)).astype(BF)
     up[half:, :] = total[half:].astype(BF)
-    total = keep_down[...] + got_down[...].astype(F32)
+    total = keep_down[...] + got_down[ROWS:, :].astype(F32)
     down[:half, :] = total[:half].astype(BF)
     down[half:, :] = (total[half:] + far_down[...].astype(F32)).astype(BF)
 
@@ -287,7 +290,7 @@
 
 
 def total_kernel(own, a, b, c, d, out):
-    total = own[...] + a[...].astype(F32) + b[...].astype(F32) + c[...].astype(F32)
+    total = own[...] + a[:ROWS, :].astype(F32) + b[:ROWS, :].astype(F32) + c[...].astype(F32)
     out[...] = (total + d[...].astype(F32)).astype(BF)
 
 
@@ -302,14 +305,17 @@
     )(*args)
 
 
-def reduce_rows(parts):
-    own, near_up, near_down, keep_up, keep_down, send_up, send_down, far_up, far_down = parts
+def reduce_rows(parts, query_own, query_far):
+    own, up, down, keep_up, keep_down, far_up, far_down = parts
     far_up, far_down = along_z(far_up, 2), along_z(far_down, -2)
-    got_up, got_down = along_z(send_up, 1), along_z(send_down, -1)
-    near_up, near_down = along_z(near_up, 1), along_z(near_down, -1)
+    got_up, got_down = along_z(up, 1), along_z(down, -1)
     up, down = middle(keep_up, keep_down, got_up, got_down, far_up, far_down)
+    up, down, query_own, query_far = barrier((up, down, query_own, query_far))
     up, down = along_z(up, 2), along_z(down, -2)
-    return add_up(own, near_up, near_down, up, down)
+    up, down, query_core, query_far_core = barrier(
+        (up, down, other_core(query_own), other_core(query_far))
+    )
+    return add_up(own, got_up, got_down, up, down), (query_own, query_core, query_far, query_far_core)
 
 
 ORIGINS = ((0, 0, ROWS), (-1, 0, ROWS), (1, 0, ROWS), (-2, 0, ROWS), (2, 0, ROWS)) + (
@@ -320,12 +326,15 @@
 )
 
 
-def gather_rows(own):
+def gather_rows(own, queries, weights):
+    own = jnp.concatenate([own, pair_x(own)], axis=1)
+    own, queries = barrier((own, queries))
     up1, down1 = along_z(own, 1), along_z(own, -1)
     up2, down2 = along_z(own, 2), along_z(own, -2)
+    up2, down2, first_out = barrier((up2, down2, first_block(queries, weights)))
     up3, down3 = along_z(up2, 1), along_z(down2, -1)
     up4, down4 = along_z(up2[: ROWS // 2], 2), along_z(down2[ROWS // 2 :], -2)
-    return [own, up1, down1, up2, down2, up3, down3, up4, down4]
+    return [own, up1, down1, up2, down2, up3, down3, up4, down4], first_out
 
 
 def pack_kernel(*refs):
@@ -518,27 +527,20 @@
 
 
 def body(queries, keys, values, rates, weights):
-    barrier = lax.optimization_barrier
     own, far1, far2, far3, query_own, query_far = prepare(queries, keys, values, rates)
     own, weights = barrier((own, weights))
-    got = [own, along_x(far1, 1), along_x(far2, 2), along_x(far3, 3)]
-    got, query_far, part = barrier((got, query_far, load(weights)))
+    got1, got2, got3 = along_x(far1, 1), along_x(far2, 2), along_x(far3, 3)
+    got2, query_far, part = barrier((got2, query_far, load(weights)))
     query_far = mirror_x(query_far)
+    got = [own, got1, got2, got3]
     got += [other_core(piece) for piece in got]
     parts, query_far = barrier((gradient(got, part), query_far))
-    own, queries, query_own, query_far = barrier(
-        (reduce_rows(parts), queries, query_own, query_far)
-    )
-    first_out = first_block(queries, weights)
-    query_core, query_far_core = other_core(query_own), other_core(query_far)
-    own, near, first_out, query_core, query_far_core = barrier(
-        (own, pair_x(own), first_out, query_core, query_far_core)
-    )
-    pieces = gather_rows(jnp.concatenate([own, near], axis=1))
+    own, late_queries = reduce_rows(parts, query_own, query_far)
+    pieces, first_out = gather_rows(own, queries, weights)
     matrix, shared = pack(pieces)
     shared_core = other_core(shared)
-    projected = project(matrix, weights, query_own, query_core, query_far, query_far_core)
-    projected, shared_core = lax.optimization_barrier((projected, shared_core))
+    projected = project(matrix, weights, *late_queries)
+    projected, shared_core = barrier((projected, shared_core))
     projected_core = other_core(projected)
     rows = renew_third(shared, shared_core, weights)
     own, core, far, far_core = down(projected, projected_core, rows)

time: 90.7 us -> 87.7 us (0.967)
  waiting for transfers between devices: 29.1 us -> 24.2 us
  starting transfers between devices: 43.4 us -> 45.4 us
    ppermute x32 -> x30, waiting for transfers between devices: 29.1 us -> 24.2 us  [move(): return lax.ppermute(array, 'ctx', perm)]
    ppermute x32 -> x30, starting transfers between devices: 43.4 us -> 45.4 us  [move(): return lax.ppermute(array, 'ctx', perm)]
    unnamed x13 -> x12, local copies, waits for them, and re-layouts: 2.81 us -> 2.81 us
  transfers between devices with their start and end apart: 32 -> 30, of which waited for: 11 -> 14; matrix products, arithmetic and copies ran while one was open for 0% -> 0% of each run, Pallas kernels for 12% -> 12%
where the time goes in v5:
time: 87.7 us; the launch traced here: 87.6 us
  starting transfers between devices  45.4 us (52%)
  waiting for transfers between devices  24.2 us (28%)
  Pallas kernels  14.9 us (17%)
  local copies, waits for them, and re-layouts  2.82 us (3%)
    ppermute x30, starting transfers between devices, move(): return lax.ppermute(array, 'ctx', perm)  45.4 us
    ppermute x30, waiting for transfers between devices, move(): return lax.ppermute(array, 'ctx', perm)  24.2 us
    pallas_call x1, Pallas kernels, project(): pl.pallas_call(project_kernel, out_shape=shape(4 * tokens, FF, dtype=F32)...  3.11 us
    unnamed x12, local copies, waits for them, and re-layouts  2.81 us
    pallas_call x1, Pallas kernels, first_block(): pl.pallas_call(first_kernel, out_shape=shape(tokens, 2 * DIM), in_specs=[...  2.75 us
    pallas_call x1, Pallas kernels, renew_third(): pl.pallas_call(third_kernel, out_shape=shape(rows, FF), in_specs=[VMEM, V...  2.43 us
    pallas_call x1, Pallas kernels, prepare(): pl.pallas_call(prepare_kernel, out_shape=(pair, pair, pair, pair, half, h...  2.15 us
    pallas_call x1, Pallas kernels, gradient(): pl.pallas_call(gradient_kernel, out_shape=(kept, sent, sent, kept, kept,...  2.11 us
  transfers between devices with their start and end apart: 30, of which 14 were waited for; matrix products, arithmetic and copies ran while one was open for 0% of the time, Pallas kernels for 12%

profile of v5, /device:TPU:1, one launch (start us, length us, event | category | flops | bytes accessed | tf_op | source)
XLA Modules:
  0.0 87.6 jit_solution(14697026890250570868)
XLA Ops:
  0.0 2.2 %prepare.1 = (bf16[128,512]{1,0:T(8,128)(2,1)}, bf16[128,512]{1,0:T(8,128)(2,1)}, bf16[128,512]{1,0:T(8,128)(2,1)}, bf16[128,512]{1,0:T(8,128)(2,1)}, bf16[64,512]{1,0:T(8,128)(2,1)}, /*index=5*/bf16[64,512]{1,0:T(8,128)(2,1)}) custom-call(bf16[2,64,1024]{2,1,0:T(8,128)(2,1)} %queries.2, bf16[1,64,1024]{2,1,0:T(8,128)(2,1)} %keys.1, ...), custom_call_target="tpu_custom_call" | custom-call | tf_op jit(solution)/shard_map/prepare/pallas_call | solution.py:124
  2.2 3.6 %collective-permute-start.1 = (bf16[128,512]{1,0:T(8,128)(2,1)}, bf16[128,512]{1,0:T(8,128)(2,1)S(1)}, u32[]{:S(2)}, u32[]{:S(2)}) collective-permute-start(bf16[128,512]{1,0:T(8,128)(2,1)} %get-tuple-element.57), channel_id=1, source_target_pairs={{0,32},{1,33},{2,34},{3,35},{4,36},{5,37},{6,38},{7,39},{8,40},{9,... | collective-permute-start | bytes 393224 | tf_op jit(solution)/shard_map/ppermute | solution.py:36
  5.8 0.3 collective-permute-start
  6.1 2.4 %collective-permute-start.2 = (bf16[128,512]{1,0:T(8,128)(2,1)}, bf16[128,512]{1,0:T(8,128)(2,1)S(1)}, u32[]{:S(2)}, u32[]{:S(2)}) collective-permute-start(bf16[128,512]{1,0:T(8,128)(2,1)} %get-tuple-element.61), channel_id=1, source_target_pairs={{0,48},{1,49},{2,50},{3,51},{4,52},{5,53},{6,54},{7,55},{8,56},{9,... | collective-permute-start | bytes 393224 | tf_op jit(solution)/shard_map/ppermute | solution.py:36
  8.5 1.5 %collective-permute-start.3 = (bf16[128,512]{1,0:T(8,128)(2,1)}, bf16[128,512]{1,0:T(8,128)(2,1)S(1)}, u32[]{:S(2)}, u32[]{:S(2)}) collective-permute-start(bf16[128,512]{1,0:T(8,128)(2,1)} %get-tuple-element.55.refs_0_), channel_id=1, source_target_pairs={{0,1},{1,0},{2,3},{3,2},{4,5},{5,4},{6,7},{7,6},{8,9},{9,8},{10,11... | collective-permute-start | bytes 393224 | tf_op jit(solution)/shard_map/ppermute | solution.py:36
  10.0 2.8 %copy-done = bf16[3,2,512,1024]{3,2,1,0:T(8,128)(2,1)S(1)} copy-done((bf16[3,2,512,1024]{3,2,1,0:T(8,128)(2,1)S(1)}, bf16[3,2,512,1024]{3,2,1,0:T(8,128)(2,1)}, u32[]{:S(2)}) %copy-start) | copy-done | bytes 6291480
  12.8 0.3 load.1.refs_8_
  13.1 0.1 collective-permute-done.refs_1_
  13.2 1.3 %collective-permute-start.4 = (bf16[128,512]{1,0:T(8,128)(2,1)S(1)}, bf16[128,512]{1,0:T(8,128)(2,1)S(1)}, u32[]{:S(2)}, u32[]{:S(2)}) collective-permute-start(bf16[128,512]{1,0:T(8,128)(2,1)S(1)} %collective-permute-done.refs_1_), channel_id=1, source_target_pairs={{0,1},{1,0},{2,3},{3,2},{4,5},{5,4},{6,7},{7,6},{8,9},{9,8},{10,11... | collective-permute-start | bytes 393224 | tf_op jit(solution)/shard_map/ppermute | solution.py:36
  14.5 0.5 collective-permute-start.5
  15.1 1.4 %collective-permute-start.7 = (bf16[64,512]{1,0:T(8,128)(2,1)S(1)}, bf16[64,512]{1,0:T(8,128)(2,1)S(1)}, u32[]{:S(2)}, u32[]{:S(2)}) collective-permute-start(bf16[64,512]{1,0:T(8,128)(2,1)S(1)} %copy-done.5), channel_id=1, source_target_pairs={{0,48},{1,49},{2,50},{3,51},{4,52},{5,53},{6,54},{7,55},{8,56},{9,... | collective-permute-start | bytes 196616 | tf_op jit(solution)/shard_map/ppermute | solution.py:36
  16.5 2.1 %gradient.1 = (f32[64,768]{1,0:T(8,128)S(1)}, bf16[128,768]{1,0:T(8,128)(2,1)S(1)}, bf16[128,768]{1,0:T(8,128)(2,1)S(1)}, f32[64,768]{1,0:T(8,128)S(1)}, f32[64,...) custom-call(bf16[128,512]{1,0:T(8,128)(2,1)S(1)} %copy-done.4, ...), custom_call_target="tpu_custom_call" | custom-call | flops 1342177280 | bytes 6291456 | tf_op jit(solution)/shard_map/gradient/pallas_call | solution.py:253
  18.6 1.4 %collective-permute-done.7.query_far = bf16[64,512]{1,0:T(8,128)(2,1)S(1)} collective-permute-done((bf16[64,512]{1,0:T(8,128)(2,1)S(1)}, bf16[64,512]{1,0:T(8,128)(2,1)S(1)}, u32[]{:S(2)}, u32[]{:S(2)}) %collective-permute-start.7) | collective-permute-done | bytes 65568 | tf_op jit(solution)/shard_map/ppermute | solution.py:36
  20.0 0.9 %collective-permute-start.8 = (bf16[128,768]{1,0:T(8,128)(2,1)S(1)}, bf16[128,768]{1,0:T(8,128)(2,1)S(1)}, u32[]{:S(2)}, u32[]{:S(2)}) collective-permute-start(bf16[128,768]{1,0:T(8,128)(2,1)S(1)} %get-tuple-element.72), channel_id=1, source_target_pairs={{0,2},{1,3},{2,4},{3,5},{4,6},{5,7},{6,8},{7,9},{8,10},{9,11},{10,... | collective-permute-start | bytes 589832 | tf_op jit(solution)/shard_map/ppermute | solution.py:36
  20.9 3.9 %collective-permute-start.9 = (bf16[128,768]{1,0:T(8,128)(2,1)S(1)}, bf16[128,768]{1,0:T(8,128)(2,1)S(1)}, u32[]{:S(2)}, u32[]{:S(2)}) collective-permute-start(bf16[128,768]{1,0:T(8,128)(2,1)S(1)} %get-tuple-element.73), channel_id=1, source_target_pairs={{0,14},{1,15},{2,0},{3,1},{4,2},{5,3},{6,4},{7,5},{8,6},{9,7},{10,... | collective-permute-start | bytes 589832 | tf_op jit(solution)/shard_map/ppermute | solution.py:36
  24.9 3.6 %collective-permute-start.11 = (bf16[32,768]{1,0:T(8,128)(2,1)S(1)}, bf16[32,768]{1,0:T(8,128)(2,1)S(1)}, u32[]{:S(2)}, u32[]{:S(2)}) collective-permute-start(bf16[32,768]{1,0:T(8,128)(2,1)S(1)} %get-tuple-element.77), channel_id=1, source_target_pairs={{0,12},{1,13},{2,14},{3,15},{4,0},{5,1},{6,2},{7,3},{8,4},{9,5},{1... | collective-permute-start | bytes 147464 | tf_op jit(solution)/shard_map/ppermute | solution.py:36
  28.4 2.9 %collective-permute-done.10.far_up = bf16[32,768]{1,0:T(8,128)(2,1)S(1)} collective-permute-done((bf16[32,768]{1,0:T(8,128)(2,1)S(1)}, bf16[32,768]{1,0:T(8,128)(2,1)S(1)}, u32[]{:S(2)}, u32[]{:S(2)}) %collective-permute-start.10) | collective-permute-done | bytes 49184 | tf_op jit(solution)/shard_map/ppermute | solution.py:36
  31.4 3.8 %collective-permute-start.12 = (bf16[64,768]{1,0:T(8,128)(2,1)S(1)}, bf16[64,768]{1,0:T(8,128)(2,1)S(1)}, u32[]{:S(2)}, u32[]{:S(2)}) collective-permute-start(bf16[64,768]{1,0:T(8,128)(2,1)S(1)} %get-tuple-element.82), channel_id=1, source_target_pairs={{0,4},{1,5},{2,6},{3,7},{4,8},{5,9},{6,10},{7,11},{8,12},{9,13},{1... | collective-permute-start | bytes 294920 | tf_op jit(solution)/shard_map/ppermute | solution.py:36
  35.2 2.7 %collective-permute-start.14 = (bf16[64,512]{1,0:T(8,128)(2,1)S(1)}, bf16[64,512]{1,0:T(8,128)(2,1)S(1)}, u32[]{:S(2)}, u32[]{:S(2)}) collective-permute-start(bf16[64,512]{1,0:T(8,128)(2,1)S(1)} %copy-done.3), channel_id=1, source_target_pairs={{0,1},{1,0},{2,3},{3,2},{4,5},{5,4},{6,7},{7,6},{8,9},{9,8},{10,11... | collective-permute-start | bytes 196616 | tf_op jit(solution)/shard_map/ppermute | solution.py:36
  37.9 0.9 %collective-permute-done.14.query_core = bf16[64,512]{1,0:T(8,128)(2,1)S(1)} collective-permute-done((bf16[64,512]{1,0:T(8,128)(2,1)S(1)}, bf16[64,512]{1,0:T(8,128)(2,1)S(1)}, u32[]{:S(2)}, u32[]{:S(2)}) %collective-permute-start.14) | collective-permute-done | bytes 65568 | tf_op jit(solution)/shard_map/ppermute | solution.py:36
  38.8 0.4 collective-permute-done.15.query_far_core
  39.2 1.0 %collective-permute-done.13.d = bf16[64,768]{1,0:T(8,128)(2,1)S(1)} collective-permute-done((bf16[64,768]{1,0:T(8,128)(2,1)S(1)}, bf16[64,768]{1,0:T(8,128)(2,1)S(1)}, u32[]{:S(2)}, u32[]{:S(2)}) %collective-permute-start.13) | collective-permute-done | bytes 98336 | tf_op jit(solution)/shard_map/ppermute | solution.py:36
  40.3 0.1 collective-permute-start.16
  40.4 3.5 %collective-permute-done.16 = bf16[64,768]{1,0:T(8,128)(2,1)S(1)} collective-permute-done((bf16[64,768]{1,0:T(8,128)(2,1)S(1)}, bf16[64,768]{1,0:T(8,128)(2,1)S(1)}, u32[]{:S(2)}, u32[]{:S(2)}) %collective-permute-start.16) | collective-permute-done | bytes 98336 | tf_op jit(solution)/shard_map/ppermute | solution.py:36
  43.8 1.8 %collective-permute-start.18 = (bf16[64,1536]{1,0:T(8,128)(2,1)S(1)}, bf16[64,1536]{1,0:T(8,128)(2,1)S(1)}, u32[]{:S(2)}, u32[]{:S(2)}) collective-permute-start(bf16[64,1536]{1,0:T(8,128)(2,1)S(1)} %pad_maximum_fusion.refs_0_), channel_id=1, source_target_pairs={{0,12},{1,13},{2,14},{3,15},{4,0},{5,1},{6,2},{7,3},{8,4},{9,5},{1... | collective-permute-start | bytes 589832 | tf_op jit(solution)/shard_map/ppermute | solution.py:36
  45.6 0.7 collective-permute-start.17
  46.3 1.1 %collective-permute-start.20 = (bf16[64,1536]{1,0:T(8,128)(2,1)S(1)}, bf16[64,1536]{1,0:T(8,128)(2,1)S(1)}, u32[]{:S(2)}, u32[]{:S(2)}) collective-permute-start(bf16[64,1536]{1,0:T(8,128)(2,1)S(1)} %pad_maximum_fusion.refs_0_), channel_id=1, source_target_pairs={{0,14},{1,15},{2,0},{3,1},{4,2},{5,3},{6,4},{7,5},{8,6},{9,7},{10,... | collective-permute-start | bytes 589832 | tf_op jit(solution)/shard_map/ppermute | solution.py:36
  47.4 0.4 collective-permute-start.19
  47.7 2.7 %first_block.1.first_out = bf16[64,1024]{1,0:T(8,128)(2,1)S(1)} custom-call(bf16[2,64,1024]{2,1,0:T(8,128)(2,1)S(1)} %copy-done.2, bf16[3,2,512,1024]{3,2,1,0:T(8,128)(2,1)S(1)} %copy-done.1), custom_call_target="tpu_custom_call" | custom-call | flops 402653184 | bytes 7340032 | tf_op jit(solution)/shard_map/first_block/pallas_call | solution.py:164
  50.5 0.3 collective-permute-done.18.refs_4_
  50.8 3.6 %collective-permute-done.17.refs_3_ = bf16[64,1536]{1,0:T(8,128)(2,1)S(1)} collective-permute-done((bf16[64,1536]{1,0:T(8,128)(2,1)S(1)}, bf16[64,1536]{1,0:T(8,128)(2,1)S(1)}, u32[]{:S(2)}, u32[]{:S(2)}) %collective-permute-start.17) | collective-permute-done | bytes 196640 | tf_op jit(solution)/shard_map/ppermute | solution.py:36
  54.4 2.7 %collective-permute-start.22 = (bf16[64,1536]{1,0:T(8,128)(2,1)S(1)}, bf16[64,1536]{1,0:T(8,128)(2,1)S(1)}, u32[]{:S(2)}, u32[]{:S(2)}) collective-permute-start(bf16[64,1536]{1,0:T(8,128)(2,1)S(1)} %collective-permute-done.18.refs_4_), channel_id=1, source_target_pairs={{0,14},{1,15},{2,0},{3,1},{4,2},{5,3},{6,4},{7,5},{8,6},{9,7},{10,... | collective-permute-start | bytes 589832 | tf_op jit(solution)/shard_map/ppermute | solution.py:36
  57.2 2.3 %collective-permute-start.23 = (bf16[32,1536]{1,0:T(8,128)(2,1)S(1)}, bf16[32,1536]{1,0:T(8,128)(2,1)S(1)}, u32[]{:S(2)}, u32[]{:S(2)}) collective-permute-start(bf16[32,1536]{1,0:T(8,128)(2,1)S(1)} %slice.6), channel_id=1, source_target_pairs={{0,4},{1,5},{2,6},{3,7},{4,8},{5,9},{6,10},{7,11},{8,12},{9,13},{1... | collective-permute-start | bytes 294920 | tf_op jit(solution)/shard_map/ppermute | solution.py:36
  59.5 3.2 %collective-permute-done.24.refs_8_ = bf16[32,1536]{1,0:T(8,128)(2,1)S(1)} collective-permute-done((bf16[32,1536]{1,0:T(8,128)(2,1)S(1)}, bf16[32,1536]{1,0:T(8,128)(2,1)S(1)}, u32[]{:S(2)}, u32[]{:S(2)}) %collective-permute-start.24) | collective-permute-done | bytes 98336 | tf_op jit(solution)/shard_map/ppermute | solution.py:36
  62.7 4.3 %collective-permute-done.23.refs_7_ = bf16[32,1536]{1,0:T(8,128)(2,1)S(1)} collective-permute-done((bf16[32,1536]{1,0:T(8,128)(2,1)S(1)}, bf16[32,1536]{1,0:T(8,128)(2,1)S(1)}, u32[]{:S(2)}, u32[]{:S(2)}) %collective-permute-start.23) | collective-permute-done | bytes 98336 | tf_op jit(solution)/shard_map/ppermute | solution.py:36
  67.0 0.7 pack.1
  67.7 6.4 %collective-permute-start.25 = (bf16[512,512]{1,0:T(8,128)(2,1)S(1)}, bf16[512,512]{1,0:T(8,128)(2,1)S(1)}, u32[]{:S(2)}, u32[]{:S(2)}) collective-permute-start(bf16[512,512]{1,0:T(8,128)(2,1)S(1)} %get-tuple-element.96.mine), channel_id=1, source_target_pairs={{0,1},{1,0},{2,3},{3,2},{4,5},{5,4},{6,7},{7,6},{8,9},{9,8},{10,11... | collective-permute-start | bytes 1572872 | tf_op jit(solution)/shard_map/ppermute | solution.py:36
  74.1 3.1 %project.1.mine = f32[256,1024]{1,0:T(8,128)S(1)} custom-call(bf16[512,1024]{1,0:T(8,128)(2,1)S(1)} %get-tuple-element.93.scaled, bf16[3,2,512,1024]{3,2,1,0:T(8,128)(2,1)S(1)} %copy-done.1, bf16[64,512]{1,0:T(8,128)(2,1)S(1)} %copy-done.3, bf16[64,512]{1,0:T(8,128)(2,1)S(1)} %collective-permute-done.14.query_core, ...), custom_call_target="tpu_custom_call" | custom-call | flops 2200000000 | bytes 5242880 | tf_op jit(solution)/shard_map/project/pallas_call | solution.py:419
  77.3 0.3 collective-permute-start.26
  77.6 2.4 %renew_third.1.rows = bf16[256,1024]{1,0:T(8,128)(2,1)S(1)} custom-call(bf16[512,512]{1,0:T(8,128)(2,1)S(1)} %get-tuple-element.96.mine, bf16[512,512]{1,0:T(8,128)(2,1)S(1)} %collective-permute-done.25.other, bf16[3,2,512,1024]{3,2,1,0:T(8,128)(2,1)S(1)} %copy-done.1), custom_call_target="tpu_custom_call" | custom-call | flops 1200000000 | bytes 4194304 | tf_op jit(solution)/shard_map/renew_third/pallas_call | solution.py:454
  80.0 0.2 collective-permute-done.26.other
  80.2 0.5 down.1
  80.8 0.4 collective-permute-start.27
  81.2 0.9 %collective-permute-start.28 = (bf16[64,256]{1,0:T(8,128)(2,1)S(1)}, bf16[64,256]{1,0:T(8,128)(2,1)S(1)}, u32[]{:S(2)}, u32[]{:S(2)}) collective-permute-start(bf16[64,256]{1,0:T(8,128)(2,1)S(1)} %get-tuple-element.101), channel_id=1, source_target_pairs={{0,48},{1,49},{2,50},{3,51},{4,52},{5,53},{6,54},{7,55},{8,56},{9,... | collective-permute-start | bytes 98312 | tf_op jit(solution)/shard_map/ppermute | solution.py:36
  82.1 2.1 %collective-permute-start.29 = (bf16[64,256]{1,0:T(8,128)(2,1)S(1)}, bf16[64,256]{1,0:T(8,128)(2,1)S(1)}, u32[]{:S(2)}, u32[]{:S(2)}) collective-permute-start(bf16[64,256]{1,0:T(8,128)(2,1)S(1)} %get-tuple-element.102), channel_id=1, source_target_pairs={{0,49},{1,48},{2,51},{3,50},{4,53},{5,52},{6,55},{7,54},{8,57},{9,... | collective-permute-start | bytes 98312 | tf_op jit(solution)/shard_map/ppermute | solution.py:36
  84.2 0.9 %collective-permute-done.28.far = bf16[64,256]{1,0:T(8,128)(2,1)S(1)} collective-permute-done((bf16[64,256]{1,0:T(8,128)(2,1)S(1)}, bf16[64,256]{1,0:T(8,128)(2,1)S(1)}, u32[]{:S(2)}, u32[]{:S(2)}) %collective-permute-start.28) | collective-permute-done | bytes 32800 | tf_op jit(solution)/shard_map/ppermute | solution.py:36
  85.2 1.7 %collective-permute-done.29.far_core = bf16[64,256]{1,0:T(8,128)(2,1)S(1)} collective-permute-done((bf16[64,256]{1,0:T(8,128)(2,1)S(1)}, bf16[64,256]{1,0:T(8,128)(2,1)S(1)}, u32[]{:S(2)}, u32[]{:S(2)}) %collective-permute-start.29) | collective-permute-done | bytes 32800 | tf_op jit(solution)/shard_map/ppermute | solution.py:36
  86.9 0.7 finish.1
  (38 shorter events, 0.3 us)
Async XLA Ops:
  2.2 10.9 %collective-permute-start.1 = (bf16[128,512]{1,0:T(8,128)(2,1)}, bf16[128,512]{1,0:T(8,128)(2,1)S(1)}, u32[]{:S(2)}, u32[]{:S(2)}) collective-permute-start(bf16[128,512]{1,0:T(8,128)(2,1)} %get-tuple-element.57), channel_id=1, source_target_pairs={{0,32},{1,33},{2,34},{3,35},{4,36},{5,37},{6,38},{7,39},{8,40},{9,... | collective-permute-start | bytes 393224 | tf_op jit(solution)/shard_map/ppermute | solution.py:36
  5.8 7.4 %collective-permute-start = (bf16[128,512]{1,0:T(8,128)(2,1)}, bf16[128,512]{1,0:T(8,128)(2,1)S(1)}, u32[]{:S(2)}, u32[]{:S(2)}) collective-permute-start(bf16[128,512]{1,0:T(8,128)(2,1)} %get-tuple-element.56), channel_id=1, source_target_pairs={{0,16},{1,17},{2,18},{3,19},{4,20},{5,21},{6,22},{7,23},{8,24},{9,... | collective-permute-start | bytes 393224 | tf_op jit(solution)/shard_map/ppermute | solution.py:36
  6.1 8.4 %collective-permute-start.2 = (bf16[128,512]{1,0:T(8,128)(2,1)}, bf16[128,512]{1,0:T(8,128)(2,1)S(1)}, u32[]{:S(2)}, u32[]{:S(2)}) collective-permute-start(bf16[128,512]{1,0:T(8,128)(2,1)} %get-tuple-element.61), channel_id=1, source_target_pairs={{0,48},{1,49},{2,50},{3,51},{4,52},{5,53},{6,54},{7,55},{8,56},{9,... | collective-permute-start | bytes 393224 | tf_op jit(solution)/shard_map/ppermute | solution.py:36
  8.5 8.0 %collective-permute-start.3 = (bf16[128,512]{1,0:T(8,128)(2,1)}, bf16[128,512]{1,0:T(8,128)(2,1)S(1)}, u32[]{:S(2)}, u32[]{:S(2)}) collective-permute-start(bf16[128,512]{1,0:T(8,128)(2,1)} %get-tuple-element.55.refs_0_), channel_id=1, source_target_pairs={{0,1},{1,0},{2,3},{3,2},{4,5},{5,4},{6,7},{7,6},{8,9},{9,8},{10,11... | collective-permute-start | bytes 393224 | tf_op jit(solution)/shard_map/ppermute | solution.py:36
  10.0 2.8 %copy-start = (bf16[3,2,512,1024]{3,2,1,0:T(8,128)(2,1)S(1)}, bf16[3,2,512,1024]{3,2,1,0:T(8,128)(2,1)}, u32[]{:S(2)}) copy-start(bf16[3,2,512,1024]{3,2,1,0:T(8,128)(2,1)} %weights.3) | copy-start | bytes 18874372
  12.8 2.3 %copy-start.5 = (bf16[64,512]{1,0:T(8,128)(2,1)S(1)}, bf16[64,512]{1,0:T(8,128)(2,1)}, u32[]{:S(2)}) copy-start(bf16[64,512]{1,0:T(8,128)(2,1)} %get-tuple-element.70) | copy-start | bytes 196612
  12.8 3.7 %copy-start.4 = (bf16[128,512]{1,0:T(8,128)(2,1)S(1)}, bf16[128,512]{1,0:T(8,128)(2,1)}, u32[]{:S(2)}) copy-start(bf16[128,512]{1,0:T(8,128)(2,1)} %get-tuple-element.55.refs_0_) | copy-start | bytes 393220
  12.8 22.4 %copy-start.3 = (bf16[64,512]{1,0:T(8,128)(2,1)S(1)}, bf16[64,512]{1,0:T(8,128)(2,1)}, u32[]{:S(2)}) copy-start(bf16[64,512]{1,0:T(8,128)(2,1)} %get-tuple-element.84.query_own) | copy-start | bytes 196612
  12.8 35.0 %copy-start.1 = (bf16[3,2,512,1024]{3,2,1,0:T(8,128)(2,1)S(1)}, bf16[3,2,512,1024]{3,2,1,0:T(8,128)(2,1)}, u32[]{:S(2)}) copy-start(bf16[3,2,512,1024]{3,2,1,0:T(8,128)(2,1)} %weights.3) | copy-start | bytes 18874372
  12.8 34.9 %copy-start.2 = (bf16[2,64,1024]{2,1,0:T(8,128)(2,1)S(1)}, bf16[2,64,1024]{2,1,0:T(8,128)(2,1)}, u32[]{:S(2)}) copy-start(bf16[2,64,1024]{2,1,0:T(8,128)(2,1)} %queries.2) | copy-start | bytes 786436
  13.2 3.3 %collective-permute-start.4 = (bf16[128,512]{1,0:T(8,128)(2,1)S(1)}, bf16[128,512]{1,0:T(8,128)(2,1)S(1)}, u32[]{:S(2)}, u32[]{:S(2)}) collective-permute-start(bf16[128,512]{1,0:T(8,128)(2,1)S(1)} %collective-permute-done.refs_1_), channel_id=1, source_target_pairs={{0,1},{1,0},{2,3},{3,2},{4,5},{5,4},{6,7},{7,6},{8,9},{9,8},{10,11... | collective-permute-start | bytes 393224 | tf_op jit(solution)/shard_map/ppermute | solution.py:36
  14.5 1.9 %collective-permute-start.6 = (bf16[128,512]{1,0:T(8,128)(2,1)S(1)}, bf16[128,512]{1,0:T(8,128)(2,1)S(1)}, u32[]{:S(2)}, u32[]{:S(2)}) collective-permute-start(bf16[128,512]{1,0:T(8,128)(2,1)S(1)} %collective-permute-done.2.refs_3_), channel_id=1, source_target_pairs={{0,1},{1,0},{2,3},{3,2},{4,5},{5,4},{6,7},{7,6},{8,9},{9,8},{10,11... | collective-permute-start | bytes 393224 | tf_op jit(solution)/shard_map/ppermute | solution.py:36
  14.5 1.9 %collective-permute-start.5 = (bf16[128,512]{1,0:T(8,128)(2,1)S(1)}, bf16[128,512]{1,0:T(8,128)(2,1)S(1)}, u32[]{:S(2)}, u32[]{:S(2)}) collective-permute-start(bf16[128,512]{1,0:T(8,128)(2,1)S(1)} %collective-permute-done.1.refs_2_), channel_id=1, source_target_pairs={{0,1},{1,0},{2,3},{3,2},{4,5},{5,4},{6,7},{7,6},{8,9},{9,8},{10,11... | collective-permute-start | bytes 393224 | tf_op jit(solution)/shard_map/ppermute | solution.py:36
  15.1 4.9 %collective-permute-start.7 = (bf16[64,512]{1,0:T(8,128)(2,1)S(1)}, bf16[64,512]{1,0:T(8,128)(2,1)S(1)}, u32[]{:S(2)}, u32[]{:S(2)}) collective-permute-start(bf16[64,512]{1,0:T(8,128)(2,1)S(1)} %copy-done.5), channel_id=1, source_target_pairs={{0,48},{1,49},{2,50},{3,51},{4,52},{5,53},{6,54},{7,55},{8,56},{9,... | collective-permute-start | bytes 196616 | tf_op jit(solution)/shard_map/ppermute | solution.py:36
  20.0 11.3 %collective-permute-start.8 = (bf16[128,768]{1,0:T(8,128)(2,1)S(1)}, bf16[128,768]{1,0:T(8,128)(2,1)S(1)}, u32[]{:S(2)}, u32[]{:S(2)}) collective-permute-start(bf16[128,768]{1,0:T(8,128)(2,1)S(1)} %get-tuple-element.72), channel_id=1, source_target_pairs={{0,2},{1,3},{2,4},{3,5},{4,6},{5,7},{6,8},{7,9},{8,10},{9,11},{10,... | collective-permute-start | bytes 589832 | tf_op jit(solution)/shard_map/ppermute | solution.py:36
  20.9 10.4 %collective-permute-start.9 = (bf16[128,768]{1,0:T(8,128)(2,1)S(1)}, bf16[128,768]{1,0:T(8,128)(2,1)S(1)}, u32[]{:S(2)}, u32[]{:S(2)}) collective-permute-start(bf16[128,768]{1,0:T(8,128)(2,1)S(1)} %get-tuple-element.73), channel_id=1, source_target_pairs={{0,14},{1,15},{2,0},{3,1},{4,2},{5,3},{6,4},{7,5},{8,6},{9,7},{10,... | collective-permute-start | bytes 589832 | tf_op jit(solution)/shard_map/ppermute | solution.py:36
  24.9 6.5 %collective-permute-start.10 = (bf16[32,768]{1,0:T(8,128)(2,1)S(1)}, bf16[32,768]{1,0:T(8,128)(2,1)S(1)}, u32[]{:S(2)}, u32[]{:S(2)}) collective-permute-start(bf16[32,768]{1,0:T(8,128)(2,1)S(1)} %get-tuple-element.76), channel_id=1, source_target_pairs={{0,4},{1,5},{2,6},{3,7},{4,8},{5,9},{6,10},{7,11},{8,12},{9,13},{1... | collective-permute-start | bytes 147464 | tf_op jit(solution)/shard_map/ppermute | solution.py:36
  24.9 6.5 %collective-permute-start.11 = (bf16[32,768]{1,0:T(8,128)(2,1)S(1)}, bf16[32,768]{1,0:T(8,128)(2,1)S(1)}, u32[]{:S(2)}, u32[]{:S(2)}) collective-permute-start(bf16[32,768]{1,0:T(8,128)(2,1)S(1)} %get-tuple-element.77), channel_id=1, source_target_pairs={{0,12},{1,13},{2,14},{3,15},{4,0},{5,1},{6,2},{7,3},{8,4},{9,5},{1... | collective-permute-start | bytes 147464 | tf_op jit(solution)/shard_map/ppermute | solution.py:36
  31.4 7.8 %collective-permute-start.12 = (bf16[64,768]{1,0:T(8,128)(2,1)S(1)}, bf16[64,768]{1,0:T(8,128)(2,1)S(1)}, u32[]{:S(2)}, u32[]{:S(2)}) collective-permute-start(bf16[64,768]{1,0:T(8,128)(2,1)S(1)} %get-tuple-element.82), channel_id=1, source_target_pairs={{0,4},{1,5},{2,6},{3,7},{4,8},{5,9},{6,10},{7,11},{8,12},{9,13},{1... | collective-permute-start | bytes 294920 | tf_op jit(solution)/shard_map/ppermute | solution.py:36
  35.2 5.0 %collective-permute-start.13 = (bf16[64,768]{1,0:T(8,128)(2,1)S(1)}, bf16[64,768]{1,0:T(8,128)(2,1)S(1)}, u32[]{:S(2)}, u32[]{:S(2)}) collective-permute-start(bf16[64,768]{1,0:T(8,128)(2,1)S(1)} %get-tuple-element.83), channel_id=1, source_target_pairs={{0,12},{1,13},{2,14},{3,15},{4,0},{5,1},{6,2},{7,3},{8,4},{9,5},{1... | collective-permute-start | bytes 294920 | tf_op jit(solution)/shard_map/ppermute | solution.py:36
  35.2 3.6 %collective-permute-start.14 = (bf16[64,512]{1,0:T(8,128)(2,1)S(1)}, bf16[64,512]{1,0:T(8,128)(2,1)S(1)}, u32[]{:S(2)}, u32[]{:S(2)}) collective-permute-start(bf16[64,512]{1,0:T(8,128)(2,1)S(1)} %copy-done.3), channel_id=1, source_target_pairs={{0,1},{1,0},{2,3},{3,2},{4,5},{5,4},{6,7},{7,6},{8,9},{9,8},{10,11... | collective-permute-start | bytes 196616 | tf_op jit(solution)/shard_map/ppermute | solution.py:36
  37.9 1.3 %collective-permute-start.15 = (bf16[64,512]{1,0:T(8,128)(2,1)S(1)}, bf16[64,512]{1,0:T(8,128)(2,1)S(1)}, u32[]{:S(2)}, u32[]{:S(2)}) collective-permute-start(bf16[64,512]{1,0:T(8,128)(2,1)S(1)} %collective-permute-done.7.query_far), channel_id=1, source_target_pairs={{0,1},{1,0},{2,3},{3,2},{4,5},{5,4},{6,7},{7,6},{8,9},{9,8},{10,11... | collective-permute-start | bytes 196616 | tf_op jit(solution)/shard_map/ppermute | solution.py:36
  40.3 3.6 %collective-permute-start.16 = (bf16[64,768]{1,0:T(8,128)(2,1)S(1)}, bf16[64,768]{1,0:T(8,128)(2,1)S(1)}, u32[]{:S(2)}, u32[]{:S(2)}) collective-permute-start(bf16[64,768]{1,0:T(8,128)(2,1)S(1)} %add_up.1), channel_id=1, source_target_pairs={{0,16},{1,17},{2,18},{3,19},{4,20},{5,21},{6,22},{7,23},{8,24},{9,... | collective-permute-start | bytes 294920 | tf_op jit(solution)/shard_map/ppermute | solution.py:36
  43.8 7.0 %collective-permute-start.18 = (bf16[64,1536]{1,0:T(8,128)(2,1)S(1)}, bf16[64,1536]{1,0:T(8,128)(2,1)S(1)}, u32[]{:S(2)}, u32[]{:S(2)}) collective-permute-start(bf16[64,1536]{1,0:T(8,128)(2,1)S(1)} %pad_maximum_fusion.refs_0_), channel_id=1, source_target_pairs={{0,12},{1,13},{2,14},{3,15},{4,0},{5,1},{6,2},{7,3},{8,4},{9,5},{1... | collective-permute-start | bytes 589832 | tf_op jit(solution)/shard_map/ppermute | solution.py:36
  45.6 8.8 %collective-permute-start.17 = (bf16[64,1536]{1,0:T(8,128)(2,1)S(1)}, bf16[64,1536]{1,0:T(8,128)(2,1)S(1)}, u32[]{:S(2)}, u32[]{:S(2)}) collective-permute-start(bf16[64,1536]{1,0:T(8,128)(2,1)S(1)} %pad_maximum_fusion.refs_0_), channel_id=1, source_target_pairs={{0,4},{1,5},{2,6},{3,7},{4,8},{5,9},{6,10},{7,11},{8,12},{9,13},{1... | collective-permute-start | bytes 589832 | tf_op jit(solution)/shard_map/ppermute | solution.py:36
  46.3 10.9 %collective-permute-start.20 = (bf16[64,1536]{1,0:T(8,128)(2,1)S(1)}, bf16[64,1536]{1,0:T(8,128)(2,1)S(1)}, u32[]{:S(2)}, u32[]{:S(2)}) collective-permute-start(bf16[64,1536]{1,0:T(8,128)(2,1)S(1)} %pad_maximum_fusion.refs_0_), channel_id=1, source_target_pairs={{0,14},{1,15},{2,0},{3,1},{4,2},{5,3},{6,4},{7,5},{8,6},{9,7},{10,... | collective-permute-start | bytes 589832 | tf_op jit(solution)/shard_map/ppermute | solution.py:36
  47.4 12.2 %collective-permute-start.19 = (bf16[64,1536]{1,0:T(8,128)(2,1)S(1)}, bf16[64,1536]{1,0:T(8,128)(2,1)S(1)}, u32[]{:S(2)}, u32[]{:S(2)}) collective-permute-start(bf16[64,1536]{1,0:T(8,128)(2,1)S(1)} %pad_maximum_fusion.refs_0_), channel_id=1, source_target_pairs={{0,2},{1,3},{2,4},{3,5},{4,6},{5,7},{6,8},{7,9},{8,10},{9,11},{10,... | collective-permute-start | bytes 589832 | tf_op jit(solution)/shard_map/ppermute | solution.py:36
  54.4 12.6 %collective-permute-start.21 = (bf16[64,1536]{1,0:T(8,128)(2,1)S(1)}, bf16[64,1536]{1,0:T(8,128)(2,1)S(1)}, u32[]{:S(2)}, u32[]{:S(2)}) collective-permute-start(bf16[64,1536]{1,0:T(8,128)(2,1)S(1)} %collective-permute-done.17.refs_3_), channel_id=1, source_target_pairs={{0,2},{1,3},{2,4},{3,5},{4,6},{5,7},{6,8},{7,9},{8,10},{9,11},{10,... | collective-permute-start | bytes 589832 | tf_op jit(solution)/shard_map/ppermute | solution.py:36
  54.4 12.6 %collective-permute-start.22 = (bf16[64,1536]{1,0:T(8,128)(2,1)S(1)}, bf16[64,1536]{1,0:T(8,128)(2,1)S(1)}, u32[]{:S(2)}, u32[]{:S(2)}) collective-permute-start(bf16[64,1536]{1,0:T(8,128)(2,1)S(1)} %collective-permute-done.18.refs_4_), channel_id=1, source_target_pairs={{0,14},{1,15},{2,0},{3,1},{4,2},{5,3},{6,4},{7,5},{8,6},{9,7},{10,... | collective-permute-start | bytes 589832 | tf_op jit(solution)/shard_map/ppermute | solution.py:36
  57.1 5.6 %collective-permute-start.24 = (bf16[32,1536]{1,0:T(8,128)(2,1)S(1)}, bf16[32,1536]{1,0:T(8,128)(2,1)S(1)}, u32[]{:S(2)}, u32[]{:S(2)}) collective-permute-start(bf16[32,1536]{1,0:T(8,128)(2,1)S(1)} %slice.7), channel_id=1, source_target_pairs={{0,12},{1,13},{2,14},{3,15},{4,0},{5,1},{6,2},{7,3},{8,4},{9,5},{1... | collective-permute-start | bytes 294920 | tf_op jit(solution)/shard_map/ppermute | solution.py:36
  57.2 9.8 %collective-permute-start.23 = (bf16[32,1536]{1,0:T(8,128)(2,1)S(1)}, bf16[32,1536]{1,0:T(8,128)(2,1)S(1)}, u32[]{:S(2)}, u32[]{:S(2)}) collective-permute-start(bf16[32,1536]{1,0:T(8,128)(2,1)S(1)} %slice.6), channel_id=1, source_target_pairs={{0,4},{1,5},{2,6},{3,7},{4,8},{5,9},{6,10},{7,11},{8,12},{9,13},{1... | collective-permute-start | bytes 294920 | tf_op jit(solution)/shard_map/ppermute | solution.py:36
  67.7 9.5 %collective-permute-start.25 = (bf16[512,512]{1,0:T(8,128)(2,1)S(1)}, bf16[512,512]{1,0:T(8,128)(2,1)S(1)}, u32[]{:S(2)}, u32[]{:S(2)}) collective-permute-start(bf16[512,512]{1,0:T(8,128)(2,1)S(1)} %get-tuple-element.96.mine), channel_id=1, source_target_pairs={{0,1},{1,0},{2,3},{3,2},{4,5},{5,4},{6,7},{7,6},{8,9},{9,8},{10,11... | collective-permute-start | bytes 1572872 | tf_op jit(solution)/shard_map/ppermute | solution.py:36
  77.3 3.0 %collective-permute-start.26 = (f32[256,1024]{1,0:T(8,128)S(1)}, f32[256,1024]{1,0:T(8,128)S(1)}, u32[]{:S(2)}, u32[]{:S(2)}) collective-permute-start(f32[256,1024]{1,0:T(8,128)S(1)} %project.1.mine), channel_id=1, source_target_pairs={{0,1},{1,0},{2,3},{3,2},{4,5},{5,4},{6,7},{7,6},{8,9},{9,8},{10,11... | collective-permute-start | bytes 3145736 | tf_op jit(solution)/shard_map/ppermute | solution.py:36
  80.8 3.4 %collective-permute-start.27 = (bf16[64,256]{1,0:T(8,128)(2,1)S(1)}, bf16[64,256]{1,0:T(8,128)(2,1)S(1)}, u32[]{:S(2)}, u32[]{:S(2)}) collective-permute-start(bf16[64,256]{1,0:T(8,128)(2,1)S(1)} %get-tuple-element.100), channel_id=1, source_target_pairs={{0,1},{1,0},{2,3},{3,2},{4,5},{5,4},{6,7},{7,6},{8,9},{9,8},{10,11... | collective-permute-start | bytes 98312 | tf_op jit(solution)/shard_map/ppermute | solution.py:36
  81.2 4.0 %collective-permute-start.28 = (bf16[64,256]{1,0:T(8,128)(2,1)S(1)}, bf16[64,256]{1,0:T(8,128)(2,1)S(1)}, u32[]{:S(2)}, u32[]{:S(2)}) collective-permute-start(bf16[64,256]{1,0:T(8,128)(2,1)S(1)} %get-tuple-element.101), channel_id=1, source_target_pairs={{0,48},{1,49},{2,50},{3,51},{4,52},{5,53},{6,54},{7,55},{8,56},{9,... | collective-permute-start | bytes 98312 | tf_op jit(solution)/shard_map/ppermute | solution.py:36
  82.1 4.8 %collective-permute-start.29 = (bf16[64,256]{1,0:T(8,128)(2,1)S(1)}, bf16[64,256]{1,0:T(8,128)(2,1)S(1)}, u32[]{:S(2)}, u32[]{:S(2)}) collective-permute-start(bf16[64,256]{1,0:T(8,128)(2,1)S(1)} %get-tuple-element.102), channel_id=1, source_target_pairs={{0,49},{1,48},{2,51},{3,50},{4,53},{5,52},{6,55},{7,54},{8,57},{9,... | collective-permute-start | bytes 98312 | tf_op jit(solution)/shard_map/ppermute | solution.py:36

commit v6 on v5

--- a/solution.py
+++ b/solution.py
@@ -42,6 +42,10 @@
 
 def along_z(array, distance):
     return move(array, lambda x, z, c: (x, z + distance, c))
+
+
+def opposite_z(array):
+    return move(array, lambda x, z, c: (x, z + 2 - 4 * c, c))
 
 
 def pair_x(array):
@@ -206,8 +210,8 @@
 
 def gradient_kernel(*refs):
     pieces, w = refs[:8], refs[8]
-    own, up, down, keep_up, keep_down, far_up, far_down = refs[9:16]
-    k, v, d, gated, total = refs[16:]
+    own, up, down, keep_up, keep_down, far = refs[9:15]
+    k, v, d, gated, total = refs[15:]
     _, z, c = place()
     tokens = pieces[0].shape[0] // 2
     for i, piece in enumerate(pieces):
@@ -242,19 +246,17 @@
     down[ROWS:, :] = rows(-3).astype(BF)
     keep_up[...] = rows(2)
     keep_down[...] = rows(-2)
-    far = rows(4).astype(BF)
-    far_up[...] = far[: ROWS // 2]
-    far_down[...] = far[ROWS // 2 :]
+    far[...] = rows(4).astype(BF)
 
 
 def gradient(pieces, weights):
     tokens = 8 * pieces[0].shape[0] // 2
-    kept, sent, half = shape(ROWS, WIDE, dtype=F32), shape(2 * ROWS, WIDE), shape(ROWS // 2, WIDE)
+    kept, sent, far = shape(ROWS, WIDE, dtype=F32), shape(2 * ROWS, WIDE), shape(ROWS, WIDE)
     return pl.pallas_call(
         gradient_kernel,
-        out_shape=(kept, sent, sent, kept, kept, half, half),
+        out_shape=(kept, sent, sent, kept, kept, far),
         in_specs=[VMEM] * 9,
-        out_specs=(VMEM,) * 7,
+        out_specs=(VMEM,) * 6,
         scratch_shapes=[
             pltpu.VMEM((tokens, DIM), BF),
             pltpu.VMEM((tokens, DIM), BF),
@@ -268,21 +270,28 @@
     )(*pieces, weights)
 
 
-def middle_kernel(keep_up, keep_down, got_up, got_down, far_up, far_down, up, down):
-    half = ROWS // 2
-    total = keep_up[...] + got_up[ROWS:, :].astype(F32)
-    up[:half, :] = (total[:half] + far_up[...].astype(F32)).astype(BF)
-    up[half:, :] = total[half:].astype(BF)
-    total = keep_down[...] + got_down[ROWS:, :].astype(F32)
-    down[:half, :] = total[:half].astype(BF)
-    down[half:, :] = (total[half:] + far_down[...].astype(F32)).astype(BF)
+def middle_kernel(keep_up, keep_down, got_up, got_down, far, up, down):
+    _, _, c = place()
+    total_up = keep_up[...] + got_up[ROWS:, :].astype(F32)
+    total_down = keep_down[...] + got_down[ROWS:, :].astype(F32)
+    last = far[...].astype(F32)
+
+    @pl.when(c == 0)
+    def _():
+        up[...] = (total_up + last).astype(BF)
+        down[...] = total_down.astype(BF)
+
+    @pl.when(c == 1)
+    def _():
+        up[...] = total_up.astype(BF)
+        down[...] = (total_down + last).astype(BF)
 
 
 def middle(*args):
     return pl.pallas_call(
         middle_kernel,
         out_shape=(shape(ROWS, WIDE), shape(ROWS, WIDE)),
-        in_specs=[VMEM] * 6,
+        in_specs=[VMEM] * 5,
         out_specs=(VMEM, VMEM),
         compiler_params=params(3),
         name="middle",
@@ -305,46 +314,35 @@
     )(*args)
 
 
-def reduce_rows(parts, query_own, query_far):
-    own, up, down, keep_up, keep_down, far_up, far_down = parts
-    far_up, far_down = along_z(far_up, 2), along_z(far_down, -2)
+def reduce_rows(parts):
+    own, up, down, keep_up, keep_down, far = parts
+    far = opposite_z(far)
     got_up, got_down = along_z(up, 1), along_z(down, -1)
-    up, down = middle(keep_up, keep_down, got_up, got_down, far_up, far_down)
-    up, down, query_own, query_far = barrier((up, down, query_own, query_far))
-    up, down = along_z(up, 2), along_z(down, -2)
-    up, down, query_core, query_far_core = barrier(
-        (up, down, other_core(query_own), other_core(query_far))
-    )
-    return add_up(own, got_up, got_down, up, down), (query_own, query_core, query_far, query_far_core)
-
-
-ORIGINS = ((0, 0, ROWS), (-1, 0, ROWS), (1, 0, ROWS), (-2, 0, ROWS), (2, 0, ROWS)) + (
-    (-3, 0, ROWS),
-    (3, 0, ROWS),
-    (-4, 0, ROWS // 2),
-    (4, ROWS // 2, ROWS // 2),
-)
+    up, down = middle(keep_up, keep_down, got_up, got_down, far)
+    return add_up(own, got_up, got_down, along_z(up, 2), along_z(down, -2))
+
+
+ORIGINS = (0, -1, 1, -2, 2, -3, 3, 4)
 
 
 def gather_rows(own, queries, weights):
-    own = jnp.concatenate([own, pair_x(own)], axis=1)
+    _, _, c = place()
     own, queries = barrier((own, queries))
     up1, down1 = along_z(own, 1), along_z(own, -1)
     up2, down2 = along_z(own, 2), along_z(own, -2)
     up2, down2, first_out = barrier((up2, down2, first_block(queries, weights)))
     up3, down3 = along_z(up2, 1), along_z(down2, -1)
-    up4, down4 = along_z(up2[: ROWS // 2], 2), along_z(down2[ROWS // 2 :], -2)
-    return [own, up1, down1, up2, down2, up3, down3, up4, down4], first_out
+    far = opposite_z(jnp.where(c == 0, up2, down2))
+    return [own, up1, down1, up2, down2, up3, down3, far], first_out
 
 
 def pack_kernel(*refs):
-    pieces = refs[:9]
-    matrix, shared, sem = refs[9:]
+    pieces = refs[:8]
+    matrix, shared, sem = refs[8:]
     x, z, _ = place()
     copies = []
     for i, piece in enumerate(pieces):
-        step, first, count = ORIGINS[i]
-        rows = at_place(lax.rem(z + step + Z, Z) * ROWS + first, count)
+        rows = at_place(lax.rem(z + ORIGINS[i] + Z, Z) * ROWS, ROWS)
         for j in range(4):
             side = lax.rem(x + j // 2, 2)
             target, size, offset = ((matrix, HALF, 0), (shared, QUARTER, HALF))[j % 2]
@@ -363,9 +361,9 @@
     return pl.pallas_call(
         pack_kernel,
         out_shape=(shape(DIM, FF), shape(DIM, HALF)),
-        in_specs=[ANY] * 9,
+        in_specs=[ANY] * 8,
         out_specs=(VMEM, VMEM),
-        scratch_shapes=[pltpu.SemaphoreType.DMA((9, 4))],
+        scratch_shapes=[pltpu.SemaphoreType.DMA((8, 4))],
         compiler_params=params(4),
         cost_estimate=cost(0, 3 << 20),
         name="pack",
@@ -530,16 +528,18 @@
     own, far1, far2, far3, query_own, query_far = prepare(queries, keys, values, rates)
     own, weights = barrier((own, weights))
     got1, got2, got3 = along_x(far1, 1), along_x(far2, 2), along_x(far3, 3)
-    got2, query_far, part = barrier((got2, query_far, load(weights)))
-    query_far = mirror_x(query_far)
+    got2, query_own, part = barrier((got2, query_own, load(weights)))
     got = [own, got1, got2, got3]
     got += [other_core(piece) for piece in got]
-    parts, query_far = barrier((gradient(got, part), query_far))
-    own, late_queries = reduce_rows(parts, query_own, query_far)
-    pieces, first_out = gather_rows(own, queries, weights)
+    got, query_core = barrier((got, other_core(query_own)))
+    own, query_far = barrier((reduce_rows(gradient(got, part)), query_far))
+    own, near, query_far, query_far_core = barrier(
+        (own, pair_x(own), mirror_x(query_far), mirror_x_core(query_far))
+    )
+    pieces, first_out = gather_rows(jnp.concatenate([own, near], axis=1), queries, weights)
     matrix, shared = pack(pieces)
     shared_core = other_core(shared)
-    projected = project(matrix, weights, *late_queries)
+    projected = project(matrix, weights, query_own, query_core, query_far, query_far_core)
     projected, shared_core = barrier((projected, shared_core))
     projected_core = other_core(projected)
     rows = renew_third(shared, shared_core, weights)

time: 87.7 us -> 91.7 us (1.046)
  waiting for transfers between devices: 24.2 us -> 30.3 us
  starting transfers between devices: 45.4 us -> 40.7 us
  local copies, waits for them, and re-layouts: 2.82 us -> 5.59 us
    ppermute x30 -> x28, waiting for transfers between devices: 24.2 us -> 30.3 us  [move(): return lax.ppermute(array, 'ctx', perm)]
    ppermute x30 -> x28, starting transfers between devices: 45.4 us -> 40.7 us  [move(): return lax.ppermute(array, 'ctx', perm)]
    unnamed x12 -> x14, local copies, waits for them, and re-layouts: 2.81 us -> 5.59 us
  transfers between devices with their start and end apart: 30 -> 28, of which waited for: 14 -> 12; matrix products, arithmetic and copies ran while one was open for 0% -> 0% of each run, Pallas kernels for 12% -> 9%
where the time goes in v6:
time: 91.7 us; the launch traced here: 91.6 us
  starting transfers between devices  40.7 us (44%)
  waiting for transfers between devices  30.3 us (33%)
  Pallas kernels  14.9 us (16%)
  local copies, waits for them, and re-layouts  5.59 us (6%)
    ppermute x28, starting transfers between devices, move(): return lax.ppermute(array, 'ctx', perm)  40.7 us
    ppermute x28, waiting for transfers between devices, move(): return lax.ppermute(array, 'ctx', perm)  30.3 us
    unnamed x14, local copies, waits for them, and re-layouts  5.59 us
    pallas_call x1, Pallas kernels, project(): pl.pallas_call(project_kernel, out_shape=shape(4 * tokens, FF, dtype=F32)...  3.12 us
    pallas_call x1, Pallas kernels, first_block(): pl.pallas_call(first_kernel, out_shape=shape(tokens, 2 * DIM), in_specs=[...  2.73 us
    pallas_call x1, Pallas kernels, renew_third(): pl.pallas_call(third_kernel, out_shape=shape(rows, FF), in_specs=[VMEM, V...  2.46 us
    pallas_call x1, Pallas kernels, prepare(): pl.pallas_call(prepare_kernel, out_shape=(pair, pair, pair, pair, half, h...  2.14 us
    pallas_call x1, Pallas kernels, gradient(): pl.pallas_call(gradient_kernel, out_shape=(kept, sent, sent, kept, kept,...  2.12 us
  transfers between devices with their start and end apart: 28, of which 12 were waited for; matrix products, arithmetic and copies ran while one was open for 0% of the time, Pallas kernels for 9%

profile of v6, /device:TPU:1, one launch (start us, length us, event | category | flops | bytes accessed | tf_op | source)
XLA Modules:
  0.0 91.6 jit_solution(4253583351928753200)
XLA Ops:
  0.0 2.1 %prepare.1 = (bf16[128,512]{1,0:T(8,128)(2,1)}, bf16[128,512]{1,0:T(8,128)(2,1)}, bf16[128,512]{1,0:T(8,128)(2,1)}, bf16[128,512]{1,0:T(8,128)(2,1)}, bf16[64,512]{1,0:T(8,128)(2,1)}, /*index=5*/bf16[64,512]{1,0:T(8,128)(2,1)}) custom-call(bf16[2,64,1024]{2,1,0:T(8,128)(2,1)} %queries.2, bf16[1,64,1024]{2,1,0:T(8,128)(2,1)} %keys.1, ...), custom_call_target="tpu_custom_call" | custom-call | tf_op jit(solution)/shard_map/prepare/pallas_call | solution.py:128
  2.2 3.6 %collective-permute-start.1 = (bf16[128,512]{1,0:T(8,128)(2,1)}, bf16[128,512]{1,0:T(8,128)(2,1)S(1)}, u32[]{:S(2)}, u32[]{:S(2)}) collective-permute-start(bf16[128,512]{1,0:T(8,128)(2,1)} %get-tuple-element.55), channel_id=1, source_target_pairs={{0,32},{1,33},{2,34},{3,35},{4,36},{5,37},{6,38},{7,39},{8,40},{9,... | collective-permute-start | bytes 393224 | tf_op jit(solution)/shard_map/ppermute | solution.py:36
  5.8 0.3 collective-permute-start
  6.1 2.4 %collective-permute-start.2 = (bf16[128,512]{1,0:T(8,128)(2,1)}, bf16[128,512]{1,0:T(8,128)(2,1)S(1)}, u32[]{:S(2)}, u32[]{:S(2)}) collective-permute-start(bf16[128,512]{1,0:T(8,128)(2,1)} %get-tuple-element.59), channel_id=1, source_target_pairs={{0,48},{1,49},{2,50},{3,51},{4,52},{5,53},{6,54},{7,55},{8,56},{9,... | collective-permute-start | bytes 393224 | tf_op jit(solution)/shard_map/ppermute | solution.py:36
  8.5 1.5 %collective-permute-start.3 = (bf16[128,512]{1,0:T(8,128)(2,1)}, bf16[128,512]{1,0:T(8,128)(2,1)S(1)}, u32[]{:S(2)}, u32[]{:S(2)}) collective-permute-start(bf16[128,512]{1,0:T(8,128)(2,1)} %get-tuple-element.61.refs_0_), channel_id=1, source_target_pairs={{0,1},{1,0},{2,3},{3,2},{4,5},{5,4},{6,7},{7,6},{8,9},{9,8},{10,11... | collective-permute-start | bytes 393224 | tf_op jit(solution)/shard_map/ppermute | solution.py:36
  10.0 2.8 %copy-done = bf16[3,2,512,1024]{3,2,1,0:T(8,128)(2,1)S(1)} copy-done((bf16[3,2,512,1024]{3,2,1,0:T(8,128)(2,1)S(1)}, bf16[3,2,512,1024]{3,2,1,0:T(8,128)(2,1)}, u32[]{:S(2)}) %copy-start) | copy-done | bytes 6291480
  12.8 0.3 load.1.refs_8_
  13.1 0.1 collective-permute-start.5
  13.2 1.3 %collective-permute-start.4 = (bf16[128,512]{1,0:T(8,128)(2,1)S(1)}, bf16[128,512]{1,0:T(8,128)(2,1)S(1)}, u32[]{:S(2)}, u32[]{:S(2)}) collective-permute-start(bf16[128,512]{1,0:T(8,128)(2,1)S(1)} %collective-permute-done.refs_1_), channel_id=1, source_target_pairs={{0,1},{1,0},{2,3},{3,2},{4,5},{5,4},{6,7},{7,6},{8,9},{9,8},{10,11... | collective-permute-start | bytes 393224 | tf_op jit(solution)/shard_map/ppermute | solution.py:36
  14.5 0.5 collective-permute-start.7
  15.1 0.9 %collective-permute-done.7.query_core = bf16[64,512]{1,0:T(8,128)(2,1)S(1)} collective-permute-done((bf16[64,512]{1,0:T(8,128)(2,1)S(1)}, bf16[64,512]{1,0:T(8,128)(2,1)S(1)}, u32[]{:S(2)}, u32[]{:S(2)}) %collective-permute-start.7) | collective-permute-done | bytes 65568 | tf_op jit(solution)/shard_map/ppermute | solution.py:36
  16.0 2.1 %gradient.1 = (f32[64,768]{1,0:T(8,128)S(1)}, bf16[128,768]{1,0:T(8,128)(2,1)S(1)}, bf16[128,768]{1,0:T(8,128)(2,1)S(1)}, f32[64,768]{1,0:T(8,128)S(1)}, f32[64,...) custom-call(bf16[128,512]{1,0:T(8,128)(2,1)S(1)} %copy-done.5, bf16[128,512]{1,0:T(8,128)(2,1)S(1)} %collective-permute-done.refs_1_, ...), custom_call_target="tpu_custom_call" | custom-call | flops 1342177280 | bytes 6291456 | tf_op jit(solution)/shard_map/gradient/pallas_call | solution.py:255
  18.1 1.0 %collective-permute-start.8 = (bf16[128,768]{1,0:T(8,128)(2,1)S(1)}, bf16[128,768]{1,0:T(8,128)(2,1)S(1)}, u32[]{:S(2)}, u32[]{:S(2)}) collective-permute-start(bf16[128,768]{1,0:T(8,128)(2,1)S(1)} %get-tuple-element.71), channel_id=1, source_target_pairs={{0,2},{1,3},{2,4},{3,5},{4,6},{5,7},{6,8},{7,9},{8,10},{9,11},{10,... | collective-permute-start | bytes 589832 | tf_op jit(solution)/shard_map/ppermute | solution.py:36
  19.1 4.0 %collective-permute-start.9 = (bf16[128,768]{1,0:T(8,128)(2,1)S(1)}, bf16[128,768]{1,0:T(8,128)(2,1)S(1)}, u32[]{:S(2)}, u32[]{:S(2)}) collective-permute-start(bf16[128,768]{1,0:T(8,128)(2,1)S(1)} %get-tuple-element.72), channel_id=1, source_target_pairs={{0,14},{1,15},{2,0},{3,1},{4,2},{5,3},{6,4},{7,5},{8,6},{9,7},{10,... | collective-permute-start | bytes 589832 | tf_op jit(solution)/shard_map/ppermute | solution.py:36
  23.2 1.8 %collective-permute-start.10 = (bf16[64,768]{1,0:T(8,128)(2,1)S(1)}, bf16[64,768]{1,0:T(8,128)(2,1)S(1)}, u32[]{:S(2)}, u32[]{:S(2)}) collective-permute-start(bf16[64,768]{1,0:T(8,128)(2,1)S(1)} %get-tuple-element.75), channel_id=1, source_target_pairs={{0,4},{1,13},{2,6},{3,15},{4,8},{5,1},{6,10},{7,3},{8,12},{9,5},{1... | collective-permute-start | bytes 294920 | tf_op jit(solution)/shard_map/ppermute | solution.py:36
  25.0 5.0 %collective-permute-done.10.far = bf16[64,768]{1,0:T(8,128)(2,1)S(1)} collective-permute-done((bf16[64,768]{1,0:T(8,128)(2,1)S(1)}, bf16[64,768]{1,0:T(8,128)(2,1)S(1)}, u32[]{:S(2)}, u32[]{:S(2)}) %collective-permute-start.10) | collective-permute-done | bytes 98336 | tf_op jit(solution)/shard_map/ppermute | solution.py:36
  30.1 4.4 %collective-permute-start.11 = (bf16[64,768]{1,0:T(8,128)(2,1)S(1)}, bf16[64,768]{1,0:T(8,128)(2,1)S(1)}, u32[]{:S(2)}, u32[]{:S(2)}) collective-permute-start(bf16[64,768]{1,0:T(8,128)(2,1)S(1)} %get-tuple-element.76), channel_id=1, source_target_pairs={{0,4},{1,5},{2,6},{3,7},{4,8},{5,9},{6,10},{7,11},{8,12},{9,13},{1... | collective-permute-start | bytes 294920 | tf_op jit(solution)/shard_map/ppermute | solution.py:36
  34.5 2.0 %collective-permute-done.11.c = bf16[64,768]{1,0:T(8,128)(2,1)S(1)} collective-permute-done((bf16[64,768]{1,0:T(8,128)(2,1)S(1)}, bf16[64,768]{1,0:T(8,128)(2,1)S(1)}, u32[]{:S(2)}, u32[]{:S(2)}) %collective-permute-start.11) | collective-permute-done | bytes 98336 | tf_op jit(solution)/shard_map/ppermute | solution.py:36
  36.5 3.6 %collective-permute-done.12.d = bf16[64,768]{1,0:T(8,128)(2,1)S(1)} collective-permute-done((bf16[64,768]{1,0:T(8,128)(2,1)S(1)}, bf16[64,768]{1,0:T(8,128)(2,1)S(1)}, u32[]{:S(2)}, u32[]{:S(2)}) %collective-permute-start.12) | collective-permute-done | bytes 98336 | tf_op jit(solution)/shard_map/ppermute | solution.py:36
  40.2 1.0 %collective-permute-start.13 = (bf16[64,768]{1,0:T(8,128)(2,1)S(1)}, bf16[64,768]{1,0:T(8,128)(2,1)S(1)}, u32[]{:S(2)}, u32[]{:S(2)}) collective-permute-start(bf16[64,768]{1,0:T(8,128)(2,1)S(1)} %add_up.1), channel_id=1, source_target_pairs={{0,16},{1,17},{2,18},{3,19},{4,20},{5,21},{6,22},{7,23},{8,24},{9,... | collective-permute-start | bytes 294920 | tf_op jit(solution)/shard_map/ppermute | solution.py:36
  41.2 1.7 %collective-permute-start.14 = (bf16[64,512]{1,0:T(8,128)(2,1)S(1)}, bf16[64,512]{1,0:T(8,128)(2,1)S(1)}, u32[]{:S(2)}, u32[]{:S(2)}) collective-permute-start(bf16[64,512]{1,0:T(8,128)(2,1)S(1)} %copy-done.6), channel_id=1, source_target_pairs={{0,48},{1,49},{2,50},{3,51},{4,52},{5,53},{6,54},{7,55},{8,56},{9,... | collective-permute-start | bytes 196616 | tf_op jit(solution)/shard_map/ppermute | solution.py:36
  42.9 1.8 %collective-permute-start.15 = (bf16[64,512]{1,0:T(8,128)(2,1)S(1)}, bf16[64,512]{1,0:T(8,128)(2,1)S(1)}, u32[]{:S(2)}, u32[]{:S(2)}) collective-permute-start(bf16[64,512]{1,0:T(8,128)(2,1)S(1)} %copy-done.6), channel_id=1, source_target_pairs={{0,49},{1,48},{2,51},{3,50},{4,53},{5,52},{6,55},{7,54},{8,57},{9,... | collective-permute-start | bytes 196616 | tf_op jit(solution)/shard_map/ppermute | solution.py:36
  44.8 0.8 collective-permute-done.14.query_far
  45.5 3.3 %collective-permute-done.15.query_far_core = bf16[64,512]{1,0:T(8,128)(2,1)S(1)} collective-permute-done((bf16[64,512]{1,0:T(8,128)(2,1)S(1)}, bf16[64,512]{1,0:T(8,128)(2,1)S(1)}, u32[]{:S(2)}, u32[]{:S(2)}) %collective-permute-start.15) | collective-permute-done | bytes 65568 | tf_op jit(solution)/shard_map/ppermute | solution.py:36
  48.8 2.6 %collective-permute-start.16 = (bf16[64,1536]{1,0:T(8,128)(2,1)S(1)}, bf16[64,1536]{1,0:T(8,128)(2,1)S(1)}, u32[]{:S(2)}, u32[]{:S(2)}) collective-permute-start(bf16[64,1536]{1,0:T(8,128)(2,1)S(1)} %pad_maximum_fusion.refs_0_), channel_id=1, source_target_pairs={{0,4},{1,5},{2,6},{3,7},{4,8},{5,9},{6,10},{7,11},{8,12},{9,13},{1... | collective-permute-start | bytes 589832 | tf_op jit(solution)/shard_map/ppermute | solution.py:36
  51.4 1.1 %collective-permute-start.17 = (bf16[64,1536]{1,0:T(8,128)(2,1)S(1)}, bf16[64,1536]{1,0:T(8,128)(2,1)S(1)}, u32[]{:S(2)}, u32[]{:S(2)}) collective-permute-start(bf16[64,1536]{1,0:T(8,128)(2,1)S(1)} %pad_maximum_fusion.refs_0_), channel_id=1, source_target_pairs={{0,12},{1,13},{2,14},{3,15},{4,0},{5,1},{6,2},{7,3},{8,4},{9,5},{1... | collective-permute-start | bytes 589832 | tf_op jit(solution)/shard_map/ppermute | solution.py:36
  52.5 1.1 %collective-permute-start.18 = (bf16[64,1536]{1,0:T(8,128)(2,1)S(1)}, bf16[64,1536]{1,0:T(8,128)(2,1)S(1)}, u32[]{:S(2)}, u32[]{:S(2)}) collective-permute-start(bf16[64,1536]{1,0:T(8,128)(2,1)S(1)} %pad_maximum_fusion.refs_0_), channel_id=1, source_target_pairs={{0,2},{1,3},{2,4},{3,5},{4,6},{5,7},{6,8},{7,9},{8,10},{9,11},{10,... | collective-permute-start | bytes 589832 | tf_op jit(solution)/shard_map/ppermute | solution.py:36
  53.5 1.6 %collective-permute-start.19 = (bf16[64,1536]{1,0:T(8,128)(2,1)S(1)}, bf16[64,1536]{1,0:T(8,128)(2,1)S(1)}, u32[]{:S(2)}, u32[]{:S(2)}) collective-permute-start(bf16[64,1536]{1,0:T(8,128)(2,1)S(1)} %pad_maximum_fusion.refs_0_), channel_id=1, source_target_pairs={{0,14},{1,15},{2,0},{3,1},{4,2},{5,3},{6,4},{7,5},{8,6},{9,7},{10,... | collective-permute-start | bytes 589832 | tf_op jit(solution)/shard_map/ppermute | solution.py:36
  55.2 2.8 %copy-done.1 = bf16[3,2,512,1024]{3,2,1,0:T(8,128)(2,1)S(1)} copy-done((bf16[3,2,512,1024]{3,2,1,0:T(8,128)(2,1)S(1)}, bf16[3,2,512,1024]{3,2,1,0:T(8,128)(2,1)}, u32[]{:S(2)}) %copy-start.1) | copy-done | bytes 6291480
  57.9 2.7 %first_block.1.first_out = bf16[64,1024]{1,0:T(8,128)(2,1)S(1)} custom-call(bf16[2,64,1024]{2,1,0:T(8,128)(2,1)S(1)} %copy-done.3, bf16[3,2,512,1024]{3,2,1,0:T(8,128)(2,1)S(1)} %copy-done.1), custom_call_target="tpu_custom_call" | custom-call | flops 402653184 | bytes 7340032 | tf_op jit(solution)/shard_map/first_block/pallas_call | solution.py:168
  60.7 0.7 collective-permute-done.17.refs_4_
  61.4 1.7 %collective-permute-start.22 = (bf16[64,1536]{1,0:T(8,128)(2,1)S(1)}, bf16[64,1536]{1,0:T(8,128)(2,1)S(1)}, u32[]{:S(2)}, u32[]{:S(2)}) collective-permute-start(bf16[64,1536]{1,0:T(8,128)(2,1)S(1)} %broadcast_select_fusion), channel_id=1, source_target_pairs={{0,4},{1,13},{2,6},{3,15},{4,8},{5,1},{6,10},{7,3},{8,12},{9,5},{1... | collective-permute-start | bytes 589832 | tf_op jit(solution)/shard_map/ppermute | solution.py:36
  63.1 1.2 %collective-permute-start.20 = (bf16[64,1536]{1,0:T(8,128)(2,1)S(1)}, bf16[64,1536]{1,0:T(8,128)(2,1)S(1)}, u32[]{:S(2)}, u32[]{:S(2)}) collective-permute-start(bf16[64,1536]{1,0:T(8,128)(2,1)S(1)} %collective-permute-done.16.refs_3_), channel_id=1, source_target_pairs={{0,2},{1,3},{2,4},{3,5},{4,6},{5,7},{6,8},{7,9},{8,10},{9,11},{10,... | collective-permute-start | bytes 589832 | tf_op jit(solution)/shard_map/ppermute | solution.py:36
  64.3 1.4 %collective-permute-start.21 = (bf16[64,1536]{1,0:T(8,128)(2,1)S(1)}, bf16[64,1536]{1,0:T(8,128)(2,1)S(1)}, u32[]{:S(2)}, u32[]{:S(2)}) collective-permute-start(bf16[64,1536]{1,0:T(8,128)(2,1)S(1)} %collective-permute-done.17.refs_4_), channel_id=1, source_target_pairs={{0,14},{1,15},{2,0},{3,1},{4,2},{5,3},{6,4},{7,5},{8,6},{9,7},{10,... | collective-permute-start | bytes 589832 | tf_op jit(solution)/shard_map/ppermute | solution.py:36
  65.7 5.4 %collective-permute-done.22.refs_7_ = bf16[64,1536]{1,0:T(8,128)(2,1)S(1)} collective-permute-done((bf16[64,1536]{1,0:T(8,128)(2,1)S(1)}, bf16[64,1536]{1,0:T(8,128)(2,1)S(1)}, u32[]{:S(2)}, u32[]{:S(2)}) %collective-permute-start.22) | collective-permute-done | bytes 196640 | tf_op jit(solution)/shard_map/ppermute | solution.py:36
  71.2 4.4 %collective-permute-done.21.refs_6_ = bf16[64,1536]{1,0:T(8,128)(2,1)S(1)} collective-permute-done((bf16[64,1536]{1,0:T(8,128)(2,1)S(1)}, bf16[64,1536]{1,0:T(8,128)(2,1)S(1)}, u32[]{:S(2)}, u32[]{:S(2)}) %collective-permute-start.21) | collective-permute-done | bytes 196640 | tf_op jit(solution)/shard_map/ppermute | solution.py:36
  75.6 0.6 pack.1
  76.2 0.5 collective-permute-start.23
  76.7 3.1 %project.1.mine = f32[256,1024]{1,0:T(8,128)S(1)} custom-call(bf16[512,1024]{1,0:T(8,128)(2,1)S(1)} %get-tuple-element.88.scaled, bf16[3,2,512,1024]{3,2,1,0:T(8,128)(2,1)S(1)} %copy-done.2, bf16[64,512]{1,0:T(8,128)(2,1)S(1)} %copy-done.4, bf16[64,512]{1,0:T(8,128)(2,1)S(1)} %collective-permute-done.7.query_core, ...), custom_call_target="tpu_custom_call" | custom-call | flops 2200000000 | bytes 5242880 | tf_op jit(solution)/shard_map/project/pallas_call | solution.py:417
  79.8 0.4 collective-permute-start.24
  80.2 2.5 %renew_third.1.rows = bf16[256,1024]{1,0:T(8,128)(2,1)S(1)} custom-call(bf16[512,512]{1,0:T(8,128)(2,1)S(1)} %get-tuple-element.92.mine, bf16[512,512]{1,0:T(8,128)(2,1)S(1)} %collective-permute-done.23.other, bf16[3,2,512,1024]{3,2,1,0:T(8,128)(2,1)S(1)} %copy-done.2), custom_call_target="tpu_custom_call" | custom-call | flops 1200000000 | bytes 4194304 | tf_op jit(solution)/shard_map/renew_third/pallas_call | solution.py:452
  82.8 0.5 down.1
  83.4 0.4 collective-permute-start.25
  83.8 2.3 %collective-permute-start.26 = (bf16[64,256]{1,0:T(8,128)(2,1)S(1)}, bf16[64,256]{1,0:T(8,128)(2,1)S(1)}, u32[]{:S(2)}, u32[]{:S(2)}) collective-permute-start(bf16[64,256]{1,0:T(8,128)(2,1)S(1)} %get-tuple-element.97), channel_id=1, source_target_pairs={{0,48},{1,49},{2,50},{3,51},{4,52},{5,53},{6,54},{7,55},{8,56},{9,... | collective-permute-start | bytes 98312 | tf_op jit(solution)/shard_map/ppermute | solution.py:36
  86.1 0.7 collective-permute-start.27
  86.8 1.0 %collective-permute-done.26.far = bf16[64,256]{1,0:T(8,128)(2,1)S(1)} collective-permute-done((bf16[64,256]{1,0:T(8,128)(2,1)S(1)}, bf16[64,256]{1,0:T(8,128)(2,1)S(1)}, u32[]{:S(2)}, u32[]{:S(2)}) %collective-permute-start.26) | collective-permute-done | bytes 32800 | tf_op jit(solution)/shard_map/ppermute | solution.py:36
  87.7 3.1 %collective-permute-done.27.far_core = bf16[64,256]{1,0:T(8,128)(2,1)S(1)} collective-permute-done((bf16[64,256]{1,0:T(8,128)(2,1)S(1)}, bf16[64,256]{1,0:T(8,128)(2,1)S(1)}, u32[]{:S(2)}, u32[]{:S(2)}) %collective-permute-start.27) | collective-permute-done | bytes 32800 | tf_op jit(solution)/shard_map/ppermute | solution.py:36
  90.8 0.7 finish.1
  (35 shorter events, 0.3 us)
Async XLA Ops:
  2.2 10.9 %collective-permute-start.1 = (bf16[128,512]{1,0:T(8,128)(2,1)}, bf16[128,512]{1,0:T(8,128)(2,1)S(1)}, u32[]{:S(2)}, u32[]{:S(2)}) collective-permute-start(bf16[128,512]{1,0:T(8,128)(2,1)} %get-tuple-element.55), channel_id=1, source_target_pairs={{0,32},{1,33},{2,34},{3,35},{4,36},{5,37},{6,38},{7,39},{8,40},{9,... | collective-permute-start | bytes 393224 | tf_op jit(solution)/shard_map/ppermute | solution.py:36
  5.8 7.4 %collective-permute-start = (bf16[128,512]{1,0:T(8,128)(2,1)}, bf16[128,512]{1,0:T(8,128)(2,1)S(1)}, u32[]{:S(2)}, u32[]{:S(2)}) collective-permute-start(bf16[128,512]{1,0:T(8,128)(2,1)} %get-tuple-element.54), channel_id=1, source_target_pairs={{0,16},{1,17},{2,18},{3,19},{4,20},{5,21},{6,22},{7,23},{8,24},{9,... | collective-permute-start | bytes 393224 | tf_op jit(solution)/shard_map/ppermute | solution.py:36
  6.1 8.4 %collective-permute-start.2 = (bf16[128,512]{1,0:T(8,128)(2,1)}, bf16[128,512]{1,0:T(8,128)(2,1)S(1)}, u32[]{:S(2)}, u32[]{:S(2)}) collective-permute-start(bf16[128,512]{1,0:T(8,128)(2,1)} %get-tuple-element.59), channel_id=1, source_target_pairs={{0,48},{1,49},{2,50},{3,51},{4,52},{5,53},{6,54},{7,55},{8,56},{9,... | collective-permute-start | bytes 393224 | tf_op jit(solution)/shard_map/ppermute | solution.py:36
  8.5 6.6 %collective-permute-start.3 = (bf16[128,512]{1,0:T(8,128)(2,1)}, bf16[128,512]{1,0:T(8,128)(2,1)S(1)}, u32[]{:S(2)}, u32[]{:S(2)}) collective-permute-start(bf16[128,512]{1,0:T(8,128)(2,1)} %get-tuple-element.61.refs_0_), channel_id=1, source_target_pairs={{0,1},{1,0},{2,3},{3,2},{4,5},{5,4},{6,7},{7,6},{8,9},{9,8},{10,11... | collective-permute-start | bytes 393224 | tf_op jit(solution)/shard_map/ppermute | solution.py:36
  10.0 2.8 %copy-start = (bf16[3,2,512,1024]{3,2,1,0:T(8,128)(2,1)S(1)}, bf16[3,2,512,1024]{3,2,1,0:T(8,128)(2,1)}, u32[]{:S(2)}) copy-start(bf16[3,2,512,1024]{3,2,1,0:T(8,128)(2,1)} %weights.3) | copy-start | bytes 18874372
  12.8 1.8 %copy-start.4 = (bf16[64,512]{1,0:T(8,128)(2,1)S(1)}, bf16[64,512]{1,0:T(8,128)(2,1)}, u32[]{:S(2)}) copy-start(bf16[64,512]{1,0:T(8,128)(2,1)} %get-tuple-element.60.query_own) | copy-start | bytes 196612
  12.8 3.2 %copy-start.5 = (bf16[128,512]{1,0:T(8,128)(2,1)S(1)}, bf16[128,512]{1,0:T(8,128)(2,1)}, u32[]{:S(2)}) copy-start(bf16[128,512]{1,0:T(8,128)(2,1)} %get-tuple-element.61.refs_0_) | copy-start | bytes 393220
  12.8 28.4 %copy-start.6 = (bf16[64,512]{1,0:T(8,128)(2,1)S(1)}, bf16[64,512]{1,0:T(8,128)(2,1)}, u32[]{:S(2)}) copy-start(bf16[64,512]{1,0:T(8,128)(2,1)} %get-tuple-element.80) | copy-start | bytes 196612
  12.8 42.4 %copy-start.3 = (bf16[2,64,1024]{2,1,0:T(8,128)(2,1)S(1)}, bf16[2,64,1024]{2,1,0:T(8,128)(2,1)}, u32[]{:S(2)}) copy-start(bf16[2,64,1024]{2,1,0:T(8,128)(2,1)} %queries.2) | copy-start | bytes 786436
  13.1 2.9 %collective-permute-start.5 = (bf16[128,512]{1,0:T(8,128)(2,1)S(1)}, bf16[128,512]{1,0:T(8,128)(2,1)S(1)}, u32[]{:S(2)}, u32[]{:S(2)}) collective-permute-start(bf16[128,512]{1,0:T(8,128)(2,1)S(1)} %collective-permute-done.1.refs_2_), channel_id=1, source_target_pairs={{0,1},{1,0},{2,3},{3,2},{4,5},{5,4},{6,7},{7,6},{8,9},{9,8},{10,11... | collective-permute-start | bytes 393224 | tf_op jit(solution)/shard_map/ppermute | solution.py:36
  13.2 2.8 %collective-permute-start.4 = (bf16[128,512]{1,0:T(8,128)(2,1)S(1)}, bf16[128,512]{1,0:T(8,128)(2,1)S(1)}, u32[]{:S(2)}, u32[]{:S(2)}) collective-permute-start(bf16[128,512]{1,0:T(8,128)(2,1)S(1)} %collective-permute-done.refs_1_), channel_id=1, source_target_pairs={{0,1},{1,0},{2,3},{3,2},{4,5},{5,4},{6,7},{7,6},{8,9},{9,8},{10,11... | collective-permute-start | bytes 393224 | tf_op jit(solution)/shard_map/ppermute | solution.py:36
  14.5 1.5 %collective-permute-start.6 = (bf16[128,512]{1,0:T(8,128)(2,1)S(1)}, bf16[128,512]{1,0:T(8,128)(2,1)S(1)}, u32[]{:S(2)}, u32[]{:S(2)}) collective-permute-start(bf16[128,512]{1,0:T(8,128)(2,1)S(1)} %collective-permute-done.2.refs_3_), channel_id=1, source_target_pairs={{0,1},{1,0},{2,3},{3,2},{4,5},{5,4},{6,7},{7,6},{8,9},{9,8},{10,11... | collective-permute-start | bytes 393224 | tf_op jit(solution)/shard_map/ppermute | solution.py:36
  14.5 1.4 %collective-permute-start.7 = (bf16[64,512]{1,0:T(8,128)(2,1)S(1)}, bf16[64,512]{1,0:T(8,128)(2,1)S(1)}, u32[]{:S(2)}, u32[]{:S(2)}) collective-permute-start(bf16[64,512]{1,0:T(8,128)(2,1)S(1)} %copy-done.4), channel_id=1, source_target_pairs={{0,1},{1,0},{2,3},{3,2},{4,5},{5,4},{6,7},{7,6},{8,9},{9,8},{10,11... | collective-permute-start | bytes 196616 | tf_op jit(solution)/shard_map/ppermute | solution.py:36
  18.1 11.9 %collective-permute-start.8 = (bf16[128,768]{1,0:T(8,128)(2,1)S(1)}, bf16[128,768]{1,0:T(8,128)(2,1)S(1)}, u32[]{:S(2)}, u32[]{:S(2)}) collective-permute-start(bf16[128,768]{1,0:T(8,128)(2,1)S(1)} %get-tuple-element.71), channel_id=1, source_target_pairs={{0,2},{1,3},{2,4},{3,5},{4,6},{5,7},{6,8},{7,9},{8,10},{9,11},{10,... | collective-permute-start | bytes 589832 | tf_op jit(solution)/shard_map/ppermute | solution.py:36
  19.1 10.9 %collective-permute-start.9 = (bf16[128,768]{1,0:T(8,128)(2,1)S(1)}, bf16[128,768]{1,0:T(8,128)(2,1)S(1)}, u32[]{:S(2)}, u32[]{:S(2)}) collective-permute-start(bf16[128,768]{1,0:T(8,128)(2,1)S(1)} %get-tuple-element.72), channel_id=1, source_target_pairs={{0,14},{1,15},{2,0},{3,1},{4,2},{5,3},{6,4},{7,5},{8,6},{9,7},{10,... | collective-permute-start | bytes 589832 | tf_op jit(solution)/shard_map/ppermute | solution.py:36
  23.2 6.8 %collective-permute-start.10 = (bf16[64,768]{1,0:T(8,128)(2,1)S(1)}, bf16[64,768]{1,0:T(8,128)(2,1)S(1)}, u32[]{:S(2)}, u32[]{:S(2)}) collective-permute-start(bf16[64,768]{1,0:T(8,128)(2,1)S(1)} %get-tuple-element.75), channel_id=1, source_target_pairs={{0,4},{1,13},{2,6},{3,15},{4,8},{5,1},{6,10},{7,3},{8,12},{9,5},{1... | collective-permute-start | bytes 294920 | tf_op jit(solution)/shard_map/ppermute | solution.py:36
  30.1 6.4 %collective-permute-start.11 = (bf16[64,768]{1,0:T(8,128)(2,1)S(1)}, bf16[64,768]{1,0:T(8,128)(2,1)S(1)}, u32[]{:S(2)}, u32[]{:S(2)}) collective-permute-start(bf16[64,768]{1,0:T(8,128)(2,1)S(1)} %get-tuple-element.76), channel_id=1, source_target_pairs={{0,4},{1,5},{2,6},{3,7},{4,8},{5,9},{6,10},{7,11},{8,12},{9,13},{1... | collective-permute-start | bytes 294920 | tf_op jit(solution)/shard_map/ppermute | solution.py:36
  34.5 5.6 %collective-permute-start.12 = (bf16[64,768]{1,0:T(8,128)(2,1)S(1)}, bf16[64,768]{1,0:T(8,128)(2,1)S(1)}, u32[]{:S(2)}, u32[]{:S(2)}) collective-permute-start(bf16[64,768]{1,0:T(8,128)(2,1)S(1)} %get-tuple-element.77), channel_id=1, source_target_pairs={{0,12},{1,13},{2,14},{3,15},{4,0},{5,1},{6,2},{7,3},{8,4},{9,5},{1... | collective-permute-start | bytes 294920 | tf_op jit(solution)/shard_map/ppermute | solution.py:36
  40.2 8.6 %collective-permute-start.13 = (bf16[64,768]{1,0:T(8,128)(2,1)S(1)}, bf16[64,768]{1,0:T(8,128)(2,1)S(1)}, u32[]{:S(2)}, u32[]{:S(2)}) collective-permute-start(bf16[64,768]{1,0:T(8,128)(2,1)S(1)} %add_up.1), channel_id=1, source_target_pairs={{0,16},{1,17},{2,18},{3,19},{4,20},{5,21},{6,22},{7,23},{8,24},{9,... | collective-permute-start | bytes 294920 | tf_op jit(solution)/shard_map/ppermute | solution.py:36
  41.2 4.3 %collective-permute-start.14 = (bf16[64,512]{1,0:T(8,128)(2,1)S(1)}, bf16[64,512]{1,0:T(8,128)(2,1)S(1)}, u32[]{:S(2)}, u32[]{:S(2)}) collective-permute-start(bf16[64,512]{1,0:T(8,128)(2,1)S(1)} %copy-done.6), channel_id=1, source_target_pairs={{0,48},{1,49},{2,50},{3,51},{4,52},{5,53},{6,54},{7,55},{8,56},{9,... | collective-permute-start | bytes 196616 | tf_op jit(solution)/shard_map/ppermute | solution.py:36
  42.9 5.9 %collective-permute-start.15 = (bf16[64,512]{1,0:T(8,128)(2,1)S(1)}, bf16[64,512]{1,0:T(8,128)(2,1)S(1)}, u32[]{:S(2)}, u32[]{:S(2)}) collective-permute-start(bf16[64,512]{1,0:T(8,128)(2,1)S(1)} %copy-done.6), channel_id=1, source_target_pairs={{0,49},{1,48},{2,51},{3,50},{4,53},{5,52},{6,55},{7,54},{8,57},{9,... | collective-permute-start | bytes 196616 | tf_op jit(solution)/shard_map/ppermute | solution.py:36
  48.8 11.9 %collective-permute-start.16 = (bf16[64,1536]{1,0:T(8,128)(2,1)S(1)}, bf16[64,1536]{1,0:T(8,128)(2,1)S(1)}, u32[]{:S(2)}, u32[]{:S(2)}) collective-permute-start(bf16[64,1536]{1,0:T(8,128)(2,1)S(1)} %pad_maximum_fusion.refs_0_), channel_id=1, source_target_pairs={{0,4},{1,5},{2,6},{3,7},{4,8},{5,9},{6,10},{7,11},{8,12},{9,13},{1... | collective-permute-start | bytes 589832 | tf_op jit(solution)/shard_map/ppermute | solution.py:36
  51.4 9.9 %collective-permute-start.17 = (bf16[64,1536]{1,0:T(8,128)(2,1)S(1)}, bf16[64,1536]{1,0:T(8,128)(2,1)S(1)}, u32[]{:S(2)}, u32[]{:S(2)}) collective-permute-start(bf16[64,1536]{1,0:T(8,128)(2,1)S(1)} %pad_maximum_fusion.refs_0_), channel_id=1, source_target_pairs={{0,12},{1,13},{2,14},{3,15},{4,0},{5,1},{6,2},{7,3},{8,4},{9,5},{1... | collective-permute-start | bytes 589832 | tf_op jit(solution)/shard_map/ppermute | solution.py:36
  52.5 13.3 %collective-permute-start.18 = (bf16[64,1536]{1,0:T(8,128)(2,1)S(1)}, bf16[64,1536]{1,0:T(8,128)(2,1)S(1)}, u32[]{:S(2)}, u32[]{:S(2)}) collective-permute-start(bf16[64,1536]{1,0:T(8,128)(2,1)S(1)} %pad_maximum_fusion.refs_0_), channel_id=1, source_target_pairs={{0,2},{1,3},{2,4},{3,5},{4,6},{5,7},{6,8},{7,9},{8,10},{9,11},{10,... | collective-permute-start | bytes 589832 | tf_op jit(solution)/shard_map/ppermute | solution.py:36
  53.5 12.2 %collective-permute-start.19 = (bf16[64,1536]{1,0:T(8,128)(2,1)S(1)}, bf16[64,1536]{1,0:T(8,128)(2,1)S(1)}, u32[]{:S(2)}, u32[]{:S(2)}) collective-permute-start(bf16[64,1536]{1,0:T(8,128)(2,1)S(1)} %pad_maximum_fusion.refs_0_), channel_id=1, source_target_pairs={{0,14},{1,15},{2,0},{3,1},{4,2},{5,3},{6,4},{7,5},{8,6},{9,7},{10,... | collective-permute-start | bytes 589832 | tf_op jit(solution)/shard_map/ppermute | solution.py:36
  55.2 2.8 %copy-start.1 = (bf16[3,2,512,1024]{3,2,1,0:T(8,128)(2,1)S(1)}, bf16[3,2,512,1024]{3,2,1,0:T(8,128)(2,1)}, u32[]{:S(2)}) copy-start(bf16[3,2,512,1024]{3,2,1,0:T(8,128)(2,1)} %weights.3) | copy-start | bytes 18874372
  57.9 18.8 %copy-start.2 = (bf16[3,2,512,1024]{3,2,1,0:T(8,128)(2,1)S(1)}, bf16[3,2,512,1024]{3,2,1,0:T(8,128)(2,1)}, u32[]{:S(2)}) copy-start(bf16[3,2,512,1024]{3,2,1,0:T(8,128)(2,1)} %weights.3) | copy-start | bytes 18874372
  61.4 9.8 %collective-permute-start.22 = (bf16[64,1536]{1,0:T(8,128)(2,1)S(1)}, bf16[64,1536]{1,0:T(8,128)(2,1)S(1)}, u32[]{:S(2)}, u32[]{:S(2)}) collective-permute-start(bf16[64,1536]{1,0:T(8,128)(2,1)S(1)} %broadcast_select_fusion), channel_id=1, source_target_pairs={{0,4},{1,13},{2,6},{3,15},{4,8},{5,1},{6,10},{7,3},{8,12},{9,5},{1... | collective-permute-start | bytes 589832 | tf_op jit(solution)/shard_map/ppermute | solution.py:36
  63.1 8.1 %collective-permute-start.20 = (bf16[64,1536]{1,0:T(8,128)(2,1)S(1)}, bf16[64,1536]{1,0:T(8,128)(2,1)S(1)}, u32[]{:S(2)}, u32[]{:S(2)}) collective-permute-start(bf16[64,1536]{1,0:T(8,128)(2,1)S(1)} %collective-permute-done.16.refs_3_), channel_id=1, source_target_pairs={{0,2},{1,3},{2,4},{3,5},{4,6},{5,7},{6,8},{7,9},{8,10},{9,11},{10,... | collective-permute-start | bytes 589832 | tf_op jit(solution)/shard_map/ppermute | solution.py:36
  64.3 11.3 %collective-permute-start.21 = (bf16[64,1536]{1,0:T(8,128)(2,1)S(1)}, bf16[64,1536]{1,0:T(8,128)(2,1)S(1)}, u32[]{:S(2)}, u32[]{:S(2)}) collective-permute-start(bf16[64,1536]{1,0:T(8,128)(2,1)S(1)} %collective-permute-done.17.refs_4_), channel_id=1, source_target_pairs={{0,14},{1,15},{2,0},{3,1},{4,2},{5,3},{6,4},{7,5},{8,6},{9,7},{10,... | collective-permute-start | bytes 589832 | tf_op jit(solution)/shard_map/ppermute | solution.py:36
  76.2 3.6 %collective-permute-start.23 = (bf16[512,512]{1,0:T(8,128)(2,1)S(1)}, bf16[512,512]{1,0:T(8,128)(2,1)S(1)}, u32[]{:S(2)}, u32[]{:S(2)}) collective-permute-start(bf16[512,512]{1,0:T(8,128)(2,1)S(1)} %get-tuple-element.92.mine), channel_id=1, source_target_pairs={{0,1},{1,0},{2,3},{3,2},{4,5},{5,4},{6,7},{7,6},{8,9},{9,8},{10,11... | collective-permute-start | bytes 1572872 | tf_op jit(solution)/shard_map/ppermute | solution.py:36
  79.8 3.0 %collective-permute-start.24 = (f32[256,1024]{1,0:T(8,128)S(1)}, f32[256,1024]{1,0:T(8,128)S(1)}, u32[]{:S(2)}, u32[]{:S(2)}) collective-permute-start(f32[256,1024]{1,0:T(8,128)S(1)} %project.1.mine), channel_id=1, source_target_pairs={{0,1},{1,0},{2,3},{3,2},{4,5},{5,4},{6,7},{7,6},{8,9},{9,8},{10,11... | collective-permute-start | bytes 3145736 | tf_op jit(solution)/shard_map/ppermute | solution.py:36
  83.4 3.4 %collective-permute-start.25 = (bf16[64,256]{1,0:T(8,128)(2,1)S(1)}, bf16[64,256]{1,0:T(8,128)(2,1)S(1)}, u32[]{:S(2)}, u32[]{:S(2)}) collective-permute-start(bf16[64,256]{1,0:T(8,128)(2,1)S(1)} %get-tuple-element.96), channel_id=1, source_target_pairs={{0,1},{1,0},{2,3},{3,2},{4,5},{5,4},{6,7},{7,6},{8,9},{9,8},{10,11... | collective-permute-start | bytes 98312 | tf_op jit(solution)/shard_map/ppermute | solution.py:36
  83.8 4.0 %collective-permute-start.26 = (bf16[64,256]{1,0:T(8,128)(2,1)S(1)}, bf16[64,256]{1,0:T(8,128)(2,1)S(1)}, u32[]{:S(2)}, u32[]{:S(2)}) collective-permute-start(bf16[64,256]{1,0:T(8,128)(2,1)S(1)} %get-tuple-element.97), channel_id=1, source_target_pairs={{0,48},{1,49},{2,50},{3,51},{4,52},{5,53},{6,54},{7,55},{8,56},{9,... | collective-permute-start | bytes 98312 | tf_op jit(solution)/shard_map/ppermute | solution.py:36
  86.1 4.7 %collective-permute-start.27 = (bf16[64,256]{1,0:T(8,128)(2,1)S(1)}, bf16[64,256]{1,0:T(8,128)(2,1)S(1)}, u32[]{:S(2)}, u32[]{:S(2)}) collective-permute-start(bf16[64,256]{1,0:T(8,128)(2,1)S(1)} %get-tuple-element.98), channel_id=1, source_target_pairs={{0,49},{1,48},{2,51},{3,50},{4,53},{5,52},{6,55},{7,54},{8,57},{9,... | collective-permute-start | bytes 98312 | tf_op jit(solution)/shard_map/ppermute | solution.py:36

commit v7 on v5

--- a/solution.py
+++ b/solution.py
@@ -50,10 +50,6 @@
 
 def mirror_x(array):
     return move(array, lambda x, z, c: (X - 1 - x, z, c))
-
-
-def mirror_x_core(array):
-    return move(array, lambda x, z, c: (X - 1 - x, z, c + 1))
 
 
 def other_core(array):
@@ -372,55 +368,57 @@
     )(*pieces)
 
 
-def gram_of(parts):
-    gram = dot(parts[0], parts[0], ((1,), (1,)))
-    for part in parts[1:]:
-        gram += dot(part, part, ((1,), (1,)))
-    gram = gram.astype(BF)
+def diagonal(value):
+    return jnp.where(
+        lax.broadcasted_iota(jnp.int32, (DIM, DIM), 0)
+        == lax.broadcasted_iota(jnp.int32, (DIM, DIM), 1),
+        value,
+        0.0,
+    )
+
+
+def gram_of(scaled):
+    gram = dot(scaled, scaled, ((1,), (1,))).astype(BF)
     gram_float = gram.astype(F32)
     level = jnp.sqrt(jnp.sum(gram_float * gram_float, keepdims=True)) + norm_eps
     half = 0.5 / level
-    diagonal = lax.broadcasted_iota(jnp.int32, (DIM, DIM), 0) == lax.broadcasted_iota(
-        jnp.int32, (DIM, DIM), 1
-    )
-    first_poly = (jnp.where(diagonal, 1.5, 0.0) - gram_float * half).astype(BF)
+    first_poly = (diagonal(1.5) - gram_float * half).astype(BF)
     return gram, first_poly, half, upd_scale / jnp.sqrt(level)
 
 
-def combine(rows, offset, gram, first_poly, half):
-    squared = dot(rows, first_poly, ((1,), (0,))).astype(BF)
+def combine(gram, first_poly, half):
+    squared = dot(first_poly, first_poly, ((1,), (0,))).astype(BF)
     moved = dot(squared, gram, ((1,), (0,)))
-    diagonal = lax.broadcasted_iota(jnp.int32, moved.shape, 0) + offset == lax.broadcasted_iota(
-        jnp.int32, moved.shape, 1
-    )
-    second_poly = (jnp.where(diagonal, 1.5, 0.0) - moved * half).astype(BF)
+    second_poly = (diagonal(1.5) - moved * half).astype(BF)
     return dot(second_poly, first_poly, ((1,), (0,))).astype(BF)
 
 
-def project_kernel(scaled, weights, query_own, query_core, query_far, query_far_core, out, w, q, sem):
+def project_kernel(scaled, weights, query_own, query_far, query_core, query_far_core, *refs):
+    mine, theirs, w, q, sem = refs
     x, _, c = place()
     load = pltpu.make_async_copy(weights.at[c, x // 2], w, sem)
     load.start()
     tokens = query_own.shape[0]
-    q[at_place(c * tokens, tokens), :] = query_own[...]
-    q[at_place((1 - c) * tokens, tokens), :] = query_core[...]
-    q[at_place((2 + c) * tokens, tokens), :] = query_far[...]
-    q[at_place((3 - c) * tokens, tokens), :] = query_far_core[...]
-    gram, first_poly, half, factor = gram_of([scaled[...]])
-    combined = combine(first_poly, 0, gram, first_poly, half)
+    for i, query in enumerate((query_own, query_far, query_core, query_far_core)):
+        q[i * tokens : (i + 1) * tokens, :] = query[...]
+    gram, first_poly, half, factor = gram_of(scaled[...])
+    combined = combine(gram, first_poly, half)
     update = dot(combined, scaled[...], ((1,), (0,))) * factor
     load.wait()
     renewed = (w[...].astype(F32) - update).astype(BF)
-    out[...] = dot(q[...], renewed, ((1,), (0,)))
+    projected = dot(q[...], renewed, ((1,), (0,)))
+    mine[...] = projected[: 2 * tokens]
+    theirs[...] = projected[2 * tokens :]
 
 
 def project(scaled, weights, *queries):
     tokens = queries[0].shape[0]
+    half = shape(2 * tokens, FF, dtype=F32)
     return pl.pallas_call(
         project_kernel,
-        out_shape=shape(4 * tokens, FF, dtype=F32),
+        out_shape=(half, half),
         in_specs=[VMEM, HBM] + [VMEM] * 4,
-        out_specs=VMEM,
+        out_specs=(VMEM, VMEM),
         scratch_shapes=[
             pltpu.VMEM((DIM, FF), BF),
             pltpu.VMEM((4 * tokens, DIM), BF),
@@ -432,43 +430,39 @@
     )(scaled, weights, *queries)
 
 
-def third_kernel(mine, other, weights, out, scaled, w, poly, sem):
+def third_kernel(mine, other, weights, out, scaled, w, sem):
     x, _, c = place()
-    rows = DIM // 2
-    load = pltpu.make_async_copy(weights.at[2, x // 2, at_place(c * rows, rows)], w, sem)
+    load = pltpu.make_async_copy(weights.at[2, x // 2], w, sem)
     load.start()
     for side in range(2):
         cols = slice(side * QUARTER, (side + 1) * QUARTER)
         scaled[:, at_place(side * HALF + c * QUARTER, QUARTER)] = mine[:, cols]
         scaled[:, at_place(side * HALF + (1 - c) * QUARTER, QUARTER)] = other[:, cols]
-    gram, first_poly, half, factor = gram_of([scaled[...]])
-    poly[...] = first_poly
-    combined = combine(poly[at_place(c * rows, rows), :], c * rows, gram, first_poly, half)
+    gram, first_poly, half, factor = gram_of(scaled[...])
+    combined = combine(gram, first_poly, half)
     update = dot(combined, scaled[...], ((1,), (0,))) * factor
     load.wait()
     out[...] = (w[...].astype(F32) - update).astype(BF)
 
 
 def renew_third(mine, other, weights):
-    rows = DIM // 2
     return pl.pallas_call(
         third_kernel,
-        out_shape=shape(rows, FF),
+        out_shape=shape(DIM, FF),
         in_specs=[VMEM, VMEM, HBM],
         out_specs=VMEM,
         scratch_shapes=[
             pltpu.VMEM((DIM, FF), BF),
-            pltpu.VMEM((rows, FF), BF),
-            pltpu.VMEM((DIM, DIM), BF),
+            pltpu.VMEM((DIM, FF), BF),
             pltpu.SemaphoreType.DMA,
         ],
-        compiler_params=params(14),
-        cost_estimate=cost(12 * 10**8, 4 << 20),
+        compiler_params=params(16),
+        cost_estimate=cost(19 * 10**8, 4 << 20),
         name="renew_third",
     )(mine, other, weights)
 
 
-def down_kernel(mine, other, rows, own, core, far, far_core, gated, result):
+def down_kernel(mine, other, weights, own, far, gated):
     _, _, c = place()
 
     @pl.when(c == 0)
@@ -481,49 +475,43 @@
         first_proj = other[...]
         gated[...] = (first_proj * jax.nn.sigmoid(first_proj) * mine[...]).astype(BF)
 
-    result[...] = dot(gated[...], rows[...], ((1,), (1,))).astype(BF)
+    result = dot(gated[...], weights[...], ((1,), (1,))).astype(BF)
     tokens = own.shape[0]
-    own[...] = result[at_place(c * tokens, tokens), :]
-    core[...] = result[at_place((1 - c) * tokens, tokens), :]
-    far[...] = result[at_place((2 + c) * tokens, tokens), :]
-    far_core[...] = result[at_place((3 - c) * tokens, tokens), :]
-
-
-def down(mine, other, rows):
-    tokens = mine.shape[0] // 4
-    part = shape(tokens, DIM // 2)
+    own[...] = result[:tokens]
+    far[...] = result[tokens:]
+
+
+def down(mine, other, weights):
+    tokens = mine.shape[0] // 2
+    part = shape(tokens, DIM)
     return pl.pallas_call(
         down_kernel,
-        out_shape=(part,) * 4,
+        out_shape=(part, part),
         in_specs=[VMEM] * 3,
-        out_specs=(VMEM,) * 4,
-        scratch_shapes=[pltpu.VMEM((4 * tokens, FF), BF), pltpu.VMEM((4 * tokens, DIM // 2), BF)],
+        out_specs=(VMEM, VMEM),
+        scratch_shapes=[pltpu.VMEM((2 * tokens, FF), BF)],
         compiler_params=params(8),
         cost_estimate=cost(3 * 10**8, 3 << 20),
         name="down",
-    )(mine, other, rows)
-
-
-def finish_kernel(first_out, own, core, far, far_core, out):
-    x, _, c = place()
-    half = DIM // 2
-    here, there = x // 2 * DIM, (1 - x // 2) * DIM
+    )(mine, other, weights)
+
+
+def finish_kernel(first_out, own, far, out):
+    x, _, _ = place()
     out[0] = first_out[...]
-    out[1, :, at_place(here + c * half, half)] = own[...]
-    out[1, :, at_place(here + (1 - c) * half, half)] = core[...]
-    out[1, :, at_place(there + c * half, half)] = far[...]
-    out[1, :, at_place(there + (1 - c) * half, half)] = far_core[...]
-
-
-def finish(first_out, *parts):
+    out[1, :, at_place(x // 2 * DIM, DIM)] = own[...]
+    out[1, :, at_place((1 - x // 2) * DIM, DIM)] = far[...]
+
+
+def finish(first_out, own, far):
     return pl.pallas_call(
         finish_kernel,
         out_shape=shape(2, *first_out.shape),
-        in_specs=[VMEM] * 5,
+        in_specs=[VMEM] * 3,
         out_specs=VMEM,
         compiler_params=params(2),
         name="finish",
-    )(first_out, *parts)
+    )(first_out, own, far)
 
 
 def body(queries, keys, values, rates, weights):
@@ -539,12 +527,12 @@
     pieces, first_out = gather_rows(own, queries, weights)
     matrix, shared = pack(pieces)
     shared_core = other_core(shared)
-    projected = project(matrix, weights, *late_queries)
-    projected, shared_core = barrier((projected, shared_core))
-    projected_core = other_core(projected)
-    rows = renew_third(shared, shared_core, weights)
-    own, core, far, far_core = down(projected, projected_core, rows)
-    return finish(first_out, own, other_core(core), mirror_x(far), mirror_x_core(far_core))
+    query_own, query_core, query_far, query_far_core = late_queries
+    mine, theirs = project(matrix, weights, query_own, query_far, query_core, query_far_core)
+    theirs, shared_core = barrier((theirs, shared_core))
+    other = other_core(theirs)
+    own, far = down(mine, other, renew_third(shared, shared_core, weights))
+    return finish(first_out, own, mirror_x(far))
 
 
 def solution(mesh):

time: 87.7 us -> 86.5 us (0.986)
  starting transfers between devices: 45.4 us -> 43 us
    ppermute x30 -> x28, starting transfers between devices: 45.4 us -> 43 us  [move(): return lax.ppermute(array, 'ctx', perm)]
    ppermute x30 -> x28, waiting for transfers between devices: 24.2 us -> 24.8 us  [move(): return lax.ppermute(array, 'ctx', perm)]
  transfers between devices with their start and end apart: 30 -> 28, of which waited for: 14 -> 12; matrix products, arithmetic and copies ran while one was open for 0% -> 0% of each run, Pallas kernels for 12% -> 13%
where the time goes in v7:
time: 86.5 us; the launch traced here: 86.3 us
  starting transfers between devices  43 us (50%)
  waiting for transfers between devices  24.8 us (29%)
  Pallas kernels  15.5 us (18%)
  local copies, waits for them, and re-layouts  2.82 us (3%)
    ppermute x28, starting transfers between devices, move(): return lax.ppermute(array, 'ctx', perm)  43 us
    ppermute x28, waiting for transfers between devices, move(): return lax.ppermute(array, 'ctx', perm)  24.8 us
    pallas_call x1, Pallas kernels, project(): pl.pallas_call(project_kernel, out_shape=(half, half), in_specs=[VMEM, HB...  3.12 us
    pallas_call x1, Pallas kernels, renew_third(): pl.pallas_call(third_kernel, out_shape=shape(DIM, FF), in_specs=[VMEM, VM...  2.93 us
    unnamed x12, local copies, waits for them, and re-layouts  2.81 us
    pallas_call x1, Pallas kernels, first_block(): pl.pallas_call(first_kernel, out_shape=shape(tokens, 2 * DIM), in_specs=[...  2.75 us
    pallas_call x1, Pallas kernels, prepare(): pl.pallas_call(prepare_kernel, out_shape=(pair, pair, pair, pair, half, h...  2.14 us
    pallas_call x1, Pallas kernels, gradient(): pl.pallas_call(gradient_kernel, out_shape=(kept, sent, sent, kept, kept,...  2.11 us
  transfers between devices with their start and end apart: 28, of which 12 were waited for; matrix products, arithmetic and copies ran while one was open for 0% of the time, Pallas kernels for 13%

profile of v7, /device:TPU:1, one launch (start us, length us, event | category | flops | bytes accessed | tf_op | source)
XLA Modules:
  0.0 86.3 jit_solution(8868056112677804006)
XLA Ops:
  0.0 2.1 %prepare.1 = (bf16[128,512]{1,0:T(8,128)(2,1)}, bf16[128,512]{1,0:T(8,128)(2,1)}, bf16[128,512]{1,0:T(8,128)(2,1)}, bf16[128,512]{1,0:T(8,128)(2,1)}, bf16[64,512]{1,0:T(8,128)(2,1)}, /*index=5*/bf16[64,512]{1,0:T(8,128)(2,1)}) custom-call(bf16[2,64,1024]{2,1,0:T(8,128)(2,1)} %queries.2, bf16[1,64,1024]{2,1,0:T(8,128)(2,1)} %keys.1, ...), custom_call_target="tpu_custom_call" | custom-call | tf_op jit(solution)/shard_map/prepare/pallas_call | solution.py:120
  2.2 3.6 %collective-permute-start.1 = (bf16[128,512]{1,0:T(8,128)(2,1)}, bf16[128,512]{1,0:T(8,128)(2,1)S(1)}, u32[]{:S(2)}, u32[]{:S(2)}) collective-permute-start(bf16[128,512]{1,0:T(8,128)(2,1)} %get-tuple-element.57), channel_id=1, source_target_pairs={{0,32},{1,33},{2,34},{3,35},{4,36},{5,37},{6,38},{7,39},{8,40},{9,... | collective-permute-start | bytes 393224 | tf_op jit(solution)/shard_map/ppermute | solution.py:36
  5.8 0.3 collective-permute-start
  6.1 2.4 %collective-permute-start.2 = (bf16[128,512]{1,0:T(8,128)(2,1)}, bf16[128,512]{1,0:T(8,128)(2,1)S(1)}, u32[]{:S(2)}, u32[]{:S(2)}) collective-permute-start(bf16[128,512]{1,0:T(8,128)(2,1)} %get-tuple-element.61), channel_id=1, source_target_pairs={{0,48},{1,49},{2,50},{3,51},{4,52},{5,53},{6,54},{7,55},{8,56},{9,... | collective-permute-start | bytes 393224 | tf_op jit(solution)/shard_map/ppermute | solution.py:36
  8.5 1.5 %collective-permute-start.3 = (bf16[128,512]{1,0:T(8,128)(2,1)}, bf16[128,512]{1,0:T(8,128)(2,1)S(1)}, u32[]{:S(2)}, u32[]{:S(2)}) collective-permute-start(bf16[128,512]{1,0:T(8,128)(2,1)} %get-tuple-element.55.refs_0_), channel_id=1, source_target_pairs={{0,1},{1,0},{2,3},{3,2},{4,5},{5,4},{6,7},{7,6},{8,9},{9,8},{10,11... | collective-permute-start | bytes 393224 | tf_op jit(solution)/shard_map/ppermute | solution.py:36
  10.0 2.8 %copy-done = bf16[3,2,512,1024]{3,2,1,0:T(8,128)(2,1)S(1)} copy-done((bf16[3,2,512,1024]{3,2,1,0:T(8,128)(2,1)S(1)}, bf16[3,2,512,1024]{3,2,1,0:T(8,128)(2,1)}, u32[]{:S(2)}) %copy-start) | copy-done | bytes 6291480
  12.8 0.3 load.1.refs_8_
  13.1 0.1 collective-permute-done.refs_1_
  13.2 1.3 %collective-permute-start.4 = (bf16[128,512]{1,0:T(8,128)(2,1)S(1)}, bf16[128,512]{1,0:T(8,128)(2,1)S(1)}, u32[]{:S(2)}, u32[]{:S(2)}) collective-permute-start(bf16[128,512]{1,0:T(8,128)(2,1)S(1)} %collective-permute-done.refs_1_), channel_id=1, source_target_pairs={{0,1},{1,0},{2,3},{3,2},{4,5},{5,4},{6,7},{7,6},{8,9},{9,8},{10,11... | collective-permute-start | bytes 393224 | tf_op jit(solution)/shard_map/ppermute | solution.py:36
  14.5 0.0 collective-permute-start.6
  14.5 0.5 collective-permute-start.5
  15.1 1.4 %collective-permute-start.7 = (bf16[64,512]{1,0:T(8,128)(2,1)S(1)}, bf16[64,512]{1,0:T(8,128)(2,1)S(1)}, u32[]{:S(2)}, u32[]{:S(2)}) collective-permute-start(bf16[64,512]{1,0:T(8,128)(2,1)S(1)} %copy-done.5), channel_id=1, source_target_pairs={{0,48},{1,49},{2,50},{3,51},{4,52},{5,53},{6,54},{7,55},{8,56},{9,... | collective-permute-start | bytes 196616 | tf_op jit(solution)/shard_map/ppermute | solution.py:36
  16.5 2.1 %gradient.1 = (f32[64,768]{1,0:T(8,128)S(1)}, bf16[128,768]{1,0:T(8,128)(2,1)S(1)}, bf16[128,768]{1,0:T(8,128)(2,1)S(1)}, f32[64,768]{1,0:T(8,128)S(1)}, f32[64,...) custom-call(bf16[128,512]{1,0:T(8,128)(2,1)S(1)} %copy-done.3, ...), custom_call_target="tpu_custom_call" | custom-call | flops 1342177280 | bytes 6291456 | tf_op jit(solution)/shard_map/gradient/pallas_call | solution.py:249
  18.6 1.4 %collective-permute-done.7.query_far = bf16[64,512]{1,0:T(8,128)(2,1)S(1)} collective-permute-done((bf16[64,512]{1,0:T(8,128)(2,1)S(1)}, bf16[64,512]{1,0:T(8,128)(2,1)S(1)}, u32[]{:S(2)}, u32[]{:S(2)}) %collective-permute-start.7) | collective-permute-done | bytes 65568 | tf_op jit(solution)/shard_map/ppermute | solution.py:36
  20.0 0.9 %collective-permute-start.8 = (bf16[128,768]{1,0:T(8,128)(2,1)S(1)}, bf16[128,768]{1,0:T(8,128)(2,1)S(1)}, u32[]{:S(2)}, u32[]{:S(2)}) collective-permute-start(bf16[128,768]{1,0:T(8,128)(2,1)S(1)} %get-tuple-element.72), channel_id=1, source_target_pairs={{0,2},{1,3},{2,4},{3,5},{4,6},{5,7},{6,8},{7,9},{8,10},{9,11},{10,... | collective-permute-start | bytes 589832 | tf_op jit(solution)/shard_map/ppermute | solution.py:36
  20.9 3.9 %collective-permute-start.9 = (bf16[128,768]{1,0:T(8,128)(2,1)S(1)}, bf16[128,768]{1,0:T(8,128)(2,1)S(1)}, u32[]{:S(2)}, u32[]{:S(2)}) collective-permute-start(bf16[128,768]{1,0:T(8,128)(2,1)S(1)} %get-tuple-element.73), channel_id=1, source_target_pairs={{0,14},{1,15},{2,0},{3,1},{4,2},{5,3},{6,4},{7,5},{8,6},{9,7},{10,... | collective-permute-start | bytes 589832 | tf_op jit(solution)/shard_map/ppermute | solution.py:36
  24.9 3.6 %collective-permute-start.11 = (bf16[32,768]{1,0:T(8,128)(2,1)S(1)}, bf16[32,768]{1,0:T(8,128)(2,1)S(1)}, u32[]{:S(2)}, u32[]{:S(2)}) collective-permute-start(bf16[32,768]{1,0:T(8,128)(2,1)S(1)} %get-tuple-element.77), channel_id=1, source_target_pairs={{0,12},{1,13},{2,14},{3,15},{4,0},{5,1},{6,2},{7,3},{8,4},{9,5},{1... | collective-permute-start | bytes 147464 | tf_op jit(solution)/shard_map/ppermute | solution.py:36
  28.4 2.9 %collective-permute-done.10.far_up = bf16[32,768]{1,0:T(8,128)(2,1)S(1)} collective-permute-done((bf16[32,768]{1,0:T(8,128)(2,1)S(1)}, bf16[32,768]{1,0:T(8,128)(2,1)S(1)}, u32[]{:S(2)}, u32[]{:S(2)}) %collective-permute-start.10) | collective-permute-done | bytes 49184 | tf_op jit(solution)/shard_map/ppermute | solution.py:36
  31.3 0.1 middle.1
  31.4 3.8 %collective-permute-start.12 = (bf16[64,768]{1,0:T(8,128)(2,1)S(1)}, bf16[64,768]{1,0:T(8,128)(2,1)S(1)}, u32[]{:S(2)}, u32[]{:S(2)}) collective-permute-start(bf16[64,768]{1,0:T(8,128)(2,1)S(1)} %get-tuple-element.82), channel_id=1, source_target_pairs={{0,4},{1,5},{2,6},{3,7},{4,8},{5,9},{6,10},{7,11},{8,12},{9,13},{1... | collective-permute-start | bytes 294920 | tf_op jit(solution)/shard_map/ppermute | solution.py:36
  35.2 2.7 %collective-permute-start.14 = (bf16[64,512]{1,0:T(8,128)(2,1)S(1)}, bf16[64,512]{1,0:T(8,128)(2,1)S(1)}, u32[]{:S(2)}, u32[]{:S(2)}) collective-permute-start(bf16[64,512]{1,0:T(8,128)(2,1)S(1)} %copy-done.4), channel_id=1, source_target_pairs={{0,1},{1,0},{2,3},{3,2},{4,5},{5,4},{6,7},{7,6},{8,9},{9,8},{10,11... | collective-permute-start | bytes 196616 | tf_op jit(solution)/shard_map/ppermute | solution.py:36
  37.9 0.9 %collective-permute-done.14.query_core = bf16[64,512]{1,0:T(8,128)(2,1)S(1)} collective-permute-done((bf16[64,512]{1,0:T(8,128)(2,1)S(1)}, bf16[64,512]{1,0:T(8,128)(2,1)S(1)}, u32[]{:S(2)}, u32[]{:S(2)}) %collective-permute-start.14) | collective-permute-done | bytes 65568 | tf_op jit(solution)/shard_map/ppermute | solution.py:36
  38.8 0.4 collective-permute-done.15.query_far_core
  39.2 1.0 %collective-permute-done.13.d = bf16[64,768]{1,0:T(8,128)(2,1)S(1)} collective-permute-done((bf16[64,768]{1,0:T(8,128)(2,1)S(1)}, bf16[64,768]{1,0:T(8,128)(2,1)S(1)}, u32[]{:S(2)}, u32[]{:S(2)}) %collective-permute-start.13) | collective-permute-done | bytes 98336 | tf_op jit(solution)/shard_map/ppermute | solution.py:36
  40.2 0.1 add_up.1
  40.2 0.1 collective-permute-start.16
  40.3 3.5 %collective-permute-done.16 = bf16[64,768]{1,0:T(8,128)(2,1)S(1)} collective-permute-done((bf16[64,768]{1,0:T(8,128)(2,1)S(1)}, bf16[64,768]{1,0:T(8,128)(2,1)S(1)}, u32[]{:S(2)}, u32[]{:S(2)}) %collective-permute-start.16) | collective-permute-done | bytes 98336 | tf_op jit(solution)/shard_map/ppermute | solution.py:36
  43.8 1.8 %collective-permute-start.18 = (bf16[64,1536]{1,0:T(8,128)(2,1)S(1)}, bf16[64,1536]{1,0:T(8,128)(2,1)S(1)}, u32[]{:S(2)}, u32[]{:S(2)}) collective-permute-start(bf16[64,1536]{1,0:T(8,128)(2,1)S(1)} %pad_maximum_fusion.refs_0_), channel_id=1, source_target_pairs={{0,12},{1,13},{2,14},{3,15},{4,0},{5,1},{6,2},{7,3},{8,4},{9,5},{1... | collective-permute-start | bytes 589832 | tf_op jit(solution)/shard_map/ppermute | solution.py:36
  45.6 0.7 collective-permute-start.17
  46.3 1.1 %collective-permute-start.20 = (bf16[64,1536]{1,0:T(8,128)(2,1)S(1)}, bf16[64,1536]{1,0:T(8,128)(2,1)S(1)}, u32[]{:S(2)}, u32[]{:S(2)}) collective-permute-start(bf16[64,1536]{1,0:T(8,128)(2,1)S(1)} %pad_maximum_fusion.refs_0_), channel_id=1, source_target_pairs={{0,14},{1,15},{2,0},{3,1},{4,2},{5,3},{6,4},{7,5},{8,6},{9,7},{10,... | collective-permute-start | bytes 589832 | tf_op jit(solution)/shard_map/ppermute | solution.py:36
  47.3 0.4 collective-permute-start.19
  47.7 2.7 %first_block.1.first_out = bf16[64,1024]{1,0:T(8,128)(2,1)S(1)} custom-call(bf16[2,64,1024]{2,1,0:T(8,128)(2,1)S(1)} %copy-done.2, bf16[3,2,512,1024]{3,2,1,0:T(8,128)(2,1)S(1)} %copy-done.1), custom_call_target="tpu_custom_call" | custom-call | flops 402653184 | bytes 7340032 | tf_op jit(solution)/shard_map/first_block/pallas_call | solution.py:160
  50.5 0.3 collective-permute-done.18.refs_4_
  50.8 3.6 %collective-permute-done.17.refs_3_ = bf16[64,1536]{1,0:T(8,128)(2,1)S(1)} collective-permute-done((bf16[64,1536]{1,0:T(8,128)(2,1)S(1)}, bf16[64,1536]{1,0:T(8,128)(2,1)S(1)}, u32[]{:S(2)}, u32[]{:S(2)}) %collective-permute-start.17) | collective-permute-done | bytes 196640 | tf_op jit(solution)/shard_map/ppermute | solution.py:36
  54.4 2.7 %collective-permute-start.22 = (bf16[64,1536]{1,0:T(8,128)(2,1)S(1)}, bf16[64,1536]{1,0:T(8,128)(2,1)S(1)}, u32[]{:S(2)}, u32[]{:S(2)}) collective-permute-start(bf16[64,1536]{1,0:T(8,128)(2,1)S(1)} %collective-permute-done.18.refs_4_), channel_id=1, source_target_pairs={{0,14},{1,15},{2,0},{3,1},{4,2},{5,3},{6,4},{7,5},{8,6},{9,7},{10,... | collective-permute-start | bytes 589832 | tf_op jit(solution)/shard_map/ppermute | solution.py:36
  57.0 0.1 collective-permute-start.24
  57.2 2.3 %collective-permute-start.23 = (bf16[32,1536]{1,0:T(8,128)(2,1)S(1)}, bf16[32,1536]{1,0:T(8,128)(2,1)S(1)}, u32[]{:S(2)}, u32[]{:S(2)}) collective-permute-start(bf16[32,1536]{1,0:T(8,128)(2,1)S(1)} %slice.6), channel_id=1, source_target_pairs={{0,4},{1,5},{2,6},{3,7},{4,8},{5,9},{6,10},{7,11},{8,12},{9,13},{1... | collective-permute-start | bytes 294920 | tf_op jit(solution)/shard_map/ppermute | solution.py:36
  59.5 3.2 %collective-permute-done.24.refs_8_ = bf16[32,1536]{1,0:T(8,128)(2,1)S(1)} collective-permute-done((bf16[32,1536]{1,0:T(8,128)(2,1)S(1)}, bf16[32,1536]{1,0:T(8,128)(2,1)S(1)}, u32[]{:S(2)}, u32[]{:S(2)}) %collective-permute-start.24) | collective-permute-done | bytes 98336 | tf_op jit(solution)/shard_map/ppermute | solution.py:36
  62.7 4.3 %collective-permute-done.23.refs_7_ = bf16[32,1536]{1,0:T(8,128)(2,1)S(1)} collective-permute-done((bf16[32,1536]{1,0:T(8,128)(2,1)S(1)}, bf16[32,1536]{1,0:T(8,128)(2,1)S(1)}, u32[]{:S(2)}, u32[]{:S(2)}) %collective-permute-start.23) | collective-permute-done | bytes 98336 | tf_op jit(solution)/shard_map/ppermute | solution.py:36
  67.0 0.7 pack.1
  67.7 6.4 %collective-permute-start.25 = (bf16[512,512]{1,0:T(8,128)(2,1)S(1)}, bf16[512,512]{1,0:T(8,128)(2,1)S(1)}, u32[]{:S(2)}, u32[]{:S(2)}) collective-permute-start(bf16[512,512]{1,0:T(8,128)(2,1)S(1)} %get-tuple-element.98.mine), channel_id=1, source_target_pairs={{0,1},{1,0},{2,3},{3,2},{4,5},{5,4},{6,7},{7,6},{8,9},{9,8},{10,11... | collective-permute-start | bytes 1572872 | tf_op jit(solution)/shard_map/ppermute | solution.py:36
  74.1 3.1 %project.1 = (f32[128,1024]{1,0:T(8,128)S(1)}, f32[128,1024]{1,0:T(8,128)S(1)}) custom-call(bf16[512,1024]{1,0:T(8,128)(2,1)S(1)} %get-tuple-element.93.scaled, bf16[3,2,512,1024]{3,2,1,0:T(8,128)(2,1)S(1)} %copy-done.1, bf16[64,512]{1,0:T(8,128)(2,1)S(1)} %copy-done.4, bf16[64,512]{1,0:T(8,128)(2,1)S(1)} %collective-permute-done.7.query_far, ...), custom_call_target="tpu_custom_call" | custom-call | flops 2200000000 | bytes 5242880 | tf_op jit(solution)/shard_map/project/pallas_call | solution.py:417
  77.3 0.3 collective-permute-start.26
  77.6 2.9 %renew_third.1.weights = bf16[512,1024]{1,0:T(8,128)(2,1)S(1)} custom-call(bf16[512,512]{1,0:T(8,128)(2,1)S(1)} %get-tuple-element.98.mine, bf16[512,512]{1,0:T(8,128)(2,1)S(1)} %collective-permute-done.25.other, bf16[3,2,512,1024]{3,2,1,0:T(8,128)(2,1)S(1)} %copy-done.1), custom_call_target="tpu_custom_call" | custom-call | flops 1900000000 | bytes 4194304 | tf_op jit(solution)/shard_map/renew_third/pallas_call | solution.py:449
  80.6 0.6 down.1
  81.2 1.0 %collective-permute-start.27 = (bf16[64,512]{1,0:T(8,128)(2,1)S(1)}, bf16[64,512]{1,0:T(8,128)(2,1)S(1)}, u32[]{:S(2)}, u32[]{:S(2)}) collective-permute-start(bf16[64,512]{1,0:T(8,128)(2,1)S(1)} %get-tuple-element.102), channel_id=1, source_target_pairs={{0,48},{1,49},{2,50},{3,51},{4,52},{5,53},{6,54},{7,55},{8,56},{9,... | collective-permute-start | bytes 196616 | tf_op jit(solution)/shard_map/ppermute | solution.py:36
  82.2 3.4 %collective-permute-done.27.far = bf16[64,512]{1,0:T(8,128)(2,1)S(1)} collective-permute-done((bf16[64,512]{1,0:T(8,128)(2,1)S(1)}, bf16[64,512]{1,0:T(8,128)(2,1)S(1)}, u32[]{:S(2)}, u32[]{:S(2)}) %collective-permute-start.27) | collective-permute-done | bytes 65568 | tf_op jit(solution)/shard_map/ppermute | solution.py:36
  85.6 0.7 finish.1
  (34 shorter events, 0.1 us)
Async XLA Ops:
  2.2 10.9 %collective-permute-start.1 = (bf16[128,512]{1,0:T(8,128)(2,1)}, bf16[128,512]{1,0:T(8,128)(2,1)S(1)}, u32[]{:S(2)}, u32[]{:S(2)}) collective-permute-start(bf16[128,512]{1,0:T(8,128)(2,1)} %get-tuple-element.57), channel_id=1, source_target_pairs={{0,32},{1,33},{2,34},{3,35},{4,36},{5,37},{6,38},{7,39},{8,40},{9,... | collective-permute-start | bytes 393224 | tf_op jit(solution)/shard_map/ppermute | solution.py:36
  5.8 7.4 %collective-permute-start = (bf16[128,512]{1,0:T(8,128)(2,1)}, bf16[128,512]{1,0:T(8,128)(2,1)S(1)}, u32[]{:S(2)}, u32[]{:S(2)}) collective-permute-start(bf16[128,512]{1,0:T(8,128)(2,1)} %get-tuple-element.56), channel_id=1, source_target_pairs={{0,16},{1,17},{2,18},{3,19},{4,20},{5,21},{6,22},{7,23},{8,24},{9,... | collective-permute-start | bytes 393224 | tf_op jit(solution)/shard_map/ppermute | solution.py:36
  6.1 8.4 %collective-permute-start.2 = (bf16[128,512]{1,0:T(8,128)(2,1)}, bf16[128,512]{1,0:T(8,128)(2,1)S(1)}, u32[]{:S(2)}, u32[]{:S(2)}) collective-permute-start(bf16[128,512]{1,0:T(8,128)(2,1)} %get-tuple-element.61), channel_id=1, source_target_pairs={{0,48},{1,49},{2,50},{3,51},{4,52},{5,53},{6,54},{7,55},{8,56},{9,... | collective-permute-start | bytes 393224 | tf_op jit(solution)/shard_map/ppermute | solution.py:36
  8.5 8.0 %collective-permute-start.3 = (bf16[128,512]{1,0:T(8,128)(2,1)}, bf16[128,512]{1,0:T(8,128)(2,1)S(1)}, u32[]{:S(2)}, u32[]{:S(2)}) collective-permute-start(bf16[128,512]{1,0:T(8,128)(2,1)} %get-tuple-element.55.refs_0_), channel_id=1, source_target_pairs={{0,1},{1,0},{2,3},{3,2},{4,5},{5,4},{6,7},{7,6},{8,9},{9,8},{10,11... | collective-permute-start | bytes 393224 | tf_op jit(solution)/shard_map/ppermute | solution.py:36
  10.0 2.8 %copy-start = (bf16[3,2,512,1024]{3,2,1,0:T(8,128)(2,1)S(1)}, bf16[3,2,512,1024]{3,2,1,0:T(8,128)(2,1)}, u32[]{:S(2)}) copy-start(bf16[3,2,512,1024]{3,2,1,0:T(8,128)(2,1)} %weights.3) | copy-start | bytes 18874372
  12.8 2.3 %copy-start.5 = (bf16[64,512]{1,0:T(8,128)(2,1)S(1)}, bf16[64,512]{1,0:T(8,128)(2,1)}, u32[]{:S(2)}) copy-start(bf16[64,512]{1,0:T(8,128)(2,1)} %get-tuple-element.70) | copy-start | bytes 196612
  12.8 3.7 %copy-start.3 = (bf16[128,512]{1,0:T(8,128)(2,1)S(1)}, bf16[128,512]{1,0:T(8,128)(2,1)}, u32[]{:S(2)}) copy-start(bf16[128,512]{1,0:T(8,128)(2,1)} %get-tuple-element.55.refs_0_) | copy-start | bytes 393220
  12.8 22.4 %copy-start.4 = (bf16[64,512]{1,0:T(8,128)(2,1)S(1)}, bf16[64,512]{1,0:T(8,128)(2,1)}, u32[]{:S(2)}) copy-start(bf16[64,512]{1,0:T(8,128)(2,1)} %get-tuple-element.84.query_own) | copy-start | bytes 196612
  12.8 35.0 %copy-start.1 = (bf16[3,2,512,1024]{3,2,1,0:T(8,128)(2,1)S(1)}, bf16[3,2,512,1024]{3,2,1,0:T(8,128)(2,1)}, u32[]{:S(2)}) copy-start(bf16[3,2,512,1024]{3,2,1,0:T(8,128)(2,1)} %weights.3) | copy-start | bytes 18874372
  12.8 34.9 %copy-start.2 = (bf16[2,64,1024]{2,1,0:T(8,128)(2,1)S(1)}, bf16[2,64,1024]{2,1,0:T(8,128)(2,1)}, u32[]{:S(2)}) copy-start(bf16[2,64,1024]{2,1,0:T(8,128)(2,1)} %queries.2) | copy-start | bytes 786436
  13.2 3.3 %collective-permute-start.4 = (bf16[128,512]{1,0:T(8,128)(2,1)S(1)}, bf16[128,512]{1,0:T(8,128)(2,1)S(1)}, u32[]{:S(2)}, u32[]{:S(2)}) collective-permute-start(bf16[128,512]{1,0:T(8,128)(2,1)S(1)} %collective-permute-done.refs_1_), channel_id=1, source_target_pairs={{0,1},{1,0},{2,3},{3,2},{4,5},{5,4},{6,7},{7,6},{8,9},{9,8},{10,11... | collective-permute-start | bytes 393224 | tf_op jit(solution)/shard_map/ppermute | solution.py:36
  14.5 1.9 %collective-permute-start.6 = (bf16[128,512]{1,0:T(8,128)(2,1)S(1)}, bf16[128,512]{1,0:T(8,128)(2,1)S(1)}, u32[]{:S(2)}, u32[]{:S(2)}) collective-permute-start(bf16[128,512]{1,0:T(8,128)(2,1)S(1)} %collective-permute-done.2.refs_3_), channel_id=1, source_target_pairs={{0,1},{1,0},{2,3},{3,2},{4,5},{5,4},{6,7},{7,6},{8,9},{9,8},{10,11... | collective-permute-start | bytes 393224 | tf_op jit(solution)/shard_map/ppermute | solution.py:36
  14.5 1.9 %collective-permute-start.5 = (bf16[128,512]{1,0:T(8,128)(2,1)S(1)}, bf16[128,512]{1,0:T(8,128)(2,1)S(1)}, u32[]{:S(2)}, u32[]{:S(2)}) collective-permute-start(bf16[128,512]{1,0:T(8,128)(2,1)S(1)} %collective-permute-done.1.refs_2_), channel_id=1, source_target_pairs={{0,1},{1,0},{2,3},{3,2},{4,5},{5,4},{6,7},{7,6},{8,9},{9,8},{10,11... | collective-permute-start | bytes 393224 | tf_op jit(solution)/shard_map/ppermute | solution.py:36
  15.1 4.9 %collective-permute-start.7 = (bf16[64,512]{1,0:T(8,128)(2,1)S(1)}, bf16[64,512]{1,0:T(8,128)(2,1)S(1)}, u32[]{:S(2)}, u32[]{:S(2)}) collective-permute-start(bf16[64,512]{1,0:T(8,128)(2,1)S(1)} %copy-done.5), channel_id=1, source_target_pairs={{0,48},{1,49},{2,50},{3,51},{4,52},{5,53},{6,54},{7,55},{8,56},{9,... | collective-permute-start | bytes 196616 | tf_op jit(solution)/shard_map/ppermute | solution.py:36
  20.0 11.3 %collective-permute-start.8 = (bf16[128,768]{1,0:T(8,128)(2,1)S(1)}, bf16[128,768]{1,0:T(8,128)(2,1)S(1)}, u32[]{:S(2)}, u32[]{:S(2)}) collective-permute-start(bf16[128,768]{1,0:T(8,128)(2,1)S(1)} %get-tuple-element.72), channel_id=1, source_target_pairs={{0,2},{1,3},{2,4},{3,5},{4,6},{5,7},{6,8},{7,9},{8,10},{9,11},{10,... | collective-permute-start | bytes 589832 | tf_op jit(solution)/shard_map/ppermute | solution.py:36
  20.9 10.4 %collective-permute-start.9 = (bf16[128,768]{1,0:T(8,128)(2,1)S(1)}, bf16[128,768]{1,0:T(8,128)(2,1)S(1)}, u32[]{:S(2)}, u32[]{:S(2)}) collective-permute-start(bf16[128,768]{1,0:T(8,128)(2,1)S(1)} %get-tuple-element.73), channel_id=1, source_target_pairs={{0,14},{1,15},{2,0},{3,1},{4,2},{5,3},{6,4},{7,5},{8,6},{9,7},{10,... | collective-permute-start | bytes 589832 | tf_op jit(solution)/shard_map/ppermute | solution.py:36
  24.9 6.5 %collective-permute-start.10 = (bf16[32,768]{1,0:T(8,128)(2,1)S(1)}, bf16[32,768]{1,0:T(8,128)(2,1)S(1)}, u32[]{:S(2)}, u32[]{:S(2)}) collective-permute-start(bf16[32,768]{1,0:T(8,128)(2,1)S(1)} %get-tuple-element.76), channel_id=1, source_target_pairs={{0,4},{1,5},{2,6},{3,7},{4,8},{5,9},{6,10},{7,11},{8,12},{9,13},{1... | collective-permute-start | bytes 147464 | tf_op jit(solution)/shard_map/ppermute | solution.py:36
  24.9 6.5 %collective-permute-start.11 = (bf16[32,768]{1,0:T(8,128)(2,1)S(1)}, bf16[32,768]{1,0:T(8,128)(2,1)S(1)}, u32[]{:S(2)}, u32[]{:S(2)}) collective-permute-start(bf16[32,768]{1,0:T(8,128)(2,1)S(1)} %get-tuple-element.77), channel_id=1, source_target_pairs={{0,12},{1,13},{2,14},{3,15},{4,0},{5,1},{6,2},{7,3},{8,4},{9,5},{1... | collective-permute-start | bytes 147464 | tf_op jit(solution)/shard_map/ppermute | solution.py:36
  31.4 7.8 %collective-permute-start.12 = (bf16[64,768]{1,0:T(8,128)(2,1)S(1)}, bf16[64,768]{1,0:T(8,128)(2,1)S(1)}, u32[]{:S(2)}, u32[]{:S(2)}) collective-permute-start(bf16[64,768]{1,0:T(8,128)(2,1)S(1)} %get-tuple-element.82), channel_id=1, source_target_pairs={{0,4},{1,5},{2,6},{3,7},{4,8},{5,9},{6,10},{7,11},{8,12},{9,13},{1... | collective-permute-start | bytes 294920 | tf_op jit(solution)/shard_map/ppermute | solution.py:36
  35.2 5.0 %collective-permute-start.13 = (bf16[64,768]{1,0:T(8,128)(2,1)S(1)}, bf16[64,768]{1,0:T(8,128)(2,1)S(1)}, u32[]{:S(2)}, u32[]{:S(2)}) collective-permute-start(bf16[64,768]{1,0:T(8,128)(2,1)S(1)} %get-tuple-element.83), channel_id=1, source_target_pairs={{0,12},{1,13},{2,14},{3,15},{4,0},{5,1},{6,2},{7,3},{8,4},{9,5},{1... | collective-permute-start | bytes 294920 | tf_op jit(solution)/shard_map/ppermute | solution.py:36
  35.2 3.6 %collective-permute-start.14 = (bf16[64,512]{1,0:T(8,128)(2,1)S(1)}, bf16[64,512]{1,0:T(8,128)(2,1)S(1)}, u32[]{:S(2)}, u32[]{:S(2)}) collective-permute-start(bf16[64,512]{1,0:T(8,128)(2,1)S(1)} %copy-done.4), channel_id=1, source_target_pairs={{0,1},{1,0},{2,3},{3,2},{4,5},{5,4},{6,7},{7,6},{8,9},{9,8},{10,11... | collective-permute-start | bytes 196616 | tf_op jit(solution)/shard_map/ppermute | solution.py:36
  37.9 1.3 %collective-permute-start.15 = (bf16[64,512]{1,0:T(8,128)(2,1)S(1)}, bf16[64,512]{1,0:T(8,128)(2,1)S(1)}, u32[]{:S(2)}, u32[]{:S(2)}) collective-permute-start(bf16[64,512]{1,0:T(8,128)(2,1)S(1)} %collective-permute-done.7.query_far), channel_id=1, source_target_pairs={{0,1},{1,0},{2,3},{3,2},{4,5},{5,4},{6,7},{7,6},{8,9},{9,8},{10,11... | collective-permute-start | bytes 196616 | tf_op jit(solution)/shard_map/ppermute | solution.py:36
  40.2 3.6 %collective-permute-start.16 = (bf16[64,768]{1,0:T(8,128)(2,1)S(1)}, bf16[64,768]{1,0:T(8,128)(2,1)S(1)}, u32[]{:S(2)}, u32[]{:S(2)}) collective-permute-start(bf16[64,768]{1,0:T(8,128)(2,1)S(1)} %add_up.1), channel_id=1, source_target_pairs={{0,16},{1,17},{2,18},{3,19},{4,20},{5,21},{6,22},{7,23},{8,24},{9,... | collective-permute-start | bytes 294920 | tf_op jit(solution)/shard_map/ppermute | solution.py:36
  43.8 7.0 %collective-permute-start.18 = (bf16[64,1536]{1,0:T(8,128)(2,1)S(1)}, bf16[64,1536]{1,0:T(8,128)(2,1)S(1)}, u32[]{:S(2)}, u32[]{:S(2)}) collective-permute-start(bf16[64,1536]{1,0:T(8,128)(2,1)S(1)} %pad_maximum_fusion.refs_0_), channel_id=1, source_target_pairs={{0,12},{1,13},{2,14},{3,15},{4,0},{5,1},{6,2},{7,3},{8,4},{9,5},{1... | collective-permute-start | bytes 589832 | tf_op jit(solution)/shard_map/ppermute | solution.py:36
  45.6 8.8 %collective-permute-start.17 = (bf16[64,1536]{1,0:T(8,128)(2,1)S(1)}, bf16[64,1536]{1,0:T(8,128)(2,1)S(1)}, u32[]{:S(2)}, u32[]{:S(2)}) collective-permute-start(bf16[64,1536]{1,0:T(8,128)(2,1)S(1)} %pad_maximum_fusion.refs_0_), channel_id=1, source_target_pairs={{0,4},{1,5},{2,6},{3,7},{4,8},{5,9},{6,10},{7,11},{8,12},{9,13},{1... | collective-permute-start | bytes 589832 | tf_op jit(solution)/shard_map/ppermute | solution.py:36
  46.3 10.9 %collective-permute-start.20 = (bf16[64,1536]{1,0:T(8,128)(2,1)S(1)}, bf16[64,1536]{1,0:T(8,128)(2,1)S(1)}, u32[]{:S(2)}, u32[]{:S(2)}) collective-permute-start(bf16[64,1536]{1,0:T(8,128)(2,1)S(1)} %pad_maximum_fusion.refs_0_), channel_id=1, source_target_pairs={{0,14},{1,15},{2,0},{3,1},{4,2},{5,3},{6,4},{7,5},{8,6},{9,7},{10,... | collective-permute-start | bytes 589832 | tf_op jit(solution)/shard_map/ppermute | solution.py:36
  47.3 12.2 %collective-permute-start.19 = (bf16[64,1536]{1,0:T(8,128)(2,1)S(1)}, bf16[64,1536]{1,0:T(8,128)(2,1)S(1)}, u32[]{:S(2)}, u32[]{:S(2)}) collective-permute-start(bf16[64,1536]{1,0:T(8,128)(2,1)S(1)} %pad_maximum_fusion.refs_0_), channel_id=1, source_target_pairs={{0,2},{1,3},{2,4},{3,5},{4,6},{5,7},{6,8},{7,9},{8,10},{9,11},{10,... | collective-permute-start | bytes 589832 | tf_op jit(solution)/shard_map/ppermute | solution.py:36
  54.4 12.6 %collective-permute-start.21 = (bf16[64,1536]{1,0:T(8,128)(2,1)S(1)}, bf16[64,1536]{1,0:T(8,128)(2,1)S(1)}, u32[]{:S(2)}, u32[]{:S(2)}) collective-permute-start(bf16[64,1536]{1,0:T(8,128)(2,1)S(1)} %collective-permute-done.17.refs_3_), channel_id=1, source_target_pairs={{0,2},{1,3},{2,4},{3,5},{4,6},{5,7},{6,8},{7,9},{8,10},{9,11},{10,... | collective-permute-start | bytes 589832 | tf_op jit(solution)/shard_map/ppermute | solution.py:36
  54.4 12.6 %collective-permute-start.22 = (bf16[64,1536]{1,0:T(8,128)(2,1)S(1)}, bf16[64,1536]{1,0:T(8,128)(2,1)S(1)}, u32[]{:S(2)}, u32[]{:S(2)}) collective-permute-start(bf16[64,1536]{1,0:T(8,128)(2,1)S(1)} %collective-permute-done.18.refs_4_), channel_id=1, source_target_pairs={{0,14},{1,15},{2,0},{3,1},{4,2},{5,3},{6,4},{7,5},{8,6},{9,7},{10,... | collective-permute-start | bytes 589832 | tf_op jit(solution)/shard_map/ppermute | solution.py:36
  57.0 5.6 %collective-permute-start.24 = (bf16[32,1536]{1,0:T(8,128)(2,1)S(1)}, bf16[32,1536]{1,0:T(8,128)(2,1)S(1)}, u32[]{:S(2)}, u32[]{:S(2)}) collective-permute-start(bf16[32,1536]{1,0:T(8,128)(2,1)S(1)} %slice.7), channel_id=1, source_target_pairs={{0,12},{1,13},{2,14},{3,15},{4,0},{5,1},{6,2},{7,3},{8,4},{9,5},{1... | collective-permute-start | bytes 294920 | tf_op jit(solution)/shard_map/ppermute | solution.py:36
  57.2 9.8 %collective-permute-start.23 = (bf16[32,1536]{1,0:T(8,128)(2,1)S(1)}, bf16[32,1536]{1,0:T(8,128)(2,1)S(1)}, u32[]{:S(2)}, u32[]{:S(2)}) collective-permute-start(bf16[32,1536]{1,0:T(8,128)(2,1)S(1)} %slice.6), channel_id=1, source_target_pairs={{0,4},{1,5},{2,6},{3,7},{4,8},{5,9},{6,10},{7,11},{8,12},{9,13},{1... | collective-permute-start | bytes 294920 | tf_op jit(solution)/shard_map/ppermute | solution.py:36
  67.7 9.6 %collective-permute-start.25 = (bf16[512,512]{1,0:T(8,128)(2,1)S(1)}, bf16[512,512]{1,0:T(8,128)(2,1)S(1)}, u32[]{:S(2)}, u32[]{:S(2)}) collective-permute-start(bf16[512,512]{1,0:T(8,128)(2,1)S(1)} %get-tuple-element.98.mine), channel_id=1, source_target_pairs={{0,1},{1,0},{2,3},{3,2},{4,5},{5,4},{6,7},{7,6},{8,9},{9,8},{10,11... | collective-permute-start | bytes 1572872 | tf_op jit(solution)/shard_map/ppermute | solution.py:36
  77.3 3.3 %collective-permute-start.26 = (f32[128,1024]{1,0:T(8,128)S(1)}, f32[128,1024]{1,0:T(8,128)S(1)}, u32[]{:S(2)}, u32[]{:S(2)}) collective-permute-start(f32[128,1024]{1,0:T(8,128)S(1)} %get-tuple-element.99), channel_id=1, source_target_pairs={{0,1},{1,0},{2,3},{3,2},{4,5},{5,4},{6,7},{7,6},{8,9},{9,8},{10,11... | collective-permute-start | bytes 1572872 | tf_op jit(solution)/shard_map/ppermute | solution.py:36
  81.2 4.4 %collective-permute-start.27 = (bf16[64,512]{1,0:T(8,128)(2,1)S(1)}, bf16[64,512]{1,0:T(8,128)(2,1)S(1)}, u32[]{:S(2)}, u32[]{:S(2)}) collective-permute-start(bf16[64,512]{1,0:T(8,128)(2,1)S(1)} %get-tuple-element.102), channel_id=1, source_target_pairs={{0,48},{1,49},{2,50},{3,51},{4,52},{5,53},{6,54},{7,55},{8,56},{9,... | collective-permute-start | bytes 196616 | tf_op jit(solution)/shard_map/ppermute | solution.py:36

commit v8 on v7

--- a/solution.py
+++ b/solution.py
@@ -44,6 +44,10 @@
     return move(array, lambda x, z, c: (x, z + distance, c))
 
 
+def opposite_z(array):
+    return move(array, lambda x, z, c: (x, z + 2 - 4 * c, c))
+
+
 def pair_x(array):
     return move(array, lambda x, z, c: (x ^ 1, z, c))
 
@@ -77,40 +81,45 @@
 
 
 def prepare_kernel(queries, keys, values, rates, *refs):
-    own, far1, far2, far3, query_own, query_far, q, k, v, r, sem = refs
-    copies = []
-    for i, (source, target) in enumerate(
-        ((rates, r), (values.at[0], v), (keys.at[0], k), (queries.at[1], q))
-    ):
-        copy = pltpu.make_async_copy(source, target, sem.at[i])
-        copy.start()
-        copies.append(copy)
+    targets, outs, (q, k, v, r, scaled, in_sem, out_sem) = refs[:4], refs[4:6], refs[6:]
     x, _, _ = place()
-    tokens = k.shape[0]
+    tokens = v.shape[0]
+    loads = [
+        pltpu.make_async_copy(source, target, in_sem.at[i])
+        for i, (source, target) in enumerate(
+            ((values.at[0], v), (rates, r), (keys.at[0], k), (queries.at[1], q))
+        )
+    ]
+    for load in loads:
+        load.start()
     diagonal = lax.broadcasted_iota(jnp.int32, (tokens, tokens), 0) == lax.broadcasted_iota(
         jnp.int32, (tokens, tokens), 1
     )
+    heads = [lax.rem(x + distance, X) // 2 for distance in range(4)]
+    copies = []
+
+    def send(source, target):
+        copy = pltpu.make_async_copy(source, target, out_sem.at[len(copies)])
+        copy.start()
+        copies.append(copy)
+
+    loads[0].wait()
+    loads[1].wait()
+    for head in range(2):
+        cols = slice(head * DIM, (head + 1) * DIM)
+        row = r[0, head : head + 1, :]
+        rate = jnp.sum(jnp.where(diagonal, row, 0.0), axis=1, keepdims=True)
+        scaled[head] = (v[:, cols].astype(F32) * rate).astype(BF)
+    for head, target in zip(heads, targets):
+        send(scaled.at[head], target.at[pl.ds(tokens, tokens)])
+    loads[2].wait()
+    for head, target in zip(heads, targets):
+        send(k.at[:, at_place(head * DIM, DIM)], target.at[pl.ds(0, tokens)])
+    loads[3].wait()
+    for head, target in zip((heads[0], 1 - heads[0]), outs):
+        send(q.at[:, at_place(head * DIM, DIM)], target)
     for copy in copies:
         copy.wait()
-    for head in range(2):
-        row = r[0, head : head + 1, :]
-        rate = jnp.sum(jnp.where(diagonal, row, 0.0), axis=1, keepdims=True)
-        cols = slice(head * DIM, (head + 1) * DIM)
-        scaled = (v[:, cols].astype(F32) * rate).astype(BF)
-        for distance, ref in enumerate((own, far1, far2, far3)):
-
-            @pl.when(lax.rem(x + distance, X) // 2 == head)
-            def _():
-                ref[:tokens, :] = k[:, cols]
-                ref[tokens:, :] = scaled
-
-        @pl.when(x // 2 == head)
-        def _():
-            query_own[...] = q[:, cols]
-
-        @pl.when(x // 2 != head)
-        def _():
-            query_far[...] = q[:, cols]
 
 
 def prepare(queries, keys, values, rates):
@@ -121,13 +130,15 @@
         prepare_kernel,
         out_shape=(pair, pair, pair, pair, half, half),
         in_specs=[HBM] * 4,
-        out_specs=(VMEM,) * 6,
+        out_specs=(ANY,) * 6,
         scratch_shapes=[
             wide,
             wide,
             wide,
             pltpu.VMEM(rates.shape, F32),
+            pltpu.VMEM((2, tokens, DIM), BF),
             pltpu.SemaphoreType.DMA((4,)),
+            pltpu.SemaphoreType.DMA((10,)),
         ],
         name="prepare",
     )(queries, keys, values, rates)
@@ -314,12 +325,7 @@
     return add_up(own, got_up, got_down, up, down), (query_own, query_core, query_far, query_far_core)
 
 
-ORIGINS = ((0, 0, ROWS), (-1, 0, ROWS), (1, 0, ROWS), (-2, 0, ROWS), (2, 0, ROWS)) + (
-    (-3, 0, ROWS),
-    (3, 0, ROWS),
-    (-4, 0, ROWS // 2),
-    (4, ROWS // 2, ROWS // 2),
-)
+ORIGINS = (0, -1, 1, -2, 2, -3, 3, 4)
 
 
 def gather_rows(own, queries, weights):
@@ -329,18 +335,18 @@
     up2, down2 = along_z(own, 2), along_z(own, -2)
     up2, down2, first_out = barrier((up2, down2, first_block(queries, weights)))
     up3, down3 = along_z(up2, 1), along_z(down2, -1)
-    up4, down4 = along_z(up2[: ROWS // 2], 2), along_z(down2[ROWS // 2 :], -2)
-    return [own, up1, down1, up2, down2, up3, down3, up4, down4], first_out
+    _, _, c = place()
+    far = opposite_z(jnp.where(c == 0, up2, down2))
+    return [own, up1, down1, up2, down2, up3, down3, far], first_out
 
 
 def pack_kernel(*refs):
-    pieces = refs[:9]
-    matrix, shared, sem = refs[9:]
+    pieces = refs[:8]
+    matrix, shared, sem = refs[8:]
     x, z, _ = place()
     copies = []
     for i, piece in enumerate(pieces):
-        step, first, count = ORIGINS[i]
-        rows = at_place(lax.rem(z + step + Z, Z) * ROWS + first, count)
+        rows = at_place(lax.rem(z + ORIGINS[i] + Z, Z) * ROWS, ROWS)
         for j in range(4):
             side = lax.rem(x + j // 2, 2)
             target, size, offset = ((matrix, HALF, 0), (shared, QUARTER, HALF))[j % 2]
@@ -359,9 +365,9 @@
     return pl.pallas_call(
         pack_kernel,
         out_shape=(shape(DIM, FF), shape(DIM, HALF)),
-        in_specs=[ANY] * 9,
+        in_specs=[ANY] * 8,
         out_specs=(VMEM, VMEM),
-        scratch_shapes=[pltpu.SemaphoreType.DMA((9, 4))],
+        scratch_shapes=[pltpu.SemaphoreType.DMA((8, 4))],
         compiler_params=params(4),
         cost_estimate=cost(0, 3 << 20),
         name="pack",
@@ -377,8 +383,11 @@
     )
 
 
-def gram_of(scaled):
-    gram = dot(scaled, scaled, ((1,), (1,))).astype(BF)
+def gram_of(*parts):
+    gram = dot(parts[0], parts[0], ((1,), (1,)))
+    for part in parts[1:]:
+        gram += dot(part, part, ((1,), (1,)))
+    gram = gram.astype(BF)
     gram_float = gram.astype(F32)
     level = jnp.sqrt(jnp.sum(gram_float * gram_float, keepdims=True)) + norm_eps
     half = 0.5 / level
@@ -430,19 +439,19 @@
     )(scaled, weights, *queries)
 
 
-def third_kernel(mine, other, weights, out, scaled, w, sem):
+def third_kernel(mine, other, weights, out, w, sem):
     x, _, c = place()
     load = pltpu.make_async_copy(weights.at[2, x // 2], w, sem)
     load.start()
-    for side in range(2):
-        cols = slice(side * QUARTER, (side + 1) * QUARTER)
-        scaled[:, at_place(side * HALF + c * QUARTER, QUARTER)] = mine[:, cols]
-        scaled[:, at_place(side * HALF + (1 - c) * QUARTER, QUARTER)] = other[:, cols]
-    gram, first_poly, half, factor = gram_of(scaled[...])
+    gram, first_poly, half, factor = gram_of(mine[...], other[...])
     combined = combine(gram, first_poly, half)
-    update = dot(combined, scaled[...], ((1,), (0,))) * factor
     load.wait()
-    out[...] = (w[...].astype(F32) - update).astype(BF)
+    for core, part in ((c, mine), (1 - c, other)):
+        update = dot(combined, part[...], ((1,), (0,))) * factor
+        for side in range(2):
+            cols = at_place(side * HALF + core * QUARTER, QUARTER)
+            change = update[:, side * QUARTER : (side + 1) * QUARTER]
+            out[:, cols] = (w[:, cols].astype(F32) - change).astype(BF)
 
 
 def renew_third(mine, other, weights):
@@ -452,7 +461,6 @@
         in_specs=[VMEM, VMEM, HBM],
         out_specs=VMEM,
         scratch_shapes=[
-            pltpu.VMEM((DIM, FF), BF),
             pltpu.VMEM((DIM, FF), BF),
             pltpu.SemaphoreType.DMA,
         ],

time: 86.5 us -> 84.5 us (0.977)
  waiting for transfers between devices: 24.8 us -> 18.5 us
  local copies, waits for them, and re-layouts: 2.82 us -> 5.59 us
  starting transfers between devices: 43 us -> 44.7 us
    ppermute x28 -> x27, waiting for transfers between devices: 24.8 us -> 18.5 us  [move(): return lax.ppermute(array, 'ctx', perm)]
    unnamed x12 -> x14, local copies, waits for them, and re-layouts: 2.81 us -> 5.59 us
    ppermute x28 -> x27, starting transfers between devices: 43 us -> 44.7 us  [move(): return lax.ppermute(array, 'ctx', perm)]
  transfers between devices with their start and end apart: 28 -> 27, of which waited for: 12 -> 10; matrix products, arithmetic and copies ran while one was open for 0% -> 0% of each run, Pallas kernels for 13% -> 13%
where the time goes in v8:
time: 84.5 us; the launch traced here: 84.2 us
  starting transfers between devices  44.7 us (53%)
  waiting for transfers between devices  18.5 us (22%)
  Pallas kernels  15.1 us (18%)
  local copies, waits for them, and re-layouts  5.59 us (7%)
    ppermute x27, starting transfers between devices, move(): return lax.ppermute(array, 'ctx', perm)  44.7 us
    ppermute x27, waiting for transfers between devices, move(): return lax.ppermute(array, 'ctx', perm)  18.5 us
    unnamed x14, local copies, waits for them, and re-layouts  5.59 us
    pallas_call x1, Pallas kernels, project(): pl.pallas_call(project_kernel, out_shape=(half, half), in_specs=[VMEM, HB...  3.12 us
    pallas_call x1, Pallas kernels, renew_third(): pl.pallas_call(third_kernel, out_shape=shape(DIM, FF), in_specs=[VMEM, VM...  2.86 us
    pallas_call x1, Pallas kernels, first_block(): pl.pallas_call(first_kernel, out_shape=shape(tokens, 2 * DIM), in_specs=[...  2.73 us
    pallas_call x1, Pallas kernels, gradient(): pl.pallas_call(gradient_kernel, out_shape=(kept, sent, sent, kept, kept,...  2.12 us
    pallas_call x1, Pallas kernels, prepare(): pl.pallas_call(prepare_kernel, out_shape=(pair, pair, pair, pair, half, h...  1.93 us
  transfers between devices with their start and end apart: 27, of which 10 were waited for; matrix products, arithmetic and copies ran while one was open for 0% of the time, Pallas kernels for 13%

profile of v8, /device:TPU:1, one launch (start us, length us, event | category | flops | bytes accessed | tf_op | source)
XLA Modules:
  0.0 84.2 jit_solution(14867238762651624299)
XLA Ops:
  0.0 1.9 %prepare.1 = (bf16[128,512]{1,0:T(8,128)(2,1)}, bf16[128,512]{1,0:T(8,128)(2,1)}, bf16[128,512]{1,0:T(8,128)(2,1)}, bf16[128,512]{1,0:T(8,128)(2,1)}, bf16[64,512]{1,0:T(8,128)(2,1)}, /*index=5*/bf16[64,512]{1,0:T(8,128)(2,1)}) custom-call(bf16[2,64,1024]{2,1,0:T(8,128)(2,1)} %queries.2, bf16[1,64,1024]{2,1,0:T(8,128)(2,1)} %keys.1, ...), custom_call_target="tpu_custom_call" | custom-call | tf_op jit(solution)/shard_map/prepare/pallas_call | solution.py:129
  1.9 3.7 %collective-permute-start.1 = (bf16[128,512]{1,0:T(8,128)(2,1)}, bf16[128,512]{1,0:T(8,128)(2,1)S(1)}, u32[]{:S(2)}, u32[]{:S(2)}) collective-permute-start(bf16[128,512]{1,0:T(8,128)(2,1)} %get-tuple-element.57), channel_id=1, source_target_pairs={{0,32},{1,33},{2,34},{3,35},{4,36},{5,37},{6,38},{7,39},{8,40},{9,... | collective-permute-start | bytes 393224 | tf_op jit(solution)/shard_map/ppermute | solution.py:36
  5.6 0.3 collective-permute-start
  5.9 2.4 %collective-permute-start.2 = (bf16[128,512]{1,0:T(8,128)(2,1)}, bf16[128,512]{1,0:T(8,128)(2,1)S(1)}, u32[]{:S(2)}, u32[]{:S(2)}) collective-permute-start(bf16[128,512]{1,0:T(8,128)(2,1)} %get-tuple-element.61), channel_id=1, source_target_pairs={{0,48},{1,49},{2,50},{3,51},{4,52},{5,53},{6,54},{7,55},{8,56},{9,... | collective-permute-start | bytes 393224 | tf_op jit(solution)/shard_map/ppermute | solution.py:36
  8.3 1.5 %collective-permute-start.3 = (bf16[128,512]{1,0:T(8,128)(2,1)}, bf16[128,512]{1,0:T(8,128)(2,1)S(1)}, u32[]{:S(2)}, u32[]{:S(2)}) collective-permute-start(bf16[128,512]{1,0:T(8,128)(2,1)} %get-tuple-element.55.refs_0_), channel_id=1, source_target_pairs={{0,1},{1,0},{2,3},{3,2},{4,5},{5,4},{6,7},{7,6},{8,9},{9,8},{10,11... | collective-permute-start | bytes 393224 | tf_op jit(solution)/shard_map/ppermute | solution.py:36
  9.8 2.8 %copy-done = bf16[3,2,512,1024]{3,2,1,0:T(8,128)(2,1)S(1)} copy-done((bf16[3,2,512,1024]{3,2,1,0:T(8,128)(2,1)S(1)}, bf16[3,2,512,1024]{3,2,1,0:T(8,128)(2,1)}, u32[]{:S(2)}) %copy-start) | copy-done | bytes 6291480
  12.6 0.3 load.1.refs_8_
  12.9 0.1 collective-permute-start.5
  13.0 0.0 collective-permute-done.refs_1_
  13.0 1.3 %collective-permute-start.4 = (bf16[128,512]{1,0:T(8,128)(2,1)S(1)}, bf16[128,512]{1,0:T(8,128)(2,1)S(1)}, u32[]{:S(2)}, u32[]{:S(2)}) collective-permute-start(bf16[128,512]{1,0:T(8,128)(2,1)S(1)} %collective-permute-done.refs_1_), channel_id=1, source_target_pairs={{0,1},{1,0},{2,3},{3,2},{4,5},{5,4},{6,7},{7,6},{8,9},{9,8},{10,11... | collective-permute-start | bytes 393224 | tf_op jit(solution)/shard_map/ppermute | solution.py:36
  14.3 0.0 collective-permute-start.6
  14.3 1.9 %collective-permute-start.7 = (bf16[64,512]{1,0:T(8,128)(2,1)S(1)}, bf16[64,512]{1,0:T(8,128)(2,1)S(1)}, u32[]{:S(2)}, u32[]{:S(2)}) collective-permute-start(bf16[64,512]{1,0:T(8,128)(2,1)S(1)} %copy-done.6), channel_id=1, source_target_pairs={{0,48},{1,49},{2,50},{3,51},{4,52},{5,53},{6,54},{7,55},{8,56},{9,... | collective-permute-start | bytes 196616 | tf_op jit(solution)/shard_map/ppermute | solution.py:36
  16.3 0.0 collective-permute-done.6.refs_7_
  16.3 2.1 %gradient.1 = (f32[64,768]{1,0:T(8,128)S(1)}, bf16[128,768]{1,0:T(8,128)(2,1)S(1)}, bf16[128,768]{1,0:T(8,128)(2,1)S(1)}, f32[64,768]{1,0:T(8,128)S(1)}, f32[64,...) custom-call(bf16[128,512]{1,0:T(8,128)(2,1)S(1)} %copy-done.4, ...), custom_call_target="tpu_custom_call" | custom-call | flops 1342177280 | bytes 6291456 | tf_op jit(solution)/shard_map/gradient/pallas_call | solution.py:260
  18.4 0.3 collective-permute-done.7.query_far
  18.8 1.4 %collective-permute-start.8 = (bf16[128,768]{1,0:T(8,128)(2,1)S(1)}, bf16[128,768]{1,0:T(8,128)(2,1)S(1)}, u32[]{:S(2)}, u32[]{:S(2)}) collective-permute-start(bf16[128,768]{1,0:T(8,128)(2,1)S(1)} %get-tuple-element.72), channel_id=1, source_target_pairs={{0,2},{1,3},{2,4},{3,5},{4,6},{5,7},{6,8},{7,9},{8,10},{9,11},{10,... | collective-permute-start | bytes 589832 | tf_op jit(solution)/shard_map/ppermute | solution.py:36
  20.1 4.0 %collective-permute-start.9 = (bf16[128,768]{1,0:T(8,128)(2,1)S(1)}, bf16[128,768]{1,0:T(8,128)(2,1)S(1)}, u32[]{:S(2)}, u32[]{:S(2)}) collective-permute-start(bf16[128,768]{1,0:T(8,128)(2,1)S(1)} %get-tuple-element.73), channel_id=1, source_target_pairs={{0,14},{1,15},{2,0},{3,1},{4,2},{5,3},{6,4},{7,5},{8,6},{9,7},{10,... | collective-permute-start | bytes 589832 | tf_op jit(solution)/shard_map/ppermute | solution.py:36
  24.2 3.6 %collective-permute-start.11 = (bf16[32,768]{1,0:T(8,128)(2,1)S(1)}, bf16[32,768]{1,0:T(8,128)(2,1)S(1)}, u32[]{:S(2)}, u32[]{:S(2)}) collective-permute-start(bf16[32,768]{1,0:T(8,128)(2,1)S(1)} %get-tuple-element.77), channel_id=1, source_target_pairs={{0,12},{1,13},{2,14},{3,15},{4,0},{5,1},{6,2},{7,3},{8,4},{9,5},{1... | collective-permute-start | bytes 147464 | tf_op jit(solution)/shard_map/ppermute | solution.py:36
  27.8 2.4 %collective-permute-done.10.far_up = bf16[32,768]{1,0:T(8,128)(2,1)S(1)} collective-permute-done((bf16[32,768]{1,0:T(8,128)(2,1)S(1)}, bf16[32,768]{1,0:T(8,128)(2,1)S(1)}, u32[]{:S(2)}, u32[]{:S(2)}) %collective-permute-start.10) | collective-permute-done | bytes 49184 | tf_op jit(solution)/shard_map/ppermute | solution.py:36
  30.2 0.4 collective-permute-done.11.far_down
  30.7 3.8 %collective-permute-start.12 = (bf16[64,768]{1,0:T(8,128)(2,1)S(1)}, bf16[64,768]{1,0:T(8,128)(2,1)S(1)}, u32[]{:S(2)}, u32[]{:S(2)}) collective-permute-start(bf16[64,768]{1,0:T(8,128)(2,1)S(1)} %get-tuple-element.82), channel_id=1, source_target_pairs={{0,4},{1,5},{2,6},{3,7},{4,8},{5,9},{6,10},{7,11},{8,12},{9,13},{1... | collective-permute-start | bytes 294920 | tf_op jit(solution)/shard_map/ppermute | solution.py:36
  34.4 3.0 %collective-permute-start.14 = (bf16[64,512]{1,0:T(8,128)(2,1)S(1)}, bf16[64,512]{1,0:T(8,128)(2,1)S(1)}, u32[]{:S(2)}, u32[]{:S(2)}) collective-permute-start(bf16[64,512]{1,0:T(8,128)(2,1)S(1)} %copy-done.5), channel_id=1, source_target_pairs={{0,1},{1,0},{2,3},{3,2},{4,5},{5,4},{6,7},{7,6},{8,9},{9,8},{10,11... | collective-permute-start | bytes 196616 | tf_op jit(solution)/shard_map/ppermute | solution.py:36
  37.4 0.0 collective-permute-start.15
  37.4 0.9 %collective-permute-done.14.query_core = bf16[64,512]{1,0:T(8,128)(2,1)S(1)} collective-permute-done((bf16[64,512]{1,0:T(8,128)(2,1)S(1)}, bf16[64,512]{1,0:T(8,128)(2,1)S(1)}, u32[]{:S(2)}, u32[]{:S(2)}) %collective-permute-start.14) | collective-permute-done | bytes 65568 | tf_op jit(solution)/shard_map/ppermute | solution.py:36
  38.3 0.4 collective-permute-done.15.query_far_core
  38.7 0.7 collective-permute-done.13.d
  39.4 0.1 add_up.1
  39.4 0.1 collective-permute-start.16
  39.5 3.5 %collective-permute-done.16 = bf16[64,768]{1,0:T(8,128)(2,1)S(1)} collective-permute-done((bf16[64,768]{1,0:T(8,128)(2,1)S(1)}, bf16[64,768]{1,0:T(8,128)(2,1)S(1)}, u32[]{:S(2)}, u32[]{:S(2)}) %collective-permute-start.16) | collective-permute-done | bytes 98336 | tf_op jit(solution)/shard_map/ppermute | solution.py:36
  43.0 1.7 %collective-permute-start.17 = (bf16[64,1536]{1,0:T(8,128)(2,1)S(1)}, bf16[64,1536]{1,0:T(8,128)(2,1)S(1)}, u32[]{:S(2)}, u32[]{:S(2)}) collective-permute-start(bf16[64,1536]{1,0:T(8,128)(2,1)S(1)} %pad_maximum_fusion.refs_0_), channel_id=1, source_target_pairs={{0,4},{1,5},{2,6},{3,7},{4,8},{5,9},{6,10},{7,11},{8,12},{9,13},{1... | collective-permute-start | bytes 589832 | tf_op jit(solution)/shard_map/ppermute | solution.py:36
  44.7 1.9 %collective-permute-start.18 = (bf16[64,1536]{1,0:T(8,128)(2,1)S(1)}, bf16[64,1536]{1,0:T(8,128)(2,1)S(1)}, u32[]{:S(2)}, u32[]{:S(2)}) collective-permute-start(bf16[64,1536]{1,0:T(8,128)(2,1)S(1)} %pad_maximum_fusion.refs_0_), channel_id=1, source_target_pairs={{0,12},{1,13},{2,14},{3,15},{4,0},{5,1},{6,2},{7,3},{8,4},{9,5},{1... | collective-permute-start | bytes 589832 | tf_op jit(solution)/shard_map/ppermute | solution.py:36
  46.6 2.7 %collective-permute-start.20 = (bf16[64,1536]{1,0:T(8,128)(2,1)S(1)}, bf16[64,1536]{1,0:T(8,128)(2,1)S(1)}, u32[]{:S(2)}, u32[]{:S(2)}) collective-permute-start(bf16[64,1536]{1,0:T(8,128)(2,1)S(1)} %pad_maximum_fusion.refs_0_), channel_id=1, source_target_pairs={{0,14},{1,15},{2,0},{3,1},{4,2},{5,3},{6,4},{7,5},{8,6},{9,7},{10,... | collective-permute-start | bytes 589832 | tf_op jit(solution)/shard_map/ppermute | solution.py:36
  49.3 2.8 %copy-done.1 = bf16[3,2,512,1024]{3,2,1,0:T(8,128)(2,1)S(1)} copy-done((bf16[3,2,512,1024]{3,2,1,0:T(8,128)(2,1)S(1)}, bf16[3,2,512,1024]{3,2,1,0:T(8,128)(2,1)}, u32[]{:S(2)}) %copy-start.1) | copy-done | bytes 6291480
  52.1 2.7 %first_block.1.first_out = bf16[64,1024]{1,0:T(8,128)(2,1)S(1)} custom-call(bf16[2,64,1024]{2,1,0:T(8,128)(2,1)S(1)} %copy-done.3, bf16[3,2,512,1024]{3,2,1,0:T(8,128)(2,1)S(1)} %copy-done.1), custom_call_target="tpu_custom_call" | custom-call | flops 402653184 | bytes 7340032 | tf_op jit(solution)/shard_map/first_block/pallas_call | solution.py:171
  54.9 0.1 collective-permute-start.23
  55.0 1.2 %collective-permute-start.21 = (bf16[64,1536]{1,0:T(8,128)(2,1)S(1)}, bf16[64,1536]{1,0:T(8,128)(2,1)S(1)}, u32[]{:S(2)}, u32[]{:S(2)}) collective-permute-start(bf16[64,1536]{1,0:T(8,128)(2,1)S(1)} %collective-permute-done.17.refs_3_), channel_id=1, source_target_pairs={{0,2},{1,3},{2,4},{3,5},{4,6},{5,7},{6,8},{7,9},{8,10},{9,11},{10,... | collective-permute-start | bytes 589832 | tf_op jit(solution)/shard_map/ppermute | solution.py:36
  56.2 1.6 %collective-permute-start.22 = (bf16[64,1536]{1,0:T(8,128)(2,1)S(1)}, bf16[64,1536]{1,0:T(8,128)(2,1)S(1)}, u32[]{:S(2)}, u32[]{:S(2)}) collective-permute-start(bf16[64,1536]{1,0:T(8,128)(2,1)S(1)} %collective-permute-done.18.refs_4_), channel_id=1, source_target_pairs={{0,14},{1,15},{2,0},{3,1},{4,2},{5,3},{6,4},{7,5},{8,6},{9,7},{10,... | collective-permute-start | bytes 589832 | tf_op jit(solution)/shard_map/ppermute | solution.py:36
  57.8 6.3 %collective-permute-done.23.refs_7_ = bf16[64,1536]{1,0:T(8,128)(2,1)S(1)} collective-permute-done((bf16[64,1536]{1,0:T(8,128)(2,1)S(1)}, bf16[64,1536]{1,0:T(8,128)(2,1)S(1)}, u32[]{:S(2)}, u32[]{:S(2)}) %collective-permute-start.23) | collective-permute-done | bytes 196640 | tf_op jit(solution)/shard_map/ppermute | solution.py:36
  64.1 1.7 %collective-permute-done.22.refs_6_ = bf16[64,1536]{1,0:T(8,128)(2,1)S(1)} collective-permute-done((bf16[64,1536]{1,0:T(8,128)(2,1)S(1)}, bf16[64,1536]{1,0:T(8,128)(2,1)S(1)}, u32[]{:S(2)}, u32[]{:S(2)}) %collective-permute-start.22) | collective-permute-done | bytes 196640 | tf_op jit(solution)/shard_map/ppermute | solution.py:36
  65.8 0.6 pack.1
  66.5 5.6 %collective-permute-start.24 = (bf16[512,512]{1,0:T(8,128)(2,1)S(1)}, bf16[512,512]{1,0:T(8,128)(2,1)S(1)}, u32[]{:S(2)}, u32[]{:S(2)}) collective-permute-start(bf16[512,512]{1,0:T(8,128)(2,1)S(1)} %get-tuple-element.98.mine), channel_id=1, source_target_pairs={{0,1},{1,0},{2,3},{3,2},{4,5},{5,4},{6,7},{7,6},{8,9},{9,8},{10,11... | collective-permute-start | bytes 1572872 | tf_op jit(solution)/shard_map/ppermute | solution.py:36
  72.0 3.1 %project.1 = (f32[128,1024]{1,0:T(8,128)S(1)}, f32[128,1024]{1,0:T(8,128)S(1)}) custom-call(bf16[512,1024]{1,0:T(8,128)(2,1)S(1)} %get-tuple-element.93.scaled, bf16[3,2,512,1024]{3,2,1,0:T(8,128)(2,1)S(1)} %copy-done.2, bf16[64,512]{1,0:T(8,128)(2,1)S(1)} %copy-done.5, bf16[64,512]{1,0:T(8,128)(2,1)S(1)} %collective-permute-done.7.query_far, ...), custom_call_target="tpu_custom_call" | custom-call | flops 2200000000 | bytes 5242880 | tf_op jit(solution)/shard_map/project/pallas_call | solution.py:426
  75.2 0.3 collective-permute-start.25
  75.5 2.9 %renew_third.1.weights = bf16[512,1024]{1,0:T(8,128)(2,1)S(1)} custom-call(bf16[512,512]{1,0:T(8,128)(2,1)S(1)} %get-tuple-element.98.mine, bf16[512,512]{1,0:T(8,128)(2,1)S(1)} %collective-permute-done.24.other, bf16[3,2,512,1024]{3,2,1,0:T(8,128)(2,1)S(1)} %copy-done.2), custom_call_target="tpu_custom_call" | custom-call | flops 1900000000 | bytes 4194304 | tf_op jit(solution)/shard_map/renew_third/pallas_call | solution.py:458
  78.4 0.6 down.1
  79.0 2.6 %collective-permute-start.26 = (bf16[64,512]{1,0:T(8,128)(2,1)S(1)}, bf16[64,512]{1,0:T(8,128)(2,1)S(1)}, u32[]{:S(2)}, u32[]{:S(2)}) collective-permute-start(bf16[64,512]{1,0:T(8,128)(2,1)S(1)} %get-tuple-element.102), channel_id=1, source_target_pairs={{0,48},{1,49},{2,50},{3,51},{4,52},{5,53},{6,54},{7,55},{8,56},{9,... | collective-permute-start | bytes 196616 | tf_op jit(solution)/shard_map/ppermute | solution.py:36
  81.6 1.8 %collective-permute-done.26.far = bf16[64,512]{1,0:T(8,128)(2,1)S(1)} collective-permute-done((bf16[64,512]{1,0:T(8,128)(2,1)S(1)}, bf16[64,512]{1,0:T(8,128)(2,1)S(1)}, u32[]{:S(2)}, u32[]{:S(2)}) %collective-permute-start.26) | collective-permute-done | bytes 65568 | tf_op jit(solution)/shard_map/ppermute | solution.py:36
  83.4 0.7 finish.1
  (33 shorter events, 0.2 us)
Async XLA Ops:
  1.9 10.9 %collective-permute-start.1 = (bf16[128,512]{1,0:T(8,128)(2,1)}, bf16[128,512]{1,0:T(8,128)(2,1)S(1)}, u32[]{:S(2)}, u32[]{:S(2)}) collective-permute-start(bf16[128,512]{1,0:T(8,128)(2,1)} %get-tuple-element.57), channel_id=1, source_target_pairs={{0,32},{1,33},{2,34},{3,35},{4,36},{5,37},{6,38},{7,39},{8,40},{9,... | collective-permute-start | bytes 393224 | tf_op jit(solution)/shard_map/ppermute | solution.py:36
  5.6 7.4 %collective-permute-start = (bf16[128,512]{1,0:T(8,128)(2,1)}, bf16[128,512]{1,0:T(8,128)(2,1)S(1)}, u32[]{:S(2)}, u32[]{:S(2)}) collective-permute-start(bf16[128,512]{1,0:T(8,128)(2,1)} %get-tuple-element.56), channel_id=1, source_target_pairs={{0,16},{1,17},{2,18},{3,19},{4,20},{5,21},{6,22},{7,23},{8,24},{9,... | collective-permute-start | bytes 393224 | tf_op jit(solution)/shard_map/ppermute | solution.py:36
  5.9 8.4 %collective-permute-start.2 = (bf16[128,512]{1,0:T(8,128)(2,1)}, bf16[128,512]{1,0:T(8,128)(2,1)S(1)}, u32[]{:S(2)}, u32[]{:S(2)}) collective-permute-start(bf16[128,512]{1,0:T(8,128)(2,1)} %get-tuple-element.61), channel_id=1, source_target_pairs={{0,48},{1,49},{2,50},{3,51},{4,52},{5,53},{6,54},{7,55},{8,56},{9,... | collective-permute-start | bytes 393224 | tf_op jit(solution)/shard_map/ppermute | solution.py:36
  8.3 8.0 %collective-permute-start.3 = (bf16[128,512]{1,0:T(8,128)(2,1)}, bf16[128,512]{1,0:T(8,128)(2,1)S(1)}, u32[]{:S(2)}, u32[]{:S(2)}) collective-permute-start(bf16[128,512]{1,0:T(8,128)(2,1)} %get-tuple-element.55.refs_0_), channel_id=1, source_target_pairs={{0,1},{1,0},{2,3},{3,2},{4,5},{5,4},{6,7},{7,6},{8,9},{9,8},{10,11... | collective-permute-start | bytes 393224 | tf_op jit(solution)/shard_map/ppermute | solution.py:36
  9.8 2.8 %copy-start = (bf16[3,2,512,1024]{3,2,1,0:T(8,128)(2,1)S(1)}, bf16[3,2,512,1024]{3,2,1,0:T(8,128)(2,1)}, u32[]{:S(2)}) copy-start(bf16[3,2,512,1024]{3,2,1,0:T(8,128)(2,1)} %weights.3) | copy-start | bytes 18874372
  12.6 1.8 %copy-start.6 = (bf16[64,512]{1,0:T(8,128)(2,1)S(1)}, bf16[64,512]{1,0:T(8,128)(2,1)}, u32[]{:S(2)}) copy-start(bf16[64,512]{1,0:T(8,128)(2,1)} %get-tuple-element.70) | copy-start | bytes 196612
  12.6 3.7 %copy-start.4 = (bf16[128,512]{1,0:T(8,128)(2,1)S(1)}, bf16[128,512]{1,0:T(8,128)(2,1)}, u32[]{:S(2)}) copy-start(bf16[128,512]{1,0:T(8,128)(2,1)} %get-tuple-element.55.refs_0_) | copy-start | bytes 393220
  12.6 21.9 %copy-start.5 = (bf16[64,512]{1,0:T(8,128)(2,1)S(1)}, bf16[64,512]{1,0:T(8,128)(2,1)}, u32[]{:S(2)}) copy-start(bf16[64,512]{1,0:T(8,128)(2,1)} %get-tuple-element.84.query_own) | copy-start | bytes 196612
  12.6 36.7 %copy-start.3 = (bf16[2,64,1024]{2,1,0:T(8,128)(2,1)S(1)}, bf16[2,64,1024]{2,1,0:T(8,128)(2,1)}, u32[]{:S(2)}) copy-start(bf16[2,64,1024]{2,1,0:T(8,128)(2,1)} %queries.2) | copy-start | bytes 786436
  12.9 3.4 %collective-permute-start.5 = (bf16[128,512]{1,0:T(8,128)(2,1)S(1)}, bf16[128,512]{1,0:T(8,128)(2,1)S(1)}, u32[]{:S(2)}, u32[]{:S(2)}) collective-permute-start(bf16[128,512]{1,0:T(8,128)(2,1)S(1)} %collective-permute-done.1.refs_2_), channel_id=1, source_target_pairs={{0,1},{1,0},{2,3},{3,2},{4,5},{5,4},{6,7},{7,6},{8,9},{9,8},{10,11... | collective-permute-start | bytes 393224 | tf_op jit(solution)/shard_map/ppermute | solution.py:36
  13.0 3.3 %collective-permute-start.4 = (bf16[128,512]{1,0:T(8,128)(2,1)S(1)}, bf16[128,512]{1,0:T(8,128)(2,1)S(1)}, u32[]{:S(2)}, u32[]{:S(2)}) collective-permute-start(bf16[128,512]{1,0:T(8,128)(2,1)S(1)} %collective-permute-done.refs_1_), channel_id=1, source_target_pairs={{0,1},{1,0},{2,3},{3,2},{4,5},{5,4},{6,7},{7,6},{8,9},{9,8},{10,11... | collective-permute-start | bytes 393224 | tf_op jit(solution)/shard_map/ppermute | solution.py:36
  14.3 1.9 %collective-permute-start.6 = (bf16[128,512]{1,0:T(8,128)(2,1)S(1)}, bf16[128,512]{1,0:T(8,128)(2,1)S(1)}, u32[]{:S(2)}, u32[]{:S(2)}) collective-permute-start(bf16[128,512]{1,0:T(8,128)(2,1)S(1)} %collective-permute-done.2.refs_3_), channel_id=1, source_target_pairs={{0,1},{1,0},{2,3},{3,2},{4,5},{5,4},{6,7},{7,6},{8,9},{9,8},{10,11... | collective-permute-start | bytes 393224 | tf_op jit(solution)/shard_map/ppermute | solution.py:36
  14.3 4.4 %collective-permute-start.7 = (bf16[64,512]{1,0:T(8,128)(2,1)S(1)}, bf16[64,512]{1,0:T(8,128)(2,1)S(1)}, u32[]{:S(2)}, u32[]{:S(2)}) collective-permute-start(bf16[64,512]{1,0:T(8,128)(2,1)S(1)} %copy-done.6), channel_id=1, source_target_pairs={{0,48},{1,49},{2,50},{3,51},{4,52},{5,53},{6,54},{7,55},{8,56},{9,... | collective-permute-start | bytes 196616 | tf_op jit(solution)/shard_map/ppermute | solution.py:36
  18.8 11.8 %collective-permute-start.8 = (bf16[128,768]{1,0:T(8,128)(2,1)S(1)}, bf16[128,768]{1,0:T(8,128)(2,1)S(1)}, u32[]{:S(2)}, u32[]{:S(2)}) collective-permute-start(bf16[128,768]{1,0:T(8,128)(2,1)S(1)} %get-tuple-element.72), channel_id=1, source_target_pairs={{0,2},{1,3},{2,4},{3,5},{4,6},{5,7},{6,8},{7,9},{8,10},{9,11},{10,... | collective-permute-start | bytes 589832 | tf_op jit(solution)/shard_map/ppermute | solution.py:36
  20.1 10.5 %collective-permute-start.9 = (bf16[128,768]{1,0:T(8,128)(2,1)S(1)}, bf16[128,768]{1,0:T(8,128)(2,1)S(1)}, u32[]{:S(2)}, u32[]{:S(2)}) collective-permute-start(bf16[128,768]{1,0:T(8,128)(2,1)S(1)} %get-tuple-element.73), channel_id=1, source_target_pairs={{0,14},{1,15},{2,0},{3,1},{4,2},{5,3},{6,4},{7,5},{8,6},{9,7},{10,... | collective-permute-start | bytes 589832 | tf_op jit(solution)/shard_map/ppermute | solution.py:36
  24.2 6.0 %collective-permute-start.10 = (bf16[32,768]{1,0:T(8,128)(2,1)S(1)}, bf16[32,768]{1,0:T(8,128)(2,1)S(1)}, u32[]{:S(2)}, u32[]{:S(2)}) collective-permute-start(bf16[32,768]{1,0:T(8,128)(2,1)S(1)} %get-tuple-element.76), channel_id=1, source_target_pairs={{0,4},{1,5},{2,6},{3,7},{4,8},{5,9},{6,10},{7,11},{8,12},{9,13},{1... | collective-permute-start | bytes 147464 | tf_op jit(solution)/shard_map/ppermute | solution.py:36
  24.2 6.4 %collective-permute-start.11 = (bf16[32,768]{1,0:T(8,128)(2,1)S(1)}, bf16[32,768]{1,0:T(8,128)(2,1)S(1)}, u32[]{:S(2)}, u32[]{:S(2)}) collective-permute-start(bf16[32,768]{1,0:T(8,128)(2,1)S(1)} %get-tuple-element.77), channel_id=1, source_target_pairs={{0,12},{1,13},{2,14},{3,15},{4,0},{5,1},{6,2},{7,3},{8,4},{9,5},{1... | collective-permute-start | bytes 147464 | tf_op jit(solution)/shard_map/ppermute | solution.py:36
  30.7 8.0 %collective-permute-start.12 = (bf16[64,768]{1,0:T(8,128)(2,1)S(1)}, bf16[64,768]{1,0:T(8,128)(2,1)S(1)}, u32[]{:S(2)}, u32[]{:S(2)}) collective-permute-start(bf16[64,768]{1,0:T(8,128)(2,1)S(1)} %get-tuple-element.82), channel_id=1, source_target_pairs={{0,4},{1,5},{2,6},{3,7},{4,8},{5,9},{6,10},{7,11},{8,12},{9,13},{1... | collective-permute-start | bytes 294920 | tf_op jit(solution)/shard_map/ppermute | solution.py:36
  34.4 4.9 %collective-permute-start.13 = (bf16[64,768]{1,0:T(8,128)(2,1)S(1)}, bf16[64,768]{1,0:T(8,128)(2,1)S(1)}, u32[]{:S(2)}, u32[]{:S(2)}) collective-permute-start(bf16[64,768]{1,0:T(8,128)(2,1)S(1)} %get-tuple-element.83), channel_id=1, source_target_pairs={{0,12},{1,13},{2,14},{3,15},{4,0},{5,1},{6,2},{7,3},{8,4},{9,5},{1... | collective-permute-start | bytes 294920 | tf_op jit(solution)/shard_map/ppermute | solution.py:36
  34.4 3.9 %collective-permute-start.14 = (bf16[64,512]{1,0:T(8,128)(2,1)S(1)}, bf16[64,512]{1,0:T(8,128)(2,1)S(1)}, u32[]{:S(2)}, u32[]{:S(2)}) collective-permute-start(bf16[64,512]{1,0:T(8,128)(2,1)S(1)} %copy-done.5), channel_id=1, source_target_pairs={{0,1},{1,0},{2,3},{3,2},{4,5},{5,4},{6,7},{7,6},{8,9},{9,8},{10,11... | collective-permute-start | bytes 196616 | tf_op jit(solution)/shard_map/ppermute | solution.py:36
  37.4 1.3 %collective-permute-start.15 = (bf16[64,512]{1,0:T(8,128)(2,1)S(1)}, bf16[64,512]{1,0:T(8,128)(2,1)S(1)}, u32[]{:S(2)}, u32[]{:S(2)}) collective-permute-start(bf16[64,512]{1,0:T(8,128)(2,1)S(1)} %collective-permute-done.7.query_far), channel_id=1, source_target_pairs={{0,1},{1,0},{2,3},{3,2},{4,5},{5,4},{6,7},{7,6},{8,9},{9,8},{10,11... | collective-permute-start | bytes 196616 | tf_op jit(solution)/shard_map/ppermute | solution.py:36
  39.4 3.6 %collective-permute-start.16 = (bf16[64,768]{1,0:T(8,128)(2,1)S(1)}, bf16[64,768]{1,0:T(8,128)(2,1)S(1)}, u32[]{:S(2)}, u32[]{:S(2)}) collective-permute-start(bf16[64,768]{1,0:T(8,128)(2,1)S(1)} %add_up.1), channel_id=1, source_target_pairs={{0,16},{1,17},{2,18},{3,19},{4,20},{5,21},{6,22},{7,23},{8,24},{9,... | collective-permute-start | bytes 294920 | tf_op jit(solution)/shard_map/ppermute | solution.py:36
  43.0 11.9 %collective-permute-start.17 = (bf16[64,1536]{1,0:T(8,128)(2,1)S(1)}, bf16[64,1536]{1,0:T(8,128)(2,1)S(1)}, u32[]{:S(2)}, u32[]{:S(2)}) collective-permute-start(bf16[64,1536]{1,0:T(8,128)(2,1)S(1)} %pad_maximum_fusion.refs_0_), channel_id=1, source_target_pairs={{0,4},{1,5},{2,6},{3,7},{4,8},{5,9},{6,10},{7,11},{8,12},{9,13},{1... | collective-permute-start | bytes 589832 | tf_op jit(solution)/shard_map/ppermute | solution.py:36
  44.7 10.2 %collective-permute-start.18 = (bf16[64,1536]{1,0:T(8,128)(2,1)S(1)}, bf16[64,1536]{1,0:T(8,128)(2,1)S(1)}, u32[]{:S(2)}, u32[]{:S(2)}) collective-permute-start(bf16[64,1536]{1,0:T(8,128)(2,1)S(1)} %pad_maximum_fusion.refs_0_), channel_id=1, source_target_pairs={{0,12},{1,13},{2,14},{3,15},{4,0},{5,1},{6,2},{7,3},{8,4},{9,5},{1... | collective-permute-start | bytes 589832 | tf_op jit(solution)/shard_map/ppermute | solution.py:36
  46.6 11.1 %collective-permute-start.19 = (bf16[64,1536]{1,0:T(8,128)(2,1)S(1)}, bf16[64,1536]{1,0:T(8,128)(2,1)S(1)}, u32[]{:S(2)}, u32[]{:S(2)}) collective-permute-start(bf16[64,1536]{1,0:T(8,128)(2,1)S(1)} %pad_maximum_fusion.refs_0_), channel_id=1, source_target_pairs={{0,2},{1,3},{2,4},{3,5},{4,6},{5,7},{6,8},{7,9},{8,10},{9,11},{10,... | collective-permute-start | bytes 589832 | tf_op jit(solution)/shard_map/ppermute | solution.py:36
  46.6 11.1 %collective-permute-start.20 = (bf16[64,1536]{1,0:T(8,128)(2,1)S(1)}, bf16[64,1536]{1,0:T(8,128)(2,1)S(1)}, u32[]{:S(2)}, u32[]{:S(2)}) collective-permute-start(bf16[64,1536]{1,0:T(8,128)(2,1)S(1)} %pad_maximum_fusion.refs_0_), channel_id=1, source_target_pairs={{0,14},{1,15},{2,0},{3,1},{4,2},{5,3},{6,4},{7,5},{8,6},{9,7},{10,... | collective-permute-start | bytes 589832 | tf_op jit(solution)/shard_map/ppermute | solution.py:36
  49.3 2.8 %copy-start.1 = (bf16[3,2,512,1024]{3,2,1,0:T(8,128)(2,1)S(1)}, bf16[3,2,512,1024]{3,2,1,0:T(8,128)(2,1)}, u32[]{:S(2)}) copy-start(bf16[3,2,512,1024]{3,2,1,0:T(8,128)(2,1)} %weights.3) | copy-start | bytes 18874372
  52.1 19.9 %copy-start.2 = (bf16[3,2,512,1024]{3,2,1,0:T(8,128)(2,1)S(1)}, bf16[3,2,512,1024]{3,2,1,0:T(8,128)(2,1)}, u32[]{:S(2)}) copy-start(bf16[3,2,512,1024]{3,2,1,0:T(8,128)(2,1)} %weights.3) | copy-start | bytes 18874372
  54.9 9.2 %collective-permute-start.23 = (bf16[64,1536]{1,0:T(8,128)(2,1)S(1)}, bf16[64,1536]{1,0:T(8,128)(2,1)S(1)}, u32[]{:S(2)}, u32[]{:S(2)}) collective-permute-start(bf16[64,1536]{1,0:T(8,128)(2,1)S(1)} %broadcast_select_fusion), channel_id=1, source_target_pairs={{0,4},{1,13},{2,6},{3,15},{4,8},{5,1},{6,10},{7,3},{8,12},{9,5},{1... | collective-permute-start | bytes 589832 | tf_op jit(solution)/shard_map/ppermute | solution.py:36
  55.0 9.1 %collective-permute-start.21 = (bf16[64,1536]{1,0:T(8,128)(2,1)S(1)}, bf16[64,1536]{1,0:T(8,128)(2,1)S(1)}, u32[]{:S(2)}, u32[]{:S(2)}) collective-permute-start(bf16[64,1536]{1,0:T(8,128)(2,1)S(1)} %collective-permute-done.17.refs_3_), channel_id=1, source_target_pairs={{0,2},{1,3},{2,4},{3,5},{4,6},{5,7},{6,8},{7,9},{8,10},{9,11},{10,... | collective-permute-start | bytes 589832 | tf_op jit(solution)/shard_map/ppermute | solution.py:36
  56.2 9.6 %collective-permute-start.22 = (bf16[64,1536]{1,0:T(8,128)(2,1)S(1)}, bf16[64,1536]{1,0:T(8,128)(2,1)S(1)}, u32[]{:S(2)}, u32[]{:S(2)}) collective-permute-start(bf16[64,1536]{1,0:T(8,128)(2,1)S(1)} %collective-permute-done.18.refs_4_), channel_id=1, source_target_pairs={{0,14},{1,15},{2,0},{3,1},{4,2},{5,3},{6,4},{7,5},{8,6},{9,7},{10,... | collective-permute-start | bytes 589832 | tf_op jit(solution)/shard_map/ppermute | solution.py:36
  66.5 8.7 %collective-permute-start.24 = (bf16[512,512]{1,0:T(8,128)(2,1)S(1)}, bf16[512,512]{1,0:T(8,128)(2,1)S(1)}, u32[]{:S(2)}, u32[]{:S(2)}) collective-permute-start(bf16[512,512]{1,0:T(8,128)(2,1)S(1)} %get-tuple-element.98.mine), channel_id=1, source_target_pairs={{0,1},{1,0},{2,3},{3,2},{4,5},{5,4},{6,7},{7,6},{8,9},{9,8},{10,11... | collective-permute-start | bytes 1572872 | tf_op jit(solution)/shard_map/ppermute | solution.py:36
  75.2 3.2 %collective-permute-start.25 = (f32[128,1024]{1,0:T(8,128)S(1)}, f32[128,1024]{1,0:T(8,128)S(1)}, u32[]{:S(2)}, u32[]{:S(2)}) collective-permute-start(f32[128,1024]{1,0:T(8,128)S(1)} %get-tuple-element.99), channel_id=1, source_target_pairs={{0,1},{1,0},{2,3},{3,2},{4,5},{5,4},{6,7},{7,6},{8,9},{9,8},{10,11... | collective-permute-start | bytes 1572872 | tf_op jit(solution)/shard_map/ppermute | solution.py:36
  79.0 4.4 %collective-permute-start.26 = (bf16[64,512]{1,0:T(8,128)(2,1)S(1)}, bf16[64,512]{1,0:T(8,128)(2,1)S(1)}, u32[]{:S(2)}, u32[]{:S(2)}) collective-permute-start(bf16[64,512]{1,0:T(8,128)(2,1)S(1)} %get-tuple-element.102), channel_id=1, source_target_pairs={{0,48},{1,49},{2,50},{3,51},{4,52},{5,53},{6,54},{7,55},{8,56},{9,... | collective-permute-start | bytes 196616 | tf_op jit(solution)/shard_map/ppermute | solution.py:36

commit v9 on v8

--- a/solution.py
+++ b/solution.py
@@ -179,7 +179,7 @@
             pltpu.SemaphoreType.DMA((2, 3)),
             pltpu.SemaphoreType.DMA,
         ],
-        compiler_params=params(12),
+        compiler_params=params(48),
         cost_estimate=cost(12 * tokens * DIM * FF, 7 << 20),
         name="first_block",
     )(queries, weights)

time: 84.5 us -> 84.8 us (level)
  local copies, waits for them, and re-layouts: 5.59 us -> 2.81 us
  starting transfers between devices: 44.7 us -> 46.6 us
    unnamed x14, local copies, waits for them, and re-layouts: 5.59 us -> 2.81 us
    ppermute x27, starting transfers between devices: 44.7 us -> 46.6 us  [move(): return lax.ppermute(array, 'ctx', perm)]
  transfers between devices with their start and end apart: 27 -> 27, of which waited for: 10 -> 10; matrix products, arithmetic and copies ran while one was open for 0% -> 0% of each run, Pallas kernels for 13% -> 14%
where the time goes in v9:
time: 84.8 us; the launch traced here: 84.4 us
  starting transfers between devices  46.6 us (55%)
  waiting for transfers between devices  18.9 us (22%)
  Pallas kernels  15.9 us (19%)
  local copies, waits for them, and re-layouts  2.81 us (3%)
    ppermute x27, starting transfers between devices, move(): return lax.ppermute(array, 'ctx', perm)  46.6 us
    ppermute x27, waiting for transfers between devices, move(): return lax.ppermute(array, 'ctx', perm)  18.9 us
    pallas_call x1, Pallas kernels, first_block(): pl.pallas_call(first_kernel, out_shape=shape(tokens, 2 * DIM), in_specs=[...  3.56 us
    pallas_call x1, Pallas kernels, project(): pl.pallas_call(project_kernel, out_shape=(half, half), in_specs=[VMEM, HB...  3.12 us
    pallas_call x1, Pallas kernels, renew_third(): pl.pallas_call(third_kernel, out_shape=shape(DIM, FF), in_specs=[VMEM, VM...  2.86 us
    unnamed x14, local copies, waits for them, and re-layouts  2.81 us
    pallas_call x1, Pallas kernels, gradient(): pl.pallas_call(gradient_kernel, out_shape=(kept, sent, sent, kept, kept,...  2.12 us
    pallas_call x1, Pallas kernels, prepare(): pl.pallas_call(prepare_kernel, out_shape=(pair, pair, pair, pair, half, h...  1.93 us
  transfers between devices with their start and end apart: 27, of which 10 were waited for; matrix products, arithmetic and copies ran while one was open for 0% of the time, Pallas kernels for 14%

profile of v9, /device:TPU:1, one launch (start us, length us, event | category | flops | bytes accessed | tf_op | source)
XLA Modules:
  0.0 84.4 jit_solution(2826620888601073075)
XLA Ops:
  0.0 1.9 %prepare.1 = (bf16[128,512]{1,0:T(8,128)(2,1)}, bf16[128,512]{1,0:T(8,128)(2,1)}, bf16[128,512]{1,0:T(8,128)(2,1)}, bf16[128,512]{1,0:T(8,128)(2,1)}, bf16[64,512]{1,0:T(8,128)(2,1)}, /*index=5*/bf16[64,512]{1,0:T(8,128)(2,1)}) custom-call(bf16[2,64,1024]{2,1,0:T(8,128)(2,1)} %queries.2, bf16[1,64,1024]{2,1,0:T(8,128)(2,1)} %keys.1, ...), custom_call_target="tpu_custom_call" | custom-call | tf_op jit(solution)/shard_map/prepare/pallas_call | solution.py:129
  1.9 3.7 %collective-permute-start.1 = (bf16[128,512]{1,0:T(8,128)(2,1)}, bf16[128,512]{1,0:T(8,128)(2,1)S(1)}, u32[]{:S(2)}, u32[]{:S(2)}) collective-permute-start(bf16[128,512]{1,0:T(8,128)(2,1)} %get-tuple-element.57), channel_id=1, source_target_pairs={{0,32},{1,33},{2,34},{3,35},{4,36},{5,37},{6,38},{7,39},{8,40},{9,... | collective-permute-start | bytes 393224 | tf_op jit(solution)/shard_map/ppermute | solution.py:36
  5.6 0.3 collective-permute-start
  5.9 2.4 %collective-permute-start.2 = (bf16[128,512]{1,0:T(8,128)(2,1)}, bf16[128,512]{1,0:T(8,128)(2,1)S(1)}, u32[]{:S(2)}, u32[]{:S(2)}) collective-permute-start(bf16[128,512]{1,0:T(8,128)(2,1)} %get-tuple-element.61), channel_id=1, source_target_pairs={{0,48},{1,49},{2,50},{3,51},{4,52},{5,53},{6,54},{7,55},{8,56},{9,... | collective-permute-start | bytes 393224 | tf_op jit(solution)/shard_map/ppermute | solution.py:36
  8.3 1.5 %collective-permute-start.3 = (bf16[128,512]{1,0:T(8,128)(2,1)}, bf16[128,512]{1,0:T(8,128)(2,1)S(1)}, u32[]{:S(2)}, u32[]{:S(2)}) collective-permute-start(bf16[128,512]{1,0:T(8,128)(2,1)} %get-tuple-element.55.refs_0_), channel_id=1, source_target_pairs={{0,1},{1,0},{2,3},{3,2},{4,5},{5,4},{6,7},{7,6},{8,9},{9,8},{10,11... | collective-permute-start | bytes 393224 | tf_op jit(solution)/shard_map/ppermute | solution.py:36
  9.8 2.8 %copy-done = bf16[3,2,512,1024]{3,2,1,0:T(8,128)(2,1)S(1)} copy-done((bf16[3,2,512,1024]{3,2,1,0:T(8,128)(2,1)S(1)}, bf16[3,2,512,1024]{3,2,1,0:T(8,128)(2,1)}, u32[]{:S(2)}) %copy-start) | copy-done | bytes 6291480
  12.6 0.3 load.1.refs_8_
  12.9 0.0 collective-permute-done.1.refs_2_
  12.9 0.1 collective-permute-start.5
  13.0 0.0 collective-permute-done.refs_1_
  13.0 1.3 %collective-permute-start.4 = (bf16[128,512]{1,0:T(8,128)(2,1)S(1)}, bf16[128,512]{1,0:T(8,128)(2,1)S(1)}, u32[]{:S(2)}, u32[]{:S(2)}) collective-permute-start(bf16[128,512]{1,0:T(8,128)(2,1)S(1)} %collective-permute-done.refs_1_), channel_id=1, source_target_pairs={{0,1},{1,0},{2,3},{3,2},{4,5},{5,4},{6,7},{7,6},{8,9},{9,8},{10,11... | collective-permute-start | bytes 393224 | tf_op jit(solution)/shard_map/ppermute | solution.py:36
  14.3 0.0 collective-permute-done.2.refs_3_
  14.3 0.0 collective-permute-start.6
  14.4 1.9 %collective-permute-start.7 = (bf16[64,512]{1,0:T(8,128)(2,1)S(1)}, bf16[64,512]{1,0:T(8,128)(2,1)S(1)}, u32[]{:S(2)}, u32[]{:S(2)}) collective-permute-start(bf16[64,512]{1,0:T(8,128)(2,1)S(1)} %copy-done.4), channel_id=1, source_target_pairs={{0,48},{1,49},{2,50},{3,51},{4,52},{5,53},{6,54},{7,55},{8,56},{9,... | collective-permute-start | bytes 196616 | tf_op jit(solution)/shard_map/ppermute | solution.py:36
  16.3 0.0 slice-start
  16.3 2.1 %gradient.1 = (f32[64,768]{1,0:T(8,128)S(1)}, bf16[128,768]{1,0:T(8,128)(2,1)S(1)}, bf16[128,768]{1,0:T(8,128)(2,1)S(1)}, f32[64,768]{1,0:T(8,128)S(1)}, f32[64,...) custom-call(bf16[128,512]{1,0:T(8,128)(2,1)S(1)} %copy-done.2, ...), custom_call_target="tpu_custom_call" | custom-call | flops 1342177280 | bytes 6291456 | tf_op jit(solution)/shard_map/gradient/pallas_call | solution.py:260
  18.4 0.3 collective-permute-done.7.query_far
  18.8 1.4 %collective-permute-start.8 = (bf16[128,768]{1,0:T(8,128)(2,1)S(1)}, bf16[128,768]{1,0:T(8,128)(2,1)S(1)}, u32[]{:S(2)}, u32[]{:S(2)}) collective-permute-start(bf16[128,768]{1,0:T(8,128)(2,1)S(1)} %get-tuple-element.72), channel_id=1, source_target_pairs={{0,2},{1,3},{2,4},{3,5},{4,6},{5,7},{6,8},{7,9},{8,10},{9,11},{10,... | collective-permute-start | bytes 589832 | tf_op jit(solution)/shard_map/ppermute | solution.py:36
  20.2 4.0 %collective-permute-start.9 = (bf16[128,768]{1,0:T(8,128)(2,1)S(1)}, bf16[128,768]{1,0:T(8,128)(2,1)S(1)}, u32[]{:S(2)}, u32[]{:S(2)}) collective-permute-start(bf16[128,768]{1,0:T(8,128)(2,1)S(1)} %get-tuple-element.73), channel_id=1, source_target_pairs={{0,14},{1,15},{2,0},{3,1},{4,2},{5,3},{6,4},{7,5},{8,6},{9,7},{10,... | collective-permute-start | bytes 589832 | tf_op jit(solution)/shard_map/ppermute | solution.py:36
  24.2 3.6 %collective-permute-start.11 = (bf16[32,768]{1,0:T(8,128)(2,1)S(1)}, bf16[32,768]{1,0:T(8,128)(2,1)S(1)}, u32[]{:S(2)}, u32[]{:S(2)}) collective-permute-start(bf16[32,768]{1,0:T(8,128)(2,1)S(1)} %get-tuple-element.77), channel_id=1, source_target_pairs={{0,12},{1,13},{2,14},{3,15},{4,0},{5,1},{6,2},{7,3},{8,4},{9,5},{1... | collective-permute-start | bytes 147464 | tf_op jit(solution)/shard_map/ppermute | solution.py:36
  27.8 2.4 %collective-permute-done.10.far_up = bf16[32,768]{1,0:T(8,128)(2,1)S(1)} collective-permute-done((bf16[32,768]{1,0:T(8,128)(2,1)S(1)}, bf16[32,768]{1,0:T(8,128)(2,1)S(1)}, u32[]{:S(2)}, u32[]{:S(2)}) %collective-permute-start.10) | collective-permute-done | bytes 49184 | tf_op jit(solution)/shard_map/ppermute | solution.py:36
  30.2 0.4 collective-permute-done.11.far_down
  30.7 3.8 %collective-permute-start.12 = (bf16[64,768]{1,0:T(8,128)(2,1)S(1)}, bf16[64,768]{1,0:T(8,128)(2,1)S(1)}, u32[]{:S(2)}, u32[]{:S(2)}) collective-permute-start(bf16[64,768]{1,0:T(8,128)(2,1)S(1)} %get-tuple-element.82), channel_id=1, source_target_pairs={{0,4},{1,5},{2,6},{3,7},{4,8},{5,9},{6,10},{7,11},{8,12},{9,13},{1... | collective-permute-start | bytes 294920 | tf_op jit(solution)/shard_map/ppermute | solution.py:36
  34.5 3.0 %collective-permute-start.14 = (bf16[64,512]{1,0:T(8,128)(2,1)S(1)}, bf16[64,512]{1,0:T(8,128)(2,1)S(1)}, u32[]{:S(2)}, u32[]{:S(2)}) collective-permute-start(bf16[64,512]{1,0:T(8,128)(2,1)S(1)} %copy-done.3), channel_id=1, source_target_pairs={{0,1},{1,0},{2,3},{3,2},{4,5},{5,4},{6,7},{7,6},{8,9},{9,8},{10,11... | collective-permute-start | bytes 196616 | tf_op jit(solution)/shard_map/ppermute | solution.py:36
  37.4 0.0 collective-permute-start.15
  37.4 0.9 %collective-permute-done.14.query_core = bf16[64,512]{1,0:T(8,128)(2,1)S(1)} collective-permute-done((bf16[64,512]{1,0:T(8,128)(2,1)S(1)}, bf16[64,512]{1,0:T(8,128)(2,1)S(1)}, u32[]{:S(2)}, u32[]{:S(2)}) %collective-permute-start.14) | collective-permute-done | bytes 65568 | tf_op jit(solution)/shard_map/ppermute | solution.py:36
  38.3 0.4 collective-permute-done.15.query_far_core
  38.7 0.7 collective-permute-done.13.d
  39.4 0.1 add_up.1
  39.4 0.1 collective-permute-start.16
  39.5 3.5 %collective-permute-done.16 = bf16[64,768]{1,0:T(8,128)(2,1)S(1)} collective-permute-done((bf16[64,768]{1,0:T(8,128)(2,1)S(1)}, bf16[64,768]{1,0:T(8,128)(2,1)S(1)}, u32[]{:S(2)}, u32[]{:S(2)}) %collective-permute-start.16) | collective-permute-done | bytes 98336 | tf_op jit(solution)/shard_map/ppermute | solution.py:36
  43.0 1.7 %collective-permute-start.17 = (bf16[64,1536]{1,0:T(8,128)(2,1)S(1)}, bf16[64,1536]{1,0:T(8,128)(2,1)S(1)}, u32[]{:S(2)}, u32[]{:S(2)}) collective-permute-start(bf16[64,1536]{1,0:T(8,128)(2,1)S(1)} %pad_maximum_fusion.refs_0_), channel_id=1, source_target_pairs={{0,4},{1,5},{2,6},{3,7},{4,8},{5,9},{6,10},{7,11},{8,12},{9,13},{1... | collective-permute-start | bytes 589832 | tf_op jit(solution)/shard_map/ppermute | solution.py:36
  44.7 2.0 %collective-permute-start.18 = (bf16[64,1536]{1,0:T(8,128)(2,1)S(1)}, bf16[64,1536]{1,0:T(8,128)(2,1)S(1)}, u32[]{:S(2)}, u32[]{:S(2)}) collective-permute-start(bf16[64,1536]{1,0:T(8,128)(2,1)S(1)} %pad_maximum_fusion.refs_0_), channel_id=1, source_target_pairs={{0,12},{1,13},{2,14},{3,15},{4,0},{5,1},{6,2},{7,3},{8,4},{9,5},{1... | collective-permute-start | bytes 589832 | tf_op jit(solution)/shard_map/ppermute | solution.py:36
  46.7 2.7 %collective-permute-start.20 = (bf16[64,1536]{1,0:T(8,128)(2,1)S(1)}, bf16[64,1536]{1,0:T(8,128)(2,1)S(1)}, u32[]{:S(2)}, u32[]{:S(2)}) collective-permute-start(bf16[64,1536]{1,0:T(8,128)(2,1)S(1)} %pad_maximum_fusion.refs_0_), channel_id=1, source_target_pairs={{0,14},{1,15},{2,0},{3,1},{4,2},{5,3},{6,4},{7,5},{8,6},{9,7},{10,... | collective-permute-start | bytes 589832 | tf_op jit(solution)/shard_map/ppermute | solution.py:36
  49.4 3.6 %first_block.1.first_out = bf16[64,1024]{1,0:T(8,128)(2,1)S(1)} custom-call(bf16[2,64,1024]{2,1,0:T(8,128)(2,1)S(1)} %copy-done.1, bf16[3,2,512,1024]{3,2,1,0:T(8,128)(2,1)} %weights.3), custom_call_target="tpu_custom_call" | custom-call | flops 402653184 | bytes 7340032 | tf_op jit(solution)/shard_map/first_block/pallas_call | solution.py:171
  53.0 1.6 %collective-permute-start.23 = (bf16[64,1536]{1,0:T(8,128)(2,1)S(1)}, bf16[64,1536]{1,0:T(8,128)(2,1)S(1)}, u32[]{:S(2)}, u32[]{:S(2)}) collective-permute-start(bf16[64,1536]{1,0:T(8,128)(2,1)S(1)} %broadcast_select_fusion), channel_id=1, source_target_pairs={{0,4},{1,13},{2,6},{3,15},{4,8},{5,1},{6,10},{7,3},{8,12},{9,5},{1... | collective-permute-start | bytes 589832 | tf_op jit(solution)/shard_map/ppermute | solution.py:36
  54.6 2.7 %collective-permute-start.22 = (bf16[64,1536]{1,0:T(8,128)(2,1)S(1)}, bf16[64,1536]{1,0:T(8,128)(2,1)S(1)}, u32[]{:S(2)}, u32[]{:S(2)}) collective-permute-start(bf16[64,1536]{1,0:T(8,128)(2,1)S(1)} %collective-permute-done.18.refs_4_), channel_id=1, source_target_pairs={{0,14},{1,15},{2,0},{3,1},{4,2},{5,3},{6,4},{7,5},{8,6},{9,7},{10,... | collective-permute-start | bytes 589832 | tf_op jit(solution)/shard_map/ppermute | solution.py:36
  57.2 5.5 %collective-permute-done.23.refs_7_ = bf16[64,1536]{1,0:T(8,128)(2,1)S(1)} collective-permute-done((bf16[64,1536]{1,0:T(8,128)(2,1)S(1)}, bf16[64,1536]{1,0:T(8,128)(2,1)S(1)}, u32[]{:S(2)}, u32[]{:S(2)}) %collective-permute-start.23) | collective-permute-done | bytes 196640 | tf_op jit(solution)/shard_map/ppermute | solution.py:36
  62.7 3.1 %collective-permute-done.22.refs_6_ = bf16[64,1536]{1,0:T(8,128)(2,1)S(1)} collective-permute-done((bf16[64,1536]{1,0:T(8,128)(2,1)S(1)}, bf16[64,1536]{1,0:T(8,128)(2,1)S(1)}, u32[]{:S(2)}, u32[]{:S(2)}) %collective-permute-start.22) | collective-permute-done | bytes 196640 | tf_op jit(solution)/shard_map/ppermute | solution.py:36
  65.8 0.6 pack.1
  66.5 5.8 %collective-permute-start.24 = (bf16[512,512]{1,0:T(8,128)(2,1)S(1)}, bf16[512,512]{1,0:T(8,128)(2,1)S(1)}, u32[]{:S(2)}, u32[]{:S(2)}) collective-permute-start(bf16[512,512]{1,0:T(8,128)(2,1)S(1)} %get-tuple-element.98.mine), channel_id=1, source_target_pairs={{0,1},{1,0},{2,3},{3,2},{4,5},{5,4},{6,7},{7,6},{8,9},{9,8},{10,11... | collective-permute-start | bytes 1572872 | tf_op jit(solution)/shard_map/ppermute | solution.py:36
  72.3 3.1 %project.1 = (f32[128,1024]{1,0:T(8,128)S(1)}, f32[128,1024]{1,0:T(8,128)S(1)}) custom-call(bf16[512,1024]{1,0:T(8,128)(2,1)S(1)} %get-tuple-element.93.scaled, bf16[3,2,512,1024]{3,2,1,0:T(8,128)(2,1)S(1)} %bitcast.1, bf16[64,512]{1,0:T(8,128)(2,1)S(1)} %copy-done.3, bf16[64,512]{1,0:T(8,128)(2,1)S(1)} %collective-permute-done.7.query_far, ...), custom_call_target="tpu_custom_call" | custom-call | flops 2200000000 | bytes 5242880 | tf_op jit(solution)/shard_map/project/pallas_call | solution.py:426
  75.4 0.4 collective-permute-start.25
  75.8 2.9 %renew_third.1.weights = bf16[512,1024]{1,0:T(8,128)(2,1)S(1)} custom-call(bf16[512,512]{1,0:T(8,128)(2,1)S(1)} %get-tuple-element.98.mine, bf16[512,512]{1,0:T(8,128)(2,1)S(1)} %collective-permute-done.24.other, bf16[3,2,512,1024]{3,2,1,0:T(8,128)(2,1)S(1)} %bitcast.1), custom_call_target="tpu_custom_call" | custom-call | flops 1900000000 | bytes 4194304 | tf_op jit(solution)/shard_map/renew_third/pallas_call | solution.py:458
  78.7 0.6 down.1
  79.3 2.8 %collective-permute-start.26 = (bf16[64,512]{1,0:T(8,128)(2,1)S(1)}, bf16[64,512]{1,0:T(8,128)(2,1)S(1)}, u32[]{:S(2)}, u32[]{:S(2)}) collective-permute-start(bf16[64,512]{1,0:T(8,128)(2,1)S(1)} %get-tuple-element.102), channel_id=1, source_target_pairs={{0,48},{1,49},{2,50},{3,51},{4,52},{5,53},{6,54},{7,55},{8,56},{9,... | collective-permute-start | bytes 196616 | tf_op jit(solution)/shard_map/ppermute | solution.py:36
  82.0 1.7 %collective-permute-done.26.far = bf16[64,512]{1,0:T(8,128)(2,1)S(1)} collective-permute-done((bf16[64,512]{1,0:T(8,128)(2,1)S(1)}, bf16[64,512]{1,0:T(8,128)(2,1)S(1)}, u32[]{:S(2)}, u32[]{:S(2)}) %collective-permute-start.26) | collective-permute-done | bytes 65568 | tf_op jit(solution)/shard_map/ppermute | solution.py:36
  83.7 0.7 finish.1
  (34 shorter events, 0.2 us)
Async XLA Ops:
  1.9 10.9 %collective-permute-start.1 = (bf16[128,512]{1,0:T(8,128)(2,1)}, bf16[128,512]{1,0:T(8,128)(2,1)S(1)}, u32[]{:S(2)}, u32[]{:S(2)}) collective-permute-start(bf16[128,512]{1,0:T(8,128)(2,1)} %get-tuple-element.57), channel_id=1, source_target_pairs={{0,32},{1,33},{2,34},{3,35},{4,36},{5,37},{6,38},{7,39},{8,40},{9,... | collective-permute-start | bytes 393224 | tf_op jit(solution)/shard_map/ppermute | solution.py:36
  5.6 7.4 %collective-permute-start = (bf16[128,512]{1,0:T(8,128)(2,1)}, bf16[128,512]{1,0:T(8,128)(2,1)S(1)}, u32[]{:S(2)}, u32[]{:S(2)}) collective-permute-start(bf16[128,512]{1,0:T(8,128)(2,1)} %get-tuple-element.56), channel_id=1, source_target_pairs={{0,16},{1,17},{2,18},{3,19},{4,20},{5,21},{6,22},{7,23},{8,24},{9,... | collective-permute-start | bytes 393224 | tf_op jit(solution)/shard_map/ppermute | solution.py:36
  5.9 8.4 %collective-permute-start.2 = (bf16[128,512]{1,0:T(8,128)(2,1)}, bf16[128,512]{1,0:T(8,128)(2,1)S(1)}, u32[]{:S(2)}, u32[]{:S(2)}) collective-permute-start(bf16[128,512]{1,0:T(8,128)(2,1)} %get-tuple-element.61), channel_id=1, source_target_pairs={{0,48},{1,49},{2,50},{3,51},{4,52},{5,53},{6,54},{7,55},{8,56},{9,... | collective-permute-start | bytes 393224 | tf_op jit(solution)/shard_map/ppermute | solution.py:36
  8.3 8.0 %collective-permute-start.3 = (bf16[128,512]{1,0:T(8,128)(2,1)}, bf16[128,512]{1,0:T(8,128)(2,1)S(1)}, u32[]{:S(2)}, u32[]{:S(2)}) collective-permute-start(bf16[128,512]{1,0:T(8,128)(2,1)} %get-tuple-element.55.refs_0_), channel_id=1, source_target_pairs={{0,1},{1,0},{2,3},{3,2},{4,5},{5,4},{6,7},{7,6},{8,9},{9,8},{10,11... | collective-permute-start | bytes 393224 | tf_op jit(solution)/shard_map/ppermute | solution.py:36
  9.8 2.8 %copy-start = (bf16[3,2,512,1024]{3,2,1,0:T(8,128)(2,1)S(1)}, bf16[3,2,512,1024]{3,2,1,0:T(8,128)(2,1)}, u32[]{:S(2)}) copy-start(bf16[3,2,512,1024]{3,2,1,0:T(8,128)(2,1)} %weights.3) | copy-start | bytes 18874372
  12.6 1.8 %copy-start.4 = (bf16[64,512]{1,0:T(8,128)(2,1)S(1)}, bf16[64,512]{1,0:T(8,128)(2,1)}, u32[]{:S(2)}) copy-start(bf16[64,512]{1,0:T(8,128)(2,1)} %get-tuple-element.70) | copy-start | bytes 196612
  12.6 3.7 %copy-start.2 = (bf16[128,512]{1,0:T(8,128)(2,1)S(1)}, bf16[128,512]{1,0:T(8,128)(2,1)}, u32[]{:S(2)}) copy-start(bf16[128,512]{1,0:T(8,128)(2,1)} %get-tuple-element.55.refs_0_) | copy-start | bytes 393220
  12.6 21.9 %copy-start.3 = (bf16[64,512]{1,0:T(8,128)(2,1)S(1)}, bf16[64,512]{1,0:T(8,128)(2,1)}, u32[]{:S(2)}) copy-start(bf16[64,512]{1,0:T(8,128)(2,1)} %get-tuple-element.84.query_own) | copy-start | bytes 196612
  12.6 36.8 %copy-start.1 = (bf16[2,64,1024]{2,1,0:T(8,128)(2,1)S(1)}, bf16[2,64,1024]{2,1,0:T(8,128)(2,1)}, u32[]{:S(2)}) copy-start(bf16[2,64,1024]{2,1,0:T(8,128)(2,1)} %queries.2) | copy-start | bytes 786436
  12.9 3.4 %collective-permute-start.5 = (bf16[128,512]{1,0:T(8,128)(2,1)S(1)}, bf16[128,512]{1,0:T(8,128)(2,1)S(1)}, u32[]{:S(2)}, u32[]{:S(2)}) collective-permute-start(bf16[128,512]{1,0:T(8,128)(2,1)S(1)} %collective-permute-done.1.refs_2_), channel_id=1, source_target_pairs={{0,1},{1,0},{2,3},{3,2},{4,5},{5,4},{6,7},{7,6},{8,9},{9,8},{10,11... | collective-permute-start | bytes 393224 | tf_op jit(solution)/shard_map/ppermute | solution.py:36
  13.0 3.3 %collective-permute-start.4 = (bf16[128,512]{1,0:T(8,128)(2,1)S(1)}, bf16[128,512]{1,0:T(8,128)(2,1)S(1)}, u32[]{:S(2)}, u32[]{:S(2)}) collective-permute-start(bf16[128,512]{1,0:T(8,128)(2,1)S(1)} %collective-permute-done.refs_1_), channel_id=1, source_target_pairs={{0,1},{1,0},{2,3},{3,2},{4,5},{5,4},{6,7},{7,6},{8,9},{9,8},{10,11... | collective-permute-start | bytes 393224 | tf_op jit(solution)/shard_map/ppermute | solution.py:36
  14.3 1.9 %collective-permute-start.6 = (bf16[128,512]{1,0:T(8,128)(2,1)S(1)}, bf16[128,512]{1,0:T(8,128)(2,1)S(1)}, u32[]{:S(2)}, u32[]{:S(2)}) collective-permute-start(bf16[128,512]{1,0:T(8,128)(2,1)S(1)} %collective-permute-done.2.refs_3_), channel_id=1, source_target_pairs={{0,1},{1,0},{2,3},{3,2},{4,5},{5,4},{6,7},{7,6},{8,9},{9,8},{10,11... | collective-permute-start | bytes 393224 | tf_op jit(solution)/shard_map/ppermute | solution.py:36
  14.4 4.4 %collective-permute-start.7 = (bf16[64,512]{1,0:T(8,128)(2,1)S(1)}, bf16[64,512]{1,0:T(8,128)(2,1)S(1)}, u32[]{:S(2)}, u32[]{:S(2)}) collective-permute-start(bf16[64,512]{1,0:T(8,128)(2,1)S(1)} %copy-done.4), channel_id=1, source_target_pairs={{0,48},{1,49},{2,50},{3,51},{4,52},{5,53},{6,54},{7,55},{8,56},{9,... | collective-permute-start | bytes 196616 | tf_op jit(solution)/shard_map/ppermute | solution.py:36
  16.3 56.0 %slice-start = ((s8[6291456]{0:T(1024)(128)(4,1)}), s8[2097152]{0:T(1024)(128)(4,1)S(1)}, s32[]{:S(2)}) async-start(s8[6291456]{0:T(1024)(128)(4,1)} %bitcast), calls=%async_computation | async-start | bytes 4194304
  18.8 11.9 %collective-permute-start.8 = (bf16[128,768]{1,0:T(8,128)(2,1)S(1)}, bf16[128,768]{1,0:T(8,128)(2,1)S(1)}, u32[]{:S(2)}, u32[]{:S(2)}) collective-permute-start(bf16[128,768]{1,0:T(8,128)(2,1)S(1)} %get-tuple-element.72), channel_id=1, source_target_pairs={{0,2},{1,3},{2,4},{3,5},{4,6},{5,7},{6,8},{7,9},{8,10},{9,11},{10,... | collective-permute-start | bytes 589832 | tf_op jit(solution)/shard_map/ppermute | solution.py:36
  20.2 10.5 %collective-permute-start.9 = (bf16[128,768]{1,0:T(8,128)(2,1)S(1)}, bf16[128,768]{1,0:T(8,128)(2,1)S(1)}, u32[]{:S(2)}, u32[]{:S(2)}) collective-permute-start(bf16[128,768]{1,0:T(8,128)(2,1)S(1)} %get-tuple-element.73), channel_id=1, source_target_pairs={{0,14},{1,15},{2,0},{3,1},{4,2},{5,3},{6,4},{7,5},{8,6},{9,7},{10,... | collective-permute-start | bytes 589832 | tf_op jit(solution)/shard_map/ppermute | solution.py:36
  24.2 6.0 %collective-permute-start.10 = (bf16[32,768]{1,0:T(8,128)(2,1)S(1)}, bf16[32,768]{1,0:T(8,128)(2,1)S(1)}, u32[]{:S(2)}, u32[]{:S(2)}) collective-permute-start(bf16[32,768]{1,0:T(8,128)(2,1)S(1)} %get-tuple-element.76), channel_id=1, source_target_pairs={{0,4},{1,5},{2,6},{3,7},{4,8},{5,9},{6,10},{7,11},{8,12},{9,13},{1... | collective-permute-start | bytes 147464 | tf_op jit(solution)/shard_map/ppermute | solution.py:36
  24.2 6.4 %collective-permute-start.11 = (bf16[32,768]{1,0:T(8,128)(2,1)S(1)}, bf16[32,768]{1,0:T(8,128)(2,1)S(1)}, u32[]{:S(2)}, u32[]{:S(2)}) collective-permute-start(bf16[32,768]{1,0:T(8,128)(2,1)S(1)} %get-tuple-element.77), channel_id=1, source_target_pairs={{0,12},{1,13},{2,14},{3,15},{4,0},{5,1},{6,2},{7,3},{8,4},{9,5},{1... | collective-permute-start | bytes 147464 | tf_op jit(solution)/shard_map/ppermute | solution.py:36
  30.7 8.0 %collective-permute-start.12 = (bf16[64,768]{1,0:T(8,128)(2,1)S(1)}, bf16[64,768]{1,0:T(8,128)(2,1)S(1)}, u32[]{:S(2)}, u32[]{:S(2)}) collective-permute-start(bf16[64,768]{1,0:T(8,128)(2,1)S(1)} %get-tuple-element.82), channel_id=1, source_target_pairs={{0,4},{1,5},{2,6},{3,7},{4,8},{5,9},{6,10},{7,11},{8,12},{9,13},{1... | collective-permute-start | bytes 294920 | tf_op jit(solution)/shard_map/ppermute | solution.py:36
  34.5 4.9 %collective-permute-start.13 = (bf16[64,768]{1,0:T(8,128)(2,1)S(1)}, bf16[64,768]{1,0:T(8,128)(2,1)S(1)}, u32[]{:S(2)}, u32[]{:S(2)}) collective-permute-start(bf16[64,768]{1,0:T(8,128)(2,1)S(1)} %get-tuple-element.83), channel_id=1, source_target_pairs={{0,12},{1,13},{2,14},{3,15},{4,0},{5,1},{6,2},{7,3},{8,4},{9,5},{1... | collective-permute-start | bytes 294920 | tf_op jit(solution)/shard_map/ppermute | solution.py:36
  34.5 3.9 %collective-permute-start.14 = (bf16[64,512]{1,0:T(8,128)(2,1)S(1)}, bf16[64,512]{1,0:T(8,128)(2,1)S(1)}, u32[]{:S(2)}, u32[]{:S(2)}) collective-permute-start(bf16[64,512]{1,0:T(8,128)(2,1)S(1)} %copy-done.3), channel_id=1, source_target_pairs={{0,1},{1,0},{2,3},{3,2},{4,5},{5,4},{6,7},{7,6},{8,9},{9,8},{10,11... | collective-permute-start | bytes 196616 | tf_op jit(solution)/shard_map/ppermute | solution.py:36
  37.4 1.3 %collective-permute-start.15 = (bf16[64,512]{1,0:T(8,128)(2,1)S(1)}, bf16[64,512]{1,0:T(8,128)(2,1)S(1)}, u32[]{:S(2)}, u32[]{:S(2)}) collective-permute-start(bf16[64,512]{1,0:T(8,128)(2,1)S(1)} %collective-permute-done.7.query_far), channel_id=1, source_target_pairs={{0,1},{1,0},{2,3},{3,2},{4,5},{5,4},{6,7},{7,6},{8,9},{9,8},{10,11... | collective-permute-start | bytes 196616 | tf_op jit(solution)/shard_map/ppermute | solution.py:36
  39.4 3.6 %collective-permute-start.16 = (bf16[64,768]{1,0:T(8,128)(2,1)S(1)}, bf16[64,768]{1,0:T(8,128)(2,1)S(1)}, u32[]{:S(2)}, u32[]{:S(2)}) collective-permute-start(bf16[64,768]{1,0:T(8,128)(2,1)S(1)} %add_up.1), channel_id=1, source_target_pairs={{0,16},{1,17},{2,18},{3,19},{4,20},{5,21},{6,22},{7,23},{8,24},{9,... | collective-permute-start | bytes 294920 | tf_op jit(solution)/shard_map/ppermute | solution.py:36
  43.0 9.9 %collective-permute-start.17 = (bf16[64,1536]{1,0:T(8,128)(2,1)S(1)}, bf16[64,1536]{1,0:T(8,128)(2,1)S(1)}, u32[]{:S(2)}, u32[]{:S(2)}) collective-permute-start(bf16[64,1536]{1,0:T(8,128)(2,1)S(1)} %pad_maximum_fusion.refs_0_), channel_id=1, source_target_pairs={{0,4},{1,5},{2,6},{3,7},{4,8},{5,9},{6,10},{7,11},{8,12},{9,13},{1... | collective-permute-start | bytes 589832 | tf_op jit(solution)/shard_map/ppermute | solution.py:36
  44.7 8.2 %collective-permute-start.18 = (bf16[64,1536]{1,0:T(8,128)(2,1)S(1)}, bf16[64,1536]{1,0:T(8,128)(2,1)S(1)}, u32[]{:S(2)}, u32[]{:S(2)}) collective-permute-start(bf16[64,1536]{1,0:T(8,128)(2,1)S(1)} %pad_maximum_fusion.refs_0_), channel_id=1, source_target_pairs={{0,12},{1,13},{2,14},{3,15},{4,0},{5,1},{6,2},{7,3},{8,4},{9,5},{1... | collective-permute-start | bytes 589832 | tf_op jit(solution)/shard_map/ppermute | solution.py:36
  46.7 25.6 %slice-start.1 = ((s8[6291456]{0:T(1024)(128)(4,1)}), s8[4194304]{0:T(1024)(128)(4,1)S(1)}, s32[]{:S(2)}) async-start(s8[6291456]{0:T(1024)(128)(4,1)} %bitcast), calls=%async_computation.1 | async-start | bytes 8388608
  46.7 10.6 %collective-permute-start.19 = (bf16[64,1536]{1,0:T(8,128)(2,1)S(1)}, bf16[64,1536]{1,0:T(8,128)(2,1)S(1)}, u32[]{:S(2)}, u32[]{:S(2)}) collective-permute-start(bf16[64,1536]{1,0:T(8,128)(2,1)S(1)} %pad_maximum_fusion.refs_0_), channel_id=1, source_target_pairs={{0,2},{1,3},{2,4},{3,5},{4,6},{5,7},{6,8},{7,9},{8,10},{9,11},{10,... | collective-permute-start | bytes 589832 | tf_op jit(solution)/shard_map/ppermute | solution.py:36
  46.7 10.6 %collective-permute-start.20 = (bf16[64,1536]{1,0:T(8,128)(2,1)S(1)}, bf16[64,1536]{1,0:T(8,128)(2,1)S(1)}, u32[]{:S(2)}, u32[]{:S(2)}) collective-permute-start(bf16[64,1536]{1,0:T(8,128)(2,1)S(1)} %pad_maximum_fusion.refs_0_), channel_id=1, source_target_pairs={{0,14},{1,15},{2,0},{3,1},{4,2},{5,3},{6,4},{7,5},{8,6},{9,7},{10,... | collective-permute-start | bytes 589832 | tf_op jit(solution)/shard_map/ppermute | solution.py:36
  53.0 9.7 %collective-permute-start.23 = (bf16[64,1536]{1,0:T(8,128)(2,1)S(1)}, bf16[64,1536]{1,0:T(8,128)(2,1)S(1)}, u32[]{:S(2)}, u32[]{:S(2)}) collective-permute-start(bf16[64,1536]{1,0:T(8,128)(2,1)S(1)} %broadcast_select_fusion), channel_id=1, source_target_pairs={{0,4},{1,13},{2,6},{3,15},{4,8},{5,1},{6,10},{7,3},{8,12},{9,5},{1... | collective-permute-start | bytes 589832 | tf_op jit(solution)/shard_map/ppermute | solution.py:36
  54.6 8.2 %collective-permute-start.21 = (bf16[64,1536]{1,0:T(8,128)(2,1)S(1)}, bf16[64,1536]{1,0:T(8,128)(2,1)S(1)}, u32[]{:S(2)}, u32[]{:S(2)}) collective-permute-start(bf16[64,1536]{1,0:T(8,128)(2,1)S(1)} %collective-permute-done.17.refs_3_), channel_id=1, source_target_pairs={{0,2},{1,3},{2,4},{3,5},{4,6},{5,7},{6,8},{7,9},{8,10},{9,11},{10,... | collective-permute-start | bytes 589832 | tf_op jit(solution)/shard_map/ppermute | solution.py:36
  54.6 11.3 %collective-permute-start.22 = (bf16[64,1536]{1,0:T(8,128)(2,1)S(1)}, bf16[64,1536]{1,0:T(8,128)(2,1)S(1)}, u32[]{:S(2)}, u32[]{:S(2)}) collective-permute-start(bf16[64,1536]{1,0:T(8,128)(2,1)S(1)} %collective-permute-done.18.refs_4_), channel_id=1, source_target_pairs={{0,14},{1,15},{2,0},{3,1},{4,2},{5,3},{6,4},{7,5},{8,6},{9,7},{10,... | collective-permute-start | bytes 589832 | tf_op jit(solution)/shard_map/ppermute | solution.py:36
  66.5 8.9 %collective-permute-start.24 = (bf16[512,512]{1,0:T(8,128)(2,1)S(1)}, bf16[512,512]{1,0:T(8,128)(2,1)S(1)}, u32[]{:S(2)}, u32[]{:S(2)}) collective-permute-start(bf16[512,512]{1,0:T(8,128)(2,1)S(1)} %get-tuple-element.98.mine), channel_id=1, source_target_pairs={{0,1},{1,0},{2,3},{3,2},{4,5},{5,4},{6,7},{7,6},{8,9},{9,8},{10,11... | collective-permute-start | bytes 1572872 | tf_op jit(solution)/shard_map/ppermute | solution.py:36
  75.4 3.2 %collective-permute-start.25 = (f32[128,1024]{1,0:T(8,128)S(1)}, f32[128,1024]{1,0:T(8,128)S(1)}, u32[]{:S(2)}, u32[]{:S(2)}) collective-permute-start(f32[128,1024]{1,0:T(8,128)S(1)} %get-tuple-element.99), channel_id=1, source_target_pairs={{0,1},{1,0},{2,3},{3,2},{4,5},{5,4},{6,7},{7,6},{8,9},{9,8},{10,11... | collective-permute-start | bytes 1572872 | tf_op jit(solution)/shard_map/ppermute | solution.py:36
  79.3 4.4 %collective-permute-start.26 = (bf16[64,512]{1,0:T(8,128)(2,1)S(1)}, bf16[64,512]{1,0:T(8,128)(2,1)S(1)}, u32[]{:S(2)}, u32[]{:S(2)}) collective-permute-start(bf16[64,512]{1,0:T(8,128)(2,1)S(1)} %get-tuple-element.102), channel_id=1, source_target_pairs={{0,48},{1,49},{2,50},{3,51},{4,52},{5,53},{6,54},{7,55},{8,56},{9,... | collective-permute-start | bytes 196616 | tf_op jit(solution)/shard_map/ppermute | solution.py:36
